TPU v7x, 32 devices: a whole 2x2x4 slice. The times are simulated.
32 devices in a mesh: grp: 4 (over z), dp: 8 (over y, x, core).
Axes of the slice: x: 2, y: 2, z: 4, core: 2. Of those that a mesh axis runs over, the one named last changes fastest.
Arguments:
- hidden: bfloat16 [8, 4, 320, 2048], P('dp', 'grp'), may hold values from -6 to 6
- cotangent: bfloat16 [8, 4, 320, 2048], P('dp', 'grp'), may hold values from -6 to 6
- segment_ids: int32 [8, 1024], P('dp'), may hold values from 0 to 3, never falling along the last dimension, each value on 1 to 512 neighbouring positions
- continuation_prompt: int32 [8, 4], P('dp', 'grp'), may hold values from 0 to 3
- gain_master: float32 [2, 2048], P(None, ('grp', 'dp')), may hold values from 0.5 to 1.5
- gain_first: float32 [2, 2048], P(None, ('grp', 'dp')), may hold values from -96 to 96
- gain_second: float32 [2, 2048], P(None, ('grp', 'dp')), may hold values from 100 to 10000
- attention_master: float32 [2048, 4096], P(('grp', 'dp')), may hold values from -0.125 to 0.125
- attention_first: float32 [2048, 4096], P(('grp', 'dp')), may hold values from -80 to 80
- attention_second: float32 [2048, 4096], P(('grp', 'dp')), may hold values from 80 to 8000
- merge_master: float32 [2048, 2048], P(('grp', 'dp')), may hold values from -1 to 1
- merge_first: float32 [2048, 2048], P(('grp', 'dp')), may hold values from -6 to 6
- merge_second: float32 [2048, 2048], P(('grp', 'dp')), may hold values from 2 to 120
- feedforward_master: float32 [2048, 24576], P(('grp', 'dp')), may hold values from -0.125 to 0.125
- feedforward_first: float32 [2048, 24576], P(('grp', 'dp')), may hold values from -48 to 48
- feedforward_second: float32 [2048, 24576], P(('grp', 'dp')), may hold values from 30 to 2000
Outputs:
- block_output: bfloat16 [8, 4, 320, 2048], P('dp', 'grp')
- input_grad: float32 [8, 4, 320, 2048], P('dp', 'grp')
- gain_grad: float32 [2, 2048], P(None, ('grp', 'dp'))
- gain_update: float32 [2, 2048], P(None, ('grp', 'dp'))
- gain_first_new: float32 [2, 2048], P(None, ('grp', 'dp'))
- gain_second_new: float32 [2, 2048], P(None, ('grp', 'dp'))
- attention_grad: float32 [2048, 4096], P(('grp', 'dp'))
- attention_update: float32 [2048, 4096], P(('grp', 'dp'))
- attention_first_new: float32 [2048, 4096], P(('grp', 'dp'))
- attention_second_new: float32 [2048, 4096], P(('grp', 'dp'))
- merge_grad: float32 [2048, 2048], P(('grp', 'dp'))
- merge_update: float32 [2048, 2048], P(('grp', 'dp'))
- merge_first_new: float32 [2048, 2048], P(('grp', 'dp'))
- merge_second_new: float32 [2048, 2048], P(('grp', 'dp'))
- feedforward_grad: float32 [2048, 24576], P(('grp', 'dp'))
- feedforward_update: float32 [2048, 24576], P(('grp', 'dp'))
- feedforward_first_new: float32 [2048, 24576], P(('grp', 'dp'))
- feedforward_second_new: float32 [2048, 24576], P(('grp', 'dp'))
Inputs may be any that keep to these rules, and one draw needn't show every extreme that they name: `segment_ids`: along a group's prompt the ids never fall; each of the 4 ids covers 1 to 512 positions, and one covers exactly 512.
All inputs are finite; a program needn't handle non-finite values.
Results may differ from a plain program's by a relative error of at most 0.025.
The roundings to bfloat16 on the way count: a program that leaves them out, or rounds other values in their place, can miss the bound.
Values may be sent and summed in bfloat16 or wider, within the bound.
A program may use at most 896 MiB of HBM per device.

v0:
```python
import jax
import jax.numpy as jnp
from jax import lax
from jax.sharding import PartitionSpec as P

D = 2048
FF = 8192
HQ = 8
HK = 4
HD = 256
PROMPT_LEN = 1024
PROMPTS = 4
CONT = 64
STEP = 10


EPS_NORM = 1e-06
ROPE_THETA = 1000042.0
MASK_FILL = -1e30
BETA_ONE = 0.9
BETA_TWO = 0.95
ADAM_EPS = 1e-08
LEARN_RATE = 0.02
WEIGHT_DECAY = 0.1


def contract(left, right, left_axis, right_axis):
    return lax.dot_general(
        left, right, (((left_axis,), (right_axis,)), ((), ())), preferred_element_type=jnp.float32
    )


def rotate(values, cosine, sine_part):
    half_width = values.shape[-1] // 2
    front_half = values[..., :half_width]
    back_half = values[..., half_width:]
    return jnp.concatenate(
        [front_half * cosine - back_half * sine_part, back_half * cosine + front_half * sine_part],
        axis=-1,
    )


def angle_table(positions):
    inverse_rate = ROPE_THETA ** (-(jnp.arange(HD // 2, dtype=jnp.float32) * 2.0) / HD)
    angles = positions.astype(jnp.float32)[..., None] * inverse_rate
    return (jnp.cos(angles), jnp.sin(angles))


def segment_positions(segment_row, source_row):
    labels = jnp.arange(PROMPTS, dtype=jnp.int32)
    member = (segment_row[None, :] == labels[:, None]).astype(jnp.int32)
    lengths = jnp.sum(member, axis=1, dtype=jnp.int32)
    starts = jnp.cumsum(lengths, dtype=jnp.int32) - lengths
    prompt_index = jnp.arange(segment_row.shape[0], dtype=jnp.int32)
    prompt_positions = prompt_index - jnp.sum(member * starts[:, None], axis=0, dtype=jnp.int32)
    source_length = jnp.sum(
        (source_row[:, None] == labels[None, :]).astype(jnp.int32) * lengths[None, :],
        axis=1,
        dtype=jnp.int32,
    )
    follow_positions = source_length[:, None] + jnp.arange(CONT, dtype=jnp.int32)[None, :]
    return (prompt_positions, follow_positions)


def norm_scale(values):
    return lax.rsqrt(jnp.mean(values * values, axis=-1, keepdims=True) + EPS_NORM)


def norm_back(values, row_scale, gain_row, normed_grad):
    scaled = normed_grad * gain_row
    return row_scale * scaled - values * row_scale**3 * jnp.mean(
        scaled * values, axis=-1, keepdims=True
    )


def masked_scores(head_queries, all_keys, visible, score_scale):
    raw_scores = (
        jnp.einsum("rkgd,skd->kgrs", head_queries, all_keys, preferred_element_type=jnp.float32)
        * score_scale
    )
    return jnp.where(visible, raw_scores, MASK_FILL)


def adam_step(master, first_moment, second_moment, gradient, decay_rate):
    first_new = BETA_ONE * first_moment + (1.0 - BETA_ONE) * gradient
    second_new = BETA_TWO * second_moment + (1.0 - BETA_TWO) * gradient * gradient
    correct_one = 1.0 - BETA_ONE**STEP
    correct_two = 1.0 - BETA_TWO**STEP
    update = first_new / correct_one / (jnp.sqrt(second_new / correct_two) + ADAM_EPS)
    return (-LEARN_RATE * (update + decay_rate * master), first_new, second_new)


def gate_parts(gate_values, up_values):
    gate_sigmoid = jax.nn.sigmoid(gate_values)
    gate_silu = gate_values * gate_sigmoid
    return (gate_sigmoid, gate_silu, (gate_silu * up_values).astype(jnp.bfloat16))


def gate_backward(activated_grad, gate_values, up_values, gate_sigmoid, gate_silu):
    gate_grad = (
        activated_grad * up_values * gate_sigmoid * (1.0 + gate_values * (1.0 - gate_sigmoid))
    ).astype(jnp.bfloat16)
    up_grad = (activated_grad * gate_silu).astype(jnp.bfloat16)
    return (gate_grad, up_grad)


def body(
    hidden,
    cotangent,
    segment_ids,
    continuation_prompt,
    gain_master,
    gain_first,
    gain_second,
    attention_master,
    attention_first,
    attention_second,
    merge_master,
    merge_first,
    merge_second,
    feedforward_master,
    feedforward_first,
    feedforward_second,
):
    group_index = lax.axis_index("grp")
    row_count = hidden.shape[2]
    prompt_rows = row_count - CONT
    query_width = HQ * HD
    key_width = HK * HD
    group_heads = HQ // HK
    score_scale = HD ** (-0.5)
    key_count = PROMPT_LEN + CONT
    gain_low = gain_master.astype(jnp.bfloat16)
    attention_low = attention_master.astype(jnp.bfloat16)
    merge_low = merge_master.astype(jnp.bfloat16)
    feedforward_low = feedforward_master.astype(jnp.bfloat16)
    gain_rows, attention_weight, merge_weight = (
        lax.all_gather(gain_low, ("grp", "dp"), axis=1, tiled=True),
        lax.all_gather(attention_low, ("grp", "dp"), axis=0, tiled=True),
        lax.all_gather(merge_low, ("grp", "dp"), axis=0, tiled=True),
    )
    feedforward_weight = lax.all_gather(feedforward_low, ("grp", "dp"), axis=0, tiled=True)
    gate_weight = feedforward_weight[:, : 2 * FF]
    down_weight = feedforward_weight[:, 2 * FF :]
    gain_float = gain_rows.astype(jnp.float32)
    segment_row = segment_ids[0]
    source_row = continuation_prompt[0]
    prompt_positions, follow_positions = segment_positions(segment_row, source_row)
    own_positions = jnp.concatenate(
        [
            lax.dynamic_slice_in_dim(prompt_positions, group_index * prompt_rows, prompt_rows),
            follow_positions[0],
        ]
    )
    cosine, sine_part = angle_table(own_positions)
    cosine = cosine[:, None, :]
    sine_part = sine_part[:, None, :]
    inputs = hidden.reshape(row_count, D).astype(jnp.float32)
    first_scale = norm_scale(inputs)
    normed = (inputs * first_scale * gain_float[0]).astype(jnp.bfloat16)
    project = jnp.dot(normed, attention_weight, preferred_element_type=jnp.float32)
    queries = rotate(project[:, :query_width].reshape(row_count, HQ, HD), cosine, sine_part).astype(
        jnp.bfloat16
    )
    key_rows = (
        rotate(
            project[:, query_width : query_width + key_width].reshape(row_count, HK, HD),
            cosine,
            sine_part,
        )
        .astype(jnp.bfloat16)
        .reshape(row_count, key_width)
    )
    value_rows = project[:, query_width + key_width :].astype(jnp.bfloat16)
    prompt_pairs = jnp.concatenate([key_rows[:prompt_rows], value_rows[:prompt_rows]], axis=1)
    gathered = lax.all_gather(prompt_pairs, "grp", axis=0, tiled=True)
    all_keys = jnp.concatenate([gathered[:, :key_width], key_rows[prompt_rows:]], axis=0).reshape(
        key_count, HK, HD
    )
    all_values = jnp.concatenate(
        [gathered[:, key_width:], value_rows[prompt_rows:]], axis=0
    ).reshape(key_count, HK, HD)
    row_index = jnp.arange(row_count, dtype=jnp.int32)
    is_prompt = row_index < prompt_rows
    global_row = group_index * prompt_rows + jnp.minimum(row_index, prompt_rows - 1)
    own_segment = lax.dynamic_slice_in_dim(segment_row, group_index * prompt_rows, prompt_rows)
    query_segment = jnp.concatenate([own_segment, jnp.broadcast_to(source_row, (CONT,))])
    key_index = jnp.arange(PROMPT_LEN, dtype=jnp.int32)
    prompt_seen = (segment_row[None, :] == query_segment[:, None]) & (
        (key_index[None, :] <= global_row[:, None]) | ~is_prompt[:, None]
    )
    follow_seen = (~is_prompt)[:, None] & (
        jnp.arange(CONT, dtype=jnp.int32)[None, :] <= (row_index - prompt_rows)[:, None]
    )
    visible = jnp.concatenate([prompt_seen, follow_seen], axis=1)
    head_queries = queries.reshape(row_count, HK, group_heads, HD)
    scores = masked_scores(head_queries, all_keys, visible, score_scale)
    row_peak = jnp.max(scores, axis=-1, keepdims=True)
    unnormed = jnp.exp(scores - row_peak)
    row_total = jnp.sum(unnormed, axis=-1, keepdims=True)
    probability_low = (unnormed / row_total).astype(jnp.bfloat16)
    row_logsum = row_peak + jnp.log(row_total)
    attended = (
        jnp.einsum(
            "kgrs,skd->rkgd", probability_low, all_values, preferred_element_type=jnp.float32
        )
        .reshape(row_count, query_width)
        .astype(jnp.bfloat16)
    )
    middle = inputs + contract(attended, merge_weight, 1, 1)
    second_scale = norm_scale(middle)
    normed_two = (middle * second_scale * gain_float[1]).astype(jnp.bfloat16)
    grad_rows = cotangent.reshape(row_count, D).astype(jnp.float32)
    down_grad = grad_rows.astype(jnp.bfloat16)
    gate_up = jnp.dot(normed_two, gate_weight, preferred_element_type=jnp.float32)
    gate_values = gate_up[:, :FF]
    up_values = gate_up[:, FF:]
    gate_sigmoid, gate_silu, activated = gate_parts(gate_values, up_values)
    result = middle + contract(activated, down_weight, 1, 1)
    activated_grad = contract(down_grad, down_weight, 1, 0)
    gate_grad, up_grad = gate_backward(
        activated_grad, gate_values, up_values, gate_sigmoid, gate_silu
    )
    gate_up_grad = jnp.concatenate([gate_grad, up_grad], axis=1)
    normed_two_grad = contract(gate_up_grad, gate_weight, 1, 1)
    feedforward_grad = lax.psum_scatter(
        jnp.concatenate(
            [contract(normed_two, gate_up_grad, 0, 0), contract(down_grad, activated, 0, 0)], axis=1
        ),
        ("grp", "dp"),
        scatter_dimension=0,
        tiled=True,
    )
    block_output = result.astype(jnp.bfloat16).reshape(hidden.shape)
    middle_grad = grad_rows + norm_back(middle, second_scale, gain_float[1], normed_two_grad)
    gain_two_part = jnp.sum(normed_two_grad * middle * second_scale, axis=0)
    branch_grad = middle_grad.astype(jnp.bfloat16)
    merge_term = contract(branch_grad, attended, 0, 0)
    attended_grad = (
        contract(branch_grad, merge_weight, 1, 0)
        .astype(jnp.bfloat16)
        .reshape(row_count, HK, group_heads, HD)
    )
    scores = masked_scores(head_queries, all_keys, visible, score_scale)
    probabilities = jnp.exp(scores - row_logsum)
    probability_grad = jnp.einsum(
        "rkgd,skd->kgrs", attended_grad, all_values, preferred_element_type=jnp.float32
    )
    row_delta = jnp.sum(probabilities * probability_grad, axis=-1, keepdims=True)
    score_grad = (probabilities * (probability_grad - row_delta)).astype(jnp.bfloat16)
    query_grad = (
        jnp.einsum("kgrs,skd->rkgd", score_grad, all_keys, preferred_element_type=jnp.float32)
        * score_scale
    )
    key_grad = (
        jnp.einsum("kgrs,rkgd->skd", score_grad, head_queries, preferred_element_type=jnp.float32)
        * score_scale
    )
    value_grad = jnp.einsum(
        "kgrs,rkgd->skd",
        probabilities.astype(jnp.bfloat16),
        attended_grad,
        preferred_element_type=jnp.float32,
    )
    prompt_grads = jnp.concatenate(
        [
            key_grad[:PROMPT_LEN].reshape(PROMPT_LEN, key_width),
            value_grad[:PROMPT_LEN].reshape(PROMPT_LEN, key_width),
        ],
        axis=1,
    )
    summed = lax.psum_scatter(
        prompt_grads.astype(jnp.bfloat16), "grp", scatter_dimension=0, tiled=True
    ).astype(jnp.float32)
    key_local = jnp.concatenate(
        [summed[:, :key_width], key_grad[PROMPT_LEN:].reshape(CONT, key_width)], axis=0
    ).reshape(row_count, HK, HD)
    value_local = jnp.concatenate(
        [summed[:, key_width:], value_grad[PROMPT_LEN:].reshape(CONT, key_width)], axis=0
    )
    project_grad = jnp.concatenate(
        [
            rotate(query_grad.reshape(row_count, HQ, HD), cosine, -sine_part).reshape(
                row_count, query_width
            ),
            rotate(key_local, cosine, -sine_part).reshape(row_count, key_width),
            value_local,
        ],
        axis=1,
    ).astype(jnp.bfloat16)
    attention_term = contract(normed, project_grad, 0, 0)
    normed_grad = contract(project_grad, attention_weight, 1, 1)
    input_grad = (middle_grad + norm_back(inputs, first_scale, gain_float[0], normed_grad)).reshape(
        hidden.shape
    )
    gain_one_part = jnp.sum(normed_grad * inputs * first_scale, axis=0)
    gain_term = jnp.stack([gain_one_part, gain_two_part])
    gain_grad, attention_grad, merge_grad = (
        lax.psum_scatter(gain_term, ("grp", "dp"), scatter_dimension=1, tiled=True),
        lax.psum_scatter(attention_term, ("grp", "dp"), scatter_dimension=0, tiled=True),
        lax.psum_scatter(merge_term, ("grp", "dp"), scatter_dimension=0, tiled=True),
    )
    gain_new = adam_step(gain_master, gain_first, gain_second, gain_grad, 0.0)
    attention_new = adam_step(
        attention_master, attention_first, attention_second, attention_grad, WEIGHT_DECAY
    )
    merge_new = adam_step(merge_master, merge_first, merge_second, merge_grad, WEIGHT_DECAY)
    feedforward_new = adam_step(
        feedforward_master, feedforward_first, feedforward_second, feedforward_grad, WEIGHT_DECAY
    )
    return (
        block_output,
        input_grad,
        gain_grad,
        gain_new[0],
        gain_new[1],
        gain_new[2],
        attention_grad,
        attention_new[0],
        attention_new[1],
        attention_new[2],
        merge_grad,
        merge_new[0],
        merge_new[1],
        merge_new[2],
        feedforward_grad,
        feedforward_new[0],
        feedforward_new[1],
        feedforward_new[2],
    )


def solution(mesh):
    placed = (
        P("dp", "grp", None, None),
        P("dp", "grp", None, None),
        P("dp", None),
        P("dp", "grp"),
        P(None, ("grp", "dp")),
        P(None, ("grp", "dp")),
        P(None, ("grp", "dp")),
        P(("grp", "dp"), None),
        P(("grp", "dp"), None),
        P(("grp", "dp"), None),
        P(("grp", "dp"), None),
        P(("grp", "dp"), None),
        P(("grp", "dp"), None),
        P(("grp", "dp"), None),
        P(("grp", "dp"), None),
        P(("grp", "dp"), None),
    )
    return jax.shard_map(
        body,
        mesh=mesh,
        in_specs=placed,
        out_specs=(
            P("dp", "grp", None, None),
            P("dp", "grp", None, None),
            P(None, ("grp", "dp")),
            P(None, ("grp", "dp")),
            P(None, ("grp", "dp")),
            P(None, ("grp", "dp")),
            P(("grp", "dp"), None),
            P(("grp", "dp"), None),
            P(("grp", "dp"), None),
            P(("grp", "dp"), None),
            P(("grp", "dp"), None),
            P(("grp", "dp"), None),
            P(("grp", "dp"), None),
            P(("grp", "dp"), None),
            P(("grp", "dp"), None),
            P(("grp", "dp"), None),
            P(("grp", "dp"), None),
            P(("grp", "dp"), None),
        ),
        check_vma=False,
    )
```

profile of v0, /device:TPU:9, one launch (start us, length us, event | category | flops | bytes accessed | tf_op | source)
XLA Modules:
  0.0 3390.2 jit_solution(11051955683111575182)
XLA Ops:
  11.8 35.7 %all-gather = bf16[32,64,2]{1,2,0:T(2,128)(2,1)S(1)} all-gather(bf16[1,64,2]{1,2,0:T(2,128)(2,1)S(1)} %convert_bitcast_fusion), channel_id=1, replica_groups=mesh['grp'=4,'dp'=8] {'grp','dp'}, dimensions={0}, use_global_device_ids=true | all-gather | bytes 8448 | tf_op jit(solution)/shard_map/all_gather | solution.py:138
  52.1 74.8 %all-gather.6.cloned.1.call-done = bf16[2048,4096]{1,0:T(8,128)(2,1)} async-done(((bf16[64,4096]{1,0:T(8,128)(2,1)}), bf16[2048,4096]{1,0:T(8,128)(2,1)}) %all-gather.6.cloned.1.call-update) | async-done | bytes 16777232 | tf_op jit(solution)/shard_map/all_gather | solution.py:139
  126.9 9.3 fusion.103
  145.6 4.8 convert_element_type.99
  159.5 62.4 %all-gather.8.cloned.1.call-done = bf16[1024,2048]{1,0:T(8,128)(2,1)} async-done(((bf16[256,2048]{1,0:T(8,128)(2,1)}), bf16[1024,2048]{1,0:T(8,128)(2,1)}) %all-gather.8.cloned.1.call-update) | async-done | bytes 4194320 | tf_op jit(solution)/shard_map/all_gather | solution.py:176
  222.0 4.0 fusion.98
  247.8 56.6 %all-gather.10.cloned.1.call-done = bf16[2048,2048]{1,0:T(8,128)(2,1)} async-done(((bf16[64,2048]{1,0:T(8,128)(2,1)}), bf16[2048,2048]{1,0:T(8,128)(2,1)}) %all-gather.10.cloned.1.call-update) | async-done | bytes 8388624 | tf_op jit(solution)/shard_map/all_gather | solution.py:140
  304.4 7.8 multiply_reduce_fusion.2
  313.4 508.1 %all-gather.12.cloned.1.call-done = bf16[2048,24576]{1,0:T(8,128)(2,1)} async-done(((bf16[64,24576]{1,0:T(8,128)(2,1)}), bf16[2048,24576]{1,0:T(8,128)(2,1)}) %all-gather.12.cloned.1.call-update) | async-done | bytes 100663312 | tf_op jit(solution)/shard_map/all_gather | solution.py:142
  821.5 37.5 %fusion.2 = f32[320,16384]{1,0:T(8,128)} fusion(bf16[2048,24576]{1,0:T(8,128)(2,1)} %all-gather.12.cloned.1.call-done, f32[320,2048]{1,0:T(8,128)} %get-tuple-element.69, f32[2048]{0:T(1024)S(1)} %bitcast.144, f32[320]{0:T(512)S(1)} %get-tuple-element.61), kind=kOutput, calls=%fused_computation.3 | convolution fusion | flops 21476802560 | bytes 90711296 | tf_op jit(solution)/shard_map/dot_general | solution.py:215
  859.0 27.3 multiply_convert_fusion.1
  886.3 32.8 multiply_reduce_fusion
  928.4 4.4 reshape.309
  932.8 7.8 fusion.25
  940.6 9.3 fusion.8
  951.4 4.0 copy.128
  955.3 9.7 fusion.10
  971.3 4.0 copy.126
  975.3 4.7 pad_maximum_fusion.4
  981.8 5.2 convolution_multiply_fusion
  991.3 65.3 %reduce-scatter.8.cloned.1.call-done = bf16[256,2048]{0,1:T(8,128)(2,1)} async-done(((bf16[1024,2048]{0,1:T(8,128)(2,1)}), bf16[256,2048]{0,1:T(8,128)(2,1)}) %reduce-scatter.8.cloned.1.call-update) | async-done | bytes 1048592 | tf_op jit(solution)/shard_map/reduce_scatter | solution.py:272
  1064.9 12.2 fusion.43
  1078.7 9.6 fusion.71
  1090.2 16.5 fusion.65
  1106.8 29.8 convolution_bitcast_fusion
  1136.6 50.9 %fusion.14 = f32[2048,16384]{1,0:T(8,128)} fusion(bf16[320,8192]{1,0:T(8,128)(2,1)} %get-tuple-element.35, bf16[320,8192]{1,0:T(8,128)(2,1)} %get-tuple-element.34, f32[320,2048]{1,0:T(8,128)S(1)} %copy-done.10, f32[2048]{0:T(1024)S(1)} %bitcast.147, f32[320]{0:T(512)S(1)} %get-tuple-element.61), kind=kOutput, calls=%fused_computation.28 | convolution fusion | flops 21497774080 | bytes 147334400 | tf_op jit(solution)/shard_map/dot_general | solution.py:28
  1187.5 133.2 %pad_maximum_fusion = f32[2048,24576]{1,0:T(8,128)} fusion(f32[2048,8192]{1,0:T(8,128)} %convolution_bitcast_fusion, f32[2048,16384]{1,0:T(8,128)} %fusion.14), kind=kLoop, calls=%fused_computation | loop fusion | flops 50331648 | bytes 402653184 | tf_op jit(solution)/shard_map/concatenate | solution.py:227
  1322.5 18.7 fusion.44
  1345.1 51.1 %reduce-scatter.12.cloned.1.call-done = f32[64,2048]{1,0:T(8,128)} async-done(((f32[2048,2048]{1,0:T(8,128)}), f32[64,2048]{1,0:T(8,128)}) %reduce-scatter.12.cloned.1.call-update) | async-done | bytes 524304 | tf_op jit(solution)/shard_map/reduce_scatter | solution.py:301
  1398.7 361.5 %reduce-scatter.10.cloned.1.call-done = f32[64,4096]{1,0:T(8,128)} async-done(((f32[2048,4096]{1,0:T(8,128)}), f32[64,4096]{1,0:T(8,128)}) %reduce-scatter.10.cloned.1.call-update) | async-done | bytes 1048592 | tf_op jit(solution)/shard_map/reduce_scatter | solution.py:300
  1763.9 1602.8 %reduce-scatter.14.cloned.1.call-done = f32[64,24576]{1,0:T(8,128)} async-done(((f32[2048,24576]{1,0:T(8,128)}), f32[64,24576]{1,0:T(8,128)}) %reduce-scatter.14.cloned.1.call-update) | async-done | bytes 6291472 | tf_op jit(solution)/shard_map/reduce_scatter | solution.py:226
  3366.7 16.7 add_multiply_fusion
  (219 shorter events, 96.5 us)
Async XLA Ops:
  7.2 42.6 %copy-start.6 = (bf16[1,1,320,2048]{3,2,1,0:T(8,128)(2,1)S(1)}, bf16[1,1,320,2048]{3,2,1,0:T(8,128)(2,1)}, u32[]{:S(2)}) copy-start(bf16[1,1,320,2048]{3,2,1,0:T(8,128)(2,1)} %param.16) | copy-start | bytes 3932164
  7.2 119.7 %all-gather.6.cloned.1.call-start = ((), (), s32[]{:S(2)}) async-start(), calls=%async_computation.5 | async-start | bytes 17301504 | tf_op jit(solution)/shard_map/all_gather | solution.py:139
  9.4 212.5 %all-gather.8.cloned.1.call-start = ((), (), s32[]{:S(2)}) async-start(), calls=%async_computation.6 | async-start | bytes 5242880 | tf_op jit(solution)/shard_map/all_gather | solution.py:176
  50.7 85.4 %copy-start.48 = (f32[320]{0:T(512)}, f32[320]{0:T(512)S(1)}, u32[]{:S(2)}) copy-start(f32[320]{0:T(512)S(1)} %get-tuple-element.59) | copy-start | bytes 3844
  52.1 105.2 %copy-start.18 = (f32[320,128]{1,0:T(8,128)}, f32[320,128]{1,0:T(8,128)S(1)}, u32[]{:S(2)}) copy-start(f32[320,128]{1,0:T(8,128)S(1)} %get-tuple-element.57) | copy-start | bytes 491524
  52.1 84.1 %copy-start.43 = (f32[1,2048]{1,0:T(1,128)}, f32[1,2048]{1,0:T(1,128)S(1)}, u32[]{:S(2)}) copy-start(f32[1,2048]{1,0:T(1,128)S(1)} %get-tuple-element.54) | copy-start | bytes 24580
  144.7 159.7 %all-gather.10.cloned.1.call-start = ((), (), s32[]{:S(2)}) async-start(), calls=%async_computation.7 | async-start | bytes 8650752 | tf_op jit(solution)/shard_map/all_gather | solution.py:140
  145.5 675.9 %all-gather.12.cloned.1.call-start = ((), (), s32[]{:S(2)}) async-start(), calls=%async_computation.8 | async-start | bytes 103809024 | tf_op jit(solution)/shard_map/all_gather | solution.py:142
  150.4 906.2 %reduce-scatter.8.cloned.1.call-start = ((), (), s32[]{:S(2)}) async-start(), calls=%async_computation.9 | async-start | bytes 5242880 | tf_op jit(solution)/shard_map/reduce_scatter | solution.py:272
  247.8 64.4 %copy-start.15 = (bf16[320,2048]{1,0:T(8,128)(2,1)}, bf16[320,2048]{1,0:T(8,128)(2,1)S(1)}, u32[]{:S(2)}) copy-start(bf16[320,2048]{1,0:T(8,128)(2,1)S(1)} %convert_element_type.96) | copy-start | bytes 3932164
  859.0 27.3 copy-start.9
  886.3 32.9 copy-start.53
  924.4 154.3 %copy-start.1 = (f32[320,2048]{1,0:T(8,128)}, f32[320,2048]{1,0:T(8,128)S(1)}, u32[]{:S(2)}) copy-start(f32[320,2048]{1,0:T(8,128)S(1)} %subtract_add_fusion) | copy-start | bytes 7864324
  955.3 9.8 copy-start.24
  980.0 363.4 %reduce-scatter.16.cloned.1.call-start = ((), (), s32[]{:S(2)}) async-start(), calls=%async_computation.13 | async-start | bytes 1081344
  989.8 71.2 %slice-start.1 = ((f32[1088,4,256]{2,0,1:T(8,128)}), f32[64,4,256]{2,0,1:T(8,128)S(1)}, s32[]{:S(2)}) async-start(f32[1088,4,256]{2,0,1:T(8,128)} %copy-done.12), calls=%async_computation.15 | async-start | bytes 524288 | tf_op jit(solution)/shard_map/slice | solution.py:276
  1078.5 317.6 %reduce-scatter.12.cloned.1.call-start = ((), (), s32[]{:S(2)}) async-start(), calls=%async_computation.11 | async-start | bytes 17301504 | tf_op jit(solution)/shard_map/reduce_scatter | solution.py:301
  1088.3 671.9 %reduce-scatter.10.cloned.1.call-start = ((), (), s32[]{:S(2)}) async-start(), calls=%async_computation.10 | async-start | bytes 34603008 | tf_op jit(solution)/shard_map/reduce_scatter | solution.py:300
  1106.7 2260.0 %reduce-scatter.14.cloned.1.call-start = ((), (), s32[]{:S(2)}) async-start(), calls=%async_computation.12 | async-start | bytes 207618048 | tf_op jit(solution)/shard_map/reduce_scatter | solution.py:226
  1106.8 29.8 copy-start.10
  1322.4 18.7 copy-start.55
  1322.4 18.7 copy-start.2
  1322.4 18.7 copy-start.8
  1322.4 18.7 copy-start.25
  1322.4 18.7 copy-start.45
  1322.4 18.7 copy-start.50
  1322.5 18.7 copy-start.52
  1341.2 54.9 %copy-start.28 = (f32[64,2048]{1,0:T(8,128)S(1)}, f32[64,2048]{1,0:T(8,128)}, u32[]{:S(2)}) copy-start(f32[64,2048]{1,0:T(8,128)} %param.26) | copy-start | bytes 1572868
  1341.3 54.9 %copy-start.40 = (f32[64,2048]{1,0:T(8,128)S(1)}, f32[64,2048]{1,0:T(8,128)}, u32[]{:S(2)}) copy-start(f32[64,2048]{1,0:T(8,128)} %param.27) | copy-start | bytes 1572868
  1343.5 416.7 %copy-start.17 = (f32[64,4096]{1,0:T(8,128)S(1)}, f32[64,4096]{1,0:T(8,128)}, u32[]{:S(2)}) copy-start(f32[64,4096]{1,0:T(8,128)} %param.23) | copy-start | bytes 3145732
  1343.5 416.7 %copy-start.38 = (f32[64,4096]{1,0:T(8,128)S(1)}, f32[64,4096]{1,0:T(8,128)}, u32[]{:S(2)}) copy-start(f32[64,4096]{1,0:T(8,128)} %param.24) | copy-start | bytes 3145732
  1344.5 419.4 %copy-start.54 = (f32[2,64]{1,0:T(2,128)}, f32[2,64]{1,0:T(2,128)S(1)}, u32[]{:S(2)}) copy-start(f32[2,64]{1,0:T(2,128)S(1)} %copy.147) | copy-start | bytes 1540
  (39 other events, 118.0 us)
Sparse Core Ops, SparseCore 0:
  11.5 115.3 all-gather.5
  144.8 77.0 all-gather.7
  225.4 78.9 all-gather.9
  307.7 513.7 all-gather.11
  980.2 76.3 reduce-scatter.7
  1078.6 111.2 reduce-scatter.15
  1192.8 203.2 reduce-scatter.11
  1399.0 361.1 reduce-scatter.9
  1767.2 1599.4 reduce-scatter.13
where the time goes:
time: 3400 us; the launch traced here: 3390 us
  waiting for transfers between devices  2780 us (82%)
  matrix products  286 us (8%)
  other arithmetic  201 us (6%)
  local copies, waits for them, and re-layouts  68.4 us (2%)
  blocking collectives  35.7 us (1%)
    reduce_scatter x1, waiting for transfers between devices, body(): lax.psum_scatter(jnp.concatenate([contract(normed_two, gate_up_grad, 0, 0...  1600 us
    all_gather x1, waiting for transfers between devices, body(): lax.all_gather(feedforward_low, ('grp', 'dp'), axis=0, tiled=True)  508 us
    reduce_scatter x1, waiting for transfers between devices, body(): lax.psum_scatter(attention_term, ('grp', 'dp'), scatter_dimension=0, tile...  361 us
    dot_general x10, matrix products, contract(): lax.dot_general(left, right, (((left_axis,), (right_axis,)), ((), ())), p...  209 us
    concatenate x1, other arithmetic, body(): jnp.concatenate([contract(normed_two, gate_up_grad, 0, 0), contract(down_...  133 us
    all_gather x1, waiting for transfers between devices, body(): lax.all_gather(attention_low, ('grp', 'dp'), axis=0, tiled=True)  74.8 us
  transfers between devices with their start and end apart: 9, of which 8 were waited for; matrix products, arithmetic and copies ran while one was open for 10% of the time, Pallas kernels for 0%

commit v1 on v0

--- a/solution.py
+++ b/solution.py
@@ -50,7 +50,9 @@
     labels = jnp.arange(PROMPTS, dtype=jnp.int32)
     member = (segment_row[None, :] == labels[:, None]).astype(jnp.int32)
     lengths = jnp.sum(member, axis=1, dtype=jnp.int32)
-    starts = jnp.cumsum(lengths, dtype=jnp.int32) - lengths
+    starts = jnp.sum(
+        jnp.where(labels[None, :] < labels[:, None], lengths[None, :], 0), axis=1, dtype=jnp.int32
+    )
     prompt_index = jnp.arange(segment_row.shape[0], dtype=jnp.int32)
     prompt_positions = prompt_index - jnp.sum(member * starts[:, None], axis=0, dtype=jnp.int32)
     source_length = jnp.sum(
@@ -133,15 +135,24 @@
     gain_low = gain_master.astype(jnp.bfloat16)
     attention_low = attention_master.astype(jnp.bfloat16)
     merge_low = merge_master.astype(jnp.bfloat16)
-    feedforward_low = feedforward_master.astype(jnp.bfloat16)
+    dp_size = lax.axis_size("dp")
+    own_rows = feedforward_master.shape[0]
+    own_hidden = FF // dp_size
     gain_rows, attention_weight, merge_weight = (
         lax.all_gather(gain_low, ("grp", "dp"), axis=1, tiled=True),
         lax.all_gather(attention_low, ("grp", "dp"), axis=0, tiled=True),
         lax.all_gather(merge_low, ("grp", "dp"), axis=0, tiled=True),
     )
-    feedforward_weight = lax.all_gather(feedforward_low, ("grp", "dp"), axis=0, tiled=True)
-    gate_weight = feedforward_weight[:, : 2 * FF]
-    down_weight = feedforward_weight[:, 2 * FF :]
+    feedforward_low = jnp.transpose(
+        feedforward_master.astype(jnp.bfloat16).reshape(own_rows, 3, dp_size, own_hidden),
+        (2, 0, 1, 3),
+    ).reshape(dp_size * own_rows, 3 * own_hidden)
+    feedforward_weight = lax.all_gather(
+        lax.all_to_all(feedforward_low, "dp", 0, 0, tiled=True), "grp", axis=0, tiled=True
+    )
+    gate_weight = feedforward_weight[:, : 2 * own_hidden]
+    down_weight = feedforward_weight[:, 2 * own_hidden :]
+    down_grad = lax.all_gather(cotangent.reshape(-1, D), "dp", axis=0, tiled=True)
     gain_float = gain_rows.astype(jnp.float32)
     segment_row = segment_ids[0]
     source_row = continuation_prompt[0]
@@ -211,25 +222,42 @@
     second_scale = norm_scale(middle)
     normed_two = (middle * second_scale * gain_float[1]).astype(jnp.bfloat16)
     grad_rows = cotangent.reshape(row_count, D).astype(jnp.float32)
-    down_grad = grad_rows.astype(jnp.bfloat16)
-    gate_up = jnp.dot(normed_two, gate_weight, preferred_element_type=jnp.float32)
-    gate_values = gate_up[:, :FF]
-    up_values = gate_up[:, FF:]
+    normed_all = lax.all_gather(normed_two, "dp", axis=0, tiled=True)
+    gate_up = jnp.dot(normed_all, gate_weight, preferred_element_type=jnp.float32)
+    gate_values = gate_up[:, :own_hidden]
+    up_values = gate_up[:, own_hidden:]
     gate_sigmoid, gate_silu, activated = gate_parts(gate_values, up_values)
-    result = middle + contract(activated, down_weight, 1, 1)
+    down_part = contract(activated, down_weight, 1, 1).astype(jnp.bfloat16)
     activated_grad = contract(down_grad, down_weight, 1, 0)
     gate_grad, up_grad = gate_backward(
         activated_grad, gate_values, up_values, gate_sigmoid, gate_silu
     )
     gate_up_grad = jnp.concatenate([gate_grad, up_grad], axis=1)
-    normed_two_grad = contract(gate_up_grad, gate_weight, 1, 1)
-    feedforward_grad = lax.psum_scatter(
-        jnp.concatenate(
-            [contract(normed_two, gate_up_grad, 0, 0), contract(down_grad, activated, 0, 0)], axis=1
-        ),
-        ("grp", "dp"),
-        scatter_dimension=0,
-        tiled=True,
+    normed_two_part = contract(gate_up_grad, gate_weight, 1, 1).astype(jnp.bfloat16)
+    normed_two_grad = lax.psum_scatter(
+        normed_two_part, "dp", scatter_dimension=0, tiled=True
+    ).astype(jnp.float32)
+    result = middle + lax.psum_scatter(
+        down_part, "dp", scatter_dimension=0, tiled=True
+    ).astype(jnp.float32)
+
+    def to_owner(left, right):
+        part = lax.psum_scatter(
+            contract(left, right, 0, 0).astype(jnp.bfloat16),
+            "grp",
+            scatter_dimension=0,
+            tiled=True,
+        )
+        spread = lax.all_to_all(part, "dp", 0, 0, tiled=True)
+        width = right.shape[1] // own_hidden
+        return (
+            jnp.transpose(spread.reshape(dp_size, own_rows, width, own_hidden), (1, 2, 0, 3))
+            .reshape(own_rows, width * FF)
+            .astype(jnp.float32)
+        )
+
+    feedforward_grad = jnp.concatenate(
+        [to_owner(normed_all, gate_up_grad), to_owner(down_grad, activated)], axis=1
     )
     block_output = result.astype(jnp.bfloat16).reshape(hidden.shape)
     middle_grad = grad_rows + norm_back(middle, second_scale, gain_float[1], normed_two_grad)
@@ -297,8 +325,12 @@
     gain_term = jnp.stack([gain_one_part, gain_two_part])
     gain_grad, attention_grad, merge_grad = (
         lax.psum_scatter(gain_term, ("grp", "dp"), scatter_dimension=1, tiled=True),
-        lax.psum_scatter(attention_term, ("grp", "dp"), scatter_dimension=0, tiled=True),
-        lax.psum_scatter(merge_term, ("grp", "dp"), scatter_dimension=0, tiled=True),
+        lax.psum_scatter(
+            attention_term.astype(jnp.bfloat16), ("grp", "dp"), scatter_dimension=0, tiled=True
+        ).astype(jnp.float32),
+        lax.psum_scatter(
+            merge_term.astype(jnp.bfloat16), ("grp", "dp"), scatter_dimension=0, tiled=True
+        ).astype(jnp.float32),
     )
     gain_new = adam_step(gain_master, gain_first, gain_second, gain_grad, 0.0)
     attention_new = adam_step(

time: 3400 us -> 1720 us (0.51)
  waiting for transfers between devices: 2780 us -> 1210 us
  other arithmetic: 201 us -> 67.8 us
  blocking collectives: 35.7 us -> 93.7 us
  matrix products: 286 us -> 232 us
    reduce_scatter x3 -> x6, waiting for transfers between devices: 2020 us -> 661 us  [the longest x1 202 us: body(): lax.psum_scatter(attention_term.astype(jnp.bfloat16), ('grp', 'dp'), scat...]
    all_gather x1 -> x3, waiting for transfers between devices: 508 us -> 308 us  [the longest x1 206 us: body(): lax.all_gather(lax.all_to_all(feedforward_low, 'dp', 0, 0, tiled=True), '...]
    concatenate x1 -> x0, other arithmetic: 133 us -> none  [body(): jnp.concatenate([contract(normed_two, gate_up_grad, 0, 0), contract(down_...]
    all_to_all x0 -> x2, blocking collectives: none -> 58.1 us  [the longest x1 40 us: body(): lax.all_to_all(feedforward_low, 'dp', 0, 0, tiled=True)]
    unnamed x10 -> x15, waiting for transfers between devices: 0.15 us -> 55.5 us
    all_gather x1, waiting for transfers between devices: 62.4 us -> 11 us  [body(): gathered = lax.all_gather(prompt_pairs, 'grp', axis=0, tiled=True)]
    reduce_scatter x1, waiting for transfers between devices: 65.3 us -> 19.7 us  [body(): lax.psum_scatter(prompt_grads.astype(jnp.bfloat16), 'grp', scatter_dimens...]
    dot_general x10, matrix products: 209 us -> 164 us  [contract(): lax.dot_general(left, right, (((left_axis,), (right_axis,)), ((), ())), p...]
  transfers between devices with their start and end apart: 9 -> 15, of which waited for: 8 -> 15; matrix products, arithmetic and copies ran while one was open for 10% -> 13% of each run, Pallas kernels for 0% -> 0%
where the time goes in v1:
time: 1720 us; the launch traced here: 1710 us
  waiting for transfers between devices  1210 us (70%)
  matrix products  232 us (13%)
  blocking collectives  93.7 us (5%)
  local copies, waits for them, and re-layouts  80.2 us (5%)
  other arithmetic  67.8 us (4%)
    all_gather x1, waiting for transfers between devices, body(): lax.all_gather(lax.all_to_all(feedforward_low, 'dp', 0, 0, tiled=True), '...  206 us
    reduce_scatter x1, waiting for transfers between devices, body(): lax.psum_scatter(attention_term.astype(jnp.bfloat16), ('grp', 'dp'), scat...  202 us
    reduce_scatter x2, waiting for transfers between devices, to_owner(): lax.psum_scatter(contract(left, right, 0, 0).astype(jnp.bfloat16), 'grp',...  167 us
    dot_general x10, matrix products, contract(): lax.dot_general(left, right, (((left_axis,), (right_axis,)), ((), ())), p...  164 us
    reduce_scatter x1, waiting for transfers between devices, body(): lax.psum_scatter(merge_term.astype(jnp.bfloat16), ('grp', 'dp'), scatter_...  146 us
    reduce_scatter x1, waiting for transfers between devices, body(): lax.psum_scatter(down_part, 'dp', scatter_dimension=0, tiled=True)  82.4 us
    all_gather x1, waiting for transfers between devices, body(): lax.all_gather(attention_low, ('grp', 'dp'), axis=0, tiled=True)  74.9 us
    all_gather x1, waiting for transfers between devices, body(): normed_all = lax.all_gather(normed_two, 'dp', axis=0, tiled=True)  67 us
  transfers between devices with their start and end apart: 15, of which 15 were waited for; matrix products, arithmetic and copies ran while one was open for 13% of the time, Pallas kernels for 0%

profile of v1, /device:TPU:9, one launch (start us, length us, event | category | flops | bytes accessed | tf_op | source)
XLA Modules:
  0.0 1710.4 jit_solution(16622388354676788680)
XLA Ops:
  10.8 35.7 %all-gather.1 = bf16[32,64,2]{1,2,0:T(2,128)(2,1)S(1)} all-gather(bf16[1,64,2]{1,2,0:T(2,128)(2,1)S(1)} %convert_bitcast_fusion.1), channel_id=1, replica_groups=mesh['grp'=4,'dp'=8] {'grp','dp'}, dimensions={0}, use_global_device_ids=true | all-gather | bytes 8448 | tf_op jit(solution)/shard_map/all_gather | solution.py:142
  52.0 74.9 %all-gather.9.cloned.1.call-done = bf16[2048,4096]{1,0:T(8,128)(2,1)} async-done(((bf16[64,4096]{1,0:T(8,128)(2,1)}), bf16[2048,4096]{1,0:T(8,128)(2,1)}) %all-gather.9.cloned.1.call-update) | async-done | bytes 16777232 | tf_op jit(solution)/shard_map/all_gather | solution.py:143
  126.9 9.3 fusion.100
  153.0 8.3 all_to_all.20
  161.4 40.0 %all_to_all.30 = bf16[8,64,3072]{2,1,0:T(8,128)(2,1)} all-to-all(bf16[8,64,3072]{2,1,0:T(8,128)(2,1)S(1)} %all_to_all.20), channel_id=1, replica_groups=mesh['grp'=4,'dp'=8] {'dp'}, dimensions={0} | all-to-all | bytes 6291456 | tf_op jit(solution)/shard_map/all_to_all | solution.py:151
  208.7 11.0 all-gather.11.cloned.1.call-done
  242.2 60.0 %all-gather.13.cloned.1.call-done = bf16[2048,2048]{1,0:T(8,128)(2,1)} async-done(((bf16[64,2048]{1,0:T(8,128)(2,1)}), bf16[2048,2048]{1,0:T(8,128)(2,1)}) %all-gather.13.cloned.1.call-update) | async-done | bytes 8388624 | tf_op jit(solution)/shard_map/all_gather | solution.py:144
  311.6 205.6 %all-gather.17.cloned.1.call-done = bf16[2048,3072]{1,0:T(8,128)(2,1)} async-done(((bf16[512,3072]{1,0:T(8,128)(2,1)}), bf16[2048,3072]{1,0:T(8,128)(2,1)}) %all-gather.17.cloned.1.call-update) | async-done | bytes 12582928 | tf_op jit(solution)/shard_map/all_gather | solution.py:150
  517.1 67.0 %all-gather.15.cloned.1.call-done = bf16[2560,2048]{1,0:T(8,128)(2,1)} async-done(((bf16[320,2048]{1,0:T(8,128)(2,1)}), bf16[2560,2048]{1,0:T(8,128)(2,1)}) %all-gather.15.cloned.1.call-update) | async-done | bytes 10485776 | tf_op jit(solution)/shard_map/all_gather | solution.py:225
  584.2 29.4 %fusion.11 = f32[2560,2048]{0,1:T(8,128)} fusion(bf16[2560,2048]{1,0:T(8,128)(2,1)} %all-gather.15.cloned.1.call-done, bf16[2048,3072]{1,0:T(8,128)(2,1)} %all-gather.17.cloned.1.call-done), kind=kOutput, calls=%fused_computation.28 | convolution fusion | flops 21474836480 | bytes 39845888 | tf_op jit(solution)/shard_map/dot_general | solution.py:226
  613.5 35.7 %all-gather.19.cloned.1.call-done = bf16[1,1,2560,2048]{3,2,1,0:T(8,128)(2,1)} async-done(((bf16[1,1,320,2048]{3,2,1,0:T(8,128)(2,1)}), bf16[1,1,2560,2048]{3,2,1,0:T(8,128)(2,1)}) %all-gather.19.cloned.1.call-update) | async-done | bytes 10485776 | tf_op jit(solution)/shard_map/all_gather | solution.py:155
  649.2 25.8 %multiply_convert_fusion.1 = (bf16[2560,1024]{0,1:T(8,128)(2,1)}, bf16[2560,1024]{0,1:T(8,128)(2,1)}, bf16[2560,1024]{0,1:T(8,128)(2,1)}) fusion(f32[2560,2048]{0,1:T(8,128)} %fusion.11, bf16[2048,3072]{1,0:T(8,128)(2,1)} %all-gather.17.cloned.1.call-done, bf16[1,1,2560,2048]{3,2,1,0:T(8,128)(2,1)} %all-gather.19.cloned.1.call-done), kind=kOutput, calls=%fused_computation.18 | convolution fusion | flops 10776739840 | bytes 51380224 | tf_op jit(solution)/shard_map/dot_general | solution.py:28
  675.1 28.5 %convolution_convert_fusion.1 = bf16[2560,2048]{1,0:T(8,128)(2,1)} fusion(bf16[2048,3072]{1,0:T(8,128)(2,1)} %all-gather.17.cloned.1.call-done, bf16[2560,1024]{0,1:T(8,128)(2,1)} %get-tuple-element.38, bf16[2560,1024]{0,1:T(8,128)(2,1)} %get-tuple-element.37), kind=kOutput, calls=%fused_computation.10 | convolution fusion | flops 21501050880 | bytes 29360128 | tf_op jit(solution)/shard_map/dot_general | solution.py:28
  703.7 17.2 %convolution_convert_fusion.2 = bf16[2560,2048]{1,0:T(8,128)(2,1)} fusion(bf16[2560,1024]{0,1:T(8,128)(2,1)} %get-tuple-element.39, bf16[2048,3072]{1,0:T(8,128)(2,1)} %all-gather.17.cloned.1.call-done), kind=kOutput, calls=%fused_computation.11 | convolution fusion | flops 10742661120 | bytes 19922944 | tf_op jit(solution)/shard_map/dot_general | solution.py:28
  721.6 63.3 %reduce-scatter.13.cloned.1.call-done = bf16[320,2048]{1,0:T(8,128)(2,1)} async-done(((bf16[2560,2048]{1,0:T(8,128)(2,1)}), bf16[320,2048]{1,0:T(8,128)(2,1)}) %reduce-scatter.13.cloned.1.call-update) | async-done | bytes 1310736 | tf_op jit(solution)/shard_map/reduce_scatter | solution.py:237
  787.6 82.4 %reduce-scatter.11.cloned.1.call-done = bf16[320,2048]{1,0:T(8,128)(2,1)} async-done(((bf16[2560,2048]{1,0:T(8,128)(2,1)}), bf16[320,2048]{1,0:T(8,128)(2,1)}) %reduce-scatter.11.cloned.1.call-update) | async-done | bytes 1310736 | tf_op jit(solution)/shard_map/reduce_scatter | solution.py:240
  890.3 9.0 fusion
  904.8 9.3 fusion.2
  928.9 17.0 convert_bitcast_fusion
  946.0 29.5 %convolution_convert_fusion.4 = bf16[2048,2048]{1,0:T(8,128)(2,1)} fusion(bf16[2560,2048]{1,0:T(8,128)(2,1)} %all-gather.15.cloned.1.call-done, bf16[2560,1024]{0,1:T(8,128)(2,1)} %get-tuple-element.38, bf16[2560,1024]{0,1:T(8,128)(2,1)} %get-tuple-element.37), kind=kOutput, calls=%fused_computation.26 | convolution fusion | flops 21500002304 | bytes 29360128 | tf_op jit(solution)/shard_map/dot_general | solution.py:28
  986.1 19.7 %reduce-scatter.15.cloned.1.call-done = bf16[256,2048]{0,1:T(8,128)(2,1)} async-done(((bf16[1024,2048]{0,1:T(8,128)(2,1)}), bf16[256,2048]{0,1:T(8,128)(2,1)}) %reduce-scatter.15.cloned.1.call-update) | async-done | bytes 1048592 | tf_op jit(solution)/shard_map/reduce_scatter | solution.py:300
  1008.9 11.8 fusion.46
  1022.3 8.1 convolution_convert_fusion.3
  1032.3 13.7 convolution_convert_fusion
  1046.0 39.3 %reduce-scatter.23.cloned.1.call-done = bf16[512,1024]{0,1:T(8,128)(2,1)} async-done(((bf16[2048,1024]{0,1:T(8,128)(2,1)}), bf16[512,1024]{0,1:T(8,128)(2,1)}) %reduce-scatter.23.cloned.1.call-update) | async-done | bytes 1048592 | tf_op jit(solution)/shard_map/reduce_scatter | solution.py:245
  1086.9 18.1 %all_to_all.31 = bf16[8,64,1024]{2,1,0:T(8,128)(2,1)S(1)} all-to-all(bf16[8,64,1024]{2,1,0:T(8,128)(2,1)S(1)} %bitcast.165), channel_id=1, replica_groups=mesh['grp'=4,'dp'=8] {'dp'}, dimensions={0} | all-to-all | bytes 2097152 | tf_op jit(solution)/shard_map/all_to_all | solution.py:251
  1105.0 127.5 %reduce-scatter.21.cloned.1.call-done = bf16[512,2048]{1,0:T(8,128)(2,1)} async-done(((bf16[2048,2048]{1,0:T(8,128)(2,1)}), bf16[512,2048]{1,0:T(8,128)(2,1)}) %reduce-scatter.21.cloned.1.call-update) | async-done | bytes 2097168 | tf_op jit(solution)/shard_map/reduce_scatter | solution.py:245
  1238.3 24.3 %all-to-all-done.1 = bf16[8,64,2048]{2,1,0:T(8,128)(2,1)} async-done(((bf16[8,64,2048]{2,1,0:T(8,128)(2,1)}), bf16[8,64,2048]{2,1,0:T(8,128)(2,1)}, u32[]{:S(2)}, u32[]{:S(2)}) %all-to-all-start.1) | async-done | bytes 2097184 | tf_op jit(solution)/shard_map/all_to_all | solution.py:251
  1273.8 13.7 add_multiply_fusion
  1292.8 54.8 %reduce-scatter.25.cloned.1.call-done = f32[64,2]{1,0:T(8,128)} async-done(((f32[2048,2]{1,0:T(8,128)}), f32[64,2]{1,0:T(8,128)}) %reduce-scatter.25.cloned.1.call-update) | async-done | bytes 528
  1349.0 146.1 %reduce-scatter.19.cloned.1.call-done = bf16[64,2048]{1,0:T(8,128)(2,1)} async-done(((bf16[2048,2048]{1,0:T(8,128)(2,1)}), bf16[64,2048]{1,0:T(8,128)(2,1)}) %reduce-scatter.19.cloned.1.call-update) | async-done | bytes 262160 | tf_op jit(solution)/shard_map/reduce_scatter | solution.py:331
  1497.7 202.1 %reduce-scatter.17.cloned.1.call-done = bf16[64,4096]{1,0:T(8,128)(2,1)} async-done(((bf16[2048,4096]{1,0:T(8,128)(2,1)}), bf16[64,4096]{1,0:T(8,128)(2,1)}) %reduce-scatter.17.cloned.1.call-update) | async-done | bytes 524304 | tf_op jit(solution)/shard_map/reduce_scatter | solution.py:328
  (249 shorter events, 156.4 us)
Async XLA Ops:
  7.2 119.7 %all-gather.9.cloned.1.call-start = ((), (), s32[]{:S(2)}) async-start(), calls=%async_computation.11 | async-start | bytes 17301504 | tf_op jit(solution)/shard_map/all_gather | solution.py:143
  9.4 210.3 %all-gather.11.cloned.1.call-start = ((), (), s32[]{:S(2)}) async-start(), calls=%async_computation.12 | async-start | bytes 5242880 | tf_op jit(solution)/shard_map/all_gather | solution.py:187
  50.6 85.5 %copy-start.53 = (f32[320]{0:T(512)}, f32[320]{0:T(512)S(1)}, u32[]{:S(2)}) copy-start(f32[320]{0:T(512)S(1)} %get-tuple-element.64) | copy-start | bytes 3844
  51.9 156.1 %copy-start.13 = (f32[320,128]{1,0:T(8,128)}, f32[320,128]{1,0:T(8,128)S(1)}, u32[]{:S(2)}) copy-start(f32[320,128]{1,0:T(8,128)S(1)} %get-tuple-element.62) | copy-start | bytes 491524
  52.0 84.2 %copy-start.49 = (f32[1,2048]{1,0:T(1,128)}, f32[1,2048]{1,0:T(1,128)S(1)}, u32[]{:S(2)}) copy-start(f32[1,2048]{1,0:T(1,128)S(1)} %get-tuple-element.59) | copy-start | bytes 24580
  52.0 256.8 %copy-start.38 = (f32[1,2048]{1,0:T(1,128)}, f32[1,2048]{1,0:T(1,128)S(1)}, u32[]{:S(2)}) copy-start(f32[1,2048]{1,0:T(1,128)S(1)} %get-tuple-element.58) | copy-start | bytes 24580
  142.5 159.7 %all-gather.13.cloned.1.call-start = ((), (), s32[]{:S(2)}) async-start(), calls=%async_computation.13 | async-start | bytes 8650752 | tf_op jit(solution)/shard_map/all_gather | solution.py:144
  143.3 373.8 %all-gather.17.cloned.1.call-start = ((), (), s32[]{:S(2)}) async-start(), calls=%async_computation.15 | async-start | bytes 15728640 | tf_op jit(solution)/shard_map/all_gather | solution.py:150
  201.4 382.8 %all-gather.15.cloned.1.call-start = ((), (), s32[]{:S(2)}) async-start(), calls=%async_computation.14 | async-start | bytes 11796480 | tf_op jit(solution)/shard_map/all_gather | solution.py:225
  239.0 63.2 %copy-start.10 = (bf16[1,1,320,2048]{3,2,1,0:T(8,128)(2,1)S(1)}, bf16[1,1,320,2048]{3,2,1,0:T(8,128)(2,1)}, u32[]{:S(2)}) copy-start(bf16[1,1,320,2048]{3,2,1,0:T(8,128)(2,1)} %param.16) | copy-start | bytes 3932164
  311.0 338.3 %all-gather.19.cloned.1.call-start = ((), (), s32[]{:S(2)}) async-start(), calls=%async_computation.23 | async-start | bytes 11796480 | tf_op jit(solution)/shard_map/all_gather | solution.py:155
  311.5 473.4 %reduce-scatter.13.cloned.1.call-start = ((), (), s32[]{:S(2)}) async-start(), calls=%async_computation.17 | async-start | bytes 11796480 | tf_op jit(solution)/shard_map/reduce_scatter | solution.py:237
  703.6 166.4 %reduce-scatter.11.cloned.1.call-start = ((), (), s32[]{:S(2)}) async-start(), calls=%async_computation.16 | async-start | bytes 11796480 | tf_op jit(solution)/shard_map/reduce_scatter | solution.py:240
  720.9 64.0 %copy-start.2 = (f32[320,2048]{1,0:T(8,128)S(1)}, f32[320,2048]{1,0:T(8,128)}, u32[]{:S(2)}) copy-start(f32[320,2048]{1,0:T(8,128)} %copy-done.1) | copy-start | bytes 7864324
  720.9 64.0 %copy-start.39 = (f32[1,2048]{1,0:T(1,128)S(1)}, f32[1,2048]{1,0:T(1,128)}, u32[]{:S(2)}) copy-start(f32[1,2048]{1,0:T(1,128)} %copy-done.38) | copy-start | bytes 24580
  720.9 64.0 %copy-start.47 = (f32[320]{0:T(512)S(1)}, f32[320]{0:T(512)}, u32[]{:S(2)}) copy-start(f32[320]{0:T(512)} %copy-done.46) | copy-start | bytes 3844
  720.9 149.1 %copy-start.51 = (f32[320]{0:T(512)S(1)}, f32[320]{0:T(512)}, u32[]{:S(2)}) copy-start(f32[320]{0:T(512)} %get-tuple-element.65) | copy-start | bytes 3844
  720.9 284.9 %reduce-scatter.15.cloned.1.call-start = ((), (), s32[]{:S(2)}) async-start(), calls=%async_computation.18 | async-start | bytes 5242880 | tf_op jit(solution)/shard_map/reduce_scatter | solution.py:300
  928.9 156.5 %reduce-scatter.23.cloned.1.call-start = ((), (), s32[]{:S(2)}) async-start(), calls=%async_computation.22 | async-start | bytes 5242880 | tf_op jit(solution)/shard_map/reduce_scatter | solution.py:245
  945.9 286.5 %reduce-scatter.21.cloned.1.call-start = ((), (), s32[]{:S(2)}) async-start(), calls=%async_computation.21 | async-start | bytes 10485760 | tf_op jit(solution)/shard_map/reduce_scatter | solution.py:245
  975.5 372.1 %reduce-scatter.25.cloned.1.call-start = ((), (), s32[]{:S(2)}) async-start(), calls=%async_computation.24 | async-start | bytes 1081344
  1022.2 472.9 %reduce-scatter.19.cloned.1.call-start = ((), (), s32[]{:S(2)}) async-start(), calls=%async_computation.20 | async-start | bytes 8650752 | tf_op jit(solution)/shard_map/reduce_scatter | solution.py:331
  1030.4 669.4 %reduce-scatter.17.cloned.1.call-start = ((), (), s32[]{:S(2)}) async-start(), calls=%async_computation.19 | async-start | bytes 17301504 | tf_op jit(solution)/shard_map/reduce_scatter | solution.py:328
  1232.4 30.2 %all-to-all-start.1 = ((bf16[8,64,2048]{2,1,0:T(8,128)(2,1)}), bf16[8,64,2048]{2,1,0:T(8,128)(2,1)}, u32[]{:S(2)}, u32[]{:S(2)}) async-start(bf16[8,64,2048]{2,1,0:T(8,128)(2,1)} %bitcast.173), calls=%async_computation.7 | async-start | bytes 4194304 | tf_op jit(solution)/shard_map/all_to_all | solution.py:251
  1287.5 60.9 %copy-start.56 = (f32[2,64]{1,0:T(2,128)S(1)}, f32[2,64]{1,0:T(2,128)}, u32[]{:S(2)}) copy-start(f32[2,64]{1,0:T(2,128)} %param.20) | copy-start | bytes 1540
  1287.5 60.9 %copy-start.57 = (f32[2,64]{1,0:T(2,128)S(1)}, f32[2,64]{1,0:T(2,128)}, u32[]{:S(2)}) copy-start(f32[2,64]{1,0:T(2,128)} %param.21) | copy-start | bytes 1540
  1287.5 60.9 %copy-start.58 = (f32[2,64]{1,0:T(2,128)S(1)}, f32[2,64]{1,0:T(2,128)}, u32[]{:S(2)}) copy-start(f32[2,64]{1,0:T(2,128)} %param.22) | copy-start | bytes 1540
  1287.6 207.6 %copy-start.21 = (f32[64,2048]{1,0:T(8,128)S(1)}, f32[64,2048]{1,0:T(8,128)}, u32[]{:S(2)}) copy-start(f32[64,2048]{1,0:T(8,128)} %param.26) | copy-start | bytes 1572868
  1287.6 207.6 %copy-start.34 = (f32[64,2048]{1,0:T(8,128)S(1)}, f32[64,2048]{1,0:T(8,128)}, u32[]{:S(2)}) copy-start(f32[64,2048]{1,0:T(8,128)} %param.27) | copy-start | bytes 1572868
  1292.8 407.1 %copy-start.12 = (f32[64,4096]{1,0:T(8,128)S(1)}, f32[64,4096]{1,0:T(8,128)}, u32[]{:S(2)}) copy-start(f32[64,4096]{1,0:T(8,128)} %param.23) | copy-start | bytes 3145732
  1292.8 407.1 %copy-start.31 = (f32[64,4096]{1,0:T(8,128)S(1)}, f32[64,4096]{1,0:T(8,128)}, u32[]{:S(2)}) copy-start(f32[64,4096]{1,0:T(8,128)} %param.24) | copy-start | bytes 3145732
  1348.4 355.0 %copy-start.55 = (f32[2,64]{1,0:T(2,128)}, f32[2,64]{1,0:T(2,128)S(1)}, u32[]{:S(2)}) copy-start(f32[2,64]{1,0:T(2,128)S(1)} %copy.183) | copy-start | bytes 1540
  (45 other events, 267.2 us)
Sparse Core Ops, SparseCore 0:
  11.5 115.3 all-gather.8
  142.6 77.0 all-gather.10
  223.2 78.9 all-gather.12
  303.6 213.5 all-gather.16
  519.4 64.6 all-gather.14
  585.9 63.2 all-gather.18
  703.7 81.1 reduce-scatter.12
  788.4 81.5 reduce-scatter.10
  929.0 76.7 reduce-scatter.14
  1008.1 77.2 reduce-scatter.22
  1087.7 144.6 reduce-scatter.20
  1235.1 112.4 reduce-scatter.24
  1350.0 145.1 reduce-scatter.18
  1497.4 202.3 reduce-scatter.16

commit v2 on v0

v2 whole, which is shorter than its diff:
```python
import functools

import jax
import jax.numpy as jnp
from jax import lax
from jax.experimental import pallas as pl
from jax.experimental.pallas import tpu as pltpu
from jax.sharding import PartitionSpec as P

D = 2048
FF = 8192
HQ = 8
HK = 4
HD = 256
PROMPT_LEN = 1024
PROMPTS = 4
CONT = 64
STEP = 10
GAIN_PAD = 128

EPS_NORM = 1e-06
ROPE_THETA = 1000042.0
MASK_FILL = -1e30
BETA_ONE = 0.9
BETA_TWO = 0.95
ADAM_EPS = 1e-08
LEARN_RATE = 0.02
WEIGHT_DECAY = 0.1
LOW = jnp.bfloat16
FULL = jnp.float32
MESH = pl.DeviceIdType.MESH


def contract(left, right, left_axis, right_axis):
    return lax.dot_general(
        left, right, (((left_axis,), (right_axis,)), ((), ())), preferred_element_type=FULL
    )


def rotate(values, cosine, sine_part):
    half_width = values.shape[-1] // 2
    front_half = values[..., :half_width]
    back_half = values[..., half_width:]
    return jnp.concatenate(
        [front_half * cosine - back_half * sine_part, back_half * cosine + front_half * sine_part],
        axis=-1,
    )


def angle_table(positions):
    inverse_rate = ROPE_THETA ** (-(jnp.arange(HD // 2, dtype=FULL) * 2.0) / HD)
    angles = positions.astype(FULL)[..., None] * inverse_rate
    return (jnp.cos(angles), jnp.sin(angles))


def segment_positions(segment_row, source_row):
    labels = jnp.arange(PROMPTS, dtype=jnp.int32)
    member = (segment_row[None, :] == labels[:, None]).astype(jnp.int32)
    lengths = jnp.sum(member, axis=1, dtype=jnp.int32)
    starts = jnp.sum(
        jnp.where(labels[None, :] < labels[:, None], lengths[None, :], 0), axis=1, dtype=jnp.int32
    )
    prompt_index = jnp.arange(segment_row.shape[0], dtype=jnp.int32)
    prompt_positions = prompt_index - jnp.sum(member * starts[:, None], axis=0, dtype=jnp.int32)
    source_length = jnp.sum(
        (source_row[:, None] == labels[None, :]).astype(jnp.int32) * lengths[None, :],
        axis=1,
        dtype=jnp.int32,
    )
    follow_positions = source_length[:, None] + jnp.arange(CONT, dtype=jnp.int32)[None, :]
    return (prompt_positions, follow_positions)


def norm_scale(values):
    return lax.rsqrt(jnp.mean(values * values, axis=-1, keepdims=True) + EPS_NORM)


def norm_back(values, row_scale, gain_row, normed_grad):
    scaled = normed_grad * gain_row
    return row_scale * scaled - values * row_scale**3 * jnp.mean(
        scaled * values, axis=-1, keepdims=True
    )


def masked_scores(head_queries, all_keys, visible, score_scale):
    raw_scores = (
        jnp.einsum("rkgd,skd->kgrs", head_queries, all_keys, preferred_element_type=FULL)
        * score_scale
    )
    return jnp.where(visible, raw_scores, MASK_FILL)


def adam_step(master, first_moment, second_moment, gradient, decay_rate):
    first_new = BETA_ONE * first_moment + (1.0 - BETA_ONE) * gradient
    second_new = BETA_TWO * second_moment + (1.0 - BETA_TWO) * gradient * gradient
    correct_one = 1.0 - BETA_ONE**STEP
    correct_two = 1.0 - BETA_TWO**STEP
    update = first_new / correct_one / (jnp.sqrt(second_new / correct_two) + ADAM_EPS)
    return (-LEARN_RATE * (update + decay_rate * master), first_new, second_new)


def gate_parts(gate_values, up_values):
    gate_sigmoid = jax.nn.sigmoid(gate_values)
    gate_silu = gate_values * gate_sigmoid
    return (gate_sigmoid, gate_silu, (gate_silu * up_values).astype(LOW))


def gate_backward(activated_grad, gate_values, up_values, gate_sigmoid, gate_silu):
    gate_grad = (
        activated_grad * up_values * gate_sigmoid * (1.0 + gate_values * (1.0 - gate_sigmoid))
    ).astype(LOW)
    up_grad = (activated_grad * gate_silu).astype(LOW)
    return (gate_grad, up_grad)


def flip(index, bits):
    bit = 1
    while bit <= bits:
        if bits & bit:
            index = index + bit - 2 * bit * lax.rem(index // bit, 2)
        bit *= 2
    return index


def remote(source, target, send, recv, there):
    return pltpu.make_async_remote_copy(
        src_ref=source,
        dst_ref=target,
        send_sem=send,
        recv_sem=recv,
        device_id=there,
        device_id_type=MESH,
    )


def gather_kernel(
    lines,
    plane,
    prompt_rows,
    weight_ref,
    hidden_ref,
    forward_ref,
    weights_ref,
    rows_ref,
    gate_ref,
    down_ref,
    local_sem,
    line_send,
    line_recv,
    rows_send,
    rows_recv,
    near_send,
    near_recv,
    half_send,
    half_recv,
    core_send,
    core_recv,
    swap_send,
    swap_recv,
):
    g = lax.axis_index("grp")
    d = lax.axis_index("dp")
    evens = range(0, plane, 2)
    forward_halves = plane == 8
    near = (2, 4) if forward_halves else tuple(evens[1:])
    width = weight_ref.shape[1]
    cut = (width // 256) * 128

    barrier = pltpu.get_barrier_semaphore()
    for offset in range(1, plane):
        pl.semaphore_signal(barrier, inc=1, device_id=(g, flip(d, offset)), device_id_type=MESH)

    for step in range(1, lines):
        there = lax.rem(g + step, lines)
        pl.semaphore_signal(barrier, inc=1, device_id=(there, d), device_id_type=MESH)
    pl.semaphore_wait(barrier, plane + lines - 2)

    copy = remote
    own_rows = hidden_ref.at[pl.ds(0, prompt_rows)]

    def line_weight(way, step):
        block = g - step + 1 if way == 0 else g + step - 1
        source = weight_ref if step == 1 else weights_ref.at[block, d]
        return copy(
            source,
            weights_ref.at[block, d],
            line_send.at[way, step],
            line_recv.at[way, step],
            (g + 1 if way == 0 else g - 1, d),
        )

    def line_rows(way, step):
        block = g - step + 1 if way == 0 else g + step - 1
        source = own_rows if step == 1 else rows_ref.at[block]
        return copy(
            source,
            rows_ref.at[block],
            rows_send.at[way, step],
            rows_recv.at[way, step],
            (g + 1 if way == 0 else g - 1, d),
        )

    def sends(way, step):
        if way == 0:
            return (g < lines - 1) & (g >= step - 1)
        return (g > 0) & (g + step - 1 < lines)

    def receives(way, step):
        return g >= step if way == 0 else g + step < lines

    def near_copy(block, offset, own):
        source = weight_ref if own else weights_ref.at[block, d]
        at = near.index(offset)
        return copy(
            source,
            weights_ref.at[block, d],
            near_send.at[block, at],
            near_recv.at[block, at],
            (g, flip(d, offset)),
        )

    def half_copy(block, part):
        columns = pl.ds(0, cut) if part == 0 else pl.ds(cut, width - cut)
        origin = flip(d, 2) if part == 0 else flip(d, 4)
        there = flip(d, 4) if part == 0 else flip(d, 2)
        piece = weights_ref.at[block, origin, :, columns]
        return copy(
            piece, piece, half_send.at[block, part], half_recv.at[block, part], (g, there)
        )

    def core_copy(block, offset, own=False):
        source = weight_ref if own else weights_ref.at[block, flip(d, offset)]
        return copy(
            source,
            weights_ref.at[block, flip(d, offset)],
            core_send.at[block, offset // 2],
            core_recv.at[block, offset // 2],
            (g, flip(d, 1)),
        )

    own_hidden = down_ref.shape[2]

    def swap_piece(owner, part, source_index):
        source = forward_ref.at[:, pl.ds(part * FF + owner * own_hidden, own_hidden)]
        if part == 2:
            return source, down_ref.at[source_index]
        return source, gate_ref.at[source_index, :, pl.ds(part * own_hidden, own_hidden)]

    def swap_copy(offset, part):
        source, target = swap_piece(flip(d, offset), part, d)
        return copy(
            source,
            target,
            swap_send.at[offset, part],
            swap_recv.at[offset, part],
            (g, flip(d, offset)),
        )

    locals_ = (
        pltpu.make_async_copy(weight_ref, weights_ref.at[g, d], local_sem.at[0]),
        pltpu.make_async_copy(own_rows, rows_ref.at[g], local_sem.at[1]),
        *(
            pltpu.make_async_copy(*swap_piece(d, part, d), local_sem.at[2 + part])
            for part in range(3)
        ),
    )

    def launch(block, own):
        for offset in near:
            near_copy(block, offset, own).start()
        core_copy(block, 0, own).start()

    def relay(block):
        for offset in near:
            near_copy(block, offset, False).wait_recv()
            core_copy(block, offset).start()
        if forward_halves:
            half_copy(block, 0).start()
            half_copy(block, 1).start()

    def finish(block):
        if forward_halves:
            half_copy(block, 0).wait_recv()
            half_copy(block, 1).wait_recv()
            core_copy(block, 6).start()

    for way in (0, 1):
        pl.when(sends(way, 1))(lambda way=way: line_weight(way, 1).start())
    launch(g, True)
    for one in locals_:
        one.start()
    for offset in range(1, plane):
        for part in range(3):
            swap_copy(offset, part).start()

    for step in range(1, lines):
        for way in (0, 1):

            @pl.when(receives(way, step))
            def _(way=way, step=step):
                line_weight(way, step).wait_recv()

            if step + 1 < lines:
                pl.when(sends(way, step + 1))(
                    lambda way=way, step=step: line_weight(way, step + 1).start()
                )
            else:
                pl.when(sends(way, 1))(lambda way=way: line_rows(way, 1).start())

            @pl.when(receives(way, step))
            def _(way=way, step=step):
                launch(g - step if way == 0 else g + step, False)

        if step == 1:
            relay(g)
        else:
            for way in (0, 1):
                pl.when(receives(way, step - 1))(
                    lambda way=way, step=step: relay(
                        g - step + 1 if way == 0 else g + step - 1
                    )
                )
    for step in range(1, lines):
        for way in (0, 1):

            @pl.when(receives(way, step))
            def _(way=way, step=step):
                line_rows(way, step).wait_recv()

            if step + 1 < lines:
                pl.when(sends(way, step + 1))(
                    lambda way=way, step=step: line_rows(way, step + 1).start()
                )
        if step == 1:
            for way in (0, 1):
                pl.when(receives(way, lines - 1))(
                    lambda way=way: relay(g - lines + 1 if way == 0 else g + lines - 1)
                )
            finish(g)
    for step in range(1, lines):
        for way in (0, 1):
            pl.when(receives(way, step))(
                lambda way=way, step=step: finish(g - step if way == 0 else g + step)
            )

    def drain(block):
        for offset in evens:
            core_copy(block, offset).wait()
        for offset in near:
            near_copy(block, offset, False).wait_send()
        if forward_halves:
            half_copy(block, 0).wait_send()
            half_copy(block, 1).wait_send()

    drain(g)
    for step in range(1, lines):
        for way in (0, 1):
            pl.when(receives(way, step))(
                lambda way=way, step=step: drain(g - step if way == 0 else g + step)
            )

            @pl.when(sends(way, step))
            def _(way=way, step=step):
                line_weight(way, step).wait_send()
                line_rows(way, step).wait_send()

    for offset in range(1, plane):
        for part in range(3):
            swap_copy(offset, part).wait()
    for one in locals_:
        one.wait()


def gather_start(weight, hidden, forward):
    lines, plane = lax.axis_size("grp"), lax.axis_size("dp")
    prompt_rows = PROMPT_LEN // lines
    own_rows, width = weight.shape
    anywhere = pl.BlockSpec(memory_space=pl.ANY)
    dma = pltpu.SemaphoreType.DMA
    near_count = 2 if plane == 8 else plane // 2 - 1
    pairs = (
        (2, lines),
        (2, lines),
        (2, lines),
        (2, lines),
        (lines, near_count),
        (lines, near_count),
        (lines, 2),
        (lines, 2),
        (lines, plane // 2),
        (lines, plane // 2),
        (plane, 3),
        (plane, 3),
    )
    own_hidden = FF // plane
    return pl.pallas_call(
        functools.partial(gather_kernel, lines, plane, prompt_rows),
        out_shape=(
            jax.ShapeDtypeStruct((lines, plane, own_rows, width), weight.dtype),
            jax.ShapeDtypeStruct((lines, prompt_rows, D), hidden.dtype),
            jax.ShapeDtypeStruct((plane, own_rows, 2 * own_hidden), forward.dtype),
            jax.ShapeDtypeStruct((plane, own_rows, own_hidden), forward.dtype),
        ),
        in_specs=[anywhere] * 3,
        out_specs=(anywhere,) * 4,
        scratch_shapes=[dma((5,))] + [dma(shape) for shape in pairs],
        compiler_params=pltpu.CompilerParams(collective_id=0, has_side_effects=True),
        name="gather_start",
    )(weight, hidden, forward)


def plane_swap(block, offset):
    size = lax.axis_size("dp")
    return lax.ppermute(block, "dp", [(i, i ^ offset) for i in range(size)])


def plane_gather(block):
    mine = [block] + [plane_swap(block, o) for o in range(2, lax.axis_size("dp"), 2)]
    pairs = [(one, plane_swap(one, 1)) for one in mine]
    return jnp.concatenate([one for pair in pairs for one in pair], axis=0)


def plane_scatter(part_of):
    size = lax.axis_size("dp")
    sums = {}
    for offset in list(range(size - 2, 0, -2)) + [0]:
        arrived = plane_swap(part_of(offset + 1).astype(LOW), 1)
        sums[offset] = part_of(offset).astype(FULL) + arrived.astype(FULL)
        if offset:
            sums[offset] = plane_swap(sums[offset].astype(LOW), offset)
    total = sums[0]
    for offset in range(2, size, 2):
        total = total + sums[offset].astype(FULL)
    return total


def plane_rows(term):
    lines, plane = lax.axis_size("grp"), lax.axis_size("dp")
    d = lax.axis_index("dp")
    blocks = term.reshape(lines, plane, -1, term.shape[1])
    mine = plane_scatter(
        lambda offset: lax.dynamic_index_in_dim(blocks, d ^ offset, 1, keepdims=False)
    )
    return mine.astype(LOW).reshape(-1, term.shape[1])


def line_scatter(term):
    return lax.psum_scatter(term, "grp", scatter_dimension=0, tiled=True)


def finish_kernel(
    lines,
    plane,
    query_ref,
    pair_ref,
    gain_ref,
    gate_ref,
    down_ref,
    a_master,
    a_first,
    a_second,
    f_master,
    f_first,
    f_second,
    a_grad,
    a_update,
    a_first_new,
    a_second_new,
    gain_out,
    f_grad,
    f_update,
    f_first_new,
    f_second_new,
    mine,
    core_in,
    plane_in,
    line_in,
    gate_in,
    down_in,
    state,
    made,
    a_state,
    a_made,
    gain_made,
    mine_sem,
    core_send,
    core_recv,
    plane_send,
    plane_recv,
    line_send,
    line_recv,
    swap_send,
    swap_recv,
    own_sem,
    state_sem,
    made_sem,
    a_sem,
    gain_sem,
):
    g = lax.axis_index("grp")
    d = lax.axis_index("dp")
    chips = plane // 2
    chip, core = lax.div(d, 2), lax.rem(d, 2)
    partner = d + 1 - 2 * core
    rows = a_master.shape[0]
    own_hidden = down_ref.shape[2]
    query_width, pair_width = query_ref.shape[4], pair_ref.shape[4]
    width = core_in.shape[3]
    parts = (
        (query_ref, pl.ds(0, query_width)),
        (pair_ref, pl.ds(query_width, pair_width)),
        (gain_ref, pl.ds(query_width + pair_width, GAIN_PAD)),
    )

    barrier = pltpu.get_barrier_semaphore()
    for step in range(1, plane):
        there = lax.rem(d + step, plane)
        pl.semaphore_signal(barrier, inc=1, device_id=(g, there), device_id_type=MESH)
    for step in range(1, lines):
        there = lax.rem(g + step, lines)
        pl.semaphore_signal(barrier, inc=1, device_id=(there, d), device_id_type=MESH)
    pl.semaphore_wait(barrier, plane + lines - 2)

    def line_at(turn):
        return lax.rem(g + turn + 1, lines)

    def core_copy(turn, part):
        line = line_at(turn)
        ref, columns = parts[part]
        return remote(
            ref.at[line, :, 1 - core],
            core_in.at[line, :, :, columns],
            core_send.at[turn, part],
            core_recv.at[turn, part],
            (g, partner),
        )

    def mine_copy(turn, part):
        line = line_at(turn)
        ref, columns = parts[part]
        return pltpu.make_async_copy(
            ref.at[line, :, core], mine.at[line, :, :, columns], mine_sem.at[turn, part]
        )

    def plane_copy(turn, step):
        line = line_at(turn)
        there = lax.rem(chip + step, chips)
        return remote(
            core_in.at[line, there],
            plane_in.at[line, chip],
            plane_send.at[turn, step],
            plane_recv.at[turn, step],
            (g, 2 * there + core),
        )

    def line_copy(turn):
        line = line_at(turn)
        return remote(
            core_in.at[line, chip],
            line_in.at[g],
            line_send.at[turn],
            line_recv.at[turn],
            (line, d),
        )

    def swap_copy(step, part):
        there = lax.rem(d + step, plane)
        source, target = (gate_ref, gate_in) if part == 0 else (down_ref, down_in)
        return remote(
            source.at[there],
            target.at[d],
            swap_send.at[step, part],
            swap_recv.at[step, part],
            (g, there),
        )

    own_swap = (
        pltpu.make_async_copy(gate_ref.at[d], gate_in.at[d], own_sem.at[0]),
        pltpu.make_async_copy(down_ref.at[d], down_in.at[d], own_sem.at[1]),
    )

    def state_copy(turn, part, which):
        source = (f_master, f_first, f_second)[which]
        block = lax.rem(d + turn, plane)
        slot = lax.rem(turn, 2)
        return pltpu.make_async_copy(
            source.at[:, pl.ds(part * FF + block * own_hidden, own_hidden)],
            state.at[slot, part, which],
            state_sem.at[slot, part, which],
        )

    def made_copy(turn, part, which):
        target = (f_grad, f_update, f_first_new, f_second_new)[which]
        block = lax.rem(d + turn, plane)
        slot = lax.rem(turn, 2)
        return pltpu.make_async_copy(
            made.at[slot, part, which],
            target.at[:, pl.ds(part * FF + block * own_hidden, own_hidden)],
            made_sem.at[slot, part, which],
        )

    def a_state_copy(which):
        return pltpu.make_async_copy(
            (a_master, a_first, a_second)[which], a_state.at[which], a_sem.at[which]
        )

    def a_made_copy(which):
        return pltpu.make_async_copy(
            a_made.at[which],
            (a_grad, a_update, a_first_new, a_second_new)[which],
            a_sem.at[3 + which],
        )

    for turn in range(lines):
        for part in range(3):
            core_copy(turn, part).start()
            mine_copy(turn, part).start()
    for step in range(1, plane):
        for part in range(2):
            swap_copy(step, part).start()
    for one in own_swap:
        one.start()
    for part in range(3):
        for which in range(3):
            state_copy(0, part, which).start()
    for which in range(3):
        a_state_copy(which).start()

    tile = 384 if width % 384 == 0 else 128
    tiles = width // tile

    for turn in range(lines):
        line = line_at(turn)
        for part in range(3):
            core_copy(turn, part).wait_recv()
            mine_copy(turn, part).wait()
        for step in range(1, chips):
            there = lax.rem(chip + step, chips)

            @pl.loop(0, tiles)
            def _(at, line=line, there=there):
                columns = pl.ds(pl.multiple_of(at * tile, tile), tile)
                total = mine[line, there, :, columns].astype(FULL) + core_in[
                    line, there, :, columns
                ].astype(FULL)
                core_in[line, there, :, columns] = total.astype(LOW)

            plane_copy(turn, step).start()

    def step_rows(slot, part, at, gradient):
        rows_at = pl.ds(pl.multiple_of(at * 16, 16), 16)
        update, first_new, second_new = adam_step(
            state[slot, part, 0, rows_at],
            state[slot, part, 1, rows_at],
            state[slot, part, 2, rows_at],
            gradient,
            WEIGHT_DECAY,
        )
        made[slot, part, 0, rows_at] = gradient
        made[slot, part, 1, rows_at] = update
        made[slot, part, 2, rows_at] = first_new
        made[slot, part, 3, rows_at] = second_new

    def forward_turn(turn):
        slot = lax.rem(turn, 2)
        block = lax.rem(d + turn, plane)

        @pl.when(turn + 1 < plane)
        def _():
            for part in range(3):
                for which in range(3):
                    state_copy(turn + 1, part, which).start()

        @pl.when(turn > 1)
        def _():
            for part in range(3):
                for which in range(4):
                    made_copy(turn - 2, part, which).wait()

        for part in range(3):
            for which in range(3):
                state_copy(turn, part, which).wait()

            @pl.loop(0, rows // 16)
            def _(at, part=part):
                rows_at = pl.ds(pl.multiple_of(at * 16, 16), 16)
                if part < 2:
                    gradient = gate_in[
                        block, rows_at, pl.ds(part * own_hidden, own_hidden)
                    ].astype(FULL)
                else:
                    gradient = down_in[block, rows_at].astype(FULL)
                step_rows(slot, part, at, gradient)

            for which in range(4):
                made_copy(turn, part, which).start()

    for one in own_swap:
        one.wait()
    for step in range(1, plane):
        for part in range(2):
            swap_copy(step, part).wait_recv()
    each = plane // lines
    for turn in range(lines):
        lax.fori_loop(turn * each, (turn + 1) * each, lambda k, c: (forward_turn(k), c)[1], 0)
        line = line_at(turn)
        for step in range(1, chips):
            plane_copy(turn, step).wait_recv()

        @pl.loop(0, tiles)
        def _(at, line=line):
            columns = pl.ds(pl.multiple_of(at * tile, tile), tile)
            total = mine[line, chip, :, columns].astype(FULL) + core_in[
                line, chip, :, columns
            ].astype(FULL)
            for step in range(1, chips):
                total = total + plane_in[line, lax.rem(chip + step, chips), :, columns].astype(FULL)
            core_in[line, chip, :, columns] = total.astype(LOW)

        if turn < lines - 1:
            line_copy(turn).start()

    for part in range(3):
        for which in range(4):
            for turn in (plane - 2, plane - 1):
                made_copy(turn, part, which).wait()
    for turn in range(lines - 1):
        line_copy(turn).wait_recv()
    for which in range(3):
        a_state_copy(which).wait()

    def owned(columns):
        total = core_in[g, chip, :, columns].astype(FULL)
        for step in range(1, lines):
            total = total + line_in[lax.rem(g + step, lines), :, columns].astype(FULL)
        return total

    @pl.loop(0, (query_width + pair_width) // 256)
    def _(at):
        columns = pl.ds(pl.multiple_of(at * 256, 256), 256)
        gradient = owned(columns)
        update, first_new, second_new = adam_step(
            a_state[0, :, columns],
            a_state[1, :, columns],
            a_state[2, :, columns],
            gradient,
            WEIGHT_DECAY,
        )
        a_made[0, :, columns] = gradient
        a_made[1, :, columns] = update
        a_made[2, :, columns] = first_new
        a_made[3, :, columns] = second_new

    for which in range(4):
        a_made_copy(which).start()
    gain_made[...] = owned(pl.ds(query_width + pair_width, GAIN_PAD))
    gain_copy = pltpu.make_async_copy(gain_made, gain_out, gain_sem.at[0])
    gain_copy.start()
    for turn in range(lines):
        for part in range(3):
            core_copy(turn, part).wait_send()
        for step in range(1, chips):
            plane_copy(turn, step).wait_send()
        if turn < lines - 1:
            line_copy(turn).wait_send()
    for step in range(1, plane):
        for part in range(2):
            swap_copy(step, part).wait_send()
    for which in range(4):
        a_made_copy(which).wait()
    gain_copy.wait()


def finish(query_term, pair_term, gain_term, gate_part, down_part, attention, forward):
    lines, plane = lax.axis_size("grp"), lax.axis_size("dp")
    chips = plane // 2
    rows, a_width = attention[0].shape
    f_width = forward[0].shape[1]
    own_hidden = down_part.shape[1]
    width = a_width + GAIN_PAD
    anywhere = pl.BlockSpec(memory_space=pl.ANY)
    dma = pltpu.SemaphoreType.DMA
    vmem = pltpu.VMEM

    def by_device(term):
        return term.reshape(lines, chips, 2, rows, term.shape[1])

    a_shape = jax.ShapeDtypeStruct((rows, a_width), FULL)
    f_shape = jax.ShapeDtypeStruct((rows, f_width), FULL)
    return pl.pallas_call(
        functools.partial(finish_kernel, lines, plane),
        out_shape=(a_shape,) * 4
        + (jax.ShapeDtypeStruct((rows, GAIN_PAD), FULL),)
        + (f_shape,) * 4,
        in_specs=[anywhere] * 11,
        out_specs=(anywhere,) * 9,
        scratch_shapes=[
            vmem((lines, chips, rows, width), LOW),
            vmem((lines, chips, rows, width), LOW),
            vmem((lines, chips, rows, width), LOW),
            vmem((lines, rows, width), LOW),
            vmem((plane, rows, 2 * own_hidden), LOW),
            vmem((plane, rows, own_hidden), LOW),
            vmem((2, 3, 3, rows, own_hidden), FULL),
            vmem((2, 3, 4, rows, own_hidden), FULL),
            vmem((3, rows, a_width), FULL),
            vmem((4, rows, a_width), FULL),
            vmem((rows, GAIN_PAD), FULL),
            dma((lines, 3)),
            dma((lines, 3)),
            dma((lines, 3)),
            dma((lines, chips)),
            dma((lines, chips)),
            dma((lines,)),
            dma((lines,)),
            dma((plane, 2)),
            dma((plane, 2)),
            dma((2,)),
            dma((2, 3, 3)),
            dma((2, 3, 4)),
            dma((7,)),
            dma((1,)),
        ],
        compiler_params=pltpu.CompilerParams(
            collective_id=1, has_side_effects=True, vmem_limit_bytes=60 * 2**20
        ),
        name="finish",
    )(
        by_device(query_term),
        by_device(pair_term),
        by_device(gain_term),
        gate_part.reshape(plane, rows, -1),
        down_part.reshape(plane, rows, -1),
        *attention,
        *forward,
    )


def body(
    hidden,
    cotangent,
    segment_ids,
    continuation_prompt,
    gain_master,
    gain_first,
    gain_second,
    attention_master,
    attention_first,
    attention_second,
    merge_master,
    merge_first,
    merge_second,
    feedforward_master,
    feedforward_first,
    feedforward_second,
):
    group_index = lax.axis_index("grp")
    dp_size = lax.axis_size("dp")
    row_count = hidden.shape[2]
    prompt_rows = row_count - CONT
    query_width = HQ * HD
    key_width = HK * HD
    qkv_width = query_width + 2 * key_width
    group_heads = HQ // HK
    score_scale = HD ** (-0.5)
    key_count = PROMPT_LEN + CONT
    own_rows = feedforward_master.shape[0]
    own_hidden = FF // dp_size
    own_inputs = hidden.reshape(row_count, D)

    gain_columns = jnp.pad(gain_master.T, ((0, 0), (0, GAIN_PAD - 2)))
    weight_low = jnp.concatenate(
        [attention_master.astype(LOW), merge_master.astype(LOW), gain_columns.astype(LOW)], axis=1
    )
    weights, group_rows, gate_rows, down_rows = gather_start(
        weight_low, own_inputs, feedforward_master.astype(LOW)
    )
    weights, late_cotangent = lax.optimization_barrier((weights, cotangent))
    weights = weights.reshape(D, -1)
    attention_weight = weights[:, :qkv_width]
    merge_weight = weights[:, qkv_width : qkv_width + D]
    gain_float = weights[:, qkv_width + D : qkv_width + D + 2].astype(FULL).T
    gate_weight = lax.all_gather(
        gate_rows.reshape(dp_size * own_rows, 2 * own_hidden), "grp", axis=0, tiled=True
    )
    gate_weight, down_rows = lax.optimization_barrier((gate_weight, down_rows))
    down_weight = lax.all_gather(
        down_rows.reshape(dp_size * own_rows, own_hidden), "grp", axis=0, tiled=True
    )
    down_grad = plane_gather(late_cotangent.reshape(row_count, D))

    segment_row = segment_ids[0]
    source_row = continuation_prompt[0]
    prompt_positions, follow_positions = segment_positions(segment_row, source_row)
    cosine, sine_part = angle_table(jnp.concatenate([prompt_positions, follow_positions[0]]))

    def own_part(table):
        return jnp.concatenate(
            [
                lax.dynamic_slice_in_dim(table, group_index * prompt_rows, prompt_rows),
                table[PROMPT_LEN:],
            ]
        )

    own_cosine = own_part(cosine)[:, None, :]
    own_sine = own_part(sine_part)[:, None, :]
    cosine = cosine[:, None, :]
    sine_part = sine_part[:, None, :]

    inputs = own_inputs.astype(FULL)
    first_scale = norm_scale(inputs)
    normed = (inputs * first_scale * gain_float[0]).astype(LOW)
    key_inputs = jnp.concatenate(
        [group_rows.reshape(PROMPT_LEN, D), own_inputs[prompt_rows:]], axis=0
    ).astype(FULL)
    key_scale = norm_scale(key_inputs)
    key_normed = (key_inputs * key_scale * gain_float[0]).astype(LOW)
    query_weight = attention_weight[:, :query_width]
    pair_weight = attention_weight[:, query_width:]
    queries = rotate(
        jnp.dot(normed, query_weight, preferred_element_type=FULL).reshape(row_count, HQ, HD),
        own_cosine,
        own_sine,
    ).astype(LOW)
    pairs = jnp.dot(key_normed, pair_weight, preferred_element_type=FULL)
    all_keys = rotate(
        pairs[:, :key_width].reshape(key_count, HK, HD), cosine, sine_part
    ).astype(LOW)
    all_values = pairs[:, key_width:].astype(LOW).reshape(key_count, HK, HD)

    row_index = jnp.arange(row_count, dtype=jnp.int32)
    is_prompt = row_index < prompt_rows
    global_row = group_index * prompt_rows + jnp.minimum(row_index, prompt_rows - 1)
    own_segment = lax.dynamic_slice_in_dim(segment_row, group_index * prompt_rows, prompt_rows)
    query_segment = jnp.concatenate([own_segment, jnp.broadcast_to(source_row, (CONT,))])
    key_index = jnp.arange(PROMPT_LEN, dtype=jnp.int32)
    prompt_seen = (segment_row[None, :] == query_segment[:, None]) & (
        (key_index[None, :] <= global_row[:, None]) | ~is_prompt[:, None]
    )
    follow_seen = (~is_prompt)[:, None] & (
        jnp.arange(CONT, dtype=jnp.int32)[None, :] <= (row_index - prompt_rows)[:, None]
    )
    visible = jnp.concatenate([prompt_seen, follow_seen], axis=1)
    head_queries = queries.reshape(row_count, HK, group_heads, HD)
    scores = masked_scores(head_queries, all_keys, visible, score_scale)
    row_peak = jnp.max(scores, axis=-1, keepdims=True)
    unnormed = jnp.exp(scores - row_peak)
    row_total = jnp.sum(unnormed, axis=-1, keepdims=True)
    probability_low = (unnormed / row_total).astype(LOW)
    row_logsum = row_peak + jnp.log(row_total)
    attended = (
        jnp.einsum("kgrs,skd->rkgd", probability_low, all_values, preferred_element_type=FULL)
        .reshape(row_count, query_width)
        .astype(LOW)
    )
    middle = inputs + contract(attended, merge_weight, 1, 1)
    second_scale = norm_scale(middle)
    normed_two = (middle * second_scale * gain_float[1]).astype(LOW)
    grad_rows = cotangent.reshape(row_count, D).astype(FULL)

    normed_two, down_grad = lax.optimization_barrier((normed_two, down_grad))
    normed_all = plane_gather(normed_two)
    gate_up = jnp.dot(normed_all, gate_weight, preferred_element_type=FULL)
    gate_values = gate_up[:, :own_hidden]
    up_values = gate_up[:, own_hidden:]
    gate_sigmoid, gate_silu, activated = gate_parts(gate_values, up_values)
    activated_grad = contract(down_grad, down_weight, 1, 0)
    gate_grad, up_grad = gate_backward(
        activated_grad, gate_values, up_values, gate_sigmoid, gate_silu
    )
    gate_up_grad = jnp.concatenate([gate_grad, up_grad], axis=1)

    def by_offset(left, right, right_axis):
        chunks = {}
        for offset in range(0, dp_size, 2):
            rows = left[offset * row_count : (offset + 2) * row_count]
            chunks[offset] = contract(rows, right, 1, right_axis).astype(LOW)
        return lambda offset: chunks[offset - offset % 2][
            (offset % 2) * row_count : (offset % 2 + 1) * row_count
        ]

    down_term = contract(down_grad, activated, 0, 0).astype(LOW)
    back_parts = by_offset(gate_up_grad, gate_weight, 1)
    gate_term = contract(normed_all, gate_up_grad, 0, 0).astype(LOW)
    normed_two_grad = plane_scatter(back_parts)
    down_part = line_scatter(down_term)
    gate_term, down_part = lax.optimization_barrier((gate_term, down_part))
    gate_part = line_scatter(gate_term)
    normed_two_grad, activated = lax.optimization_barrier((normed_two_grad, activated))
    result = middle + plane_scatter(by_offset(activated, down_weight, 1))
    block_output = result.astype(LOW).reshape(hidden.shape)
    middle_grad = grad_rows + norm_back(middle, second_scale, gain_float[1], normed_two_grad)
    gain_two_part = jnp.sum(normed_two_grad * middle * second_scale, axis=0)
    branch_grad = middle_grad.astype(LOW)
    merge_part = plane_rows(contract(branch_grad, attended, 0, 0).astype(LOW))
    merge_part, gate_part = lax.optimization_barrier((merge_part, gate_part))
    merge_grad = line_scatter(merge_part).astype(FULL)
    attended_grad = (
        contract(branch_grad, merge_weight, 1, 0)
        .astype(LOW)
        .reshape(row_count, HK, group_heads, HD)
    )
    scores = masked_scores(head_queries, all_keys, visible, score_scale)
    probabilities = jnp.exp(scores - row_logsum)
    probability_grad = jnp.einsum(
        "rkgd,skd->kgrs", attended_grad, all_values, preferred_element_type=FULL
    )
    row_delta = jnp.sum(probabilities * probability_grad, axis=-1, keepdims=True)
    score_grad = (probabilities * (probability_grad - row_delta)).astype(LOW)
    query_grad = (
        jnp.einsum("kgrs,skd->rkgd", score_grad, all_keys, preferred_element_type=FULL)
        * score_scale
    )
    key_grad = (
        jnp.einsum("kgrs,rkgd->skd", score_grad, head_queries, preferred_element_type=FULL)
        * score_scale
    )
    value_grad = jnp.einsum(
        "kgrs,rkgd->skd", probabilities.astype(LOW), attended_grad, preferred_element_type=FULL
    )
    query_project = (
        rotate(query_grad.reshape(row_count, HQ, HD), own_cosine, -own_sine)
        .reshape(row_count, query_width)
        .astype(LOW)
    )
    pair_project = jnp.concatenate(
        [
            rotate(key_grad, cosine, -sine_part).reshape(key_count, key_width),
            value_grad.reshape(key_count, key_width),
        ],
        axis=1,
    ).astype(LOW)
    query_back = contract(query_project, query_weight, 1, 1)
    pair_back = contract(pair_project, pair_weight, 1, 1)
    gain_one_part = jnp.sum(query_back * inputs * first_scale, axis=0) + jnp.sum(
        pair_back * key_inputs * key_scale, axis=0
    )
    gain_term = jnp.pad(
        jnp.stack([gain_one_part, gain_two_part], axis=1), ((0, 0), (0, GAIN_PAD - 2))
    )
    pair_low = pair_back[:PROMPT_LEN].astype(LOW)
    pair_low, merge_grad = lax.optimization_barrier((pair_low, merge_grad))
    finished = finish(
        contract(normed, query_project, 0, 0).astype(LOW),
        contract(key_normed, pair_project, 0, 0).astype(LOW),
        gain_term.astype(LOW),
        gate_part,
        down_part,
        (attention_master, attention_first, attention_second),
        (feedforward_master, feedforward_first, feedforward_second),
    )
    gain_grad = finished[4][:, :2].T
    pair_sum = lax.psum_scatter(
        pair_low, "grp", scatter_dimension=0, tiled=True
    ).astype(FULL)
    normed_grad = query_back + jnp.concatenate([pair_sum, pair_back[PROMPT_LEN:]], axis=0)
    input_grad = (middle_grad + norm_back(inputs, first_scale, gain_float[0], normed_grad)).reshape(
        hidden.shape
    )
    gain_new = adam_step(gain_master, gain_first, gain_second, gain_grad, 0.0)
    merge_new = adam_step(merge_master, merge_first, merge_second, merge_grad, WEIGHT_DECAY)
    return (
        block_output,
        input_grad,
        gain_grad,
        *gain_new,
        *finished[:4],
        merge_grad,
        *merge_new,
        *finished[5:],
    )


def solution(mesh):
    tokens = P("dp", "grp", None, None)
    gains = P(None, ("grp", "dp"))
    matrix = P(("grp", "dp"), None)
    return jax.shard_map(
        body,
        mesh=mesh,
        in_specs=(tokens, tokens, P("dp", None), P("dp", "grp")) + (gains,) * 3 + (matrix,) * 9,
        out_specs=(tokens, tokens) + (gains,) * 4 + (matrix,) * 12,
        check_vma=False,
    )
```

time: 3400 us -> 1120 us (0.33)
  waiting for transfers between devices: 2780 us -> 285 us
  Pallas kernels: 0 us -> 297 us
  other arithmetic: 201 us -> 79.6 us
  local copies, waits for them, and re-layouts: 68.4 us -> 133 us
  blocking collectives: 35.7 us -> 0 us
    reduce_scatter x4, waiting for transfers between devices: 2080 us -> 55.6 us  [the longest x1 46.6 us: body(): lax.psum_scatter(pair_low, 'grp', scatter_dimension=0, tiled=True)]
    all_gather x4 -> x2, waiting for transfers between devices: 702 us -> 42.8 us  [the longest x1 42.8 us: body(): lax.all_gather(down_rows.reshape(dp_size * own_rows, own_hidden), 'grp',...]
    pallas_call x0 -> x2, Pallas kernels: none -> 297 us  [the longest x1 161 us: gather_start(): pl.pallas_call(functools.partial(gather_kernel, lines, plane, prompt_rows...]
    ppermute x0 -> x35, waiting for transfers between devices: none -> 186 us  [plane_swap(): return lax.ppermute(block, 'dp', [(i, i ^ offset) for i in range(size)])]
    concatenate x5 -> x2, other arithmetic: 139 us -> 1.89 us  [the longest x1 0.95 us: own_part(): jnp.concatenate([lax.dynamic_slice_in_dim(table, group_index * prompt_row...]
    unnamed x124 -> x220, local copies, waits for them, and re-layouts: 20.6 us -> 61.3 us
    all_gather x1 -> x0, blocking collectives: 35.7 us -> none  [body(): lax.all_gather(gain_low, ('grp', 'dp'), axis=1, tiled=True)]
    dot_general x10 -> x18, matrix products: 209 us -> 192 us  [contract(): lax.dot_general(left, right, (((left_axis,), (right_axis,)), ((), ())), p...]
  transfers between devices with their start and end apart: 9 -> 41, of which waited for: 8 -> 14; matrix products, arithmetic and copies ran while one was open for 10% -> 33% of each run, Pallas kernels for 0% -> 0%
where the time goes in v2:
time: 1120 us; the launch traced here: 1100 us
  Pallas kernels  297 us (27%)
  waiting for transfers between devices  285 us (25%)
  matrix products  263 us (23%)
  local copies, waits for them, and re-layouts  133 us (12%)
  other arithmetic  79.6 us (7%)
  starting transfers between devices  29.2 us (3%)
  between operations  16.8 us (2%)
    dot_general x18, matrix products, contract(): lax.dot_general(left, right, (((left_axis,), (right_axis,)), ((), ())), p...  192 us
    ppermute x35, waiting for transfers between devices, plane_swap(): return lax.ppermute(block, 'dp', [(i, i ^ offset) for i in range(size)])  186 us
    pallas_call x1, Pallas kernels, gather_start(): pl.pallas_call(functools.partial(gather_kernel, lines, plane, prompt_rows...  161 us
    pallas_call x1, Pallas kernels, finish(): pl.pallas_call(functools.partial(finish_kernel, lines, plane), out_shape=...  135 us
    unnamed x220, local copies, waits for them, and re-layouts  61.3 us
    reduce_scatter x1, waiting for transfers between devices, body(): lax.psum_scatter(pair_low, 'grp', scatter_dimension=0, tiled=True)  46.6 us
    all_gather x1, waiting for transfers between devices, body(): lax.all_gather(down_rows.reshape(dp_size * own_rows, own_hidden), 'grp',...  42.8 us
    ppermute x35, starting transfers between devices, plane_swap(): return lax.ppermute(block, 'dp', [(i, i ^ offset) for i in range(size)])  28.8 us
  transfers between devices with their start and end apart: 41, of which 14 were waited for; matrix products, arithmetic and copies ran while one was open for 33% of the time, Pallas kernels for 0%

profile of v2, /device:TPU:9, one launch (start us, length us, event | category | flops | bytes accessed | tf_op | source)
XLA Modules:
  0.0 1102.9 jit_solution(13500280527866451776)
XLA Ops:
  13.3 161.4 %gather_start.1 = (bf16[4,8,64,6272]{3,2,1,0:T(8,128)(2,1)}, bf16[4,256,2048]{2,1,0:T(8,128)(2,1)}, bf16[8,64,2048]{2,1,0:T(8,128)(2,1)}, bf16[8,64,1024]{2,1,0:T(8,128)(2,1)}) custom-call(bf16[64,6272]{1,0:T(8,128)(2,1)} %fusion.85.weight_ref, bf16[320,2048]{1,0:T(8,128)(2,1)} %bitcast.157, bf16[64,24576]{1,0:T(8,128)(2,1)} %convert_element_type.300.forward_ref), custom_call_target="tpu_custom_call" | custom-call | tf_op jit(solution)/shard_map/gather_start/pallas_call | solution.py:396
  182.0 8.4 slice_bitcast_fusion
  195.9 12.3 %fusion.21 = f32[1088,2048]{1,0:T(8,128)S(1)} fusion(bf16[2048,6272]{1,0:T(8,128)(2,1)} %bitcast.179, f32[2048]{0:T(1024)S(1)} %bitcast.215, f32[1088]{0:T(1024)S(1)} %add_rsqrt_fusion, bf16[64,2048]{1,0:T(8,128)(2,1)S(1)} %slice_bitcast_fusion.1, bf16[1024,2048]{1,0:T(8,128)(2,1)S(1)} %bitcast.175), kind=kOutput, calls=%fused_computation.48 | convolution fusion | flops 9142403072 | bytes 21770496 | tf_op jit(solution)/shard_map/dot_general | solution.py:925
  221.1 12.3 %copy.119 = bf16[2048,2048]{1,0:T(8,128)(2,1)} copy(bf16[2048,2048]{0,1:T(8,128)(2,1)} %slice_bitcast_fusion) | data formatting | bytes 16777216 | tf_op jit(solution)/shard_map/dot_general | solution.py:921
  233.4 6.2 reshape.377
  290.1 27.0 %collective-permute-done.8 = bf16[320,2048]{1,0:T(8,128)(2,1)} collective-permute-done((bf16[320,2048]{1,0:T(8,128)(2,1)S(1)}, bf16[320,2048]{1,0:T(8,128)(2,1)}, u32[]{:S(2)}, u32[]{:S(2)}) %collective-permute-start.8) | collective-permute-done | bytes 1310752 | tf_op jit(solution)/shard_map/ppermute | solution.py:414
  318.3 28.0 %collective-permute-done.10 = bf16[320,2048]{1,0:T(8,128)(2,1)} collective-permute-done((bf16[320,2048]{1,0:T(8,128)(2,1)S(1)}, bf16[320,2048]{1,0:T(8,128)(2,1)}, u32[]{:S(2)}, u32[]{:S(2)}) %collective-permute-start.10) | collective-permute-done | bytes 1310752 | tf_op jit(solution)/shard_map/ppermute | solution.py:414
  359.1 27.0 %fusion.112 = f32[2560,2048]{0,1:T(8,128)} fusion(bf16[2560,2048]{1,0:T(8,128)(2,1)S(1)} %constant_dynamic-update-slice_fusion.8, bf16[2048,2048]{1,0:T(8,128)(2,1)} %all-gather.3.cloned.1.call-done), kind=kOutput, calls=%fused_computation.237 | convolution fusion | flops 21474836480 | bytes 39845888 | tf_op jit(solution)/shard_map/dot_general | solution.py:963
  386.2 42.8 %all-gather.5.cloned.1.call-done = bf16[2048,1024]{1,0:T(8,128)(2,1)} async-done(((bf16[512,1024]{1,0:T(8,128)(2,1)}), bf16[2048,1024]{1,0:T(8,128)(2,1)}) %all-gather.5.cloned.1.call-update) | async-done | bytes 4194320 | tf_op jit(solution)/shard_map/all_gather | solution.py:887
  428.9 25.8 %multiply_convert_fusion.1 = (bf16[2560,1024]{0,1:T(8,128)(2,1)}, bf16[2560,1024]{0,1:T(8,128)(2,1)}, bf16[2560,1024]{0,1:T(8,128)(2,1)}) fusion(f32[2560,2048]{0,1:T(8,128)} %fusion.112, bf16[2560,2048]{1,0:T(8,128)(2,1)} %copy-done.54, bf16[2048,1024]{1,0:T(8,128)(2,1)} %all-gather.5.cloned.1.call-done), kind=kOutput, calls=%fused_computation.23 | convolution fusion | flops 10776739840 | bytes 51380224 | tf_op jit(solution)/shard_map/dot_general | solution.py:35
  454.7 9.5 convolution_convert_fusion.6
  467.5 15.1 %convolution_convert_fusion.3 = bf16[2048,1024]{1,0:T(8,128)(2,1)} fusion(bf16[2560,2048]{1,0:T(8,128)(2,1)} %copy-done.54, bf16[2560,1024]{0,1:T(8,128)(2,1)S(1)} %copy-done.77), kind=kOutput, calls=%fused_computation.64 | convolution fusion | flops 10739515392 | bytes 19922944 | tf_op jit(solution)/shard_map/dot_general | solution.py:35
  482.7 8.9 convolution_convert_fusion.5
  493.6 9.7 convolution_convert_fusion.4
  506.5 29.4 %fusion.12 = bf16[2048,2048]{1,0:T(8,128)(2,1)} fusion(bf16[2560,2048]{1,0:T(8,128)(2,1)S(1)} %bitcast.204, bf16[2560,1024]{0,1:T(8,128)(2,1)S(1)} %bitcast.225, bf16[2560,1024]{0,1:T(8,128)(2,1)} %get-tuple-element.156), kind=kOutput, calls=%fused_computation.35 | convolution fusion | flops 21500002304 | bytes 29360128 | tf_op jit(solution)/shard_map/dot_general | solution.py:35
  535.8 8.9 convolution_convert_fusion.7
  564.9 15.5 %collective-permute-done.16 = bf16[320,2048]{1,0:T(8,128)(2,1)} collective-permute-done((bf16[320,2048]{1,0:T(8,128)(2,1)}, bf16[320,2048]{1,0:T(8,128)(2,1)}, u32[]{:S(2)}, u32[]{:S(2)}) %collective-permute-start.16) | collective-permute-done | bytes 1310752 | tf_op jit(solution)/shard_map/ppermute | solution.py:414
  580.4 32.1 %collective-permute-done.18 = bf16[320,2048]{1,0:T(8,128)(2,1)} collective-permute-done((bf16[320,2048]{1,0:T(8,128)(2,1)}, bf16[320,2048]{1,0:T(8,128)(2,1)}, u32[]{:S(2)}, u32[]{:S(2)}) %collective-permute-start.18) | collective-permute-done | bytes 1310752 | tf_op jit(solution)/shard_map/ppermute | solution.py:414
  645.1 21.7 %collective-permute-done.23 = bf16[320,2048]{1,0:T(8,128)(2,1)} collective-permute-done((bf16[320,2048]{1,0:T(8,128)(2,1)}, bf16[320,2048]{1,0:T(8,128)(2,1)}, u32[]{:S(2)}, u32[]{:S(2)}) %collective-permute-start.23) | collective-permute-done | bytes 1310752 | tf_op jit(solution)/shard_map/ppermute | solution.py:414
  666.8 28.5 %collective-permute-done.25 = bf16[320,2048]{1,0:T(8,128)(2,1)} collective-permute-done((bf16[320,2048]{1,0:T(8,128)(2,1)}, bf16[320,2048]{1,0:T(8,128)(2,1)}, u32[]{:S(2)}, u32[]{:S(2)}) %collective-permute-start.25) | collective-permute-done | bytes 1310752 | tf_op jit(solution)/shard_map/ppermute | solution.py:414
  702.7 7.4 fusion.35
  714.6 10.1 convolution_convert_fusion.2
  737.2 6.3 fusion.2
  757.0 7.3 fusion.30
  766.8 9.4 collective-permute-done.30
  777.3 22.6 %collective-permute-done.34 = bf16[4,64,2048]{2,1,0:T(8,128)(2,1)} collective-permute-done((bf16[4,64,2048]{2,1,0:T(8,128)(2,1)}, bf16[4,64,2048]{2,1,0:T(8,128)(2,1)}, u32[]{:S(2)}, u32[]{:S(2)}) %collective-permute-start.34) | collective-permute-done | bytes 1048608 | tf_op jit(solution)/shard_map/ppermute | solution.py:414
  804.4 16.1 %fusion.11 = (f32[2048]{0:T(1024)S(1)}, f32[1088,2048]{1,0:T(8,128)S(1)}) fusion(f32[1088]{0:T(1024)S(1)} %copy-done.69, bf16[64,2048]{1,0:T(8,128)(2,1)S(1)} %copy-done.45, bf16[1024,2048]{1,0:T(8,128)(2,1)} %bitcast.174, bf16[2048,6272]{1,0:T(8,128)(2,1)} %bitcast.182, bf16[1088,1024]{0,1:T(8,128)(2,1)} %bitcast.191, bf16[1088,1024]{0,1:T(8,128)(2,1)} %bitcast.189), kind=kOutput, calls=%fused_computation.33 | convolution fusion | flops 9151313920 | bytes 26489088 | tf_op jit(solution)/shard_map/dot_general | solution.py:35
  840.6 7.0 convolution_convert_fusion.1
  847.6 15.4 %convolution_convert_fusion = bf16[2048,2048]{1,0:T(8,128)(2,1)} fusion(bf16[1088,1024]{0,1:T(8,128)(2,1)} %bitcast.192, bf16[1088,1024]{0,1:T(8,128)(2,1)S(1)} %bitcast.190, f32[2048]{0:T(1024)S(1)} %bitcast.218, f32[1088]{0:T(1024)S(1)} %copy-done.69, bf16[64,2048]{1,0:T(8,128)(2,1)S(1)} %copy-done.45, bf16[1024,2048]{1,0:T(8,128)(2,1)S(1)} %bitcast.176), kind=kOutput, calls=%fused_computation.36 | convolution fusion | flops 9155510272 | bytes 17314048 | tf_op jit(solution)/shard_map/dot_general | solution.py:35
  864.4 46.6 %reduce-scatter.11.cloned.1.call-done = bf16[256,2048]{1,0:T(8,128)(2,1)} async-done(((bf16[1024,2048]{1,0:T(8,128)(2,1)}), bf16[256,2048]{1,0:T(8,128)(2,1)}) %reduce-scatter.11.cloned.1.call-update) | async-done | bytes 1048592 | tf_op jit(solution)/shard_map/reduce_scatter | solution.py:1053
  912.4 9.3 fusion.45
  924.8 135.1 %finish.1 = (f32[64,4096]{1,0:T(8,128)}, f32[64,4096]{1,0:T(8,128)}, f32[64,4096]{1,0:T(8,128)}, f32[64,4096]{1,0:T(8,128)}, f32[64,128]{1,0:T(8,128)}, /*index=...) custom-call(bf16[4,4,2,64,2048]{4,3,2,1,0:T(8,128)(2,1)} %bitcast.164, ...), custom_call_target="tpu_custom_call" | custom-call | tf_op jit(solution)/shard_map/finish/pallas_call | solution.py:790
  (418 shorter events, 263.2 us)
Async XLA Ops:
  7.2 340.2 %all-gather.3.cloned.1.call-start = ((), (), s32[]{:S(2)}) async-start(), calls=%async_computation.4 | async-start | bytes 10485760 | tf_op jit(solution)/shard_map/all_gather | solution.py:883
  174.8 105.7 %collective-permute-start = (bf16[320,2048]{1,0:T(8,128)(2,1)}, bf16[320,2048]{1,0:T(8,128)(2,1)}, u32[]{:S(2)}, u32[]{:S(2)}) collective-permute-start(bf16[320,2048]{1,0:T(8,128)(2,1)} %bitcast.22), channel_id=1, source_target_pairs={{0,1},{1,0},{2,3},{3,2},{4,5},{5,4},{6,7},{7,6},{8,9},{9,8},{10,11... | collective-permute-start | bytes 3932168 | tf_op jit(solution)/shard_map/ppermute | solution.py:414
  177.6 99.4 %collective-permute-start.1 = (bf16[320,2048]{1,0:T(8,128)(2,1)}, bf16[320,2048]{1,0:T(8,128)(2,1)}, u32[]{:S(2)}, u32[]{:S(2)}) collective-permute-start(bf16[320,2048]{1,0:T(8,128)(2,1)} %bitcast.22), channel_id=1, source_target_pairs={{0,2},{1,3},{2,0},{3,1},{4,6},{5,7},{6,4},{7,5},{8,10},{9,11},{10,... | collective-permute-start | bytes 3932168 | tf_op jit(solution)/shard_map/ppermute | solution.py:414
  179.0 99.4 %collective-permute-start.3 = (bf16[320,2048]{1,0:T(8,128)(2,1)}, bf16[320,2048]{1,0:T(8,128)(2,1)}, u32[]{:S(2)}, u32[]{:S(2)}) collective-permute-start(bf16[320,2048]{1,0:T(8,128)(2,1)} %bitcast.22), channel_id=1, source_target_pairs={{0,4},{1,5},{2,6},{3,7},{4,0},{5,1},{6,2},{7,3},{8,12},{9,13},{10,... | collective-permute-start | bytes 3932168 | tf_op jit(solution)/shard_map/ppermute | solution.py:414
  179.0 100.9 %collective-permute-start.5 = (bf16[320,2048]{1,0:T(8,128)(2,1)}, bf16[320,2048]{1,0:T(8,128)(2,1)}, u32[]{:S(2)}, u32[]{:S(2)}) collective-permute-start(bf16[320,2048]{1,0:T(8,128)(2,1)} %bitcast.22), channel_id=1, source_target_pairs={{0,6},{1,7},{2,4},{3,5},{4,2},{5,3},{6,0},{7,1},{8,14},{9,15},{10,... | collective-permute-start | bytes 3932168 | tf_op jit(solution)/shard_map/ppermute | solution.py:414
  180.3 248.6 %all-gather.5.cloned.1.call-start = ((), (), s32[]{:S(2)}) async-start(), calls=%async_computation.5 | async-start | bytes 5242880 | tf_op jit(solution)/shard_map/all_gather | solution.py:887
  286.6 30.6 %collective-permute-start.8 = (bf16[320,2048]{1,0:T(8,128)(2,1)S(1)}, bf16[320,2048]{1,0:T(8,128)(2,1)}, u32[]{:S(2)}, u32[]{:S(2)}) collective-permute-start(bf16[320,2048]{1,0:T(8,128)(2,1)S(1)} %multiply_convert_fusion.3), channel_id=1, source_target_pairs={{0,2},{1,3},{2,0},{3,1},{4,6},{5,7},{6,4},{7,5},{8,10},{9,11},{10,... | collective-permute-start | bytes 3932168 | tf_op jit(solution)/shard_map/ppermute | solution.py:414
  288.1 58.3 %collective-permute-start.10 = (bf16[320,2048]{1,0:T(8,128)(2,1)S(1)}, bf16[320,2048]{1,0:T(8,128)(2,1)}, u32[]{:S(2)}, u32[]{:S(2)}) collective-permute-start(bf16[320,2048]{1,0:T(8,128)(2,1)S(1)} %multiply_convert_fusion.3), channel_id=1, source_target_pairs={{0,4},{1,5},{2,6},{3,7},{4,0},{5,1},{6,2},{7,3},{8,12},{9,13},{10,... | collective-permute-start | bytes 3932168 | tf_op jit(solution)/shard_map/ppermute | solution.py:414
  288.1 59.6 %collective-permute-start.12 = (bf16[320,2048]{1,0:T(8,128)(2,1)S(1)}, bf16[320,2048]{1,0:T(8,128)(2,1)S(1)}, u32[]{:S(2)}, u32[]{:S(2)}) collective-permute-start(bf16[320,2048]{1,0:T(8,128)(2,1)S(1)} %multiply_convert_fusion.3), channel_id=1, source_target_pairs={{0,6},{1,7},{2,4},{3,5},{4,2},{5,3},{6,0},{7,1},{8,14},{9,15},{10,... | collective-permute-start | bytes 3932168 | tf_op jit(solution)/shard_map/ppermute | solution.py:414
  289.3 58.4 %collective-permute-start.7 = (bf16[320,2048]{1,0:T(8,128)(2,1)S(1)}, bf16[320,2048]{1,0:T(8,128)(2,1)}, u32[]{:S(2)}, u32[]{:S(2)}) collective-permute-start(bf16[320,2048]{1,0:T(8,128)(2,1)S(1)} %multiply_convert_fusion.3), channel_id=1, source_target_pairs={{0,1},{1,0},{2,3},{3,2},{4,5},{5,4},{6,7},{7,6},{8,9},{9,8},{10,11... | collective-permute-start | bytes 3932168 | tf_op jit(solution)/shard_map/ppermute | solution.py:414
  317.1 33.4 %collective-permute-start.9 = (bf16[320,2048]{1,0:T(8,128)(2,1)}, bf16[320,2048]{1,0:T(8,128)(2,1)}, u32[]{:S(2)}, u32[]{:S(2)}) collective-permute-start(bf16[320,2048]{1,0:T(8,128)(2,1)} %collective-permute-done.8), channel_id=1, source_target_pairs={{0,1},{1,0},{2,3},{3,2},{4,5},{5,4},{6,7},{7,6},{8,9},{9,8},{10,11... | collective-permute-start | bytes 3932168 | tf_op jit(solution)/shard_map/ppermute | solution.py:414
  347.5 212.8 %reduce-scatter.5.cloned.1.call-start = ((), (), s32[]{:S(2)}) async-start(), calls=%async_computation.6 | async-start | bytes 5242880 | tf_op jit(solution)/shard_map/reduce_scatter | solution.py:448
  467.0 79.0 %collective-permute-start.15 = (bf16[320,2048]{1,0:T(8,128)(2,1)}, bf16[320,2048]{1,0:T(8,128)(2,1)}, u32[]{:S(2)}, u32[]{:S(2)}) collective-permute-start(bf16[320,2048]{1,0:T(8,128)(2,1)} %slice.227), channel_id=1, source_target_pairs={{0,1},{1,0},{2,3},{3,2},{4,5},{5,4},{6,7},{7,6},{8,9},{9,8},{10,11... | collective-permute-start | bytes 3932168 | tf_op jit(solution)/shard_map/ppermute | solution.py:414
  482.6 321.7 %reduce-scatter.7.cloned.1.call-start = ((), (), s32[]{:S(2)}) async-start(), calls=%async_computation.7 | async-start | bytes 10485760 | tf_op jit(solution)/shard_map/reduce_scatter | solution.py:448
  493.6 57.6 %collective-permute-start.17 = (bf16[320,2048]{1,0:T(8,128)(2,1)}, bf16[320,2048]{1,0:T(8,128)(2,1)}, u32[]{:S(2)}, u32[]{:S(2)}) collective-permute-start(bf16[320,2048]{1,0:T(8,128)(2,1)} %slice.231), channel_id=1, source_target_pairs={{0,1},{1,0},{2,3},{3,2},{4,5},{5,4},{6,7},{7,6},{8,9},{9,8},{10,11... | collective-permute-start | bytes 3932168 | tf_op jit(solution)/shard_map/ppermute | solution.py:414
  506.0 54.6 %collective-permute-start.19 = (bf16[320,2048]{1,0:T(8,128)(2,1)}, bf16[320,2048]{1,0:T(8,128)(2,1)}, u32[]{:S(2)}, u32[]{:S(2)}) collective-permute-start(bf16[320,2048]{1,0:T(8,128)(2,1)} %slice.235), channel_id=1, source_target_pairs={{0,1},{1,0},{2,3},{3,2},{4,5},{5,4},{6,7},{7,6},{8,9},{9,8},{10,11... | collective-permute-start | bytes 3932168 | tf_op jit(solution)/shard_map/ppermute | solution.py:414
  545.9 19.1 %collective-permute-start.14 = (bf16[320,2048]{1,0:T(8,128)(2,1)}, bf16[320,2048]{1,0:T(8,128)(2,1)}, u32[]{:S(2)}, u32[]{:S(2)}) collective-permute-start(bf16[320,2048]{1,0:T(8,128)(2,1)} %slice.223), channel_id=1, source_target_pairs={{0,1},{1,0},{2,3},{3,2},{4,5},{5,4},{6,7},{7,6},{8,9},{9,8},{10,11... | collective-permute-start | bytes 3932168 | tf_op jit(solution)/shard_map/ppermute | solution.py:414
  549.8 30.7 %collective-permute-start.16 = (bf16[320,2048]{1,0:T(8,128)(2,1)}, bf16[320,2048]{1,0:T(8,128)(2,1)}, u32[]{:S(2)}, u32[]{:S(2)}) collective-permute-start(bf16[320,2048]{1,0:T(8,128)(2,1)} %add_convert_fusion.6), channel_id=1, source_target_pairs={{0,2},{1,3},{2,0},{3,1},{4,6},{5,7},{6,4},{7,5},{8,10},{9,11},{10,... | collective-permute-start | bytes 3932168 | tf_op jit(solution)/shard_map/ppermute | solution.py:414
  554.1 58.5 %collective-permute-start.18 = (bf16[320,2048]{1,0:T(8,128)(2,1)}, bf16[320,2048]{1,0:T(8,128)(2,1)}, u32[]{:S(2)}, u32[]{:S(2)}) collective-permute-start(bf16[320,2048]{1,0:T(8,128)(2,1)} %add_convert_fusion.5), channel_id=1, source_target_pairs={{0,4},{1,5},{2,6},{3,7},{4,0},{5,1},{6,2},{7,3},{8,12},{9,13},{10,... | collective-permute-start | bytes 3932168 | tf_op jit(solution)/shard_map/ppermute | solution.py:414
  560.3 270.4 %reduce-scatter.9.cloned.1.call-start = ((), (), s32[]{:S(2)}) async-start(), calls=%async_computation.8 | async-start | bytes 1310720 | tf_op jit(solution)/shard_map/reduce_scatter | solution.py:448
  562.8 49.8 %collective-permute-start.20 = (bf16[320,2048]{1,0:T(8,128)(2,1)S(1)}, bf16[320,2048]{1,0:T(8,128)(2,1)S(1)}, u32[]{:S(2)}, u32[]{:S(2)}) collective-permute-start(bf16[320,2048]{1,0:T(8,128)(2,1)S(1)} %add_convert_fusion.4), channel_id=1, source_target_pairs={{0,6},{1,7},{2,4},{3,5},{4,2},{5,3},{6,0},{7,1},{8,14},{9,15},{10,... | collective-permute-start | bytes 3932168 | tf_op jit(solution)/shard_map/ppermute | solution.py:414
  636.6 30.2 %collective-permute-start.23 = (bf16[320,2048]{1,0:T(8,128)(2,1)}, bf16[320,2048]{1,0:T(8,128)(2,1)}, u32[]{:S(2)}, u32[]{:S(2)}) collective-permute-start(bf16[320,2048]{1,0:T(8,128)(2,1)} %add_convert_fusion.3), channel_id=1, source_target_pairs={{0,2},{1,3},{2,0},{3,1},{4,6},{5,7},{6,4},{7,5},{8,10},{9,11},{10,... | collective-permute-start | bytes 3932168 | tf_op jit(solution)/shard_map/ppermute | solution.py:414
  638.2 57.1 %collective-permute-start.25 = (bf16[320,2048]{1,0:T(8,128)(2,1)}, bf16[320,2048]{1,0:T(8,128)(2,1)}, u32[]{:S(2)}, u32[]{:S(2)}) collective-permute-start(bf16[320,2048]{1,0:T(8,128)(2,1)} %add_convert_fusion.2), channel_id=1, source_target_pairs={{0,4},{1,5},{2,6},{3,7},{4,0},{5,1},{6,2},{7,3},{8,12},{9,13},{10,... | collective-permute-start | bytes 3932168 | tf_op jit(solution)/shard_map/ppermute | solution.py:414
  641.3 54.6 %collective-permute-start.27 = (bf16[320,2048]{1,0:T(8,128)(2,1)}, bf16[320,2048]{1,0:T(8,128)(2,1)}, u32[]{:S(2)}, u32[]{:S(2)}) collective-permute-start(bf16[320,2048]{1,0:T(8,128)(2,1)} %add_convert_fusion.1), channel_id=1, source_target_pairs={{0,6},{1,7},{2,4},{3,5},{4,2},{5,3},{6,0},{7,1},{8,14},{9,15},{10,... | collective-permute-start | bytes 3932168 | tf_op jit(solution)/shard_map/ppermute | solution.py:414
  728.8 17.8 %collective-permute-start.29 = (bf16[4,64,2048]{2,1,0:T(8,128)(2,1)}, bf16[4,64,2048]{2,1,0:T(8,128)(2,1)S(1)}, u32[]{:S(2)}, u32[]{:S(2)}) collective-permute-start(bf16[4,64,2048]{2,1,0:T(8,128)(2,1)} %get-tuple-element.160), channel_id=1, source_target_pairs={{0,1},{1,0},{2,3},{3,2},{4,5},{5,4},{6,7},{7,6},{8,9},{9,8},{10,11... | collective-permute-start | bytes 3145736 | tf_op jit(solution)/shard_map/ppermute | solution.py:414
  730.8 15.8 %collective-permute-start.31 = (bf16[4,64,2048]{2,1,0:T(8,128)(2,1)}, bf16[4,64,2048]{2,1,0:T(8,128)(2,1)}, u32[]{:S(2)}, u32[]{:S(2)}) collective-permute-start(bf16[4,64,2048]{2,1,0:T(8,128)(2,1)} %get-tuple-element.159), channel_id=1, source_target_pairs={{0,1},{1,0},{2,3},{3,2},{4,5},{5,4},{6,7},{7,6},{8,9},{9,8},{10,11... | collective-permute-start | bytes 3145736 | tf_op jit(solution)/shard_map/ppermute | solution.py:414
  730.8 15.8 %collective-permute-start.33 = (bf16[4,64,2048]{2,1,0:T(8,128)(2,1)S(1)}, bf16[4,64,2048]{2,1,0:T(8,128)(2,1)}, u32[]{:S(2)}, u32[]{:S(2)}) collective-permute-start(bf16[4,64,2048]{2,1,0:T(8,128)(2,1)S(1)} %get-tuple-element.161), channel_id=1, source_target_pairs={{0,1},{1,0},{2,3},{3,2},{4,5},{5,4},{6,7},{7,6},{8,9},{9,8},{10,11... | collective-permute-start | bytes 3145736 | tf_op jit(solution)/shard_map/ppermute | solution.py:414
  731.3 35.5 %collective-permute-start.28 = (bf16[4,64,2048]{2,1,0:T(8,128)(2,1)}, bf16[4,64,2048]{2,1,0:T(8,128)(2,1)}, u32[]{:S(2)}, u32[]{:S(2)}) collective-permute-start(bf16[4,64,2048]{2,1,0:T(8,128)(2,1)} %get-tuple-element.158), channel_id=1, source_target_pairs={{0,1},{1,0},{2,3},{3,2},{4,5},{5,4},{6,7},{7,6},{8,9},{9,8},{10,11... | collective-permute-start | bytes 3145736 | tf_op jit(solution)/shard_map/ppermute | solution.py:414
  751.7 24.5 %collective-permute-start.30 = (bf16[4,64,2048]{2,1,0:T(8,128)(2,1)}, bf16[4,64,2048]{2,1,0:T(8,128)(2,1)}, u32[]{:S(2)}, u32[]{:S(2)}) collective-permute-start(bf16[4,64,2048]{2,1,0:T(8,128)(2,1)} %get-tuple-element.162), channel_id=1, source_target_pairs={{0,2},{1,3},{2,0},{3,1},{4,6},{5,7},{6,4},{7,5},{8,10},{9,11},{10,... | collective-permute-start | bytes 3145736 | tf_op jit(solution)/shard_map/ppermute | solution.py:414
  753.1 24.2 %collective-permute-start.32 = (bf16[4,64,2048]{2,1,0:T(8,128)(2,1)}, bf16[4,64,2048]{2,1,0:T(8,128)(2,1)}, u32[]{:S(2)}, u32[]{:S(2)}) collective-permute-start(bf16[4,64,2048]{2,1,0:T(8,128)(2,1)} %get-tuple-element.164), channel_id=1, source_target_pairs={{0,4},{1,5},{2,6},{3,7},{4,0},{5,1},{6,2},{7,3},{8,12},{9,13},{10,... | collective-permute-start | bytes 3145736 | tf_op jit(solution)/shard_map/ppermute | solution.py:414
  754.3 45.6 %collective-permute-start.34 = (bf16[4,64,2048]{2,1,0:T(8,128)(2,1)}, bf16[4,64,2048]{2,1,0:T(8,128)(2,1)}, u32[]{:S(2)}, u32[]{:S(2)}) collective-permute-start(bf16[4,64,2048]{2,1,0:T(8,128)(2,1)} %get-tuple-element.163), channel_id=1, source_target_pairs={{0,6},{1,7},{2,4},{3,5},{4,2},{5,3},{6,0},{7,1},{8,14},{9,15},{10,... | collective-permute-start | bytes 3145736 | tf_op jit(solution)/shard_map/ppermute | solution.py:414
  804.4 106.6 %reduce-scatter.11.cloned.1.call-start = ((), (), s32[]{:S(2)}) async-start(), calls=%async_computation.9 | async-start | bytes 5242880 | tf_op jit(solution)/shard_map/reduce_scatter | solution.py:1053
  (105 other events, 1204.6 us)
Sparse Core Ops, SparseCore 0:
  180.4 151.9 all-gather.2
  347.6 81.2 all-gather.4
  482.8 77.4 reduce-scatter.4
  562.6 144.6 reduce-scatter.6
  804.5 26.1 reduce-scatter.8
  833.4 77.4 reduce-scatter.10

commit v3 on v2

--- a/solution.py
+++ b/solution.py
@@ -37,16 +37,6 @@
     )
 
 
-def rotate(values, cosine, sine_part):
-    half_width = values.shape[-1] // 2
-    front_half = values[..., :half_width]
-    back_half = values[..., half_width:]
-    return jnp.concatenate(
-        [front_half * cosine - back_half * sine_part, back_half * cosine + front_half * sine_part],
-        axis=-1,
-    )
-
-
 def angle_table(positions):
     inverse_rate = ROPE_THETA ** (-(jnp.arange(HD // 2, dtype=FULL) * 2.0) / HD)
     angles = positions.astype(FULL)[..., None] * inverse_rate
@@ -80,14 +70,6 @@
     return row_scale * scaled - values * row_scale**3 * jnp.mean(
         scaled * values, axis=-1, keepdims=True
     )
-
-
-def masked_scores(head_queries, all_keys, visible, score_scale):
-    raw_scores = (
-        jnp.einsum("rkgd,skd->kgrs", head_queries, all_keys, preferred_element_type=FULL)
-        * score_scale
-    )
-    return jnp.where(visible, raw_scores, MASK_FILL)
 
 
 def adam_step(master, first_moment, second_moment, gradient, decay_rate):
@@ -409,6 +391,354 @@
     )(weight, hidden, forward)
 
 
+def project_kernel(
+    place_ref,
+    group_ref,
+    own_ref,
+    gain_ref,
+    cosine_ref,
+    sine_ref,
+    weight_ref,
+    query_ref,
+    pair_ref,
+    normed_ref,
+    own_normed_ref,
+    scale_ref,
+):
+    step = pl.program_id(0)
+    own_rows = own_ref.shape[0]
+    prompt_rows = own_rows - CONT
+    start = pl.multiple_of(place_ref[0] * prompt_rows, 16)
+    tile = 32
+
+    def norm_tile(values, at):
+        values = values.astype(FULL)
+        scale = lax.rsqrt(jnp.mean(values * values, axis=-1, keepdims=True) + EPS_NORM)
+        normed_ref[pl.ds(at, tile)] = (values * scale * gain_ref[...]).astype(LOW)
+        scale_ref[pl.ds(at, tile)] = jnp.broadcast_to(scale, (tile, 128))
+
+    @pl.when(step == 0)
+    def _():
+        @pl.loop(0, PROMPT_LEN // tile)
+        def _(at):
+            first = pl.multiple_of(at * tile, tile)
+            norm_tile(group_ref[pl.ds(first, tile)], first)
+
+        for at in range(0, CONT, tile):
+            norm_tile(own_ref[prompt_rows + at : prompt_rows + at + tile], PROMPT_LEN + at)
+        own_normed_ref[:prompt_rows] = normed_ref[pl.ds(start, prompt_rows)]
+        own_normed_ref[prompt_rows:] = normed_ref[PROMPT_LEN:]
+
+    def turn(values, cosine, sine_part):
+        front, back = values[:, : HD // 2], values[:, HD // 2 :]
+        return front * cosine - back * sine_part, back * cosine + front * sine_part
+
+    def project(rows):
+        return jnp.dot(rows, weight_ref[...], preferred_element_type=FULL)
+
+    @pl.when(step < HQ)
+    def _():
+        for first, count, table in ((0, prompt_rows, start), (prompt_rows, CONT, PROMPT_LEN)):
+            values = project(own_normed_ref[first : first + count])
+            front, back = turn(
+                values, cosine_ref[pl.ds(table, count)], sine_ref[pl.ds(table, count)]
+            )
+            query_ref[first : first + count, : HD // 2] = front.astype(LOW)
+            query_ref[first : first + count, HD // 2 :] = back.astype(LOW)
+
+    key_count = PROMPT_LEN + CONT
+    part = key_count // 4
+
+    @pl.when((step >= HQ) & (step < HQ + HK))
+    def _():
+        @pl.loop(0, 4)
+        def _(at):
+            rows = pl.ds(pl.multiple_of(at * part, 16), part)
+            front, back = turn(project(normed_ref[rows]), cosine_ref[rows], sine_ref[rows])
+            pair_ref[rows, : HD // 2] = front.astype(LOW)
+            pair_ref[rows, HD // 2 :] = back.astype(LOW)
+
+    @pl.when(step >= HQ + HK)
+    def _():
+        @pl.loop(0, 4)
+        def _(at):
+            rows = pl.ds(pl.multiple_of(at * part, 16), part)
+            pair_ref[rows] = project(normed_ref[rows]).astype(LOW)
+
+
+VMEM_LIMIT = 60 * 2**20
+
+
+def project_heads(place, group_rows, own_inputs, gain_row, cosine, sine_part, weights):
+    own_rows = own_inputs.shape[0]
+    key_count = PROMPT_LEN + CONT
+    whole = lambda shape: pl.BlockSpec(shape, lambda j, p: (0, 0))
+    return pl.pallas_call(
+        project_kernel,
+        grid_spec=pltpu.PrefetchScalarGridSpec(
+            num_scalar_prefetch=1,
+            grid=(HQ + 2 * HK,),
+            in_specs=[
+                whole((PROMPT_LEN, D)),
+                whole((own_rows, D)),
+                whole((1, D)),
+                whole((key_count, HD // 2)),
+                whole((key_count, HD // 2)),
+                pl.BlockSpec((D, HD), lambda j, p: (0, j)),
+            ],
+            out_specs=[
+                pl.BlockSpec((own_rows, HD), lambda j, p: (0, jnp.minimum(j, HQ - 1))),
+                pl.BlockSpec((key_count, HD), lambda j, p: (0, jnp.maximum(j - HQ, 0))),
+                whole((key_count, D)),
+                whole((own_rows, D)),
+                whole((key_count, 128)),
+            ],
+        ),
+        out_shape=[
+            jax.ShapeDtypeStruct((own_rows, HQ * HD), LOW),
+            jax.ShapeDtypeStruct((key_count, 2 * HK * HD), LOW),
+            jax.ShapeDtypeStruct((key_count, D), LOW),
+            jax.ShapeDtypeStruct((own_rows, D), LOW),
+            jax.ShapeDtypeStruct((key_count, 128), FULL),
+        ],
+        compiler_params=pltpu.CompilerParams(vmem_limit_bytes=VMEM_LIMIT),
+        name="project_heads",
+    )(place, group_rows, own_inputs, gain_row, cosine, sine_part, weights)
+
+
+def across(left, right):
+    return lax.dot_general(left, right, (((1,), (1,)), ((), ())), preferred_element_type=FULL)
+
+
+def along(left, right):
+    return lax.dot_general(left, right, (((0,), (0,)), ((), ())), preferred_element_type=FULL)
+
+
+def attend_kernel(query_ref, key_ref, value_ref, seen_ref, attended_ref, logsum_ref):
+    group_heads = HQ // HK
+    for head in range(group_heads):
+        columns = slice(head * HD, (head + 1) * HD)
+        scores = across(query_ref[:, columns], key_ref[...]) * HD ** (-0.5)
+        scores = jnp.where(seen_ref[...] > 0, scores, MASK_FILL)
+        peak = jnp.max(scores, axis=-1, keepdims=True)
+        unnormed = jnp.exp(scores - peak)
+        total = jnp.sum(unnormed, axis=-1, keepdims=True)
+        low = (unnormed / total).astype(LOW)
+        attended_ref[:, columns] = jnp.dot(
+            low, value_ref[...], preferred_element_type=FULL
+        ).astype(LOW)
+        logsum_ref[:, head * 128 : (head + 1) * 128] = jnp.broadcast_to(
+            peak + jnp.log(total), (query_ref.shape[0], 128)
+        )
+
+
+def attend(queries, pairs, seen):
+    rows, key_count = seen.shape
+    group_heads = HQ // HK
+    return pl.pallas_call(
+        attend_kernel,
+        grid=(HK,),
+        in_specs=[
+            pl.BlockSpec((rows, group_heads * HD), lambda j: (0, j)),
+            pl.BlockSpec((key_count, HD), lambda j: (0, j)),
+            pl.BlockSpec((key_count, HD), lambda j: (0, HK + j)),
+            pl.BlockSpec((rows, key_count), lambda j: (0, 0)),
+        ],
+        out_specs=[
+            pl.BlockSpec((rows, group_heads * HD), lambda j: (0, j)),
+            pl.BlockSpec((rows, group_heads * 128), lambda j: (0, j)),
+        ],
+        out_shape=[
+            jax.ShapeDtypeStruct((rows, HQ * HD), LOW),
+            jax.ShapeDtypeStruct((rows, HQ * 128), FULL),
+        ],
+        compiler_params=pltpu.CompilerParams(vmem_limit_bytes=VMEM_LIMIT),
+        name="attend",
+    )(queries, pairs, pairs, seen)
+
+
+def attend_back_kernel(
+    place_ref,
+    query_ref,
+    key_ref,
+    value_ref,
+    seen_ref,
+    logsum_ref,
+    grad_ref,
+    cosine_ref,
+    sine_ref,
+    query_out,
+    pair_out,
+):
+    step = pl.program_id(0)
+    group_heads = HQ // HK
+    rows = query_ref.shape[0]
+    prompt_rows = rows - CONT
+    start = pl.multiple_of(place_ref[0] * prompt_rows, 16)
+    score_scale = HD ** (-0.5)
+    key_grad = value_grad = 0.0
+
+    def turn_back(values, cosine, sine_part):
+        front, back = values[:, : HD // 2], values[:, HD // 2 :]
+        return jnp.concatenate(
+            [front * cosine + back * sine_part, back * cosine - front * sine_part], axis=1
+        ).astype(LOW)
+
+    for head in range(group_heads):
+        columns = slice(head * HD, (head + 1) * HD)
+        scores = across(query_ref[:, columns], key_ref[...]) * score_scale
+        scores = jnp.where(seen_ref[...] > 0, scores, MASK_FILL)
+        probabilities = jnp.exp(scores - logsum_ref[:, head * 128 : head * 128 + 1])
+        grads = grad_ref[:, columns]
+        probability_grad = across(grads, value_ref[...])
+        delta = jnp.sum(probabilities * probability_grad, axis=-1, keepdims=True)
+        score_grad = (probabilities * (probability_grad - delta)).astype(LOW)
+        query_grad = jnp.dot(score_grad, key_ref[...], preferred_element_type=FULL) * score_scale
+        key_grad = key_grad + along(score_grad, query_ref[:, columns])
+        value_grad = value_grad + along(probabilities.astype(LOW), grads)
+        query_out[:prompt_rows, columns] = turn_back(
+            query_grad[:prompt_rows],
+            cosine_ref[pl.ds(start, prompt_rows)],
+            sine_ref[pl.ds(start, prompt_rows)],
+        )
+        query_out[prompt_rows:, columns] = turn_back(
+            query_grad[prompt_rows:], cosine_ref[PROMPT_LEN:], sine_ref[PROMPT_LEN:]
+        )
+    pair_out[:, pl.ds(pl.multiple_of(step * HD, HD), HD)] = turn_back(
+        key_grad * score_scale, cosine_ref[...], sine_ref[...]
+    )
+    pair_out[:, pl.ds(pl.multiple_of((HK + step) * HD, HD), HD)] = value_grad.astype(LOW)
+
+
+def attend_back(place, queries, pairs, seen, logsum, grads, cosine, sine_part):
+    rows, key_count = seen.shape
+    group_heads = HQ // HK
+    whole = lambda shape: pl.BlockSpec(shape, lambda j, p: (0, 0))
+    return pl.pallas_call(
+        attend_back_kernel,
+        grid_spec=pltpu.PrefetchScalarGridSpec(
+            num_scalar_prefetch=1,
+            grid=(HK,),
+            in_specs=[
+                pl.BlockSpec((rows, group_heads * HD), lambda j, p: (0, j)),
+                pl.BlockSpec((key_count, HD), lambda j, p: (0, j)),
+                pl.BlockSpec((key_count, HD), lambda j, p: (0, HK + j)),
+                whole((rows, key_count)),
+                pl.BlockSpec((rows, group_heads * 128), lambda j, p: (0, j)),
+                pl.BlockSpec((rows, group_heads * HD), lambda j, p: (0, j)),
+                whole((key_count, HD // 2)),
+                whole((key_count, HD // 2)),
+            ],
+            out_specs=[
+                pl.BlockSpec((rows, group_heads * HD), lambda j, p: (0, j)),
+                whole((key_count, 2 * HK * HD)),
+            ],
+        ),
+        out_shape=[
+            jax.ShapeDtypeStruct((rows, HQ * HD), LOW),
+            jax.ShapeDtypeStruct((key_count, 2 * HK * HD), LOW),
+        ],
+        compiler_params=pltpu.CompilerParams(vmem_limit_bytes=VMEM_LIMIT),
+        name="attend_back",
+    )(place, queries, pairs, pairs, seen, logsum, grads, cosine, sine_part)
+
+
+def weights_back_kernel(
+    place_ref,
+    query_ref,
+    pair_ref,
+    branch_ref,
+    attended_ref,
+    normed_ref,
+    own_normed_ref,
+    group_ref,
+    own_ref,
+    scale_ref,
+    query_weight_ref,
+    pair_weight_ref,
+    query_term,
+    pair_term,
+    merge_term,
+    back_out,
+    pair_back_out,
+    gain_out,
+):
+    rows = query_ref.shape[0]
+    prompt_rows = rows - CONT
+    start = pl.multiple_of(place_ref[0] * prompt_rows, 16)
+    query_term[...] = along(own_normed_ref[...], query_ref[...]).astype(LOW)
+    pair_term[...] = along(normed_ref[...], pair_ref[...]).astype(LOW)
+    merge_term[...] = along(branch_ref[...], attended_ref[...]).astype(LOW)
+    query_back = across(query_ref[...], query_weight_ref[...])
+    pair_back = across(pair_ref[...], pair_weight_ref[...])
+    own_values = own_ref[prompt_rows:].astype(FULL) * scale_ref[PROMPT_LEN:, :1]
+    tail = query_back[prompt_rows:] + pair_back[PROMPT_LEN:]
+    group_values = group_ref[...].astype(FULL) * scale_ref[:PROMPT_LEN, :1]
+    own_prompt = own_ref[:prompt_rows].astype(FULL) * scale_ref[pl.ds(start, prompt_rows), :1]
+    gain_out[...] = (
+        jnp.sum(pair_back[:PROMPT_LEN] * group_values, axis=0, keepdims=True)
+        + jnp.sum(query_back[:prompt_rows] * own_prompt, axis=0, keepdims=True)
+        + jnp.sum(tail * own_values, axis=0, keepdims=True)
+    )
+    back_out[:prompt_rows] = query_back[:prompt_rows]
+    back_out[prompt_rows:] = tail
+    pair_back_out[...] = pair_back[:PROMPT_LEN].astype(LOW)
+
+
+def weights_back(
+    place, queries, pairs, branch, attended, normed, own_normed, group_rows, own_inputs, scale, weights
+):
+    rows, key_count = queries.shape[0], pairs.shape[0]
+    wide, tile = HQ * HD, 256
+    whole = lambda shape: pl.BlockSpec(shape, lambda j, p: (0, 0))
+    tall = lambda count: pl.BlockSpec((count, tile), lambda j, p: (0, j))
+    flat = lambda at: pl.BlockSpec((tile, wide), lambda j, p: (j, at))
+    return pl.pallas_call(
+        weights_back_kernel,
+        grid_spec=pltpu.PrefetchScalarGridSpec(
+            num_scalar_prefetch=1,
+            grid=(D // tile,),
+            in_specs=[
+                whole((rows, wide)),
+                whole((key_count, wide)),
+                tall(rows),
+                whole((rows, wide)),
+                tall(key_count),
+                tall(rows),
+                tall(PROMPT_LEN),
+                tall(rows),
+                whole((key_count, 128)),
+                flat(0),
+                flat(1),
+            ],
+            out_specs=[flat(0), flat(0), flat(0), tall(rows), tall(PROMPT_LEN), tall(1)],
+        ),
+        out_shape=[
+            jax.ShapeDtypeStruct((D, wide), LOW),
+            jax.ShapeDtypeStruct((D, wide), LOW),
+            jax.ShapeDtypeStruct((D, wide), LOW),
+            jax.ShapeDtypeStruct((rows, D), FULL),
+            jax.ShapeDtypeStruct((PROMPT_LEN, D), LOW),
+            jax.ShapeDtypeStruct((1, D), FULL),
+        ],
+        compiler_params=pltpu.CompilerParams(vmem_limit_bytes=VMEM_LIMIT),
+        name="weights_back",
+    )(
+        place,
+        queries,
+        pairs,
+        branch,
+        attended,
+        normed,
+        own_normed,
+        group_rows,
+        own_inputs,
+        scale,
+        weights,
+        weights,
+    )
+
+
 def plane_swap(block, offset):
     size = lax.axis_size("dp")
     return lax.ppermute(block, "dp", [(i, i ^ offset) for i in range(size)])
@@ -434,16 +764,6 @@
     return total
 
 
-def plane_rows(term):
-    lines, plane = lax.axis_size("grp"), lax.axis_size("dp")
-    d = lax.axis_index("dp")
-    blocks = term.reshape(lines, plane, -1, term.shape[1])
-    mine = plane_scatter(
-        lambda offset: lax.dynamic_index_in_dim(blocks, d ^ offset, 1, keepdims=False)
-    )
-    return mine.astype(LOW).reshape(-1, term.shape[1])
-
-
 def line_scatter(term):
     return lax.psum_scatter(term, "grp", scatter_dimension=0, tiled=True)
 
@@ -453,12 +773,17 @@
     plane,
     query_ref,
     pair_ref,
+    merge_ref,
     gain_ref,
     gate_ref,
     down_ref,
+    back_ref,
     a_master,
     a_first,
     a_second,
+    m_master,
+    m_first,
+    m_second,
     f_master,
     f_first,
     f_second,
@@ -466,7 +791,12 @@
     a_update,
     a_first_new,
     a_second_new,
+    m_grad,
+    m_update,
+    m_first_new,
+    m_second_new,
     gain_out,
+    back_out,
     f_grad,
     f_update,
     f_first_new,
@@ -496,6 +826,8 @@
     made_sem,
     a_sem,
     gain_sem,
+    back_send,
+    back_recv,
 ):
     g = lax.axis_index("grp")
     d = lax.axis_index("dp")
@@ -504,13 +836,13 @@
     partner = d + 1 - 2 * core
     rows = a_master.shape[0]
     own_hidden = down_ref.shape[2]
-    query_width, pair_width = query_ref.shape[4], pair_ref.shape[4]
     width = core_in.shape[3]
-    parts = (
-        (query_ref, pl.ds(0, query_width)),
-        (pair_ref, pl.ds(query_width, pair_width)),
-        (gain_ref, pl.ds(query_width + pair_width, GAIN_PAD)),
-    )
+    a_width, m_width = a_master.shape[1], m_master.shape[1]
+    parts, begin = [], 0
+    for ref in (query_ref, pair_ref, merge_ref, gain_ref):
+        parts.append((ref, pl.ds(begin, ref.shape[4])))
+        begin += ref.shape[4]
+    prompt_rows = back_out.shape[1]
 
     barrier = pltpu.get_barrier_semaphore()
     for step in range(1, plane):
@@ -539,7 +871,7 @@
         line = line_at(turn)
         ref, columns = parts[part]
         return pltpu.make_async_copy(
-            ref.at[line, :, core], mine.at[line, :, :, columns], mine_sem.at[turn, part]
+            ref.at[line, :, core], mine.at[turn % 2, :, :, columns], mine_sem.at[turn, part]
         )
 
     def plane_copy(turn, step):
@@ -579,128 +911,152 @@
         pltpu.make_async_copy(down_ref.at[d], down_in.at[d], own_sem.at[1]),
     )
 
-    def state_copy(turn, part, which):
-        source = (f_master, f_first, f_second)[which]
-        block = lax.rem(d + turn, plane)
+    def f_columns(turn):
+        block = lax.rem(d + lax.div(turn, 3), plane)
+        return pl.ds(
+            pl.multiple_of(lax.rem(turn, 3) * FF + block * own_hidden, own_hidden), own_hidden
+        )
+
+    def state_copy(turn, which):
         slot = lax.rem(turn, 2)
         return pltpu.make_async_copy(
-            source.at[:, pl.ds(part * FF + block * own_hidden, own_hidden)],
-            state.at[slot, part, which],
-            state_sem.at[slot, part, which],
-        )
-
-    def made_copy(turn, part, which):
-        target = (f_grad, f_update, f_first_new, f_second_new)[which]
-        block = lax.rem(d + turn, plane)
+            (f_master, f_first, f_second)[which].at[:, f_columns(turn)],
+            state.at[slot, which],
+            state_sem.at[slot, which],
+        )
+
+    def made_copy(turn, which):
         slot = lax.rem(turn, 2)
         return pltpu.make_async_copy(
-            made.at[slot, part, which],
-            target.at[:, pl.ds(part * FF + block * own_hidden, own_hidden)],
-            made_sem.at[slot, part, which],
-        )
-
-    def a_state_copy(which):
+            made.at[slot, which],
+            (f_grad, f_update, f_first_new, f_second_new)[which].at[:, f_columns(turn)],
+            made_sem.at[slot, which],
+        )
+
+    def back_copy(step):
+        there = lax.rem(g + step, lines)
+        return remote(
+            back_ref.at[there],
+            back_out.at[g],
+            back_send.at[step],
+            back_recv.at[step],
+            (there, d),
+        )
+
+    own_back = pltpu.make_async_copy(back_ref.at[g], back_out.at[g], own_sem.at[2])
+
+    slabs = (pl.ds(0, a_width), pl.ds(a_width, m_width))
+
+    def a_state_copy(which, slab):
+        source = ((a_master, a_first, a_second), (m_master, m_first, m_second))[slab][which]
         return pltpu.make_async_copy(
-            (a_master, a_first, a_second)[which], a_state.at[which], a_sem.at[which]
-        )
-
-    def a_made_copy(which):
+            source, a_state.at[which, :, slabs[slab]], a_sem.at[slab, which]
+        )
+
+    def a_made_copy(which, slab):
+        target = (
+            (a_grad, a_update, a_first_new, a_second_new),
+            (m_grad, m_update, m_first_new, m_second_new),
+        )[slab][which]
         return pltpu.make_async_copy(
-            a_made.at[which],
-            (a_grad, a_update, a_first_new, a_second_new)[which],
-            a_sem.at[3 + which],
-        )
-
+            a_made.at[which, :, slabs[slab]], target, a_sem.at[slab, 3 + which]
+        )
+
+    every = range(len(parts))
     for turn in range(lines):
-        for part in range(3):
+        for part in every:
             core_copy(turn, part).start()
-            mine_copy(turn, part).start()
+            if turn < 2:
+                mine_copy(turn, part).start()
+    for step in range(1, lines):
+        back_copy(step).start()
     for step in range(1, plane):
         for part in range(2):
             swap_copy(step, part).start()
     for one in own_swap:
         one.start()
-    for part in range(3):
-        for which in range(3):
-            state_copy(0, part, which).start()
+    own_back.start()
     for which in range(3):
-        a_state_copy(which).start()
-
-    tile = 384 if width % 384 == 0 else 128
+        state_copy(0, which).start()
+        for slab in range(2):
+            a_state_copy(which, slab).start()
+
+    tile = 896 if width % 896 == 0 else 128
     tiles = width // tile
 
     for turn in range(lines):
         line = line_at(turn)
-        for part in range(3):
+        for part in every:
             core_copy(turn, part).wait_recv()
             mine_copy(turn, part).wait()
-        for step in range(1, chips):
+        for step in range(1, chips + 1):
             there = lax.rem(chip + step, chips)
 
             @pl.loop(0, tiles)
-            def _(at, line=line, there=there):
+            def _(at, line=line, there=there, turn=turn):
                 columns = pl.ds(pl.multiple_of(at * tile, tile), tile)
-                total = mine[line, there, :, columns].astype(FULL) + core_in[
+                total = mine[turn % 2, there, :, columns].astype(FULL) + core_in[
                     line, there, :, columns
                 ].astype(FULL)
                 core_in[line, there, :, columns] = total.astype(LOW)
 
-            plane_copy(turn, step).start()
-
-    def step_rows(slot, part, at, gradient):
-        rows_at = pl.ds(pl.multiple_of(at * 16, 16), 16)
-        update, first_new, second_new = adam_step(
-            state[slot, part, 0, rows_at],
-            state[slot, part, 1, rows_at],
-            state[slot, part, 2, rows_at],
-            gradient,
-            WEIGHT_DECAY,
-        )
-        made[slot, part, 0, rows_at] = gradient
-        made[slot, part, 1, rows_at] = update
-        made[slot, part, 2, rows_at] = first_new
-        made[slot, part, 3, rows_at] = second_new
+            if step < chips:
+                plane_copy(turn, step).start()
+        if turn + 2 < lines:
+            for part in every:
+                mine_copy(turn + 2, part).start()
 
     def forward_turn(turn):
         slot = lax.rem(turn, 2)
-        block = lax.rem(d + turn, plane)
-
-        @pl.when(turn + 1 < plane)
+        block = lax.rem(d + lax.div(turn, 3), plane)
+        part = lax.rem(turn, 3)
+
+        @pl.when(turn + 1 < 3 * plane)
         def _():
-            for part in range(3):
-                for which in range(3):
-                    state_copy(turn + 1, part, which).start()
+            for which in range(3):
+                state_copy(turn + 1, which).start()
 
         @pl.when(turn > 1)
         def _():
-            for part in range(3):
-                for which in range(4):
-                    made_copy(turn - 2, part, which).wait()
-
-        for part in range(3):
-            for which in range(3):
-                state_copy(turn, part, which).wait()
-
+            for which in range(4):
+                made_copy(turn - 2, which).wait()
+
+        for which in range(3):
+            state_copy(turn, which).wait()
+
+        def rows_step(read):
             @pl.loop(0, rows // 16)
-            def _(at, part=part):
+            def _(at):
                 rows_at = pl.ds(pl.multiple_of(at * 16, 16), 16)
-                if part < 2:
-                    gradient = gate_in[
-                        block, rows_at, pl.ds(part * own_hidden, own_hidden)
-                    ].astype(FULL)
-                else:
-                    gradient = down_in[block, rows_at].astype(FULL)
-                step_rows(slot, part, at, gradient)
-
-            for which in range(4):
-                made_copy(turn, part, which).start()
+                gradient = read(rows_at).astype(FULL)
+                update, first_new, second_new = adam_step(
+                    state[slot, 0, rows_at],
+                    state[slot, 1, rows_at],
+                    state[slot, 2, rows_at],
+                    gradient,
+                    WEIGHT_DECAY,
+                )
+                made[slot, 0, rows_at] = gradient
+                made[slot, 1, rows_at] = update
+                made[slot, 2, rows_at] = first_new
+                made[slot, 3, rows_at] = second_new
+
+        for own in range(2):
+            pl.when(part == own)(
+                lambda own=own: rows_step(
+                    lambda at: gate_in[block, at, pl.ds(own * own_hidden, own_hidden)]
+                )
+            )
+        pl.when(part == 2)(lambda: rows_step(lambda at: down_in[block, at]))
+        for which in range(4):
+            made_copy(turn, which).start()
 
     for one in own_swap:
         one.wait()
     for step in range(1, plane):
         for part in range(2):
             swap_copy(step, part).wait_recv()
-    each = plane // lines
+    each = 3 * plane // lines
     for turn in range(lines):
         lax.fori_loop(turn * each, (turn + 1) * each, lambda k, c: (forward_turn(k), c)[1], 0)
         line = line_at(turn)
@@ -710,9 +1066,7 @@
         @pl.loop(0, tiles)
         def _(at, line=line):
             columns = pl.ds(pl.multiple_of(at * tile, tile), tile)
-            total = mine[line, chip, :, columns].astype(FULL) + core_in[
-                line, chip, :, columns
-            ].astype(FULL)
+            total = core_in[line, chip, :, columns].astype(FULL)
             for step in range(1, chips):
                 total = total + plane_in[line, lax.rem(chip + step, chips), :, columns].astype(FULL)
             core_in[line, chip, :, columns] = total.astype(LOW)
@@ -720,14 +1074,14 @@
         if turn < lines - 1:
             line_copy(turn).start()
 
-    for part in range(3):
-        for which in range(4):
-            for turn in (plane - 2, plane - 1):
-                made_copy(turn, part, which).wait()
+    for which in range(4):
+        for turn in (3 * plane - 2, 3 * plane - 1):
+            made_copy(turn, which).wait()
     for turn in range(lines - 1):
         line_copy(turn).wait_recv()
     for which in range(3):
-        a_state_copy(which).wait()
+        for slab in range(2):
+            a_state_copy(which, slab).wait()
 
     def owned(columns):
         total = core_in[g, chip, :, columns].astype(FULL)
@@ -735,7 +1089,7 @@
             total = total + line_in[lax.rem(g + step, lines), :, columns].astype(FULL)
         return total
 
-    @pl.loop(0, (query_width + pair_width) // 256)
+    @pl.loop(0, (a_width + m_width) // 256)
     def _(at):
         columns = pl.ds(pl.multiple_of(at * 256, 256), 256)
         gradient = owned(columns)
@@ -752,12 +1106,13 @@
         a_made[3, :, columns] = second_new
 
     for which in range(4):
-        a_made_copy(which).start()
-    gain_made[...] = owned(pl.ds(query_width + pair_width, GAIN_PAD))
+        for slab in range(2):
+            a_made_copy(which, slab).start()
+    gain_made[...] = owned(pl.ds(a_width + m_width, GAIN_PAD))
     gain_copy = pltpu.make_async_copy(gain_made, gain_out, gain_sem.at[0])
     gain_copy.start()
     for turn in range(lines):
-        for part in range(3):
+        for part in every:
             core_copy(turn, part).wait_send()
         for step in range(1, chips):
             plane_copy(turn, step).wait_send()
@@ -766,72 +1121,78 @@
     for step in range(1, plane):
         for part in range(2):
             swap_copy(step, part).wait_send()
+    for step in range(1, lines):
+        back_copy(step).wait()
+    own_back.wait()
     for which in range(4):
-        a_made_copy(which).wait()
+        for slab in range(2):
+            a_made_copy(which, slab).wait()
     gain_copy.wait()
 
 
-def finish(query_term, pair_term, gain_term, gate_part, down_part, attention, forward):
+def finish(terms, gate_part, down_part, pair_back, attention, merge, forward):
     lines, plane = lax.axis_size("grp"), lax.axis_size("dp")
     chips = plane // 2
     rows, a_width = attention[0].shape
-    f_width = forward[0].shape[1]
+    m_width = merge[0].shape[1]
     own_hidden = down_part.shape[1]
-    width = a_width + GAIN_PAD
+    width = a_width + m_width + GAIN_PAD
     anywhere = pl.BlockSpec(memory_space=pl.ANY)
     dma = pltpu.SemaphoreType.DMA
     vmem = pltpu.VMEM
-
-    def by_device(term):
-        return term.reshape(lines, chips, 2, rows, term.shape[1])
-
-    a_shape = jax.ShapeDtypeStruct((rows, a_width), FULL)
-    f_shape = jax.ShapeDtypeStruct((rows, f_width), FULL)
+    back = pair_back.reshape(lines, PROMPT_LEN // lines, D)
+
+    def like(array):
+        return jax.ShapeDtypeStruct(array.shape, array.dtype)
+
     return pl.pallas_call(
         functools.partial(finish_kernel, lines, plane),
-        out_shape=(a_shape,) * 4
-        + (jax.ShapeDtypeStruct((rows, GAIN_PAD), FULL),)
-        + (f_shape,) * 4,
-        in_specs=[anywhere] * 11,
-        out_specs=(anywhere,) * 9,
+        out_shape=(like(attention[0]),) * 4
+        + (like(merge[0]),) * 4
+        + (jax.ShapeDtypeStruct((rows, GAIN_PAD), FULL), like(back))
+        + (like(forward[0]),) * 4,
+        in_specs=[anywhere] * 16,
+        out_specs=(anywhere,) * 14,
         scratch_shapes=[
-            vmem((lines, chips, rows, width), LOW),
+            vmem((2, chips, rows, width), LOW),
             vmem((lines, chips, rows, width), LOW),
             vmem((lines, chips, rows, width), LOW),
             vmem((lines, rows, width), LOW),
             vmem((plane, rows, 2 * own_hidden), LOW),
             vmem((plane, rows, own_hidden), LOW),
-            vmem((2, 3, 3, rows, own_hidden), FULL),
-            vmem((2, 3, 4, rows, own_hidden), FULL),
-            vmem((3, rows, a_width), FULL),
-            vmem((4, rows, a_width), FULL),
+            vmem((2, 3, rows, own_hidden), FULL),
+            vmem((2, 4, rows, own_hidden), FULL),
+            vmem((3, rows, a_width + m_width), FULL),
+            vmem((4, rows, a_width + m_width), FULL),
             vmem((rows, GAIN_PAD), FULL),
-            dma((lines, 3)),
-            dma((lines, 3)),
-            dma((lines, 3)),
+            dma((lines, 4)),
+            dma((lines, 4)),
+            dma((lines, 4)),
             dma((lines, chips)),
             dma((lines, chips)),
             dma((lines,)),
             dma((lines,)),
             dma((plane, 2)),
             dma((plane, 2)),
-            dma((2,)),
-            dma((2, 3, 3)),
-            dma((2, 3, 4)),
-            dma((7,)),
+            dma((3,)),
+            dma((2, 3)),
+            dma((2, 4)),
+            dma((2, 7)),
             dma((1,)),
+            dma((lines,)),
+            dma((lines,)),
         ],
         compiler_params=pltpu.CompilerParams(
-            collective_id=1, has_side_effects=True, vmem_limit_bytes=60 * 2**20
+            collective_id=1, has_side_effects=True, vmem_limit_bytes=VMEM_LIMIT
         ),
         name="finish",
     )(
-        by_device(query_term),
-        by_device(pair_term),
-        by_device(gain_term),
+        *(term.reshape(lines, chips, 2, rows, term.shape[1]) for term in terms),
         gate_part.reshape(plane, rows, -1),
         down_part.reshape(plane, rows, -1),
+        back,
         *attention,
+        *merge,
         *forward,
     )
 
@@ -858,12 +1219,7 @@
     dp_size = lax.axis_size("dp")
     row_count = hidden.shape[2]
     prompt_rows = row_count - CONT
-    query_width = HQ * HD
-    key_width = HK * HD
-    qkv_width = query_width + 2 * key_width
-    group_heads = HQ // HK
-    score_scale = HD ** (-0.5)
-    key_count = PROMPT_LEN + CONT
+    qkv_width = (HQ + 2 * HK) * HD
     own_rows = feedforward_master.shape[0]
     own_hidden = FF // dp_size
     own_inputs = hidden.reshape(row_count, D)
@@ -877,7 +1233,6 @@
     )
     weights, late_cotangent = lax.optimization_barrier((weights, cotangent))
     weights = weights.reshape(D, -1)
-    attention_weight = weights[:, :qkv_width]
     merge_weight = weights[:, qkv_width : qkv_width + D]
     gain_float = weights[:, qkv_width + D : qkv_width + D + 2].astype(FULL).T
     gate_weight = lax.all_gather(
@@ -894,39 +1249,13 @@
     prompt_positions, follow_positions = segment_positions(segment_row, source_row)
     cosine, sine_part = angle_table(jnp.concatenate([prompt_positions, follow_positions[0]]))
 
-    def own_part(table):
-        return jnp.concatenate(
-            [
-                lax.dynamic_slice_in_dim(table, group_index * prompt_rows, prompt_rows),
-                table[PROMPT_LEN:],
-            ]
-        )
-
-    own_cosine = own_part(cosine)[:, None, :]
-    own_sine = own_part(sine_part)[:, None, :]
-    cosine = cosine[:, None, :]
-    sine_part = sine_part[:, None, :]
-
+    place = jnp.reshape(group_index, (1,)).astype(jnp.int32)
+    group_rows = group_rows.reshape(PROMPT_LEN, D)
+    queries, pairs, key_normed, normed, key_scale = project_heads(
+        place, group_rows, own_inputs, gain_float[:1], cosine, sine_part, weights
+    )
     inputs = own_inputs.astype(FULL)
     first_scale = norm_scale(inputs)
-    normed = (inputs * first_scale * gain_float[0]).astype(LOW)
-    key_inputs = jnp.concatenate(
-        [group_rows.reshape(PROMPT_LEN, D), own_inputs[prompt_rows:]], axis=0
-    ).astype(FULL)
-    key_scale = norm_scale(key_inputs)
-    key_normed = (key_inputs * key_scale * gain_float[0]).astype(LOW)
-    query_weight = attention_weight[:, :query_width]
-    pair_weight = attention_weight[:, query_width:]
-    queries = rotate(
-        jnp.dot(normed, query_weight, preferred_element_type=FULL).reshape(row_count, HQ, HD),
-        own_cosine,
-        own_sine,
-    ).astype(LOW)
-    pairs = jnp.dot(key_normed, pair_weight, preferred_element_type=FULL)
-    all_keys = rotate(
-        pairs[:, :key_width].reshape(key_count, HK, HD), cosine, sine_part
-    ).astype(LOW)
-    all_values = pairs[:, key_width:].astype(LOW).reshape(key_count, HK, HD)
 
     row_index = jnp.arange(row_count, dtype=jnp.int32)
     is_prompt = row_index < prompt_rows
@@ -941,34 +1270,12 @@
         jnp.arange(CONT, dtype=jnp.int32)[None, :] <= (row_index - prompt_rows)[:, None]
     )
     visible = jnp.concatenate([prompt_seen, follow_seen], axis=1)
-    head_queries = queries.reshape(row_count, HK, group_heads, HD)
-    scores = masked_scores(head_queries, all_keys, visible, score_scale)
-    row_peak = jnp.max(scores, axis=-1, keepdims=True)
-    unnormed = jnp.exp(scores - row_peak)
-    row_total = jnp.sum(unnormed, axis=-1, keepdims=True)
-    probability_low = (unnormed / row_total).astype(LOW)
-    row_logsum = row_peak + jnp.log(row_total)
-    attended = (
-        jnp.einsum("kgrs,skd->rkgd", probability_low, all_values, preferred_element_type=FULL)
-        .reshape(row_count, query_width)
-        .astype(LOW)
-    )
+    seen = visible.astype(FULL)
+    attended, row_logsum = attend(queries, pairs, seen)
     middle = inputs + contract(attended, merge_weight, 1, 1)
     second_scale = norm_scale(middle)
     normed_two = (middle * second_scale * gain_float[1]).astype(LOW)
     grad_rows = cotangent.reshape(row_count, D).astype(FULL)
-
-    normed_two, down_grad = lax.optimization_barrier((normed_two, down_grad))
-    normed_all = plane_gather(normed_two)
-    gate_up = jnp.dot(normed_all, gate_weight, preferred_element_type=FULL)
-    gate_values = gate_up[:, :own_hidden]
-    up_values = gate_up[:, own_hidden:]
-    gate_sigmoid, gate_silu, activated = gate_parts(gate_values, up_values)
-    activated_grad = contract(down_grad, down_weight, 1, 0)
-    gate_grad, up_grad = gate_backward(
-        activated_grad, gate_values, up_values, gate_sigmoid, gate_silu
-    )
-    gate_up_grad = jnp.concatenate([gate_grad, up_grad], axis=1)
 
     def by_offset(left, right, right_axis):
         chunks = {}
@@ -979,95 +1286,79 @@
             (offset % 2) * row_count : (offset % 2 + 1) * row_count
         ]
 
+    normed_two, down_grad = lax.optimization_barrier((normed_two, down_grad))
+    normed_all = plane_gather(normed_two)
+    gate_up = jnp.dot(normed_all, gate_weight, preferred_element_type=FULL)
+    gate_values = gate_up[:, :own_hidden]
+    up_values = gate_up[:, own_hidden:]
+    gate_sigmoid, gate_silu, activated = gate_parts(gate_values, up_values)
     down_term = contract(down_grad, activated, 0, 0).astype(LOW)
+    down_term, down_weight = lax.optimization_barrier((down_term, down_weight))
+    out_parts = by_offset(activated, down_weight, 1)
+    out_chunks = [out_parts(offset) for offset in range(dp_size)]
+    out_chunks, down_grad = lax.optimization_barrier((out_chunks, down_grad))
+    out_sum = plane_scatter(lambda offset: out_chunks[offset])
+    activated_grad = contract(down_grad, down_weight, 1, 0)
+    gate_grad, up_grad = gate_backward(
+        activated_grad, gate_values, up_values, gate_sigmoid, gate_silu
+    )
+    gate_up_grad = jnp.concatenate([gate_grad, up_grad], axis=1)
+
     back_parts = by_offset(gate_up_grad, gate_weight, 1)
-    gate_term = contract(normed_all, gate_up_grad, 0, 0).astype(LOW)
     normed_two_grad = plane_scatter(back_parts)
     down_part = line_scatter(down_term)
+    gate_term = contract(normed_all, gate_up_grad, 0, 0).astype(LOW)
+    normed_two_grad, gate_term = lax.optimization_barrier((normed_two_grad, gate_term))
     gate_term, down_part = lax.optimization_barrier((gate_term, down_part))
     gate_part = line_scatter(gate_term)
-    normed_two_grad, activated = lax.optimization_barrier((normed_two_grad, activated))
-    result = middle + plane_scatter(by_offset(activated, down_weight, 1))
+    result = middle + out_sum
     block_output = result.astype(LOW).reshape(hidden.shape)
     middle_grad = grad_rows + norm_back(middle, second_scale, gain_float[1], normed_two_grad)
     gain_two_part = jnp.sum(normed_two_grad * middle * second_scale, axis=0)
     branch_grad = middle_grad.astype(LOW)
-    merge_part = plane_rows(contract(branch_grad, attended, 0, 0).astype(LOW))
-    merge_part, gate_part = lax.optimization_barrier((merge_part, gate_part))
-    merge_grad = line_scatter(merge_part).astype(FULL)
-    attended_grad = (
-        contract(branch_grad, merge_weight, 1, 0)
-        .astype(LOW)
-        .reshape(row_count, HK, group_heads, HD)
-    )
-    scores = masked_scores(head_queries, all_keys, visible, score_scale)
-    probabilities = jnp.exp(scores - row_logsum)
-    probability_grad = jnp.einsum(
-        "rkgd,skd->kgrs", attended_grad, all_values, preferred_element_type=FULL
-    )
-    row_delta = jnp.sum(probabilities * probability_grad, axis=-1, keepdims=True)
-    score_grad = (probabilities * (probability_grad - row_delta)).astype(LOW)
-    query_grad = (
-        jnp.einsum("kgrs,skd->rkgd", score_grad, all_keys, preferred_element_type=FULL)
-        * score_scale
-    )
-    key_grad = (
-        jnp.einsum("kgrs,rkgd->skd", score_grad, head_queries, preferred_element_type=FULL)
-        * score_scale
-    )
-    value_grad = jnp.einsum(
-        "kgrs,rkgd->skd", probabilities.astype(LOW), attended_grad, preferred_element_type=FULL
-    )
-    query_project = (
-        rotate(query_grad.reshape(row_count, HQ, HD), own_cosine, -own_sine)
-        .reshape(row_count, query_width)
-        .astype(LOW)
-    )
-    pair_project = jnp.concatenate(
-        [
-            rotate(key_grad, cosine, -sine_part).reshape(key_count, key_width),
-            value_grad.reshape(key_count, key_width),
-        ],
-        axis=1,
-    ).astype(LOW)
-    query_back = contract(query_project, query_weight, 1, 1)
-    pair_back = contract(pair_project, pair_weight, 1, 1)
-    gain_one_part = jnp.sum(query_back * inputs * first_scale, axis=0) + jnp.sum(
-        pair_back * key_inputs * key_scale, axis=0
+    attended_grad = contract(branch_grad, merge_weight, 1, 0).astype(LOW)
+    query_project, pair_project = attend_back(
+        place, queries, pairs, seen, row_logsum, attended_grad, cosine, sine_part
+    )
+    query_term, pair_term, merge_term, normed_grad, pair_back, gain_one_part = weights_back(
+        place,
+        query_project,
+        pair_project,
+        branch_grad,
+        attended,
+        key_normed,
+        normed,
+        group_rows,
+        own_inputs,
+        key_scale,
+        weights,
     )
     gain_term = jnp.pad(
-        jnp.stack([gain_one_part, gain_two_part], axis=1), ((0, 0), (0, GAIN_PAD - 2))
-    )
-    pair_low = pair_back[:PROMPT_LEN].astype(LOW)
-    pair_low, merge_grad = lax.optimization_barrier((pair_low, merge_grad))
+        jnp.stack([gain_one_part[0], gain_two_part], axis=1), ((0, 0), (0, GAIN_PAD - 2))
+    )
     finished = finish(
-        contract(normed, query_project, 0, 0).astype(LOW),
-        contract(key_normed, pair_project, 0, 0).astype(LOW),
-        gain_term.astype(LOW),
+        (query_term, pair_term, merge_term, gain_term.astype(LOW)),
         gate_part,
         down_part,
+        pair_back,
         (attention_master, attention_first, attention_second),
+        (merge_master, merge_first, merge_second),
         (feedforward_master, feedforward_first, feedforward_second),
     )
-    gain_grad = finished[4][:, :2].T
-    pair_sum = lax.psum_scatter(
-        pair_low, "grp", scatter_dimension=0, tiled=True
-    ).astype(FULL)
-    normed_grad = query_back + jnp.concatenate([pair_sum, pair_back[PROMPT_LEN:]], axis=0)
+    gain_grad = finished[8][:, :2].T
+    pair_sum = jnp.sum(finished[9].astype(FULL), axis=0)
+    normed_grad = normed_grad + jnp.pad(pair_sum, ((0, CONT), (0, 0)))
     input_grad = (middle_grad + norm_back(inputs, first_scale, gain_float[0], normed_grad)).reshape(
         hidden.shape
     )
     gain_new = adam_step(gain_master, gain_first, gain_second, gain_grad, 0.0)
-    merge_new = adam_step(merge_master, merge_first, merge_second, merge_grad, WEIGHT_DECAY)
     return (
         block_output,
         input_grad,
         gain_grad,
         *gain_new,
-        *finished[:4],
-        merge_grad,
-        *merge_new,
-        *finished[5:],
+        *finished[:8],
+        *finished[10:],
     )
 
 

time: 1120 us -> 953 us (0.85)
  Pallas kernels: 297 us -> 449 us
  waiting for transfers between devices: 285 us -> 147 us
  matrix products: 263 us -> 158 us
  local copies, waits for them, and re-layouts: 133 us -> 58.8 us
  starting transfers between devices: 29.2 us -> 50.3 us
  other arithmetic: 79.6 us -> 60.3 us
    pallas_call x0 -> x4, Pallas kernels: none -> 105 us  [the longest x1 40.3 us: weights_back(): pl.pallas_call(weights_back_kernel, grid_spec=pltpu.PrefetchScalarGridSpe...]
    ppermute x35 -> x28, waiting for transfers between devices: 186 us -> 113 us  [plane_swap(): return lax.ppermute(block, 'dp', [(i, i ^ offset) for i in range(size)])]
    dot_general x18 -> x13, matrix products: 192 us -> 129 us  [contract(): lax.dot_general(left, right, (((left_axis,), (right_axis,)), ((), ())), p...]
    pallas_call x1, Pallas kernels: 135 us -> 182 us  [finish(): pl.pallas_call(functools.partial(finish_kernel, lines, plane), out_shape=...]
    reduce_scatter x1 -> x0, waiting for transfers between devices: 46.6 us -> none  [body(): lax.psum_scatter(pair_low, 'grp', scatter_dimension=0, tiled=True)]
    dot_general x8 -> x0, matrix products: 43.3 us -> none  [the longest x1 12.3 us: body(): pairs = jnp.dot(key_normed, pair_weight, preferred_element_type=FULL)]
    ppermute x35 -> x28, starting transfers between devices: 28.8 us -> 50 us  [plane_swap(): return lax.ppermute(block, 'dp', [(i, i ^ offset) for i in range(size)])]
    dot_general x2 -> x0, local copies, waits for them, and re-layouts: 20.7 us -> none  [body(): jnp.dot(normed, query_weight, preferred_element_type=FULL)]
  transfers between devices with their start and end apart: 41 -> 32, of which waited for: 14 -> 9; matrix products, arithmetic and copies ran while one was open for 33% -> 17% of each run, Pallas kernels for 0% -> 11%
where the time goes in v3:
time: 953 us; the launch traced here: 939 us
  Pallas kernels  449 us (47%)
  matrix products  158 us (17%)
  waiting for transfers between devices  147 us (15%)
  other arithmetic  60.3 us (6%)
  local copies, waits for them, and re-layouts  58.8 us (6%)
  starting transfers between devices  50.3 us (5%)
  between operations  15.4 us (2%)
    pallas_call x1, Pallas kernels, finish(): pl.pallas_call(functools.partial(finish_kernel, lines, plane), out_shape=...  182 us
    pallas_call x1, Pallas kernels, gather_start(): pl.pallas_call(functools.partial(gather_kernel, lines, plane, prompt_rows...  161 us
    dot_general x13, matrix products, contract(): lax.dot_general(left, right, (((left_axis,), (right_axis,)), ((), ())), p...  129 us
    ppermute x28, waiting for transfers between devices, plane_swap(): return lax.ppermute(block, 'dp', [(i, i ^ offset) for i in range(size)])  113 us
    ppermute x28, starting transfers between devices, plane_swap(): return lax.ppermute(block, 'dp', [(i, i ^ offset) for i in range(size)])  50 us
    unnamed x139, local copies, waits for them, and re-layouts  43.8 us
    pallas_call x1, Pallas kernels, weights_back(): pl.pallas_call(weights_back_kernel, grid_spec=pltpu.PrefetchScalarGridSpe...  40.3 us
    pallas_call x1, Pallas kernels, project_heads(): pl.pallas_call(project_kernel, grid_spec=pltpu.PrefetchScalarGridSpec(num...  35.1 us
  transfers between devices with their start and end apart: 32, of which 9 were waited for; matrix products, arithmetic and copies ran while one was open for 17% of the time, Pallas kernels for 11%

profile of v3, /device:TPU:9, one launch (start us, length us, event | category | flops | bytes accessed | tf_op | source)
XLA Modules:
  0.0 938.8 jit_solution(10540019928389838150)
XLA Ops:
  10.4 4.8 convert_element_type.182.forward_ref
  16.1 161.4 %gather_start.1 = (bf16[4,8,64,6272]{3,2,1,0:T(8,128)(2,1)}, bf16[4,256,2048]{2,1,0:T(8,128)(2,1)}, bf16[8,64,2048]{2,1,0:T(8,128)(2,1)}, bf16[8,64,1024]{2,1,0:T(8,128)(2,1)}) custom-call(bf16[64,6272]{1,0:T(8,128)(2,1)} %fusion.34.weight_ref, bf16[320,2048]{1,0:T(8,128)(2,1)} %bitcast.68, bf16[64,24576]{1,0:T(8,128)(2,1)} %convert_element_type.182.forward_ref), custom_call_target="tpu_custom_call" | custom-call | tf_op jit(solution)/shard_map/gather_start/pallas_call | solution.py:378
  180.4 3.6 collective-permute-start
  192.7 35.1 %project_heads.1 = (bf16[320,2048]{1,0:T(8,128)(2,1)}, bf16[1088,2048]{1,0:T(8,128)(2,1)}, bf16[1088,2048]{1,0:T(8,128)(2,1)}, bf16[320,2048]{1,0:T(8,128)(2,1)}, f32[1088,128]{1,0:T(8,128)}) custom-call(s32[1]{0:T(128)} %bitcast.1.place_ref, bf16[1024,2048]{1,0:T(8,128)(2,1)} %bitcast.71, bf16[320,2048]{1,0:T(8,128)(2,1)} %bitcast.69, ...), custom_call_target="tpu_custom_call" | custom-call | tf_op jit(solution)/shard_map/project_heads/pallas_call | solution.py:476
  229.7 11.4 %attend.1 = (bf16[320,2048]{1,0:T(8,128)(2,1)}, f32[320,1024]{1,0:T(8,128)}) custom-call(bf16[320,2048]{1,0:T(8,128)(2,1)} %get-tuple-element.75.query_ref, bf16[1088,2048]{1,0:T(8,128)(2,1)} %get-tuple-element.76.key_ref.value_ref, bf16[1088,2048]{1,0:T(8,128)(2,1)} %get-tuple-element.76.key_ref.value_ref, f32[320,1088]{1,0:T(8,128)} %add_convert_fusion.7.seen_ref), custom_call_target="tpu_custom_call" | custom-call | tf_op jit(solution)/shard_map/attend/pallas_call | solution.py:538
  241.1 6.0 multiply_reduce_fusion.2
  259.0 26.0 %collective-permute-done.8 = bf16[320,2048]{1,0:T(8,128)(2,1)S(1)} collective-permute-done((bf16[320,2048]{1,0:T(8,128)(2,1)S(1)}, bf16[320,2048]{1,0:T(8,128)(2,1)S(1)}, u32[]{:S(2)}, u32[]{:S(2)}) %collective-permute-start.8) | collective-permute-done | bytes 1310752 | tf_op jit(solution)/shard_map/ppermute | solution.py:744
  287.2 28.5 %collective-permute-start.11 = (bf16[320,2048]{1,0:T(8,128)(2,1)S(1)}, bf16[320,2048]{1,0:T(8,128)(2,1)S(1)}, u32[]{:S(2)}, u32[]{:S(2)}) collective-permute-start(bf16[320,2048]{1,0:T(8,128)(2,1)S(1)} %collective-permute-done.10), channel_id=1, source_target_pairs={{0,1},{1,0},{2,3},{3,2},{4,5},{5,4},{6,7},{7,6},{8,9},{9,8},{10,11... | collective-permute-start | bytes 3932168 | tf_op jit(solution)/shard_map/ppermute | solution.py:744
  325.5 5.7 all-gather.3.cloned.1.call-done
  331.5 29.0 %fusion.50 = f32[2560,2048]{0,1:T(8,128)} fusion(bf16[2560,2048]{1,0:T(8,128)(2,1)} %constant_dynamic-update-slice_fusion.8, bf16[2048,2048]{1,0:T(8,128)(2,1)} %all-gather.3.cloned.1.call-done), kind=kOutput, calls=%fused_computation.138 | convolution fusion | flops 21474836480 | bytes 39845888 | tf_op jit(solution)/shard_map/dot_general | solution.py:1291
  360.5 8.6 multiply_convert_fusion.2
  372.0 13.7 %convolution_convert_fusion = bf16[2048,1024]{1,0:T(8,128)(2,1)} fusion(bf16[2560,2048]{1,0:T(8,128)(2,1)S(1)} %copy-done.28, bf16[2560,1024]{0,1:T(8,128)(2,1)S(1)} %multiply_convert_fusion.2), kind=kOutput, calls=%fused_computation.25 | convolution fusion | flops 10739515392 | bytes 19922944 | tf_op jit(solution)/shard_map/dot_general | solution.py:35
  385.7 26.4 %all-gather.5.cloned.1.call-done = bf16[2048,1024]{1,0:T(8,128)(2,1)} async-done(((bf16[512,1024]{1,0:T(8,128)(2,1)}), bf16[2048,1024]{1,0:T(8,128)(2,1)}) %all-gather.5.cloned.1.call-update) | async-done | bytes 4194320 | tf_op jit(solution)/shard_map/all_gather | solution.py:1242
  412.1 5.7 convolution_convert_fusion.5
  432.0 24.9 %multiply_convert_fusion = (bf16[2560,1024]{0,1:T(8,128)(2,1)}, bf16[2560,1024]{0,1:T(8,128)(2,1)}) fusion(f32[2560,2048]{0,1:T(8,128)} %fusion.50, bf16[2560,2048]{1,0:T(8,128)(2,1)} %copy-done.27, bf16[2048,1024]{1,0:T(8,128)(2,1)} %all-gather.5.cloned.1.call-done), kind=kOutput, calls=%fused_computation.10 | convolution fusion | flops 10771496960 | bytes 46137344 | tf_op jit(solution)/shard_map/dot_general | solution.py:35
  457.0 10.1 %convolution_convert_fusion.3 = bf16[640,2048]{1,0:T(8,128)(2,1)} fusion(bf16[2048,2048]{1,0:T(8,128)(2,1)} %all-gather.3.cloned.1.call-done, bf16[2560,1024]{0,1:T(8,128)(2,1)} %get-tuple-element.211, bf16[2560,1024]{0,1:T(8,128)(2,1)} %get-tuple-element.210), kind=kOutput, calls=%fused_computation.28 | convolution fusion | flops 5375262720 | bytes 21495808 | tf_op jit(solution)/shard_map/dot_general | solution.py:35
  467.1 8.3 convolution_convert_fusion.1
  478.6 9.0 convolution_convert_fusion.2
  488.4 8.1 convolution_convert_fusion.4
  506.1 26.0 %fusion.2 = bf16[2048,2048]{1,0:T(8,128)(2,1)} fusion(bf16[2560,2048]{1,0:T(8,128)(2,1)} %constant_dynamic-update-slice_fusion.8, bf16[2560,1024]{0,1:T(8,128)(2,1)S(1)} %bitcast.100, bf16[2560,1024]{0,1:T(8,128)(2,1)S(1)} %bitcast.102), kind=kOutput, calls=%fused_computation.16 | convolution fusion | flops 21500002304 | bytes 29360128 | tf_op jit(solution)/shard_map/dot_general | solution.py:35
  532.1 29.6 %collective-permute-done.25 = bf16[320,2048]{1,0:T(8,128)(2,1)} collective-permute-done((bf16[320,2048]{1,0:T(8,128)(2,1)}, bf16[320,2048]{1,0:T(8,128)(2,1)}, u32[]{:S(2)}, u32[]{:S(2)}) %collective-permute-start.25) | collective-permute-done | bytes 1310752 | tf_op jit(solution)/shard_map/ppermute | solution.py:744
  561.7 5.2 convert_add_fusion.2
  572.6 3.8 collective-permute-done.17
  583.7 19.1 %collective-permute-done.16 = bf16[320,2048]{1,0:T(8,128)(2,1)} collective-permute-done((bf16[320,2048]{1,0:T(8,128)(2,1)}, bf16[320,2048]{1,0:T(8,128)(2,1)}, u32[]{:S(2)}, u32[]{:S(2)}) %collective-permute-start.16) | collective-permute-done | bytes 1310752 | tf_op jit(solution)/shard_map/ppermute | solution.py:744
  602.8 33.6 %collective-permute-done.18 = bf16[320,2048]{1,0:T(8,128)(2,1)} collective-permute-done((bf16[320,2048]{1,0:T(8,128)(2,1)}, bf16[320,2048]{1,0:T(8,128)(2,1)}, u32[]{:S(2)}, u32[]{:S(2)}) %collective-permute-start.18) | collective-permute-done | bytes 1310752 | tf_op jit(solution)/shard_map/ppermute | solution.py:744
  636.5 5.5 fusion.45
  641.9 8.1 fusion.9.grad_ref
  650.1 18.6 %attend_back.1 = (bf16[320,2048]{1,0:T(8,128)(2,1)}, bf16[1088,2048]{1,0:T(8,128)(2,1)}) custom-call(s32[1]{0:T(128)} %bitcast.1.place_ref, bf16[320,2048]{1,0:T(8,128)(2,1)} %get-tuple-element.75.query_ref, bf16[1088,2048]{1,0:T(8,128)(2,1)} %get-tuple-element.76.key_ref.value_ref, bf16[1088,2048]{1,0:T(8,128)(2,1)} %get-tuple-element.76.key_ref.value_ref, ...), custom_call_target="tpu_custom_call" | custom-call | tf_op jit(solution)/shard_map/attend_back/pallas_call | solution.py:617
  668.7 40.3 %weights_back.1 = (bf16[2048,2048]{1,0:T(8,128)(2,1)}, bf16[2048,2048]{1,0:T(8,128)(2,1)}, bf16[2048,2048]{1,0:T(8,128)(2,1)}, f32[320,2048]{1,0:T(8,128)}, bf16...) custom-call(s32[1]{0:T(128)} %bitcast.1.place_ref, bf16[320,2048]{1,0:T(8,128)(2,1)} %get-tuple-element.97.query_ref, ...), custom_call_target="tpu_custom_call" | custom-call | tf_op jit(solution)/shard_map/weights_back/pallas_call | solution.py:696
  712.2 182.1 %finish.1 = (f32[64,4096]{1,0:T(8,128)}, f32[64,4096]{1,0:T(8,128)}, f32[64,4096]{1,0:T(8,128)}, f32[64,4096]{1,0:T(8,128)}, f32[64,2048]{1,0:T(8,128)}, /*index...) custom-call(bf16[4,4,2,64,2048]{4,3,2,1,0:T(8,128)(2,1)} %bitcast.73, ...), custom_call_target="tpu_custom_call" | custom-call | tf_op jit(solution)/shard_map/finish/pallas_call | solution.py:1148
  894.3 3.3 convert_reduce_fusion
  905.5 5.0 fusion.16
  (268 shorter events, 117.0 us)
Async XLA Ops:
  7.2 324.0 %all-gather.3.cloned.1.call-start = ((), (), s32[]{:S(2)}) async-start(), calls=%async_computation.2 | async-start | bytes 10485760 | tf_op jit(solution)/shard_map/all_gather | solution.py:1238
  177.6 234.6 %all-gather.5.cloned.1.call-start = ((), (), s32[]{:S(2)}) async-start(), calls=%async_computation.3 | async-start | bytes 5242880 | tf_op jit(solution)/shard_map/all_gather | solution.py:1242
  177.6 71.1 %collective-permute-start.5 = (bf16[320,2048]{1,0:T(8,128)(2,1)S(1)}, bf16[320,2048]{1,0:T(8,128)(2,1)}, u32[]{:S(2)}, u32[]{:S(2)}) collective-permute-start(bf16[320,2048]{1,0:T(8,128)(2,1)S(1)} %bitcast.84), channel_id=1, source_target_pairs={{0,6},{1,7},{2,4},{3,5},{4,2},{5,3},{6,0},{7,1},{8,14},{9,15},{10,... | collective-permute-start | bytes 3932168 | tf_op jit(solution)/shard_map/ppermute | solution.py:744
  178.7 69.4 %collective-permute-start.3 = (bf16[320,2048]{1,0:T(8,128)(2,1)S(1)}, bf16[320,2048]{1,0:T(8,128)(2,1)}, u32[]{:S(2)}, u32[]{:S(2)}) collective-permute-start(bf16[320,2048]{1,0:T(8,128)(2,1)S(1)} %bitcast.85), channel_id=1, source_target_pairs={{0,4},{1,5},{2,6},{3,7},{4,0},{5,1},{6,2},{7,3},{8,12},{9,13},{10,... | collective-permute-start | bytes 3932168 | tf_op jit(solution)/shard_map/ppermute | solution.py:744
  180.4 67.4 %collective-permute-start.1 = (bf16[320,2048]{1,0:T(8,128)(2,1)S(1)}, bf16[320,2048]{1,0:T(8,128)(2,1)}, u32[]{:S(2)}, u32[]{:S(2)}) collective-permute-start(bf16[320,2048]{1,0:T(8,128)(2,1)S(1)} %bitcast.86), channel_id=1, source_target_pairs={{0,2},{1,3},{2,0},{3,1},{4,6},{5,7},{6,4},{7,5},{8,10},{9,11},{10,... | collective-permute-start | bytes 3932168 | tf_op jit(solution)/shard_map/ppermute | solution.py:744
  180.4 68.5 %collective-permute-start = (bf16[320,2048]{1,0:T(8,128)(2,1)S(1)}, bf16[320,2048]{1,0:T(8,128)(2,1)}, u32[]{:S(2)}, u32[]{:S(2)}) collective-permute-start(bf16[320,2048]{1,0:T(8,128)(2,1)S(1)} %bitcast.87), channel_id=1, source_target_pairs={{0,1},{1,0},{2,3},{3,2},{4,5},{5,4},{6,7},{7,6},{8,9},{9,8},{10,11... | collective-permute-start | bytes 3932168 | tf_op jit(solution)/shard_map/ppermute | solution.py:744
  247.8 3.9 collective-permute-start.2
  248.1 5.2 collective-permute-start.4
  248.8 6.1 collective-permute-start.6
  255.0 30.0 %collective-permute-start.8 = (bf16[320,2048]{1,0:T(8,128)(2,1)S(1)}, bf16[320,2048]{1,0:T(8,128)(2,1)S(1)}, u32[]{:S(2)}, u32[]{:S(2)}) collective-permute-start(bf16[320,2048]{1,0:T(8,128)(2,1)S(1)} %multiply_convert_fusion.3), channel_id=1, source_target_pairs={{0,2},{1,3},{2,0},{3,1},{4,6},{5,7},{6,4},{7,5},{8,10},{9,11},{10,... | collective-permute-start | bytes 3932168 | tf_op jit(solution)/shard_map/ppermute | solution.py:744
  256.4 30.8 %collective-permute-start.10 = (bf16[320,2048]{1,0:T(8,128)(2,1)S(1)}, bf16[320,2048]{1,0:T(8,128)(2,1)S(1)}, u32[]{:S(2)}, u32[]{:S(2)}) collective-permute-start(bf16[320,2048]{1,0:T(8,128)(2,1)S(1)} %multiply_convert_fusion.3), channel_id=1, source_target_pairs={{0,4},{1,5},{2,6},{3,7},{4,0},{5,1},{6,2},{7,3},{8,12},{9,13},{10,... | collective-permute-start | bytes 3932168 | tf_op jit(solution)/shard_map/ppermute | solution.py:744
  256.6 60.3 %collective-permute-start.12 = (bf16[320,2048]{1,0:T(8,128)(2,1)S(1)}, bf16[320,2048]{1,0:T(8,128)(2,1)S(1)}, u32[]{:S(2)}, u32[]{:S(2)}) collective-permute-start(bf16[320,2048]{1,0:T(8,128)(2,1)S(1)} %multiply_convert_fusion.3), channel_id=1, source_target_pairs={{0,6},{1,7},{2,4},{3,5},{4,2},{5,3},{6,0},{7,1},{8,14},{9,15},{10,... | collective-permute-start | bytes 3932168 | tf_op jit(solution)/shard_map/ppermute | solution.py:744
  257.7 59.1 %collective-permute-start.7 = (bf16[320,2048]{1,0:T(8,128)(2,1)S(1)}, bf16[320,2048]{1,0:T(8,128)(2,1)S(1)}, u32[]{:S(2)}, u32[]{:S(2)}) collective-permute-start(bf16[320,2048]{1,0:T(8,128)(2,1)S(1)} %multiply_convert_fusion.3), channel_id=1, source_target_pairs={{0,1},{1,0},{2,3},{3,2},{4,5},{5,4},{6,7},{7,6},{8,9},{9,8},{10,11... | collective-permute-start | bytes 3932168 | tf_op jit(solution)/shard_map/ppermute | solution.py:744
  285.0 34.3 %collective-permute-start.9 = (bf16[320,2048]{1,0:T(8,128)(2,1)S(1)}, bf16[320,2048]{1,0:T(8,128)(2,1)S(1)}, u32[]{:S(2)}, u32[]{:S(2)}) collective-permute-start(bf16[320,2048]{1,0:T(8,128)(2,1)S(1)} %collective-permute-done.8), channel_id=1, source_target_pairs={{0,1},{1,0},{2,3},{3,2},{4,5},{5,4},{6,7},{7,6},{8,9},{9,8},{10,11... | collective-permute-start | bytes 3932168 | tf_op jit(solution)/shard_map/ppermute | solution.py:744
  287.2 34.6 %collective-permute-start.11 = (bf16[320,2048]{1,0:T(8,128)(2,1)S(1)}, bf16[320,2048]{1,0:T(8,128)(2,1)S(1)}, u32[]{:S(2)}, u32[]{:S(2)}) collective-permute-start(bf16[320,2048]{1,0:T(8,128)(2,1)S(1)} %collective-permute-done.10), channel_id=1, source_target_pairs={{0,1},{1,0},{2,3},{3,2},{4,5},{5,4},{6,7},{7,6},{8,9},{9,8},{10,11... | collective-permute-start | bytes 3932168 | tf_op jit(solution)/shard_map/ppermute | solution.py:744
  316.9 7.4 collective-permute-start.13
  331.3 235.6 %reduce-scatter.3.cloned.1.call-start = ((), (), s32[]{:S(2)}) async-start(), calls=%async_computation.4 | async-start | bytes 5242880 | tf_op jit(solution)/shard_map/reduce_scatter | solution.py:768
  475.5 236.7 %reduce-scatter.5.cloned.1.call-start = ((), (), s32[]{:S(2)}) async-start(), calls=%async_computation.5 | async-start | bytes 10485760 | tf_op jit(solution)/shard_map/reduce_scatter | solution.py:768
  477.8 19.9 %collective-permute-start.22 = (bf16[320,2048]{1,0:T(8,128)(2,1)S(1)}, bf16[320,2048]{1,0:T(8,128)(2,1)S(1)}, u32[]{:S(2)}, u32[]{:S(2)}) collective-permute-start(bf16[320,2048]{1,0:T(8,128)(2,1)S(1)} %slice.151), channel_id=1, source_target_pairs={{0,1},{1,0},{2,3},{3,2},{4,5},{5,4},{6,7},{7,6},{8,9},{9,8},{10,11... | collective-permute-start | bytes 3932168 | tf_op jit(solution)/shard_map/ppermute | solution.py:744
  487.8 13.9 %collective-permute-start.24 = (bf16[320,2048]{1,0:T(8,128)(2,1)S(1)}, bf16[320,2048]{1,0:T(8,128)(2,1)S(1)}, u32[]{:S(2)}, u32[]{:S(2)}) collective-permute-start(bf16[320,2048]{1,0:T(8,128)(2,1)S(1)} %slice.155), channel_id=1, source_target_pairs={{0,1},{1,0},{2,3},{3,2},{4,5},{5,4},{6,7},{7,6},{8,9},{9,8},{10,11... | collective-permute-start | bytes 3932168 | tf_op jit(solution)/shard_map/ppermute | solution.py:744
  487.9 16.6 %collective-permute-start.26 = (bf16[320,2048]{1,0:T(8,128)(2,1)S(1)}, bf16[320,2048]{1,0:T(8,128)(2,1)S(1)}, u32[]{:S(2)}, u32[]{:S(2)}) collective-permute-start(bf16[320,2048]{1,0:T(8,128)(2,1)S(1)} %slice.159), channel_id=1, source_target_pairs={{0,1},{1,0},{2,3},{3,2},{4,5},{5,4},{6,7},{7,6},{8,9},{9,8},{10,11... | collective-permute-start | bytes 3932168 | tf_op jit(solution)/shard_map/ppermute | solution.py:744
  497.6 34.5 %collective-permute-start.21 = (bf16[320,2048]{1,0:T(8,128)(2,1)}, bf16[320,2048]{1,0:T(8,128)(2,1)}, u32[]{:S(2)}, u32[]{:S(2)}) collective-permute-start(bf16[320,2048]{1,0:T(8,128)(2,1)} %slice.147), channel_id=1, source_target_pairs={{0,1},{1,0},{2,3},{3,2},{4,5},{5,4},{6,7},{7,6},{8,9},{9,8},{10,11... | collective-permute-start | bytes 3932168 | tf_op jit(solution)/shard_map/ppermute | solution.py:744
  500.2 31.8 %collective-permute-start.23 = (bf16[320,2048]{1,0:T(8,128)(2,1)}, bf16[320,2048]{1,0:T(8,128)(2,1)}, u32[]{:S(2)}, u32[]{:S(2)}) collective-permute-start(bf16[320,2048]{1,0:T(8,128)(2,1)} %add_convert_fusion.2), channel_id=1, source_target_pairs={{0,2},{1,3},{2,0},{3,1},{4,6},{5,7},{6,4},{7,5},{8,10},{9,11},{10,... | collective-permute-start | bytes 3932168 | tf_op jit(solution)/shard_map/ppermute | solution.py:744
  503.2 58.4 %collective-permute-start.25 = (bf16[320,2048]{1,0:T(8,128)(2,1)}, bf16[320,2048]{1,0:T(8,128)(2,1)}, u32[]{:S(2)}, u32[]{:S(2)}) collective-permute-start(bf16[320,2048]{1,0:T(8,128)(2,1)} %add_convert_fusion.1), channel_id=1, source_target_pairs={{0,4},{1,5},{2,6},{3,7},{4,0},{5,1},{6,2},{7,3},{8,12},{9,13},{10,... | collective-permute-start | bytes 3932168 | tf_op jit(solution)/shard_map/ppermute | solution.py:744
  506.0 55.7 %collective-permute-start.27 = (bf16[320,2048]{1,0:T(8,128)(2,1)}, bf16[320,2048]{1,0:T(8,128)(2,1)}, u32[]{:S(2)}, u32[]{:S(2)}) collective-permute-start(bf16[320,2048]{1,0:T(8,128)(2,1)} %add_convert_fusion), channel_id=1, source_target_pairs={{0,6},{1,7},{2,4},{3,5},{4,2},{5,3},{6,0},{7,1},{8,14},{9,15},{10,... | collective-permute-start | bytes 3932168 | tf_op jit(solution)/shard_map/ppermute | solution.py:744
  566.9 4.1 collective-permute-start.15
  568.1 8.3 collective-permute-start.17
  569.3 9.9 %collective-permute-start.19 = (bf16[320,2048]{1,0:T(8,128)(2,1)}, bf16[320,2048]{1,0:T(8,128)(2,1)S(1)}, u32[]{:S(2)}, u32[]{:S(2)}) collective-permute-start(bf16[320,2048]{1,0:T(8,128)(2,1)} %get-tuple-element.93), channel_id=1, source_target_pairs={{0,1},{1,0},{2,3},{3,2},{4,5},{5,4},{6,7},{7,6},{8,9},{9,8},{10,11... | collective-permute-start | bytes 3932168 | tf_op jit(solution)/shard_map/ppermute | solution.py:744
  569.3 14.4 %collective-permute-start.14 = (bf16[320,2048]{1,0:T(8,128)(2,1)}, bf16[320,2048]{1,0:T(8,128)(2,1)}, u32[]{:S(2)}, u32[]{:S(2)}) collective-permute-start(bf16[320,2048]{1,0:T(8,128)(2,1)} %get-tuple-element.87), channel_id=1, source_target_pairs={{0,1},{1,0},{2,3},{3,2},{4,5},{5,4},{6,7},{7,6},{8,9},{9,8},{10,11... | collective-permute-start | bytes 3932168 | tf_op jit(solution)/shard_map/ppermute | solution.py:744
  572.5 30.3 %collective-permute-start.16 = (bf16[320,2048]{1,0:T(8,128)(2,1)}, bf16[320,2048]{1,0:T(8,128)(2,1)}, u32[]{:S(2)}, u32[]{:S(2)}) collective-permute-start(bf16[320,2048]{1,0:T(8,128)(2,1)} %add_convert_fusion.6), channel_id=1, source_target_pairs={{0,2},{1,3},{2,0},{3,1},{4,6},{5,7},{6,4},{7,5},{8,10},{9,11},{10,... | collective-permute-start | bytes 3932168 | tf_op jit(solution)/shard_map/ppermute | solution.py:744
  578.0 58.5 %collective-permute-start.18 = (bf16[320,2048]{1,0:T(8,128)(2,1)}, bf16[320,2048]{1,0:T(8,128)(2,1)}, u32[]{:S(2)}, u32[]{:S(2)}) collective-permute-start(bf16[320,2048]{1,0:T(8,128)(2,1)} %add_convert_fusion.5), channel_id=1, source_target_pairs={{0,4},{1,5},{2,6},{3,7},{4,0},{5,1},{6,2},{7,3},{8,12},{9,13},{10,... | collective-permute-start | bytes 3932168 | tf_op jit(solution)/shard_map/ppermute | solution.py:744
  580.8 55.7 %collective-permute-start.20 = (bf16[320,2048]{1,0:T(8,128)(2,1)}, bf16[320,2048]{1,0:T(8,128)(2,1)}, u32[]{:S(2)}, u32[]{:S(2)}) collective-permute-start(bf16[320,2048]{1,0:T(8,128)(2,1)} %add_convert_fusion.4), channel_id=1, source_target_pairs={{0,6},{1,7},{2,4},{3,5},{4,2},{5,3},{6,0},{7,1},{8,14},{9,15},{10,... | collective-permute-start | bytes 3932168 | tf_op jit(solution)/shard_map/ppermute | solution.py:744
  (54 other events, 758.2 us)
Sparse Core Ops, SparseCore 0:
  177.7 153.5 all-gather.2
  332.8 79.2 all-gather.4
  475.6 77.8 reduce-scatter.2
  567.0 145.1 reduce-scatter.4

commit v4 on v3

--- a/solution.py
+++ b/solution.py
@@ -266,15 +266,29 @@
             half_copy(block, 1).wait_recv()
             core_copy(block, 6).start()
 
+    def both(step, act):
+        for way in (0, 1):
+            pl.when(receives(way, step))(
+                lambda way=way: act(g - step if way == 0 else g + step)
+            )
+
+    def take_rows(step):
+        for way in (0, 1):
+
+            @pl.when(receives(way, step))
+            def _(way=way):
+                line_rows(way, step).wait_recv()
+
+            if step + 1 < lines:
+                pl.when(sends(way, step + 1))(
+                    lambda way=way: line_rows(way, step + 1).start()
+                )
+
     for way in (0, 1):
         pl.when(sends(way, 1))(lambda way=way: line_weight(way, 1).start())
     launch(g, True)
     for one in locals_:
         one.start()
-    for offset in range(1, plane):
-        for part in range(3):
-            swap_copy(offset, part).start()
-
     for step in range(1, lines):
         for way in (0, 1):
 
@@ -289,41 +303,20 @@
             else:
                 pl.when(sends(way, 1))(lambda way=way: line_rows(way, 1).start())
 
-            @pl.when(receives(way, step))
-            def _(way=way, step=step):
-                launch(g - step if way == 0 else g + step, False)
-
+        both(step, lambda block: launch(block, False))
         if step == 1:
             relay(g)
+            for offset in range(1, plane):
+                for part in range(3):
+                    swap_copy(offset, part).start()
+    for step in range(1, lines):
+        take_rows(step)
+        both(step, relay)
+        if step == 1:
+            finish(g)
         else:
-            for way in (0, 1):
-                pl.when(receives(way, step - 1))(
-                    lambda way=way, step=step: relay(
-                        g - step + 1 if way == 0 else g + step - 1
-                    )
-                )
-    for step in range(1, lines):
-        for way in (0, 1):
-
-            @pl.when(receives(way, step))
-            def _(way=way, step=step):
-                line_rows(way, step).wait_recv()
-
-            if step + 1 < lines:
-                pl.when(sends(way, step + 1))(
-                    lambda way=way, step=step: line_rows(way, step + 1).start()
-                )
-        if step == 1:
-            for way in (0, 1):
-                pl.when(receives(way, lines - 1))(
-                    lambda way=way: relay(g - lines + 1 if way == 0 else g + lines - 1)
-                )
-            finish(g)
-    for step in range(1, lines):
-        for way in (0, 1):
-            pl.when(receives(way, step))(
-                lambda way=way, step=step: finish(g - step if way == 0 else g + step)
-            )
+            both(step - 1, finish)
+    both(lines - 1, finish)
 
     def drain(block):
         for offset in evens:
@@ -776,6 +769,7 @@
     merge_ref,
     gain_ref,
     gate_ref,
+    up_ref,
     down_ref,
     back_ref,
     a_master,
@@ -805,8 +799,7 @@
     core_in,
     plane_in,
     line_in,
-    gate_in,
-    down_in,
+    swap_in,
     state,
     made,
     a_state,
@@ -835,7 +828,7 @@
     chip, core = lax.div(d, 2), lax.rem(d, 2)
     partner = d + 1 - 2 * core
     rows = a_master.shape[0]
-    own_hidden = down_ref.shape[2]
+    own_hidden = gate_ref.shape[2]
     width = core_in.shape[3]
     a_width, m_width = a_master.shape[1], m_master.shape[1]
     parts, begin = [], 0
@@ -874,6 +867,9 @@
             ref.at[line, :, core], mine.at[turn % 2, :, :, columns], mine_sem.at[turn, part]
         )
 
+    cut = width // 256 * 128
+    columns_of = (pl.ds(0, cut), pl.ds(cut, width - cut))
+
     def plane_copy(turn, step):
         line = line_at(turn)
         there = lax.rem(chip + step, chips)
@@ -885,6 +881,29 @@
             (g, 2 * there + core),
         )
 
+    def near_copy(turn, part, relayed):
+        line = line_at(turn)
+        there = flip(chip, part + 1)
+        owner = flip(chip, 3) if relayed else there
+        return remote(
+            core_in.at[line, owner, :, columns_of[part]],
+            plane_in.at[line, 1 if relayed else 0, :, columns_of[part]],
+            plane_send.at[turn, 2 * relayed + part],
+            plane_recv.at[turn, 2 * relayed + part],
+            (g, 2 * there + core),
+        )
+
+    def relay_copy(turn, part):
+        line = line_at(turn)
+        there = flip(chip, 2 - part)
+        return remote(
+            core_in.at[line, there, :, columns_of[part]],
+            plane_in.at[line, 2, :, columns_of[part]],
+            plane_send.at[turn, 4 + part],
+            plane_recv.at[turn, 4 + part],
+            (g, 2 * there + core),
+        )
+
     def line_copy(turn):
         line = line_at(turn)
         return remote(
@@ -895,21 +914,22 @@
             (line, d),
         )
 
+    forward_refs = (gate_ref, up_ref, down_ref)
+
     def swap_copy(step, part):
         there = lax.rem(d + step, plane)
-        source, target = (gate_ref, gate_in) if part == 0 else (down_ref, down_in)
         return remote(
-            source.at[there],
-            target.at[d],
+            forward_refs[part].at[there],
+            swap_in.at[part, d],
             swap_send.at[step, part],
             swap_recv.at[step, part],
             (g, there),
         )
 
-    own_swap = (
-        pltpu.make_async_copy(gate_ref.at[d], gate_in.at[d], own_sem.at[0]),
-        pltpu.make_async_copy(down_ref.at[d], down_in.at[d], own_sem.at[1]),
-    )
+    own_swap = [
+        pltpu.make_async_copy(forward_refs[part].at[d], swap_in.at[part, d], own_sem.at[part])
+        for part in range(3)
+    ]
 
     def f_columns(turn):
         block = lax.rem(d + lax.div(turn, 3), plane)
@@ -943,7 +963,7 @@
             (there, d),
         )
 
-    own_back = pltpu.make_async_copy(back_ref.at[g], back_out.at[g], own_sem.at[2])
+    own_back = pltpu.make_async_copy(back_ref.at[g], back_out.at[g], own_sem.at[3])
 
     slabs = (pl.ds(0, a_width), pl.ds(a_width, m_width))
 
@@ -971,7 +991,7 @@
     for step in range(1, lines):
         back_copy(step).start()
     for step in range(1, plane):
-        for part in range(2):
+        for part in range(3):
             swap_copy(step, part).start()
     for one in own_swap:
         one.start()
@@ -982,30 +1002,52 @@
             a_state_copy(which, slab).start()
 
     tile = 896 if width % 896 == 0 else 128
-    tiles = width // tile
+    halves = plane == 8
+
+    def add_into(line, there, other, columns=None):
+        first, count = (0, width) if columns is None else columns
+        step = tile if columns is None else 128
+
+        @pl.loop(0, count // step)
+        def _(at):
+            here = pl.ds(pl.multiple_of(first + at * step, 128), step)
+            total = core_in[line, there, :, here].astype(FULL) + other(here).astype(FULL)
+            core_in[line, there, :, here] = total.astype(LOW)
 
     for turn in range(lines):
         line = line_at(turn)
         for part in every:
             core_copy(turn, part).wait_recv()
             mine_copy(turn, part).wait()
-        for step in range(1, chips + 1):
-            there = lax.rem(chip + step, chips)
-
-            @pl.loop(0, tiles)
-            def _(at, line=line, there=there, turn=turn):
-                columns = pl.ds(pl.multiple_of(at * tile, tile), tile)
-                total = mine[turn % 2, there, :, columns].astype(FULL) + core_in[
-                    line, there, :, columns
-                ].astype(FULL)
-                core_in[line, there, :, columns] = total.astype(LOW)
-
-            if step < chips:
+        order = (3, 1, 2, 0) if halves else tuple(range(1, chips + 1))
+        for step in order:
+            there = flip(chip, step) if halves else lax.rem(chip + step, chips)
+            add_into(
+                line, there, lambda here, there=there, turn=turn: mine[turn % 2, there, :, here]
+            )
+            if halves and step == 3:
+                for part in range(2):
+                    near_copy(turn, part, True).start()
+            elif halves and step:
+                near_copy(turn, step - 1, False).start()
+            elif not halves and step < chips:
                 plane_copy(turn, step).start()
         if turn + 2 < lines:
             for part in every:
                 mine_copy(turn + 2, part).start()
 
+    def pass_on(turn):
+        line = line_at(turn)
+        for part, columns in enumerate(((0, cut), (cut, width - cut))):
+            near_copy(turn, part, True).wait_recv()
+            add_into(
+                line,
+                flip(chip, 2 - part),
+                lambda here, line=line: plane_in[line, 1, :, here],
+                columns,
+            )
+            relay_copy(turn, part).start()
+
     def forward_turn(turn):
         slot = lax.rem(turn, 2)
         block = lax.rem(d + lax.div(turn, 3), plane)
@@ -1024,51 +1066,54 @@
         for which in range(3):
             state_copy(turn, which).wait()
 
-        def rows_step(read):
-            @pl.loop(0, rows // 16)
-            def _(at):
-                rows_at = pl.ds(pl.multiple_of(at * 16, 16), 16)
-                gradient = read(rows_at).astype(FULL)
-                update, first_new, second_new = adam_step(
-                    state[slot, 0, rows_at],
-                    state[slot, 1, rows_at],
-                    state[slot, 2, rows_at],
-                    gradient,
-                    WEIGHT_DECAY,
-                )
-                made[slot, 0, rows_at] = gradient
-                made[slot, 1, rows_at] = update
-                made[slot, 2, rows_at] = first_new
-                made[slot, 3, rows_at] = second_new
-
-        for own in range(2):
-            pl.when(part == own)(
-                lambda own=own: rows_step(
-                    lambda at: gate_in[block, at, pl.ds(own * own_hidden, own_hidden)]
-                )
+        @pl.loop(0, rows // 16)
+        def _(at):
+            rows_at = pl.ds(pl.multiple_of(at * 16, 16), 16)
+            gradient = swap_in[part, block, rows_at].astype(FULL)
+            update, first_new, second_new = adam_step(
+                state[slot, 0, rows_at],
+                state[slot, 1, rows_at],
+                state[slot, 2, rows_at],
+                gradient,
+                WEIGHT_DECAY,
             )
-        pl.when(part == 2)(lambda: rows_step(lambda at: down_in[block, at]))
+            made[slot, 0, rows_at] = gradient
+            made[slot, 1, rows_at] = update
+            made[slot, 2, rows_at] = first_new
+            made[slot, 3, rows_at] = second_new
+
         for which in range(4):
             made_copy(turn, which).start()
 
+    if halves:
+        pass_on(0)
     for one in own_swap:
         one.wait()
     for step in range(1, plane):
-        for part in range(2):
+        for part in range(3):
             swap_copy(step, part).wait_recv()
     each = 3 * plane // lines
     for turn in range(lines):
         lax.fori_loop(turn * each, (turn + 1) * each, lambda k, c: (forward_turn(k), c)[1], 0)
         line = line_at(turn)
-        for step in range(1, chips):
-            plane_copy(turn, step).wait_recv()
-
-        @pl.loop(0, tiles)
-        def _(at, line=line):
+        if halves:
+            if turn + 1 < lines:
+                pass_on(turn + 1)
+            for part in range(2):
+                near_copy(turn, part, False).wait_recv()
+                relay_copy(turn, part).wait_recv()
+            arrived = (0, 2)
+        else:
+            for step in range(1, chips):
+                plane_copy(turn, step).wait_recv()
+            arrived = tuple(lax.rem(chip + step, chips) for step in range(1, chips))
+
+        @pl.loop(0, width // tile)
+        def _(at, line=line, arrived=arrived):
             columns = pl.ds(pl.multiple_of(at * tile, tile), tile)
             total = core_in[line, chip, :, columns].astype(FULL)
-            for step in range(1, chips):
-                total = total + plane_in[line, lax.rem(chip + step, chips), :, columns].astype(FULL)
+            for block in arrived:
+                total = total + plane_in[line, block, :, columns].astype(FULL)
             core_in[line, chip, :, columns] = total.astype(LOW)
 
         if turn < lines - 1:
@@ -1114,12 +1159,18 @@
     for turn in range(lines):
         for part in every:
             core_copy(turn, part).wait_send()
-        for step in range(1, chips):
-            plane_copy(turn, step).wait_send()
+        if halves:
+            for part in range(2):
+                near_copy(turn, part, False).wait_send()
+                near_copy(turn, part, True).wait_send()
+                relay_copy(turn, part).wait_send()
+        else:
+            for step in range(1, chips):
+                plane_copy(turn, step).wait_send()
         if turn < lines - 1:
             line_copy(turn).wait_send()
     for step in range(1, plane):
-        for part in range(2):
+        for part in range(3):
             swap_copy(step, part).wait_send()
     for step in range(1, lines):
         back_copy(step).wait()
@@ -1130,12 +1181,12 @@
     gain_copy.wait()
 
 
-def finish(terms, gate_part, down_part, pair_back, attention, merge, forward):
+def finish(terms, forward_parts, pair_back, attention, merge, forward):
     lines, plane = lax.axis_size("grp"), lax.axis_size("dp")
     chips = plane // 2
     rows, a_width = attention[0].shape
     m_width = merge[0].shape[1]
-    own_hidden = down_part.shape[1]
+    own_hidden = forward_parts[0].shape[1]
     width = a_width + m_width + GAIN_PAD
     anywhere = pl.BlockSpec(memory_space=pl.ANY)
     dma = pltpu.SemaphoreType.DMA
@@ -1151,15 +1202,14 @@
         + (like(merge[0]),) * 4
         + (jax.ShapeDtypeStruct((rows, GAIN_PAD), FULL), like(back))
         + (like(forward[0]),) * 4,
-        in_specs=[anywhere] * 16,
+        in_specs=[anywhere] * 17,
         out_specs=(anywhere,) * 14,
         scratch_shapes=[
             vmem((2, chips, rows, width), LOW),
             vmem((lines, chips, rows, width), LOW),
-            vmem((lines, chips, rows, width), LOW),
+            vmem((lines, 3 if plane == 8 else chips, rows, width), LOW),
             vmem((lines, rows, width), LOW),
-            vmem((plane, rows, 2 * own_hidden), LOW),
-            vmem((plane, rows, own_hidden), LOW),
+            vmem((3, plane, rows, own_hidden), LOW),
             vmem((2, 3, rows, own_hidden), FULL),
             vmem((2, 4, rows, own_hidden), FULL),
             vmem((3, rows, a_width + m_width), FULL),
@@ -1168,13 +1218,13 @@
             dma((lines, 4)),
             dma((lines, 4)),
             dma((lines, 4)),
-            dma((lines, chips)),
-            dma((lines, chips)),
+            dma((lines, max(6, chips))),
+            dma((lines, max(6, chips))),
             dma((lines,)),
             dma((lines,)),
-            dma((plane, 2)),
-            dma((plane, 2)),
-            dma((3,)),
+            dma((plane, 3)),
+            dma((plane, 3)),
+            dma((4,)),
             dma((2, 3)),
             dma((2, 4)),
             dma((2, 7)),
@@ -1188,8 +1238,7 @@
         name="finish",
     )(
         *(term.reshape(lines, chips, 2, rows, term.shape[1]) for term in terms),
-        gate_part.reshape(plane, rows, -1),
-        down_part.reshape(plane, rows, -1),
+        *(part.reshape(plane, rows, -1) for part in forward_parts),
         back,
         *attention,
         *merge,
@@ -1277,10 +1326,12 @@
     normed_two = (middle * second_scale * gain_float[1]).astype(LOW)
     grad_rows = cotangent.reshape(row_count, D).astype(FULL)
 
-    def by_offset(left, right, right_axis):
+    def by_offset(left, right, right_axis, after=None):
         chunks = {}
-        for offset in range(0, dp_size, 2):
+        for offset in list(range(2, dp_size, 2)) + [0]:
             rows = left[offset * row_count : (offset + 2) * row_count]
+            if offset == 0 and after is not None:
+                rows, _ = lax.optimization_barrier((rows, after))
             chunks[offset] = contract(rows, right, 1, right_axis).astype(LOW)
         return lambda offset: chunks[offset - offset % 2][
             (offset % 2) * row_count : (offset % 2 + 1) * row_count
@@ -1297,26 +1348,38 @@
     out_parts = by_offset(activated, down_weight, 1)
     out_chunks = [out_parts(offset) for offset in range(dp_size)]
     out_chunks, down_grad = lax.optimization_barrier((out_chunks, down_grad))
-    out_sum = plane_scatter(lambda offset: out_chunks[offset])
+    out_swapped = [plane_swap(out_chunks[offset + 1], 1) for offset in range(0, dp_size, 2)]
     activated_grad = contract(down_grad, down_weight, 1, 0)
     gate_grad, up_grad = gate_backward(
         activated_grad, gate_values, up_values, gate_sigmoid, gate_silu
     )
     gate_up_grad = jnp.concatenate([gate_grad, up_grad], axis=1)
 
-    back_parts = by_offset(gate_up_grad, gate_weight, 1)
+    gate_up_grad, out_swapped = lax.optimization_barrier((gate_up_grad, out_swapped))
+    out_sums = [
+        out_chunks[2 * at].astype(FULL) + one.astype(FULL) for at, one in enumerate(out_swapped)
+    ]
+    out_arrived = [plane_swap(one.astype(LOW), 2 * at) for at, one in enumerate(out_sums) if at]
+    down_part = line_scatter(down_term)
+    back_parts = by_offset(gate_up_grad, gate_weight, 1, down_part)
     normed_two_grad = plane_scatter(back_parts)
-    down_part = line_scatter(down_term)
-    gate_term = contract(normed_all, gate_up_grad, 0, 0).astype(LOW)
-    normed_two_grad, gate_term = lax.optimization_barrier((normed_two_grad, gate_term))
-    gate_term, down_part = lax.optimization_barrier((gate_term, down_part))
+    gate_term = contract(normed_all, gate_up_grad[:, :own_hidden], 0, 0).astype(LOW)
+    normed_all, out_arrived = lax.optimization_barrier((normed_all, out_arrived))
+    up_term = contract(normed_all, gate_up_grad[:, own_hidden:], 0, 0).astype(LOW)
     gate_part = line_scatter(gate_term)
-    result = middle + out_sum
+    normed_two_grad, gate_term, up_term = lax.optimization_barrier(
+        (normed_two_grad, gate_term, up_term)
+    )
+    result = middle + out_sums[0]
+    for one in out_arrived:
+        result = result + one.astype(FULL)
     block_output = result.astype(LOW).reshape(hidden.shape)
     middle_grad = grad_rows + norm_back(middle, second_scale, gain_float[1], normed_two_grad)
     gain_two_part = jnp.sum(normed_two_grad * middle * second_scale, axis=0)
     branch_grad = middle_grad.astype(LOW)
     attended_grad = contract(branch_grad, merge_weight, 1, 0).astype(LOW)
+    attended_grad, gate_part = lax.optimization_barrier((attended_grad, gate_part))
+    up_part = line_scatter(up_term)
     query_project, pair_project = attend_back(
         place, queries, pairs, seen, row_logsum, attended_grad, cosine, sine_part
     )
@@ -1338,8 +1401,7 @@
     )
     finished = finish(
         (query_term, pair_term, merge_term, gain_term.astype(LOW)),
-        gate_part,
-        down_part,
+        (gate_part, up_part, down_part),
         pair_back,
         (attention_master, attention_first, attention_second),
         (merge_master, merge_first, merge_second),

time: 953 us -> 916 us (0.961)
  waiting for transfers between devices: 147 us -> 85.4 us
  other arithmetic: 60.3 us -> 73.9 us
    ppermute x28, waiting for transfers between devices: 113 us -> 57.5 us  [plane_swap(): return lax.ppermute(block, 'dp', [(i, i ^ offset) for i in range(size)])]
    pallas_call x1, Pallas kernels: 182 us -> 197 us  [finish(): pl.pallas_call(functools.partial(finish_kernel, lines, plane), out_shape=...]
    pallas_call x1, Pallas kernels: 161 us -> 149 us  [gather_start(): pl.pallas_call(functools.partial(gather_kernel, lines, plane, prompt_rows...]
    convert_element_type x0 -> x3, other arithmetic: none -> 9.98 us  [body(): one.astype(LOW)]
    dot_general x13 -> x14, matrix products: 129 us -> 137 us  [contract(): lax.dot_general(left, right, (((left_axis,), (right_axis,)), ((), ())), p...]
    unnamed x139 -> x129, local copies, waits for them, and re-layouts: 43.8 us -> 47.5 us
  transfers between devices with their start and end apart: 32 -> 33, of which waited for: 9 -> 5; matrix products, arithmetic and copies ran while one was open for 17% -> 25% of each run, Pallas kernels for 11% -> 12%
where the time goes in v4:
time: 916 us; the launch traced here: 906 us
  Pallas kernels  450 us (49%)
  matrix products  166 us (18%)
  waiting for transfers between devices  85.4 us (9%)
  other arithmetic  73.9 us (8%)
  local copies, waits for them, and re-layouts  64.9 us (7%)
  starting transfers between devices  50.1 us (5%)
  between operations  15.5 us (2%)
    pallas_call x1, Pallas kernels, finish(): pl.pallas_call(functools.partial(finish_kernel, lines, plane), out_shape=...  197 us
    pallas_call x1, Pallas kernels, gather_start(): pl.pallas_call(functools.partial(gather_kernel, lines, plane, prompt_rows...  149 us
    dot_general x14, matrix products, contract(): lax.dot_general(left, right, (((left_axis,), (right_axis,)), ((), ())), p...  137 us
    ppermute x28, waiting for transfers between devices, plane_swap(): return lax.ppermute(block, 'dp', [(i, i ^ offset) for i in range(size)])  57.5 us
    ppermute x28, starting transfers between devices, plane_swap(): return lax.ppermute(block, 'dp', [(i, i ^ offset) for i in range(size)])  49.7 us
    unnamed x129, local copies, waits for them, and re-layouts  47.5 us
    pallas_call x1, Pallas kernels, weights_back(): pl.pallas_call(weights_back_kernel, grid_spec=pltpu.PrefetchScalarGridSpe...  40.3 us
    pallas_call x1, Pallas kernels, project_heads(): pl.pallas_call(project_kernel, grid_spec=pltpu.PrefetchScalarGridSpec(num...  34.3 us
  transfers between devices with their start and end apart: 33, of which 5 were waited for; matrix products, arithmetic and copies ran while one was open for 25% of the time, Pallas kernels for 12%

profile of v4, /device:TPU:9, one launch (start us, length us, event | category | flops | bytes accessed | tf_op | source)
XLA Modules:
  0.0 906.1 jit_solution(16814388471111816902)
XLA Ops:
  10.4 4.8 convert_element_type.185.forward_ref
  16.1 148.6 %gather_start.1 = (bf16[4,8,64,6272]{3,2,1,0:T(8,128)(2,1)}, bf16[4,256,2048]{2,1,0:T(8,128)(2,1)}, bf16[8,64,2048]{2,1,0:T(8,128)(2,1)}, bf16[8,64,1024]{2,1,0:T(8,128)(2,1)}) custom-call(bf16[64,6272]{1,0:T(8,128)(2,1)} %fusion.37.weight_ref, bf16[320,2048]{1,0:T(8,128)(2,1)} %bitcast.71, bf16[64,24576]{1,0:T(8,128)(2,1)} %convert_element_type.185.forward_ref), custom_call_target="tpu_custom_call" | custom-call | tf_op jit(solution)/shard_map/gather_start/pallas_call | solution.py:371
  177.3 34.3 %project_heads.1 = (bf16[320,2048]{1,0:T(8,128)(2,1)}, bf16[1088,2048]{1,0:T(8,128)(2,1)}, bf16[1088,2048]{1,0:T(8,128)(2,1)}, bf16[320,2048]{1,0:T(8,128)(2,1)}, f32[1088,128]{1,0:T(8,128)}) custom-call(s32[1]{0:T(128)} %bitcast.1.place_ref, bf16[1024,2048]{1,0:T(8,128)(2,1)} %bitcast.74, bf16[320,2048]{1,0:T(8,128)(2,1)} %bitcast.72, ...), custom_call_target="tpu_custom_call" | custom-call | tf_op jit(solution)/shard_map/project_heads/pallas_call | solution.py:469
  213.5 11.4 %attend.1 = (bf16[320,2048]{1,0:T(8,128)(2,1)}, f32[320,1024]{1,0:T(8,128)}) custom-call(bf16[320,2048]{1,0:T(8,128)(2,1)} %get-tuple-element.85.query_ref, bf16[1088,2048]{1,0:T(8,128)(2,1)} %get-tuple-element.86.key_ref.value_ref, bf16[1088,2048]{1,0:T(8,128)(2,1)} %get-tuple-element.86.key_ref.value_ref, f32[320,1088]{1,0:T(8,128)} %add_convert_fusion.7.seen_ref), custom_call_target="tpu_custom_call" | custom-call | tf_op jit(solution)/shard_map/attend/pallas_call | solution.py:531
  224.9 5.9 multiply_reduce_fusion.2
  242.7 26.1 %collective-permute-done.8 = bf16[320,2048]{1,0:T(8,128)(2,1)S(1)} collective-permute-done((bf16[320,2048]{1,0:T(8,128)(2,1)S(1)}, bf16[320,2048]{1,0:T(8,128)(2,1)S(1)}, u32[]{:S(2)}, u32[]{:S(2)}) %collective-permute-start.8) | collective-permute-done | bytes 1310752 | tf_op jit(solution)/shard_map/ppermute | solution.py:737
  270.9 28.4 %collective-permute-start.11 = (bf16[320,2048]{1,0:T(8,128)(2,1)S(1)}, bf16[320,2048]{1,0:T(8,128)(2,1)S(1)}, u32[]{:S(2)}, u32[]{:S(2)}) collective-permute-start(bf16[320,2048]{1,0:T(8,128)(2,1)S(1)} %collective-permute-done.10), channel_id=1, source_target_pairs={{0,1},{1,0},{2,3},{3,2},{4,5},{5,4},{6,7},{7,6},{8,9},{9,8},{10,11... | collective-permute-start | bytes 3932168 | tf_op jit(solution)/shard_map/ppermute | solution.py:737
  310.7 28.9 %fusion.48 = f32[2560,2048]{0,1:T(8,128)} fusion(bf16[2560,2048]{1,0:T(8,128)(2,1)} %constant_dynamic-update-slice_fusion.8, bf16[2048,2048]{1,0:T(8,128)(2,1)} %all-gather.3.cloned.1.call-done), kind=kOutput, calls=%fused_computation.128 | convolution fusion | flops 21474836480 | bytes 39845888 | tf_op jit(solution)/shard_map/dot_general | solution.py:1342
  339.5 8.6 multiply_convert_fusion.2
  351.1 13.7 %convolution_convert_fusion = bf16[2048,1024]{1,0:T(8,128)(2,1)} fusion(bf16[2560,2048]{1,0:T(8,128)(2,1)S(1)} %copy-done.29, bf16[2560,1024]{0,1:T(8,128)(2,1)S(1)} %multiply_convert_fusion.2), kind=kOutput, calls=%fused_computation.19 | convolution fusion | flops 10739515392 | bytes 19922944 | tf_op jit(solution)/shard_map/dot_general | solution.py:35
  364.7 26.5 %all-gather.5.cloned.1.call-done = bf16[2048,1024]{1,0:T(8,128)(2,1)} async-done(((bf16[512,1024]{1,0:T(8,128)(2,1)}), bf16[2048,1024]{1,0:T(8,128)(2,1)}) %all-gather.5.cloned.1.call-update) | async-done | bytes 4194320 | tf_op jit(solution)/shard_map/all_gather | solution.py:1291
  391.3 7.2 convolution_convert_fusion.5
  406.8 4.2 convolution_convert_fusion.8
  411.2 4.8 fusion.44
  419.5 24.9 %multiply_convert_fusion.1 = (bf16[2560,1024]{0,1:T(8,128)(2,1)}, bf16[2560,1024]{0,1:T(8,128)(2,1)}) fusion(f32[2560,2048]{0,1:T(8,128)} %fusion.48, bf16[2560,2048]{1,0:T(8,128)(2,1)} %copy-done.28, bf16[2048,1024]{1,0:T(8,128)(2,1)} %all-gather.5.cloned.1.call-done), kind=kOutput, calls=%fused_computation.2 | convolution fusion | flops 10771496960 | bytes 46137344 | tf_op jit(solution)/shard_map/dot_general | solution.py:35
  444.4 5.5 pad_maximum_fusion
  449.9 4.2 add_convert_fusion.6
  462.6 8.1 convolution_convert_fusion.1
  473.3 8.3 convolution_convert_fusion.2
  482.7 15.1 %fusion.9 = bf16[2048,1024]{1,0:T(8,128)(2,1)} fusion(bf16[2560,2048]{1,0:T(8,128)(2,1)} %constant_dynamic-update-slice_fusion.8, bf16[2560,2048]{0,1:T(8,128)(2,1)S(1)} %pad_maximum_fusion), kind=kOutput, calls=%fused_computation.20 | convolution fusion | flops 10739515392 | bytes 19922944 | tf_op jit(solution)/shard_map/dot_general | solution.py:35
  497.9 9.3 %convolution_convert_fusion.3 = bf16[640,2048]{1,0:T(8,128)(2,1)S(1)} fusion(bf16[2048,2048]{1,0:T(8,128)(2,1)} %all-gather.3.cloned.1.call-done, bf16[2560,2048]{0,1:T(8,128)(2,1)} %copy-done.5), kind=kOutput, calls=%fused_computation.24 | convolution fusion | flops 5370019840 | bytes 13631488 | tf_op jit(solution)/shard_map/dot_general | solution.py:35
  508.0 8.4 collective-permute-done.19
  526.4 8.1 convolution_convert_fusion.4
  539.5 16.9 %fusion.12 = bf16[2048,1024]{1,0:T(8,128)(2,1)} fusion(bf16[2560,2048]{1,0:T(8,128)(2,1)} %constant_dynamic-update-slice_fusion.8, bf16[2560,2048]{0,1:T(8,128)(2,1)} %copy-done.5), kind=kOutput, calls=%fused_computation.21 | convolution fusion | flops 10739515392 | bytes 19922944 | tf_op jit(solution)/shard_map/dot_general | solution.py:35
  556.4 22.9 %collective-permute-done.25 = bf16[320,2048]{1,0:T(8,128)(2,1)} collective-permute-done((bf16[320,2048]{1,0:T(8,128)(2,1)}, bf16[320,2048]{1,0:T(8,128)(2,1)}, u32[]{:S(2)}, u32[]{:S(2)}) %collective-permute-start.25) | collective-permute-done | bytes 1310752 | tf_op jit(solution)/shard_map/ppermute | solution.py:737
  579.3 5.1 convert_add_fusion.2
  589.5 5.6 fusion.43
  596.2 7.3 fusion.17.grad_ref
  603.5 18.9 %attend_back.1 = (bf16[320,2048]{1,0:T(8,128)(2,1)}, bf16[1088,2048]{1,0:T(8,128)(2,1)}) custom-call(s32[1]{0:T(128)} %bitcast.1.place_ref, bf16[320,2048]{1,0:T(8,128)(2,1)} %get-tuple-element.85.query_ref, bf16[1088,2048]{1,0:T(8,128)(2,1)} %get-tuple-element.86.key_ref.value_ref, bf16[1088,2048]{1,0:T(8,128)(2,1)} %get-tuple-element.86.key_ref.value_ref, ...), custom_call_target="tpu_custom_call" | custom-call | tf_op jit(solution)/shard_map/attend_back/pallas_call | solution.py:610
  622.4 40.3 %weights_back.1 = (bf16[2048,2048]{1,0:T(8,128)(2,1)}, bf16[2048,2048]{1,0:T(8,128)(2,1)}, bf16[2048,2048]{1,0:T(8,128)(2,1)}, f32[320,2048]{1,0:T(8,128)}, bf16...) custom-call(s32[1]{0:T(128)} %bitcast.1.place_ref, bf16[320,2048]{1,0:T(8,128)(2,1)} %get-tuple-element.119.query_ref, ...), custom_call_target="tpu_custom_call" | custom-call | tf_op jit(solution)/shard_map/weights_back/pallas_call | solution.py:689
  664.7 196.6 %finish.1 = (f32[64,4096]{1,0:T(8,128)}, f32[64,4096]{1,0:T(8,128)}, f32[64,4096]{1,0:T(8,128)}, f32[64,4096]{1,0:T(8,128)}, f32[64,2048]{1,0:T(8,128)}, /*index...) custom-call(bf16[4,4,2,64,2048]{4,3,2,1,0:T(8,128)(2,1)} %bitcast.76, ...), custom_call_target="tpu_custom_call" | custom-call | tf_op jit(solution)/shard_map/finish/pallas_call | solution.py:1199
  872.6 5.0 fusion.24
  (263 shorter events, 126.6 us)
Async XLA Ops:
  7.2 303.2 %all-gather.3.cloned.1.call-start = ((), (), s32[]{:S(2)}) async-start(), calls=%async_computation.3 | async-start | bytes 10485760 | tf_op jit(solution)/shard_map/all_gather | solution.py:1287
  164.7 226.6 %all-gather.5.cloned.1.call-start = ((), (), s32[]{:S(2)}) async-start(), calls=%async_computation.4 | async-start | bytes 5242880 | tf_op jit(solution)/shard_map/all_gather | solution.py:1291
  164.8 67.7 %collective-permute-start.5 = (bf16[320,2048]{1,0:T(8,128)(2,1)S(1)}, bf16[320,2048]{1,0:T(8,128)(2,1)}, u32[]{:S(2)}, u32[]{:S(2)}) collective-permute-start(bf16[320,2048]{1,0:T(8,128)(2,1)S(1)} %bitcast.87), channel_id=1, source_target_pairs={{0,6},{1,7},{2,4},{3,5},{4,2},{5,3},{6,0},{7,1},{8,14},{9,15},{10,... | collective-permute-start | bytes 3932168 | tf_op jit(solution)/shard_map/ppermute | solution.py:737
  166.0 65.9 %collective-permute-start.3 = (bf16[320,2048]{1,0:T(8,128)(2,1)S(1)}, bf16[320,2048]{1,0:T(8,128)(2,1)}, u32[]{:S(2)}, u32[]{:S(2)}) collective-permute-start(bf16[320,2048]{1,0:T(8,128)(2,1)S(1)} %bitcast.88), channel_id=1, source_target_pairs={{0,4},{1,5},{2,6},{3,7},{4,0},{5,1},{6,2},{7,3},{8,12},{9,13},{10,... | collective-permute-start | bytes 3932168 | tf_op jit(solution)/shard_map/ppermute | solution.py:737
  167.3 64.2 %collective-permute-start.1 = (bf16[320,2048]{1,0:T(8,128)(2,1)S(1)}, bf16[320,2048]{1,0:T(8,128)(2,1)}, u32[]{:S(2)}, u32[]{:S(2)}) collective-permute-start(bf16[320,2048]{1,0:T(8,128)(2,1)S(1)} %bitcast.89), channel_id=1, source_target_pairs={{0,2},{1,3},{2,0},{3,1},{4,6},{5,7},{6,4},{7,5},{8,10},{9,11},{10,... | collective-permute-start | bytes 3932168 | tf_op jit(solution)/shard_map/ppermute | solution.py:737
  167.5 65.1 %collective-permute-start = (bf16[320,2048]{1,0:T(8,128)(2,1)S(1)}, bf16[320,2048]{1,0:T(8,128)(2,1)}, u32[]{:S(2)}, u32[]{:S(2)}) collective-permute-start(bf16[320,2048]{1,0:T(8,128)(2,1)S(1)} %bitcast.90), channel_id=1, source_target_pairs={{0,1},{1,0},{2,3},{3,2},{4,5},{5,4},{6,7},{7,6},{8,9},{9,8},{10,11... | collective-permute-start | bytes 3932168 | tf_op jit(solution)/shard_map/ppermute | solution.py:737
  231.8 5.2 collective-permute-start.4
  232.5 6.1 collective-permute-start.6
  238.7 30.1 %collective-permute-start.8 = (bf16[320,2048]{1,0:T(8,128)(2,1)S(1)}, bf16[320,2048]{1,0:T(8,128)(2,1)S(1)}, u32[]{:S(2)}, u32[]{:S(2)}) collective-permute-start(bf16[320,2048]{1,0:T(8,128)(2,1)S(1)} %multiply_convert_fusion.3), channel_id=1, source_target_pairs={{0,2},{1,3},{2,0},{3,1},{4,6},{5,7},{6,4},{7,5},{8,10},{9,11},{10,... | collective-permute-start | bytes 3932168 | tf_op jit(solution)/shard_map/ppermute | solution.py:737
  240.0 30.8 %collective-permute-start.10 = (bf16[320,2048]{1,0:T(8,128)(2,1)S(1)}, bf16[320,2048]{1,0:T(8,128)(2,1)S(1)}, u32[]{:S(2)}, u32[]{:S(2)}) collective-permute-start(bf16[320,2048]{1,0:T(8,128)(2,1)S(1)} %multiply_convert_fusion.3), channel_id=1, source_target_pairs={{0,4},{1,5},{2,6},{3,7},{4,0},{5,1},{6,2},{7,3},{8,12},{9,13},{10,... | collective-permute-start | bytes 3932168 | tf_op jit(solution)/shard_map/ppermute | solution.py:737
  240.5 60.0 %collective-permute-start.12 = (bf16[320,2048]{1,0:T(8,128)(2,1)S(1)}, bf16[320,2048]{1,0:T(8,128)(2,1)S(1)}, u32[]{:S(2)}, u32[]{:S(2)}) collective-permute-start(bf16[320,2048]{1,0:T(8,128)(2,1)S(1)} %multiply_convert_fusion.3), channel_id=1, source_target_pairs={{0,6},{1,7},{2,4},{3,5},{4,2},{5,3},{6,0},{7,1},{8,14},{9,15},{10,... | collective-permute-start | bytes 3932168 | tf_op jit(solution)/shard_map/ppermute | solution.py:737
  241.5 59.0 %collective-permute-start.7 = (bf16[320,2048]{1,0:T(8,128)(2,1)S(1)}, bf16[320,2048]{1,0:T(8,128)(2,1)S(1)}, u32[]{:S(2)}, u32[]{:S(2)}) collective-permute-start(bf16[320,2048]{1,0:T(8,128)(2,1)S(1)} %multiply_convert_fusion.3), channel_id=1, source_target_pairs={{0,1},{1,0},{2,3},{3,2},{4,5},{5,4},{6,7},{7,6},{8,9},{9,8},{10,11... | collective-permute-start | bytes 3932168 | tf_op jit(solution)/shard_map/ppermute | solution.py:737
  268.8 34.1 %collective-permute-start.9 = (bf16[320,2048]{1,0:T(8,128)(2,1)S(1)}, bf16[320,2048]{1,0:T(8,128)(2,1)S(1)}, u32[]{:S(2)}, u32[]{:S(2)}) collective-permute-start(bf16[320,2048]{1,0:T(8,128)(2,1)S(1)} %collective-permute-done.8), channel_id=1, source_target_pairs={{0,1},{1,0},{2,3},{3,2},{4,5},{5,4},{6,7},{7,6},{8,9},{9,8},{10,11... | collective-permute-start | bytes 3932168 | tf_op jit(solution)/shard_map/ppermute | solution.py:737
  270.9 34.6 %collective-permute-start.11 = (bf16[320,2048]{1,0:T(8,128)(2,1)S(1)}, bf16[320,2048]{1,0:T(8,128)(2,1)S(1)}, u32[]{:S(2)}, u32[]{:S(2)}) collective-permute-start(bf16[320,2048]{1,0:T(8,128)(2,1)S(1)} %collective-permute-done.10), channel_id=1, source_target_pairs={{0,1},{1,0},{2,3},{3,2},{4,5},{5,4},{6,7},{7,6},{8,9},{9,8},{10,11... | collective-permute-start | bytes 3932168 | tf_op jit(solution)/shard_map/ppermute | solution.py:737
  300.5 7.4 collective-permute-start.13
  310.4 216.0 %reduce-scatter.4.cloned.1.call-start = ((), (), s32[]{:S(2)}) async-start(), calls=%async_computation.5 | async-start | bytes 5242880 | tf_op jit(solution)/shard_map/reduce_scatter | solution.py:761
  411.1 192.4 %reduce-scatter.6.cloned.1.call-start = ((), (), s32[]{:S(2)}) async-start(), calls=%async_computation.6 | async-start | bytes 5242880 | tf_op jit(solution)/shard_map/reduce_scatter | solution.py:761
  418.4 31.5 %collective-permute-start.14 = (bf16[320,2048]{1,0:T(8,128)(2,1)}, bf16[320,2048]{1,0:T(8,128)(2,1)}, u32[]{:S(2)}, u32[]{:S(2)}) collective-permute-start(bf16[320,2048]{1,0:T(8,128)(2,1)} %get-tuple-element.98), channel_id=1, source_target_pairs={{0,1},{1,0},{2,3},{3,2},{4,5},{5,4},{6,7},{7,6},{8,9},{9,8},{10,11... | collective-permute-start | bytes 3932168 | tf_op jit(solution)/shard_map/ppermute | solution.py:737
  419.0 30.9 %collective-permute-start.15 = (bf16[320,2048]{1,0:T(8,128)(2,1)}, bf16[320,2048]{1,0:T(8,128)(2,1)}, u32[]{:S(2)}, u32[]{:S(2)}) collective-permute-start(bf16[320,2048]{1,0:T(8,128)(2,1)} %get-tuple-element.99), channel_id=1, source_target_pairs={{0,1},{1,0},{2,3},{3,2},{4,5},{5,4},{6,7},{7,6},{8,9},{9,8},{10,11... | collective-permute-start | bytes 3932168 | tf_op jit(solution)/shard_map/ppermute | solution.py:737
  419.0 30.9 %collective-permute-start.16 = (bf16[320,2048]{1,0:T(8,128)(2,1)}, bf16[320,2048]{1,0:T(8,128)(2,1)}, u32[]{:S(2)}, u32[]{:S(2)}) collective-permute-start(bf16[320,2048]{1,0:T(8,128)(2,1)} %get-tuple-element.100), channel_id=1, source_target_pairs={{0,1},{1,0},{2,3},{3,2},{4,5},{5,4},{6,7},{7,6},{8,9},{9,8},{10,11... | collective-permute-start | bytes 3932168 | tf_op jit(solution)/shard_map/ppermute | solution.py:737
  419.5 30.4 %collective-permute-start.17 = (bf16[320,2048]{1,0:T(8,128)(2,1)}, bf16[320,2048]{1,0:T(8,128)(2,1)}, u32[]{:S(2)}, u32[]{:S(2)}) collective-permute-start(bf16[320,2048]{1,0:T(8,128)(2,1)} %get-tuple-element.101), channel_id=1, source_target_pairs={{0,1},{1,0},{2,3},{3,2},{4,5},{5,4},{6,7},{7,6},{8,9},{9,8},{10,11... | collective-permute-start | bytes 3932168 | tf_op jit(solution)/shard_map/ppermute | solution.py:737
  454.1 53.3 %collective-permute-start.18 = (bf16[320,2048]{1,0:T(8,128)(2,1)}, bf16[320,2048]{1,0:T(8,128)(2,1)}, u32[]{:S(2)}, u32[]{:S(2)}) collective-permute-start(bf16[320,2048]{1,0:T(8,128)(2,1)} %add_convert_fusion.6), channel_id=1, source_target_pairs={{0,2},{1,3},{2,0},{3,1},{4,6},{5,7},{6,4},{7,5},{8,10},{9,11},{10,... | collective-permute-start | bytes 3932168 | tf_op jit(solution)/shard_map/ppermute | solution.py:737
  458.4 58.0 %collective-permute-start.19 = (bf16[320,2048]{1,0:T(8,128)(2,1)}, bf16[320,2048]{1,0:T(8,128)(2,1)}, u32[]{:S(2)}, u32[]{:S(2)}) collective-permute-start(bf16[320,2048]{1,0:T(8,128)(2,1)} %add_convert_fusion.5), channel_id=1, source_target_pairs={{0,4},{1,5},{2,6},{3,7},{4,0},{5,1},{6,2},{7,3},{8,12},{9,13},{10,... | collective-permute-start | bytes 3932168 | tf_op jit(solution)/shard_map/ppermute | solution.py:737
  462.5 54.0 %collective-permute-start.20 = (bf16[320,2048]{1,0:T(8,128)(2,1)}, bf16[320,2048]{1,0:T(8,128)(2,1)}, u32[]{:S(2)}, u32[]{:S(2)}) collective-permute-start(bf16[320,2048]{1,0:T(8,128)(2,1)} %add_convert_fusion.4), channel_id=1, source_target_pairs={{0,6},{1,7},{2,4},{3,5},{4,2},{5,3},{6,0},{7,1},{8,14},{9,15},{10,... | collective-permute-start | bytes 3932168 | tf_op jit(solution)/shard_map/ppermute | solution.py:737
  472.0 44.5 %collective-permute-start.26 = (bf16[320,2048]{1,0:T(8,128)(2,1)}, bf16[320,2048]{1,0:T(8,128)(2,1)}, u32[]{:S(2)}, u32[]{:S(2)}) collective-permute-start(bf16[320,2048]{1,0:T(8,128)(2,1)} %slice.159), channel_id=1, source_target_pairs={{0,1},{1,0},{2,3},{3,2},{4,5},{5,4},{6,7},{7,6},{8,9},{9,8},{10,11... | collective-permute-start | bytes 3932168 | tf_op jit(solution)/shard_map/ppermute | solution.py:737
  482.7 37.7 %collective-permute-start.24 = (bf16[320,2048]{1,0:T(8,128)(2,1)}, bf16[320,2048]{1,0:T(8,128)(2,1)}, u32[]{:S(2)}, u32[]{:S(2)}) collective-permute-start(bf16[320,2048]{1,0:T(8,128)(2,1)} %slice.157), channel_id=1, source_target_pairs={{0,1},{1,0},{2,3},{3,2},{4,5},{5,4},{6,7},{7,6},{8,9},{9,8},{10,11... | collective-permute-start | bytes 3932168 | tf_op jit(solution)/shard_map/ppermute | solution.py:737
  497.9 166.8 %reduce-scatter.8.cloned.1.call-start = ((), (), s32[]{:S(2)}) async-start(), calls=%async_computation.7 | async-start | bytes 5242880 | tf_op jit(solution)/shard_map/reduce_scatter | solution.py:761
  507.4 16.2 %collective-permute-start.22 = (bf16[320,2048]{1,0:T(8,128)(2,1)S(1)}, bf16[320,2048]{1,0:T(8,128)(2,1)S(1)}, u32[]{:S(2)}, u32[]{:S(2)}) collective-permute-start(bf16[320,2048]{1,0:T(8,128)(2,1)S(1)} %slice.155), channel_id=1, source_target_pairs={{0,1},{1,0},{2,3},{3,2},{4,5},{5,4},{6,7},{7,6},{8,9},{9,8},{10,11... | collective-permute-start | bytes 3932168 | tf_op jit(solution)/shard_map/ppermute | solution.py:737
  519.3 37.1 %collective-permute-start.27 = (bf16[320,2048]{1,0:T(8,128)(2,1)}, bf16[320,2048]{1,0:T(8,128)(2,1)}, u32[]{:S(2)}, u32[]{:S(2)}) collective-permute-start(bf16[320,2048]{1,0:T(8,128)(2,1)} %add_convert_fusion), channel_id=1, source_target_pairs={{0,6},{1,7},{2,4},{3,5},{4,2},{5,3},{6,0},{7,1},{8,14},{9,15},{10,... | collective-permute-start | bytes 3932168 | tf_op jit(solution)/shard_map/ppermute | solution.py:737
  523.2 56.0 %collective-permute-start.25 = (bf16[320,2048]{1,0:T(8,128)(2,1)}, bf16[320,2048]{1,0:T(8,128)(2,1)}, u32[]{:S(2)}, u32[]{:S(2)}) collective-permute-start(bf16[320,2048]{1,0:T(8,128)(2,1)} %add_convert_fusion.1), channel_id=1, source_target_pairs={{0,4},{1,5},{2,6},{3,7},{4,0},{5,1},{6,2},{7,3},{8,12},{9,13},{10,... | collective-permute-start | bytes 3932168 | tf_op jit(solution)/shard_map/ppermute | solution.py:737
  525.1 54.2 %collective-permute-start.23 = (bf16[320,2048]{1,0:T(8,128)(2,1)}, bf16[320,2048]{1,0:T(8,128)(2,1)}, u32[]{:S(2)}, u32[]{:S(2)}) collective-permute-start(bf16[320,2048]{1,0:T(8,128)(2,1)} %add_convert_fusion.2), channel_id=1, source_target_pairs={{0,2},{1,3},{2,0},{3,1},{4,6},{5,7},{6,4},{7,5},{8,10},{9,11},{10,... | collective-permute-start | bytes 3932168 | tf_op jit(solution)/shard_map/ppermute | solution.py:737
  537.1 42.2 %collective-permute-start.21 = (bf16[320,2048]{1,0:T(8,128)(2,1)}, bf16[320,2048]{1,0:T(8,128)(2,1)}, u32[]{:S(2)}, u32[]{:S(2)}) collective-permute-start(bf16[320,2048]{1,0:T(8,128)(2,1)} %slice.153), channel_id=1, source_target_pairs={{0,1},{1,0},{2,3},{3,2},{4,5},{5,4},{6,7},{7,6},{8,9},{9,8},{10,11... | collective-permute-start | bytes 3932168 | tf_op jit(solution)/shard_map/ppermute | solution.py:737
  (51 other events, 550.4 us)
Sparse Core Ops, SparseCore 0:
  164.8 145.5 all-gather.2
  312.0 79.2 all-gather.4
  411.2 77.8 reduce-scatter.3
  498.0 77.7 reduce-scatter.5
  584.6 76.7 reduce-scatter.7

commit v5 on v4

--- a/solution.py
+++ b/solution.py
@@ -771,7 +771,6 @@
     gate_ref,
     up_ref,
     down_ref,
-    back_ref,
     a_master,
     a_first,
     a_second,
@@ -790,7 +789,6 @@
     m_first_new,
     m_second_new,
     gain_out,
-    back_out,
     f_grad,
     f_update,
     f_first_new,
@@ -819,8 +817,6 @@
     made_sem,
     a_sem,
     gain_sem,
-    back_send,
-    back_recv,
 ):
     g = lax.axis_index("grp")
     d = lax.axis_index("dp")
@@ -835,7 +831,6 @@
     for ref in (query_ref, pair_ref, merge_ref, gain_ref):
         parts.append((ref, pl.ds(begin, ref.shape[4])))
         begin += ref.shape[4]
-    prompt_rows = back_out.shape[1]
 
     barrier = pltpu.get_barrier_semaphore()
     for step in range(1, plane):
@@ -953,18 +948,6 @@
             made_sem.at[slot, which],
         )
 
-    def back_copy(step):
-        there = lax.rem(g + step, lines)
-        return remote(
-            back_ref.at[there],
-            back_out.at[g],
-            back_send.at[step],
-            back_recv.at[step],
-            (there, d),
-        )
-
-    own_back = pltpu.make_async_copy(back_ref.at[g], back_out.at[g], own_sem.at[3])
-
     slabs = (pl.ds(0, a_width), pl.ds(a_width, m_width))
 
     def a_state_copy(which, slab):
@@ -988,14 +971,11 @@
             core_copy(turn, part).start()
             if turn < 2:
                 mine_copy(turn, part).start()
-    for step in range(1, lines):
-        back_copy(step).start()
     for step in range(1, plane):
         for part in range(3):
             swap_copy(step, part).start()
     for one in own_swap:
         one.start()
-    own_back.start()
     for which in range(3):
         state_copy(0, which).start()
         for slab in range(2):
@@ -1172,16 +1152,13 @@
     for step in range(1, plane):
         for part in range(3):
             swap_copy(step, part).wait_send()
-    for step in range(1, lines):
-        back_copy(step).wait()
-    own_back.wait()
     for which in range(4):
         for slab in range(2):
             a_made_copy(which, slab).wait()
     gain_copy.wait()
 
 
-def finish(terms, forward_parts, pair_back, attention, merge, forward):
+def finish(terms, forward_parts, attention, merge, forward):
     lines, plane = lax.axis_size("grp"), lax.axis_size("dp")
     chips = plane // 2
     rows, a_width = attention[0].shape
@@ -1191,7 +1168,6 @@
     anywhere = pl.BlockSpec(memory_space=pl.ANY)
     dma = pltpu.SemaphoreType.DMA
     vmem = pltpu.VMEM
-    back = pair_back.reshape(lines, PROMPT_LEN // lines, D)
 
     def like(array):
         return jax.ShapeDtypeStruct(array.shape, array.dtype)
@@ -1200,10 +1176,10 @@
         functools.partial(finish_kernel, lines, plane),
         out_shape=(like(attention[0]),) * 4
         + (like(merge[0]),) * 4
-        + (jax.ShapeDtypeStruct((rows, GAIN_PAD), FULL), like(back))
+        + (jax.ShapeDtypeStruct((rows, GAIN_PAD), FULL),)
         + (like(forward[0]),) * 4,
-        in_specs=[anywhere] * 17,
-        out_specs=(anywhere,) * 14,
+        in_specs=[anywhere] * 16,
+        out_specs=(anywhere,) * 13,
         scratch_shapes=[
             vmem((2, chips, rows, width), LOW),
             vmem((lines, chips, rows, width), LOW),
@@ -1224,13 +1200,11 @@
             dma((lines,)),
             dma((plane, 3)),
             dma((plane, 3)),
-            dma((4,)),
+            dma((3,)),
             dma((2, 3)),
             dma((2, 4)),
             dma((2, 7)),
             dma((1,)),
-            dma((lines,)),
-            dma((lines,)),
         ],
         compiler_params=pltpu.CompilerParams(
             collective_id=1, has_side_effects=True, vmem_limit_bytes=VMEM_LIMIT
@@ -1239,7 +1213,6 @@
     )(
         *(term.reshape(lines, chips, 2, rows, term.shape[1]) for term in terms),
         *(part.reshape(plane, rows, -1) for part in forward_parts),
-        back,
         *attention,
         *merge,
         *forward,
@@ -1399,16 +1372,18 @@
     gain_term = jnp.pad(
         jnp.stack([gain_one_part[0], gain_two_part], axis=1), ((0, 0), (0, GAIN_PAD - 2))
     )
+    pair_back, up_part = lax.optimization_barrier((pair_back, up_part))
+    pair_sum = line_scatter(pair_back)
     finished = finish(
         (query_term, pair_term, merge_term, gain_term.astype(LOW)),
         (gate_part, up_part, down_part),
-        pair_back,
         (attention_master, attention_first, attention_second),
         (merge_master, merge_first, merge_second),
         (feedforward_master, feedforward_first, feedforward_second),
     )
     gain_grad = finished[8][:, :2].T
-    pair_sum = jnp.sum(finished[9].astype(FULL), axis=0)
+    pair_sum, gain_grad = lax.optimization_barrier((pair_sum, gain_grad))
+    pair_sum = pair_sum.astype(FULL)
     normed_grad = normed_grad + jnp.pad(pair_sum, ((0, CONT), (0, 0)))
     input_grad = (middle_grad + norm_back(inputs, first_scale, gain_float[0], normed_grad)).reshape(
         hidden.shape
@@ -1420,7 +1395,7 @@
         gain_grad,
         *gain_new,
         *finished[:8],
-        *finished[10:],
+        *finished[9:],
     )
 
 

time: 916 us -> 911 us (level)
    unnamed x129 -> x131, local copies, waits for them, and re-layouts: 47.5 us -> 47.4 us
  transfers between devices with their start and end apart: 33 -> 34, of which waited for: 5 -> 5; matrix products, arithmetic and copies ran while one was open for 25% -> 26% of each run, Pallas kernels for 12% -> 33%
where the time goes in v5:
time: 911 us; the launch traced here: 901 us
  Pallas kernels  450 us (49%)
  matrix products  166 us (18%)
  waiting for transfers between devices  85.5 us (9%)
  other arithmetic  70.3 us (8%)
  local copies, waits for them, and re-layouts  64 us (7%)
  starting transfers between devices  50.2 us (6%)
  between operations  15.7 us (2%)
    pallas_call x1, Pallas kernels, finish(): pl.pallas_call(functools.partial(finish_kernel, lines, plane), out_shape=...  196 us
    pallas_call x1, Pallas kernels, gather_start(): pl.pallas_call(functools.partial(gather_kernel, lines, plane, prompt_rows...  149 us
    dot_general x14, matrix products, contract(): lax.dot_general(left, right, (((left_axis,), (right_axis,)), ((), ())), p...  137 us
    ppermute x28, waiting for transfers between devices, plane_swap(): return lax.ppermute(block, 'dp', [(i, i ^ offset) for i in range(size)])  57.5 us
    ppermute x28, starting transfers between devices, plane_swap(): return lax.ppermute(block, 'dp', [(i, i ^ offset) for i in range(size)])  49.8 us
    unnamed x131, local copies, waits for them, and re-layouts  47.4 us
    pallas_call x1, Pallas kernels, weights_back(): pl.pallas_call(weights_back_kernel, grid_spec=pltpu.PrefetchScalarGridSpe...  40.3 us
    pallas_call x1, Pallas kernels, project_heads(): pl.pallas_call(project_kernel, grid_spec=pltpu.PrefetchScalarGridSpec(num...  34.3 us
  transfers between devices with their start and end apart: 34, of which 5 were waited for; matrix products, arithmetic and copies ran while one was open for 26% of the time, Pallas kernels for 33%

profile of v5, /device:TPU:9, one launch (start us, length us, event | category | flops | bytes accessed | tf_op | source)
XLA Modules:
  0.0 901.4 jit_solution(18027979886763243779)
XLA Ops:
  10.4 4.8 convert_element_type.183.forward_ref
  16.1 148.6 %gather_start.1 = (bf16[4,8,64,6272]{3,2,1,0:T(8,128)(2,1)}, bf16[4,256,2048]{2,1,0:T(8,128)(2,1)}, bf16[8,64,2048]{2,1,0:T(8,128)(2,1)}, bf16[8,64,1024]{2,1,0:T(8,128)(2,1)}) custom-call(bf16[64,6272]{1,0:T(8,128)(2,1)} %fusion.37.weight_ref, bf16[320,2048]{1,0:T(8,128)(2,1)} %bitcast.64, bf16[64,24576]{1,0:T(8,128)(2,1)} %convert_element_type.183.forward_ref), custom_call_target="tpu_custom_call" | custom-call | tf_op jit(solution)/shard_map/gather_start/pallas_call | solution.py:371
  177.3 34.3 %project_heads.1 = (bf16[320,2048]{1,0:T(8,128)(2,1)}, bf16[1088,2048]{1,0:T(8,128)(2,1)}, bf16[1088,2048]{1,0:T(8,128)(2,1)}, bf16[320,2048]{1,0:T(8,128)(2,1)}, f32[1088,128]{1,0:T(8,128)}) custom-call(s32[1]{0:T(128)} %bitcast.1.place_ref, bf16[1024,2048]{1,0:T(8,128)(2,1)} %bitcast.67, bf16[320,2048]{1,0:T(8,128)(2,1)} %bitcast.65, ...), custom_call_target="tpu_custom_call" | custom-call | tf_op jit(solution)/shard_map/project_heads/pallas_call | solution.py:469
  213.5 11.4 %attend.1 = (bf16[320,2048]{1,0:T(8,128)(2,1)}, f32[320,1024]{1,0:T(8,128)}) custom-call(bf16[320,2048]{1,0:T(8,128)(2,1)} %get-tuple-element.88.query_ref, bf16[1088,2048]{1,0:T(8,128)(2,1)} %get-tuple-element.89.key_ref.value_ref, bf16[1088,2048]{1,0:T(8,128)(2,1)} %get-tuple-element.89.key_ref.value_ref, f32[320,1088]{1,0:T(8,128)} %add_convert_fusion.7.seen_ref), custom_call_target="tpu_custom_call" | custom-call | tf_op jit(solution)/shard_map/attend/pallas_call | solution.py:531
  224.9 5.9 multiply_reduce_fusion.2
  242.7 26.1 %collective-permute-done.8 = bf16[320,2048]{1,0:T(8,128)(2,1)S(1)} collective-permute-done((bf16[320,2048]{1,0:T(8,128)(2,1)S(1)}, bf16[320,2048]{1,0:T(8,128)(2,1)S(1)}, u32[]{:S(2)}, u32[]{:S(2)}) %collective-permute-start.8) | collective-permute-done | bytes 1310752 | tf_op jit(solution)/shard_map/ppermute | solution.py:737
  270.9 28.5 %collective-permute-start.11 = (bf16[320,2048]{1,0:T(8,128)(2,1)S(1)}, bf16[320,2048]{1,0:T(8,128)(2,1)S(1)}, u32[]{:S(2)}, u32[]{:S(2)}) collective-permute-start(bf16[320,2048]{1,0:T(8,128)(2,1)S(1)} %collective-permute-done.10), channel_id=1, source_target_pairs={{0,1},{1,0},{2,3},{3,2},{4,5},{5,4},{6,7},{7,6},{8,9},{9,8},{10,11... | collective-permute-start | bytes 3932168 | tf_op jit(solution)/shard_map/ppermute | solution.py:737
  310.6 29.0 %fusion.48 = f32[2560,2048]{0,1:T(8,128)} fusion(bf16[2560,2048]{1,0:T(8,128)(2,1)} %constant_dynamic-update-slice_fusion.8, bf16[2048,2048]{1,0:T(8,128)(2,1)} %all-gather.3.cloned.1.call-done), kind=kOutput, calls=%fused_computation.127 | convolution fusion | flops 21474836480 | bytes 39845888 | tf_op jit(solution)/shard_map/dot_general | solution.py:1315
  339.6 8.6 multiply_convert_fusion.2
  351.1 13.5 %convolution_convert_fusion = bf16[2048,1024]{1,0:T(8,128)(2,1)} fusion(bf16[2560,2048]{1,0:T(8,128)(2,1)S(1)} %copy-done.29, bf16[2560,1024]{0,1:T(8,128)(2,1)S(1)} %multiply_convert_fusion.2), kind=kOutput, calls=%fused_computation.18 | convolution fusion | flops 10739515392 | bytes 19922944 | tf_op jit(solution)/shard_map/dot_general | solution.py:35
  364.6 26.7 %all-gather.5.cloned.1.call-done = bf16[2048,1024]{1,0:T(8,128)(2,1)} async-done(((bf16[512,1024]{1,0:T(8,128)(2,1)}), bf16[2048,1024]{1,0:T(8,128)(2,1)}) %all-gather.5.cloned.1.call-update) | async-done | bytes 4194320 | tf_op jit(solution)/shard_map/all_gather | solution.py:1264
  391.3 7.2 convolution_convert_fusion.5
  406.9 4.2 convolution_convert_fusion.8
  411.2 4.8 fusion.44
  419.5 25.1 %multiply_convert_fusion.1 = (bf16[2560,1024]{0,1:T(8,128)(2,1)}, bf16[2560,1024]{0,1:T(8,128)(2,1)}) fusion(f32[2560,2048]{0,1:T(8,128)} %fusion.48, bf16[2560,2048]{1,0:T(8,128)(2,1)} %copy-done.28, bf16[2048,1024]{1,0:T(8,128)(2,1)} %all-gather.5.cloned.1.call-done), kind=kOutput, calls=%fused_computation.2 | convolution fusion | flops 10771496960 | bytes 46137344 | tf_op jit(solution)/shard_map/dot_general | solution.py:35
  444.5 5.5 pad_maximum_fusion
  450.1 4.2 add_convert_fusion.6
  462.8 8.1 convolution_convert_fusion.1
  473.5 8.2 convolution_convert_fusion.2
  482.9 15.1 %fusion.9 = bf16[2048,1024]{1,0:T(8,128)(2,1)} fusion(bf16[2560,2048]{1,0:T(8,128)(2,1)} %constant_dynamic-update-slice_fusion.8, bf16[2560,2048]{0,1:T(8,128)(2,1)S(1)} %pad_maximum_fusion), kind=kOutput, calls=%fused_computation.19 | convolution fusion | flops 10739515392 | bytes 19922944 | tf_op jit(solution)/shard_map/dot_general | solution.py:35
  498.1 9.1 %convolution_convert_fusion.3 = bf16[640,2048]{1,0:T(8,128)(2,1)S(1)} fusion(bf16[2048,2048]{1,0:T(8,128)(2,1)} %all-gather.3.cloned.1.call-done, bf16[2560,2048]{0,1:T(8,128)(2,1)} %copy-done.5), kind=kOutput, calls=%fused_computation.23 | convolution fusion | flops 5370019840 | bytes 13631488 | tf_op jit(solution)/shard_map/dot_general | solution.py:35
  507.9 8.7 collective-permute-done.19
  526.5 8.1 convolution_convert_fusion.4
  539.7 17.1 %fusion.12 = bf16[2048,1024]{1,0:T(8,128)(2,1)} fusion(bf16[2560,2048]{1,0:T(8,128)(2,1)} %constant_dynamic-update-slice_fusion.8, bf16[2560,2048]{0,1:T(8,128)(2,1)} %copy-done.5), kind=kOutput, calls=%fused_computation.20 | convolution fusion | flops 10739515392 | bytes 19922944 | tf_op jit(solution)/shard_map/dot_general | solution.py:35
  556.8 22.7 %collective-permute-done.25 = bf16[320,2048]{1,0:T(8,128)(2,1)} collective-permute-done((bf16[320,2048]{1,0:T(8,128)(2,1)}, bf16[320,2048]{1,0:T(8,128)(2,1)}, u32[]{:S(2)}, u32[]{:S(2)}) %collective-permute-start.25) | collective-permute-done | bytes 1310752 | tf_op jit(solution)/shard_map/ppermute | solution.py:737
  579.5 5.1 convert_add_fusion.2
  589.7 5.8 fusion.43
  596.5 7.3 fusion.17.grad_ref
  603.8 18.7 %attend_back.1 = (bf16[320,2048]{1,0:T(8,128)(2,1)}, bf16[1088,2048]{1,0:T(8,128)(2,1)}) custom-call(s32[1]{0:T(128)} %bitcast.1.place_ref, bf16[320,2048]{1,0:T(8,128)(2,1)} %get-tuple-element.88.query_ref, bf16[1088,2048]{1,0:T(8,128)(2,1)} %get-tuple-element.89.key_ref.value_ref, bf16[1088,2048]{1,0:T(8,128)(2,1)} %get-tuple-element.89.key_ref.value_ref, ...), custom_call_target="tpu_custom_call" | custom-call | tf_op jit(solution)/shard_map/attend_back/pallas_call | solution.py:610
  622.5 40.3 %weights_back.1 = (bf16[2048,2048]{1,0:T(8,128)(2,1)}, bf16[2048,2048]{1,0:T(8,128)(2,1)}, bf16[2048,2048]{1,0:T(8,128)(2,1)}, f32[320,2048]{1,0:T(8,128)}, bf16...) custom-call(s32[1]{0:T(128)} %bitcast.1.place_ref, bf16[320,2048]{1,0:T(8,128)(2,1)} %get-tuple-element.122.query_ref, ...), custom_call_target="tpu_custom_call" | custom-call | tf_op jit(solution)/shard_map/weights_back/pallas_call | solution.py:689
  665.1 196.2 %finish.1 = (f32[64,4096]{1,0:T(8,128)}, f32[64,4096]{1,0:T(8,128)}, f32[64,4096]{1,0:T(8,128)}, f32[64,4096]{1,0:T(8,128)}, f32[64,2048]{1,0:T(8,128)}, /*index...) custom-call(bf16[4,4,2,64,2048]{4,3,2,1,0:T(8,128)(2,1)} %bitcast.69, ...), custom_call_target="tpu_custom_call" | custom-call | tf_op jit(solution)/shard_map/finish/pallas_call | solution.py:1175
  867.8 5.0 fusion.24
  (267 shorter events, 122.0 us)
Async XLA Ops:
  7.2 303.2 %all-gather.3.cloned.1.call-start = ((), (), s32[]{:S(2)}) async-start(), calls=%async_computation.4 | async-start | bytes 10485760 | tf_op jit(solution)/shard_map/all_gather | solution.py:1260
  164.7 226.6 %all-gather.5.cloned.1.call-start = ((), (), s32[]{:S(2)}) async-start(), calls=%async_computation.5 | async-start | bytes 5242880 | tf_op jit(solution)/shard_map/all_gather | solution.py:1264
  164.8 67.7 %collective-permute-start.5 = (bf16[320,2048]{1,0:T(8,128)(2,1)S(1)}, bf16[320,2048]{1,0:T(8,128)(2,1)}, u32[]{:S(2)}, u32[]{:S(2)}) collective-permute-start(bf16[320,2048]{1,0:T(8,128)(2,1)S(1)} %bitcast.80), channel_id=1, source_target_pairs={{0,6},{1,7},{2,4},{3,5},{4,2},{5,3},{6,0},{7,1},{8,14},{9,15},{10,... | collective-permute-start | bytes 3932168 | tf_op jit(solution)/shard_map/ppermute | solution.py:737
  166.0 65.9 %collective-permute-start.3 = (bf16[320,2048]{1,0:T(8,128)(2,1)S(1)}, bf16[320,2048]{1,0:T(8,128)(2,1)}, u32[]{:S(2)}, u32[]{:S(2)}) collective-permute-start(bf16[320,2048]{1,0:T(8,128)(2,1)S(1)} %bitcast.81), channel_id=1, source_target_pairs={{0,4},{1,5},{2,6},{3,7},{4,0},{5,1},{6,2},{7,3},{8,12},{9,13},{10,... | collective-permute-start | bytes 3932168 | tf_op jit(solution)/shard_map/ppermute | solution.py:737
  167.3 64.2 %collective-permute-start.1 = (bf16[320,2048]{1,0:T(8,128)(2,1)S(1)}, bf16[320,2048]{1,0:T(8,128)(2,1)}, u32[]{:S(2)}, u32[]{:S(2)}) collective-permute-start(bf16[320,2048]{1,0:T(8,128)(2,1)S(1)} %bitcast.82), channel_id=1, source_target_pairs={{0,2},{1,3},{2,0},{3,1},{4,6},{5,7},{6,4},{7,5},{8,10},{9,11},{10,... | collective-permute-start | bytes 3932168 | tf_op jit(solution)/shard_map/ppermute | solution.py:737
  167.5 65.1 %collective-permute-start = (bf16[320,2048]{1,0:T(8,128)(2,1)S(1)}, bf16[320,2048]{1,0:T(8,128)(2,1)}, u32[]{:S(2)}, u32[]{:S(2)}) collective-permute-start(bf16[320,2048]{1,0:T(8,128)(2,1)S(1)} %bitcast.83), channel_id=1, source_target_pairs={{0,1},{1,0},{2,3},{3,2},{4,5},{5,4},{6,7},{7,6},{8,9},{9,8},{10,11... | collective-permute-start | bytes 3932168 | tf_op jit(solution)/shard_map/ppermute | solution.py:737
  232.5 6.1 collective-permute-start.6
  238.7 30.1 %collective-permute-start.8 = (bf16[320,2048]{1,0:T(8,128)(2,1)S(1)}, bf16[320,2048]{1,0:T(8,128)(2,1)S(1)}, u32[]{:S(2)}, u32[]{:S(2)}) collective-permute-start(bf16[320,2048]{1,0:T(8,128)(2,1)S(1)} %multiply_convert_fusion.3), channel_id=1, source_target_pairs={{0,2},{1,3},{2,0},{3,1},{4,6},{5,7},{6,4},{7,5},{8,10},{9,11},{10,... | collective-permute-start | bytes 3932168 | tf_op jit(solution)/shard_map/ppermute | solution.py:737
  240.1 30.8 %collective-permute-start.10 = (bf16[320,2048]{1,0:T(8,128)(2,1)S(1)}, bf16[320,2048]{1,0:T(8,128)(2,1)S(1)}, u32[]{:S(2)}, u32[]{:S(2)}) collective-permute-start(bf16[320,2048]{1,0:T(8,128)(2,1)S(1)} %multiply_convert_fusion.3), channel_id=1, source_target_pairs={{0,4},{1,5},{2,6},{3,7},{4,0},{5,1},{6,2},{7,3},{8,12},{9,13},{10,... | collective-permute-start | bytes 3932168 | tf_op jit(solution)/shard_map/ppermute | solution.py:737
  240.5 60.0 %collective-permute-start.12 = (bf16[320,2048]{1,0:T(8,128)(2,1)S(1)}, bf16[320,2048]{1,0:T(8,128)(2,1)S(1)}, u32[]{:S(2)}, u32[]{:S(2)}) collective-permute-start(bf16[320,2048]{1,0:T(8,128)(2,1)S(1)} %multiply_convert_fusion.3), channel_id=1, source_target_pairs={{0,6},{1,7},{2,4},{3,5},{4,2},{5,3},{6,0},{7,1},{8,14},{9,15},{10,... | collective-permute-start | bytes 3932168 | tf_op jit(solution)/shard_map/ppermute | solution.py:737
  241.5 59.1 %collective-permute-start.7 = (bf16[320,2048]{1,0:T(8,128)(2,1)S(1)}, bf16[320,2048]{1,0:T(8,128)(2,1)S(1)}, u32[]{:S(2)}, u32[]{:S(2)}) collective-permute-start(bf16[320,2048]{1,0:T(8,128)(2,1)S(1)} %multiply_convert_fusion.3), channel_id=1, source_target_pairs={{0,1},{1,0},{2,3},{3,2},{4,5},{5,4},{6,7},{7,6},{8,9},{9,8},{10,11... | collective-permute-start | bytes 3932168 | tf_op jit(solution)/shard_map/ppermute | solution.py:737
  268.8 34.2 %collective-permute-start.9 = (bf16[320,2048]{1,0:T(8,128)(2,1)S(1)}, bf16[320,2048]{1,0:T(8,128)(2,1)S(1)}, u32[]{:S(2)}, u32[]{:S(2)}) collective-permute-start(bf16[320,2048]{1,0:T(8,128)(2,1)S(1)} %collective-permute-done.8), channel_id=1, source_target_pairs={{0,1},{1,0},{2,3},{3,2},{4,5},{5,4},{6,7},{7,6},{8,9},{9,8},{10,11... | collective-permute-start | bytes 3932168 | tf_op jit(solution)/shard_map/ppermute | solution.py:737
  270.9 34.6 %collective-permute-start.11 = (bf16[320,2048]{1,0:T(8,128)(2,1)S(1)}, bf16[320,2048]{1,0:T(8,128)(2,1)S(1)}, u32[]{:S(2)}, u32[]{:S(2)}) collective-permute-start(bf16[320,2048]{1,0:T(8,128)(2,1)S(1)} %collective-permute-done.10), channel_id=1, source_target_pairs={{0,1},{1,0},{2,3},{3,2},{4,5},{5,4},{6,7},{7,6},{8,9},{9,8},{10,11... | collective-permute-start | bytes 3932168 | tf_op jit(solution)/shard_map/ppermute | solution.py:737
  300.5 7.4 collective-permute-start.13
  310.4 216.1 %reduce-scatter.5.cloned.1.call-start = ((), (), s32[]{:S(2)}) async-start(), calls=%async_computation.6 | async-start | bytes 5242880 | tf_op jit(solution)/shard_map/reduce_scatter | solution.py:761
  411.1 192.7 %reduce-scatter.7.cloned.1.call-start = ((), (), s32[]{:S(2)}) async-start(), calls=%async_computation.7 | async-start | bytes 5242880 | tf_op jit(solution)/shard_map/reduce_scatter | solution.py:761
  418.4 31.7 %collective-permute-start.14 = (bf16[320,2048]{1,0:T(8,128)(2,1)}, bf16[320,2048]{1,0:T(8,128)(2,1)}, u32[]{:S(2)}, u32[]{:S(2)}) collective-permute-start(bf16[320,2048]{1,0:T(8,128)(2,1)} %get-tuple-element.101), channel_id=1, source_target_pairs={{0,1},{1,0},{2,3},{3,2},{4,5},{5,4},{6,7},{7,6},{8,9},{9,8},{10,11... | collective-permute-start | bytes 3932168 | tf_op jit(solution)/shard_map/ppermute | solution.py:737
  418.9 31.1 %collective-permute-start.15 = (bf16[320,2048]{1,0:T(8,128)(2,1)}, bf16[320,2048]{1,0:T(8,128)(2,1)}, u32[]{:S(2)}, u32[]{:S(2)}) collective-permute-start(bf16[320,2048]{1,0:T(8,128)(2,1)} %get-tuple-element.102), channel_id=1, source_target_pairs={{0,1},{1,0},{2,3},{3,2},{4,5},{5,4},{6,7},{7,6},{8,9},{9,8},{10,11... | collective-permute-start | bytes 3932168 | tf_op jit(solution)/shard_map/ppermute | solution.py:737
  419.0 31.1 %collective-permute-start.16 = (bf16[320,2048]{1,0:T(8,128)(2,1)}, bf16[320,2048]{1,0:T(8,128)(2,1)}, u32[]{:S(2)}, u32[]{:S(2)}) collective-permute-start(bf16[320,2048]{1,0:T(8,128)(2,1)} %get-tuple-element.103), channel_id=1, source_target_pairs={{0,1},{1,0},{2,3},{3,2},{4,5},{5,4},{6,7},{7,6},{8,9},{9,8},{10,11... | collective-permute-start | bytes 3932168 | tf_op jit(solution)/shard_map/ppermute | solution.py:737
  419.5 30.6 %collective-permute-start.17 = (bf16[320,2048]{1,0:T(8,128)(2,1)}, bf16[320,2048]{1,0:T(8,128)(2,1)}, u32[]{:S(2)}, u32[]{:S(2)}) collective-permute-start(bf16[320,2048]{1,0:T(8,128)(2,1)} %get-tuple-element.104), channel_id=1, source_target_pairs={{0,1},{1,0},{2,3},{3,2},{4,5},{5,4},{6,7},{7,6},{8,9},{9,8},{10,11... | collective-permute-start | bytes 3932168 | tf_op jit(solution)/shard_map/ppermute | solution.py:737
  454.3 53.0 %collective-permute-start.18 = (bf16[320,2048]{1,0:T(8,128)(2,1)}, bf16[320,2048]{1,0:T(8,128)(2,1)}, u32[]{:S(2)}, u32[]{:S(2)}) collective-permute-start(bf16[320,2048]{1,0:T(8,128)(2,1)} %add_convert_fusion.6), channel_id=1, source_target_pairs={{0,2},{1,3},{2,0},{3,1},{4,6},{5,7},{6,4},{7,5},{8,10},{9,11},{10,... | collective-permute-start | bytes 3932168 | tf_op jit(solution)/shard_map/ppermute | solution.py:737
  458.6 58.0 %collective-permute-start.19 = (bf16[320,2048]{1,0:T(8,128)(2,1)}, bf16[320,2048]{1,0:T(8,128)(2,1)}, u32[]{:S(2)}, u32[]{:S(2)}) collective-permute-start(bf16[320,2048]{1,0:T(8,128)(2,1)} %add_convert_fusion.5), channel_id=1, source_target_pairs={{0,4},{1,5},{2,6},{3,7},{4,0},{5,1},{6,2},{7,3},{8,12},{9,13},{10,... | collective-permute-start | bytes 3932168 | tf_op jit(solution)/shard_map/ppermute | solution.py:737
  462.7 53.9 %collective-permute-start.20 = (bf16[320,2048]{1,0:T(8,128)(2,1)}, bf16[320,2048]{1,0:T(8,128)(2,1)}, u32[]{:S(2)}, u32[]{:S(2)}) collective-permute-start(bf16[320,2048]{1,0:T(8,128)(2,1)} %add_convert_fusion.4), channel_id=1, source_target_pairs={{0,6},{1,7},{2,4},{3,5},{4,2},{5,3},{6,0},{7,1},{8,14},{9,15},{10,... | collective-permute-start | bytes 3932168 | tf_op jit(solution)/shard_map/ppermute | solution.py:737
  472.1 44.5 %collective-permute-start.26 = (bf16[320,2048]{1,0:T(8,128)(2,1)}, bf16[320,2048]{1,0:T(8,128)(2,1)}, u32[]{:S(2)}, u32[]{:S(2)}) collective-permute-start(bf16[320,2048]{1,0:T(8,128)(2,1)} %slice.159), channel_id=1, source_target_pairs={{0,1},{1,0},{2,3},{3,2},{4,5},{5,4},{6,7},{7,6},{8,9},{9,8},{10,11... | collective-permute-start | bytes 3932168 | tf_op jit(solution)/shard_map/ppermute | solution.py:737
  482.9 37.7 %collective-permute-start.24 = (bf16[320,2048]{1,0:T(8,128)(2,1)}, bf16[320,2048]{1,0:T(8,128)(2,1)}, u32[]{:S(2)}, u32[]{:S(2)}) collective-permute-start(bf16[320,2048]{1,0:T(8,128)(2,1)} %slice.157), channel_id=1, source_target_pairs={{0,1},{1,0},{2,3},{3,2},{4,5},{5,4},{6,7},{7,6},{8,9},{9,8},{10,11... | collective-permute-start | bytes 3932168 | tf_op jit(solution)/shard_map/ppermute | solution.py:737
  498.0 164.9 %reduce-scatter.9.cloned.1.call-start = ((), (), s32[]{:S(2)}) async-start(), calls=%async_computation.8 | async-start | bytes 5242880 | tf_op jit(solution)/shard_map/reduce_scatter | solution.py:761
  507.3 16.3 %collective-permute-start.22 = (bf16[320,2048]{1,0:T(8,128)(2,1)S(1)}, bf16[320,2048]{1,0:T(8,128)(2,1)S(1)}, u32[]{:S(2)}, u32[]{:S(2)}) collective-permute-start(bf16[320,2048]{1,0:T(8,128)(2,1)S(1)} %slice.155), channel_id=1, source_target_pairs={{0,1},{1,0},{2,3},{3,2},{4,5},{5,4},{6,7},{7,6},{8,9},{9,8},{10,11... | collective-permute-start | bytes 3932168 | tf_op jit(solution)/shard_map/ppermute | solution.py:737
  519.5 37.3 %collective-permute-start.27 = (bf16[320,2048]{1,0:T(8,128)(2,1)}, bf16[320,2048]{1,0:T(8,128)(2,1)}, u32[]{:S(2)}, u32[]{:S(2)}) collective-permute-start(bf16[320,2048]{1,0:T(8,128)(2,1)} %add_convert_fusion), channel_id=1, source_target_pairs={{0,6},{1,7},{2,4},{3,5},{4,2},{5,3},{6,0},{7,1},{8,14},{9,15},{10,... | collective-permute-start | bytes 3932168 | tf_op jit(solution)/shard_map/ppermute | solution.py:737
  523.4 56.0 %collective-permute-start.25 = (bf16[320,2048]{1,0:T(8,128)(2,1)}, bf16[320,2048]{1,0:T(8,128)(2,1)}, u32[]{:S(2)}, u32[]{:S(2)}) collective-permute-start(bf16[320,2048]{1,0:T(8,128)(2,1)} %add_convert_fusion.1), channel_id=1, source_target_pairs={{0,4},{1,5},{2,6},{3,7},{4,0},{5,1},{6,2},{7,3},{8,12},{9,13},{10,... | collective-permute-start | bytes 3932168 | tf_op jit(solution)/shard_map/ppermute | solution.py:737
  525.2 54.3 %collective-permute-start.23 = (bf16[320,2048]{1,0:T(8,128)(2,1)}, bf16[320,2048]{1,0:T(8,128)(2,1)}, u32[]{:S(2)}, u32[]{:S(2)}) collective-permute-start(bf16[320,2048]{1,0:T(8,128)(2,1)} %add_convert_fusion.2), channel_id=1, source_target_pairs={{0,2},{1,3},{2,0},{3,1},{4,6},{5,7},{6,4},{7,5},{8,10},{9,11},{10,... | collective-permute-start | bytes 3932168 | tf_op jit(solution)/shard_map/ppermute | solution.py:737
  537.3 42.2 %collective-permute-start.21 = (bf16[320,2048]{1,0:T(8,128)(2,1)}, bf16[320,2048]{1,0:T(8,128)(2,1)}, u32[]{:S(2)}, u32[]{:S(2)}) collective-permute-start(bf16[320,2048]{1,0:T(8,128)(2,1)} %slice.153), channel_id=1, source_target_pairs={{0,1},{1,0},{2,3},{3,2},{4,5},{5,4},{6,7},{7,6},{8,9},{9,8},{10,11... | collective-permute-start | bytes 3932168 | tf_op jit(solution)/shard_map/ppermute | solution.py:737
  584.7 277.4 %reduce-scatter.11.cloned.1.call-start = ((), (), s32[]{:S(2)}) async-start(), calls=%async_computation.9 | async-start | bytes 5242880 | tf_op jit(solution)/shard_map/reduce_scatter | solution.py:761
  (53 other events, 950.8 us)
Sparse Core Ops, SparseCore 0:
  164.8 145.5 all-gather.2
  312.0 79.2 all-gather.4
  411.2 77.8 reduce-scatter.4
  498.2 77.7 reduce-scatter.6
  584.8 76.8 reduce-scatter.8
  664.5 77.2 reduce-scatter.10

commit v6 on v5

--- a/solution.py
+++ b/solution.py
@@ -732,6 +732,255 @@
     )
 
 
+def forward_back_kernel(
+    activated_ref, grad_ref, gate_up_ref, down_ref, out_ref, gate_up_grad_ref
+):
+    own_hidden = activated_ref.shape[1]
+    part = down_ref.shape[0] // 4
+
+    @pl.loop(0, 4)
+    def _(at):
+        columns = pl.ds(pl.multiple_of(at * part, part), part)
+        out_ref[:, columns] = across(activated_ref[...], down_ref[columns]).astype(LOW)
+
+    piece = own_hidden // 2
+    for at in range(2):
+        columns = slice(at * piece, (at + 1) * piece)
+        upper = slice(own_hidden + at * piece, own_hidden + (at + 1) * piece)
+        activated_grad = jnp.dot(
+            grad_ref[...], down_ref[:, columns], preferred_element_type=FULL
+        )
+        gate_values, up_values = gate_up_ref[:, columns], gate_up_ref[:, upper]
+        gate_sigmoid = jax.nn.sigmoid(gate_values)
+        gate_grad, up_grad = gate_backward(
+            activated_grad, gate_values, up_values, gate_sigmoid, gate_values * gate_sigmoid
+        )
+        gate_up_grad_ref[:, columns] = gate_grad
+        gate_up_grad_ref[:, upper] = up_grad
+
+
+def forward_back(rows, activated, grads, gate_up, down_weight):
+    count, own_hidden = activated.shape
+    block = lambda width: pl.BlockSpec((rows, width), lambda j: (j, 0))
+    return pl.pallas_call(
+        forward_back_kernel,
+        grid=(count // rows,),
+        in_specs=[
+            block(own_hidden),
+            block(D),
+            block(2 * own_hidden),
+            pl.BlockSpec(down_weight.shape, lambda j: (0, 0)),
+        ],
+        out_specs=[block(D), block(2 * own_hidden)],
+        out_shape=[
+            jax.ShapeDtypeStruct((count, D), LOW),
+            jax.ShapeDtypeStruct((count, 2 * own_hidden), LOW),
+        ],
+        compiler_params=pltpu.CompilerParams(vmem_limit_bytes=VMEM_LIMIT),
+        name="forward_back",
+    )(activated, grads, gate_up, down_weight)
+
+
+def plane_back_kernel(
+    plane,
+    rows_ref,
+    weight_ref,
+    out_ref,
+    weight,
+    tiles,
+    keep,
+    give,
+    core_in,
+    plane_in,
+    total,
+    load_sem,
+    tile_sem,
+    core_send,
+    core_recv,
+    plane_send,
+    plane_recv,
+    out_sem,
+):
+    g = lax.axis_index("grp")
+    d = lax.axis_index("dp")
+    chips = plane // 2
+    halves = plane == 8
+    order = (3, 1, 2, 0) if halves else tuple(range(chips - 1, -1, -1))
+    cut = D // 2
+    half_of = (pl.ds(0, cut), pl.ds(cut, D - cut))
+
+    barrier = pltpu.get_barrier_semaphore()
+    for offset in range(1, plane):
+        pl.semaphore_signal(
+            barrier, inc=1, device_id=(g, flip(d, offset)), device_id_type=MESH
+        )
+
+    load = pltpu.make_async_copy(weight_ref, weight, load_sem.at[0])
+    load.start()
+
+    def tile_copy(turn):
+        at = order[turn]
+        return pltpu.make_async_copy(
+            rows_ref.at[pl.ds(2 * at, 2)], tiles.at[turn % 2], tile_sem.at[turn % 2]
+        )
+
+    def core_copy(at):
+        return remote(
+            give.at[at], core_in.at[at], core_send.at[at], core_recv.at[at], (g, flip(d, 1))
+        )
+
+    def plane_copy(at):
+        return remote(
+            keep.at[at],
+            plane_in.at[at],
+            plane_send.at[at],
+            plane_recv.at[at],
+            (g, flip(d, 2 * at)),
+        )
+
+    def near_copy(part, relayed):
+        there = part + 1
+        return remote(
+            keep.at[3 if relayed else there, :, half_of[part]],
+            plane_in.at[1 if relayed else 0, :, half_of[part]],
+            plane_send.at[2 * relayed + part],
+            plane_recv.at[2 * relayed + part],
+            (g, flip(d, 2 * there)),
+        )
+
+    def relay_copy(part):
+        there = 2 - part
+        return remote(
+            keep.at[there, :, half_of[part]],
+            plane_in.at[2, :, half_of[part]],
+            plane_send.at[4 + part],
+            plane_recv.at[4 + part],
+            (g, flip(d, 2 * there)),
+        )
+
+    tile_copy(0).start()
+    tile_copy(1).start()
+    pl.semaphore_wait(barrier, plane - 1)
+    load.wait()
+    part_width = 512
+
+    def product(turn, which, target):
+        @pl.loop(0, D // part_width)
+        def _(at):
+            columns = pl.ds(pl.multiple_of(at * part_width, part_width), part_width)
+            target[order[turn], :, columns] = across(
+                tiles[turn % 2, which], weight[columns]
+            ).astype(LOW)
+
+    def add_into(at, other, first, count):
+        step = 256
+
+        @pl.loop(0, count // step)
+        def _(k):
+            here = pl.ds(pl.multiple_of(first + k * step, step), step)
+            keep[at, :, here] = (
+                keep[at, :, here].astype(FULL) + other(here).astype(FULL)
+            ).astype(LOW)
+
+    def settle(turn):
+        at = order[turn]
+        core_copy(at).wait_recv()
+        add_into(at, lambda here: core_in[at, :, here], 0, D)
+        if halves and at == 3:
+            near_copy(0, True).start()
+            near_copy(1, True).start()
+        elif halves and at:
+            near_copy(at - 1, False).start()
+        elif at:
+            plane_copy(at).start()
+
+    for turn in range(chips):
+        tile_copy(turn).wait()
+        product(turn, 1, give)
+        core_copy(order[turn]).start()
+        if turn:
+            settle(turn - 1)
+        product(turn, 0, keep)
+        if turn + 2 < chips:
+            tile_copy(turn + 2).start()
+        if halves and turn == chips - 1:
+            for part in range(2):
+                near_copy(part, True).wait_recv()
+                add_into(
+                    2 - part,
+                    lambda here: plane_in[1, :, here],
+                    part * cut,
+                    cut,
+                )
+                relay_copy(part).start()
+    settle(chips - 1)
+    if halves:
+        for part in range(2):
+            near_copy(part, False).wait_recv()
+            relay_copy(part).wait_recv()
+        arrived = (0, 2)
+    else:
+        for at in range(1, chips):
+            plane_copy(at).wait_recv()
+        arrived = tuple(range(1, chips))
+
+    @pl.loop(0, D // 256)
+    def _(k):
+        here = pl.ds(pl.multiple_of(k * 256, 256), 256)
+        value = keep[0, :, here].astype(FULL)
+        for at in arrived:
+            value = value + plane_in[at, :, here].astype(FULL)
+        total[:, here] = value
+
+    out = pltpu.make_async_copy(total, out_ref, out_sem.at[0])
+    out.start()
+    for at in range(chips):
+        core_copy(at).wait_send()
+    if halves:
+        for part in range(2):
+            near_copy(part, False).wait_send()
+            near_copy(part, True).wait_send()
+            relay_copy(part).wait_send()
+    else:
+        for at in range(1, chips):
+            plane_copy(at).wait_send()
+    out.wait()
+
+
+def plane_back(rows, gate_up_grad, gate_weight):
+    plane = lax.axis_size("dp")
+    chips = plane // 2
+    inner = gate_up_grad.shape[1]
+    anywhere = pl.BlockSpec(memory_space=pl.ANY)
+    dma = pltpu.SemaphoreType.DMA
+    return pl.pallas_call(
+        functools.partial(plane_back_kernel, plane),
+        out_shape=jax.ShapeDtypeStruct((rows, D), FULL),
+        in_specs=[anywhere] * 2,
+        out_specs=anywhere,
+        scratch_shapes=[
+            pltpu.VMEM((D, inner), LOW),
+            pltpu.VMEM((2, 2, rows, inner), LOW),
+            pltpu.VMEM((chips, rows, D), LOW),
+            pltpu.VMEM((chips, rows, D), LOW),
+            pltpu.VMEM((chips, rows, D), LOW),
+            pltpu.VMEM((3 if plane == 8 else chips, rows, D), LOW),
+            pltpu.VMEM((rows, D), FULL),
+            dma((1,)),
+            dma((2,)),
+            dma((chips,)),
+            dma((chips,)),
+            dma((max(6, chips),)),
+            dma((max(6, chips),)),
+            dma((1,)),
+        ],
+        compiler_params=pltpu.CompilerParams(
+            collective_id=2, has_side_effects=True, vmem_limit_bytes=VMEM_LIMIT
+        ),
+        name="plane_back",
+    )(gate_up_grad.reshape(plane, rows, inner), gate_weight)
+
+
 def plane_swap(block, offset):
     size = lax.axis_size("dp")
     return lax.ppermute(block, "dp", [(i, i ^ offset) for i in range(size)])
@@ -741,20 +990,6 @@
     mine = [block] + [plane_swap(block, o) for o in range(2, lax.axis_size("dp"), 2)]
     pairs = [(one, plane_swap(one, 1)) for one in mine]
     return jnp.concatenate([one for pair in pairs for one in pair], axis=0)
-
-
-def plane_scatter(part_of):
-    size = lax.axis_size("dp")
-    sums = {}
-    for offset in list(range(size - 2, 0, -2)) + [0]:
-        arrived = plane_swap(part_of(offset + 1).astype(LOW), 1)
-        sums[offset] = part_of(offset).astype(FULL) + arrived.astype(FULL)
-        if offset:
-            sums[offset] = plane_swap(sums[offset].astype(LOW), offset)
-    total = sums[0]
-    for offset in range(2, size, 2):
-        total = total + sums[offset].astype(FULL)
-    return total
 
 
 def line_scatter(term):
@@ -971,11 +1206,12 @@
             core_copy(turn, part).start()
             if turn < 2:
                 mine_copy(turn, part).start()
-    for step in range(1, plane):
-        for part in range(3):
-            swap_copy(step, part).start()
-    for one in own_swap:
-        one.start()
+        if turn == 0:
+            for step in range(1, plane):
+                for part in range(3):
+                    swap_copy(step, part).start()
+            for one in own_swap:
+                one.start()
     for which in range(3):
         state_copy(0, which).start()
         for slab in range(2):
@@ -994,27 +1230,30 @@
             total = core_in[line, there, :, here].astype(FULL) + other(here).astype(FULL)
             core_in[line, there, :, here] = total.astype(LOW)
 
+    def near_start(turn):
+        if halves:
+            for relayed in (True, False):
+                for part in range(2):
+                    near_copy(turn, part, relayed).start()
+        else:
+            for step in range(1, chips):
+                plane_copy(turn, step).start()
+
     for turn in range(lines):
         line = line_at(turn)
         for part in every:
             core_copy(turn, part).wait_recv()
             mine_copy(turn, part).wait()
-        order = (3, 1, 2, 0) if halves else tuple(range(1, chips + 1))
-        for step in order:
-            there = flip(chip, step) if halves else lax.rem(chip + step, chips)
+        for step in range(1, chips + 1):
+            there = lax.rem(chip + step, chips)
             add_into(
                 line, there, lambda here, there=there, turn=turn: mine[turn % 2, there, :, here]
             )
-            if halves and step == 3:
-                for part in range(2):
-                    near_copy(turn, part, True).start()
-            elif halves and step:
-                near_copy(turn, step - 1, False).start()
-            elif not halves and step < chips:
-                plane_copy(turn, step).start()
         if turn + 2 < lines:
             for part in every:
                 mine_copy(turn + 2, part).start()
+        if turn < 2:
+            near_start(turn)
 
     def pass_on(turn):
         line = line_at(turn)
@@ -1065,31 +1304,28 @@
         for which in range(4):
             made_copy(turn, which).start()
 
-    if halves:
-        pass_on(0)
-    for one in own_swap:
-        one.wait()
-    for step in range(1, plane):
-        for part in range(3):
-            swap_copy(step, part).wait_recv()
-    each = 3 * plane // lines
-    for turn in range(lines):
-        lax.fori_loop(turn * each, (turn + 1) * each, lambda k, c: (forward_turn(k), c)[1], 0)
+    def near_done(turn):
+        if halves:
+            pass_on(turn)
+            for part in range(2):
+                near_copy(turn, part, False).wait_recv()
+        else:
+            for step in range(1, chips):
+                plane_copy(turn, step).wait_recv()
+        if turn + 2 < lines:
+            near_start(turn + 2)
+
+    def line_done(turn):
         line = line_at(turn)
         if halves:
-            if turn + 1 < lines:
-                pass_on(turn + 1)
             for part in range(2):
-                near_copy(turn, part, False).wait_recv()
                 relay_copy(turn, part).wait_recv()
             arrived = (0, 2)
         else:
-            for step in range(1, chips):
-                plane_copy(turn, step).wait_recv()
             arrived = tuple(lax.rem(chip + step, chips) for step in range(1, chips))
 
         @pl.loop(0, width // tile)
-        def _(at, line=line, arrived=arrived):
+        def _(at):
             columns = pl.ds(pl.multiple_of(at * tile, tile), tile)
             total = core_in[line, chip, :, columns].astype(FULL)
             for block in arrived:
@@ -1099,6 +1335,24 @@
         if turn < lines - 1:
             line_copy(turn).start()
 
+    each = 3 * plane // lines
+
+    def forward_some(turn):
+        lax.fori_loop(turn * each, (turn + 1) * each, lambda k, c: (forward_turn(k), c)[1], 0)
+
+    near_done(0)
+    for turn in range(1, lines):
+        if turn == 1:
+            for one in own_swap:
+                one.wait()
+            for step in range(1, plane):
+                for part in range(3):
+                    swap_copy(step, part).wait_recv()
+        near_done(turn)
+        line_done(turn - 1)
+        forward_some(turn - 1)
+    line_done(lines - 1)
+    forward_some(lines - 1)
     for which in range(4):
         for turn in (3 * plane - 2, 3 * plane - 1):
             made_copy(turn, which).wait()
@@ -1299,17 +1553,6 @@
     normed_two = (middle * second_scale * gain_float[1]).astype(LOW)
     grad_rows = cotangent.reshape(row_count, D).astype(FULL)
 
-    def by_offset(left, right, right_axis, after=None):
-        chunks = {}
-        for offset in list(range(2, dp_size, 2)) + [0]:
-            rows = left[offset * row_count : (offset + 2) * row_count]
-            if offset == 0 and after is not None:
-                rows, _ = lax.optimization_barrier((rows, after))
-            chunks[offset] = contract(rows, right, 1, right_axis).astype(LOW)
-        return lambda offset: chunks[offset - offset % 2][
-            (offset % 2) * row_count : (offset % 2 + 1) * row_count
-        ]
-
     normed_two, down_grad = lax.optimization_barrier((normed_two, down_grad))
     normed_all = plane_gather(normed_two)
     gate_up = jnp.dot(normed_all, gate_weight, preferred_element_type=FULL)
@@ -1318,31 +1561,24 @@
     gate_sigmoid, gate_silu, activated = gate_parts(gate_values, up_values)
     down_term = contract(down_grad, activated, 0, 0).astype(LOW)
     down_term, down_weight = lax.optimization_barrier((down_term, down_weight))
-    out_parts = by_offset(activated, down_weight, 1)
-    out_chunks = [out_parts(offset) for offset in range(dp_size)]
-    out_chunks, down_grad = lax.optimization_barrier((out_chunks, down_grad))
+    out_term, gate_up_grad = forward_back(row_count, activated, down_grad, gate_up, down_weight)
+    out_chunks = out_term.reshape(dp_size, row_count, D)
     out_swapped = [plane_swap(out_chunks[offset + 1], 1) for offset in range(0, dp_size, 2)]
-    activated_grad = contract(down_grad, down_weight, 1, 0)
-    gate_grad, up_grad = gate_backward(
-        activated_grad, gate_values, up_values, gate_sigmoid, gate_silu
-    )
-    gate_up_grad = jnp.concatenate([gate_grad, up_grad], axis=1)
-
-    gate_up_grad, out_swapped = lax.optimization_barrier((gate_up_grad, out_swapped))
+    down_part = line_scatter(down_term)
+    gate_term = contract(normed_all, gate_up_grad[:, :own_hidden], 0, 0).astype(LOW)
+    gate_term, out_swapped = lax.optimization_barrier((gate_term, out_swapped))
     out_sums = [
         out_chunks[2 * at].astype(FULL) + one.astype(FULL) for at, one in enumerate(out_swapped)
     ]
-    out_arrived = [plane_swap(one.astype(LOW), 2 * at) for at, one in enumerate(out_sums) if at]
-    down_part = line_scatter(down_term)
-    back_parts = by_offset(gate_up_grad, gate_weight, 1, down_part)
-    normed_two_grad = plane_scatter(back_parts)
-    gate_term = contract(normed_all, gate_up_grad[:, :own_hidden], 0, 0).astype(LOW)
-    normed_all, out_arrived = lax.optimization_barrier((normed_all, out_arrived))
+    out_low = [one.astype(LOW) for one in out_sums[1:]]
+    normed_all, out_low = lax.optimization_barrier((normed_all, out_low))
+    out_arrived = [plane_swap(one, 2 * at + 2) for at, one in enumerate(out_low)]
     up_term = contract(normed_all, gate_up_grad[:, own_hidden:], 0, 0).astype(LOW)
+    gate_term, down_part = lax.optimization_barrier((gate_term, down_part))
     gate_part = line_scatter(gate_term)
-    normed_two_grad, gate_term, up_term = lax.optimization_barrier(
-        (normed_two_grad, gate_term, up_term)
-    )
+    gate_up_grad, up_term = lax.optimization_barrier((gate_up_grad, up_term))
+    normed_two_grad = plane_back(row_count, gate_up_grad, gate_weight)
+    normed_two_grad, out_arrived = lax.optimization_barrier((normed_two_grad, out_arrived))
     result = middle + out_sums[0]
     for one in out_arrived:
         result = result + one.astype(FULL)

time: 911 us -> 895 us (0.982)
  Pallas kernels: 450 us -> 559 us
  matrix products: 166 us -> 86.8 us
  other arithmetic: 70.3 us -> 40.3 us
    pallas_call x0 -> x2, Pallas kernels: none -> 137 us  [the longest x1 101 us: plane_back(): pl.pallas_call(functools.partial(plane_back_kernel, plane), out_shape=jax...]
    dot_general x14 -> x5, matrix products: 137 us -> 60.1 us  [contract(): lax.dot_general(left, right, (((left_axis,), (right_axis,)), ((), ())), p...]
    ppermute x28 -> x21, waiting for transfers between devices: 57.5 us -> 27 us  [plane_swap(): return lax.ppermute(block, 'dp', [(i, i ^ offset) for i in range(size)])]
    pallas_call x1, Pallas kernels: 196 us -> 168 us  [finish(): pl.pallas_call(functools.partial(finish_kernel, lines, plane), out_shape=...]
    reduce_scatter x4, waiting for transfers between devices: 0.03 us -> 21.2 us  [line_scatter(): return lax.psum_scatter(term, 'grp', scatter_dimension=0, tiled=True)]
    convert_element_type x6 -> x1, other arithmetic: 17.2 us -> 6.7 us  [body(): out_low = [one.astype(LOW) for one in out_sums[1:]]]
    ppermute x28 -> x21, starting transfers between devices: 49.8 us -> 41.9 us  [plane_swap(): return lax.ppermute(block, 'dp', [(i, i ^ offset) for i in range(size)])]
    unnamed x131 -> x127, local copies, waits for them, and re-layouts: 47.4 us -> 49.3 us
  transfers between devices with their start and end apart: 34 -> 27, of which waited for: 5 -> 4; matrix products, arithmetic and copies ran while one was open for 26% -> 16% of each run, Pallas kernels for 33% -> 46%
where the time goes in v6:
time: 895 us; the launch traced here: 883 us
  Pallas kernels  559 us (62%)
  matrix products  86.8 us (10%)
  waiting for transfers between devices  77.9 us (9%)
  local copies, waits for them, and re-layouts  60 us (7%)
  starting transfers between devices  43.1 us (5%)
  other arithmetic  40.3 us (5%)
  between operations  15.9 us (2%)
    pallas_call x1, Pallas kernels, finish(): pl.pallas_call(functools.partial(finish_kernel, lines, plane), out_shape=...  168 us
    pallas_call x1, Pallas kernels, gather_start(): pl.pallas_call(functools.partial(gather_kernel, lines, plane, prompt_rows...  149 us
    pallas_call x1, Pallas kernels, plane_back(): pl.pallas_call(functools.partial(plane_back_kernel, plane), out_shape=jax...  101 us
    dot_general x5, matrix products, contract(): lax.dot_general(left, right, (((left_axis,), (right_axis,)), ((), ())), p...  60.1 us
    unnamed x127, local copies, waits for them, and re-layouts  49.3 us
    ppermute x21, starting transfers between devices, plane_swap(): return lax.ppermute(block, 'dp', [(i, i ^ offset) for i in range(size)])  41.9 us
    pallas_call x1, Pallas kernels, weights_back(): pl.pallas_call(weights_back_kernel, grid_spec=pltpu.PrefetchScalarGridSpe...  40.2 us
    pallas_call x1, Pallas kernels, forward_back(): pl.pallas_call(forward_back_kernel, grid=(count // rows,), in_specs=[bloc...  36.9 us
  transfers between devices with their start and end apart: 27, of which 4 were waited for; matrix products, arithmetic and copies ran while one was open for 16% of the time, Pallas kernels for 46%

profile of v6, /device:TPU:9, one launch (start us, length us, event | category | flops | bytes accessed | tf_op | source)
XLA Modules:
  0.0 882.7 jit_solution(6035448352098670924)
XLA Ops:
  7.3 4.9 convert_element_type.111.forward_ref
  13.3 148.6 %gather_start.1 = (bf16[4,8,64,6272]{3,2,1,0:T(8,128)(2,1)}, bf16[4,256,2048]{2,1,0:T(8,128)(2,1)}, bf16[8,64,2048]{2,1,0:T(8,128)(2,1)}, bf16[8,64,1024]{2,1,0:T(8,128)(2,1)}) custom-call(bf16[64,6272]{1,0:T(8,128)(2,1)} %fusion.30.weight_ref, bf16[320,2048]{1,0:T(8,128)(2,1)} %bitcast.54, bf16[64,24576]{1,0:T(8,128)(2,1)} %convert_element_type.111.forward_ref), custom_call_target="tpu_custom_call" | custom-call | tf_op jit(solution)/shard_map/gather_start/pallas_call | solution.py:371
  170.5 3.1 multiply_sine_fusion
  173.7 34.5 %project_heads.1 = (bf16[320,2048]{1,0:T(8,128)(2,1)}, bf16[1088,2048]{1,0:T(8,128)(2,1)}, bf16[1088,2048]{1,0:T(8,128)(2,1)}, bf16[320,2048]{1,0:T(8,128)(2,1)}, f32[1088,128]{1,0:T(8,128)}) custom-call(s32[1]{0:T(128)} %bitcast.1.place_ref, bf16[1024,2048]{1,0:T(8,128)(2,1)} %bitcast.57, bf16[320,2048]{1,0:T(8,128)(2,1)} %bitcast.55, ...), custom_call_target="tpu_custom_call" | custom-call | tf_op jit(solution)/shard_map/project_heads/pallas_call | solution.py:469
  210.0 11.4 %attend.1 = (bf16[320,2048]{1,0:T(8,128)(2,1)}, f32[320,1024]{1,0:T(8,128)}) custom-call(bf16[320,2048]{1,0:T(8,128)(2,1)} %get-tuple-element.86.query_ref, bf16[1088,2048]{1,0:T(8,128)(2,1)} %get-tuple-element.87.key_ref.value_ref, bf16[1088,2048]{1,0:T(8,128)(2,1)} %get-tuple-element.87.key_ref.value_ref, f32[320,1088]{1,0:T(8,128)} %add_convert_fusion.4.seen_ref), custom_call_target="tpu_custom_call" | custom-call | tf_op jit(solution)/shard_map/attend/pallas_call | solution.py:531
  221.4 5.9 multiply_reduce_fusion.2
  240.1 27.0 %collective-permute-done.8 = bf16[320,2048]{1,0:T(8,128)(2,1)S(1)} collective-permute-done((bf16[320,2048]{1,0:T(8,128)(2,1)S(1)}, bf16[320,2048]{1,0:T(8,128)(2,1)S(1)}, u32[]{:S(2)}, u32[]{:S(2)}) %collective-permute-start.8) | collective-permute-done | bytes 1310752 | tf_op jit(solution)/shard_map/ppermute | solution.py:986
  268.1 28.9 %collective-permute-start.11 = (bf16[320,2048]{1,0:T(8,128)(2,1)S(1)}, bf16[320,2048]{1,0:T(8,128)(2,1)S(1)}, u32[]{:S(2)}, u32[]{:S(2)}) collective-permute-start(bf16[320,2048]{1,0:T(8,128)(2,1)S(1)} %collective-permute-done.10), channel_id=1, source_target_pairs={{0,1},{1,0},{2,3},{3,2},{4,5},{5,4},{6,7},{7,6},{8,9},{9,8},{10,11... | collective-permute-start | bytes 3932168 | tf_op jit(solution)/shard_map/ppermute | solution.py:986
  307.9 26.7 %fusion.38.gate_up_ref = f32[2560,2048]{1,0:T(8,128)S(1)} fusion(bf16[2560,2048]{1,0:T(8,128)(2,1)} %constant_dynamic-update-slice_fusion.8, bf16[2048,2048]{1,0:T(8,128)(2,1)} %all-gather.3.cloned.1.call-done.weight_ref), kind=kOutput, calls=%fused_computation.101 | convolution fusion | flops 21474836480 | bytes 39845888 | tf_op jit(solution)/shard_map/dot_general | solution.py:1558
  334.7 3.6 fusion.activated_ref
  338.2 3.5 copy-done
  344.1 15.4 %convolution_convert_fusion = bf16[2048,1024]{1,0:T(8,128)(2,1)} fusion(bf16[2560,2048]{1,0:T(8,128)(2,1)} %copy-done.7, bf16[2560,1024]{1,0:T(8,128)(2,1)S(1)} %fusion.activated_ref), kind=kOutput, calls=%fused_computation.14 | convolution fusion | flops 10739515392 | bytes 19922944 | tf_op jit(solution)/shard_map/dot_general | solution.py:35
  359.5 29.0 %all-gather.5.cloned.1.call-done.down_ref = bf16[2048,1024]{1,0:T(8,128)(2,1)} async-done(((bf16[512,1024]{1,0:T(8,128)(2,1)}), bf16[2048,1024]{1,0:T(8,128)(2,1)}) %all-gather.5.cloned.1.call-update) | async-done | bytes 4194320 | tf_op jit(solution)/shard_map/all_gather | solution.py:1518
  389.0 36.9 %forward_back.1 = (bf16[2560,2048]{1,0:T(8,128)(2,1)}, bf16[2560,2048]{1,0:T(8,128)(2,1)}) custom-call(bf16[2560,1024]{1,0:T(8,128)(2,1)} %copy-done.6, bf16[2560,2048]{1,0:T(8,128)(2,1)} %copy-done.7, f32[2560,2048]{1,0:T(8,128)} %copy-done, bf16[2048,1024]{1,0:T(8,128)(2,1)} %all-gather.5.cloned.1.call-done.down_ref), custom_call_target="tpu_custom_call" | custom-call | tf_op jit(solution)/shard_map/forward_back/pallas_call | solution.py:765
  425.8 4.9 fusion.37
  432.9 15.2 %fusion.9 = bf16[2048,1024]{1,0:T(8,128)(2,1)} fusion(bf16[2560,2048]{1,0:T(8,128)(2,1)} %constant_dynamic-update-slice_fusion.8, bf16[2560,2048]{1,0:T(8,128)(2,1)S(1)} %copy-done.8), kind=kOutput, calls=%fused_computation.15 | convolution fusion | flops 10739515392 | bytes 19922944 | tf_op jit(solution)/shard_map/dot_general | solution.py:35
  448.2 21.1 %reduce-scatter.5.cloned.1.call-done = bf16[512,1024]{1,0:T(8,128)(2,1)} async-done(((bf16[2048,1024]{1,0:T(8,128)(2,1)}), bf16[512,1024]{1,0:T(8,128)(2,1)}) %reduce-scatter.5.cloned.1.call-update) | async-done | bytes 1048592 | tf_op jit(solution)/shard_map/reduce_scatter | solution.py:996
  469.5 6.7 add_convert_fusion.1
  477.2 15.7 %fusion.12 = bf16[2048,1024]{1,0:T(8,128)(2,1)} fusion(bf16[2560,2048]{1,0:T(8,128)(2,1)} %constant_dynamic-update-slice_fusion.8, bf16[2560,2048]{1,0:T(8,128)(2,1)S(1)} %copy-done.9), kind=kOutput, calls=%fused_computation.16 | convolution fusion | flops 10739515392 | bytes 19922944 | tf_op jit(solution)/shard_map/dot_general | solution.py:35
  495.9 100.5 %plane_back.1 = f32[320,2048]{1,0:T(8,128)} custom-call(bf16[8,320,2048]{2,1,0:T(8,128)(2,1)} %bitcast.59, bf16[2048,2048]{1,0:T(8,128)(2,1)} %all-gather.3.cloned.1.call-done.weight_ref), custom_call_target="tpu_custom_call" | custom-call | tf_op jit(solution)/shard_map/plane_back/pallas_call | solution.py:956
  596.6 3.0 multiply_reduce_fusion
  600.2 5.3 fusion.36
  605.6 7.8 fusion.17.grad_ref
  613.4 18.9 %attend_back.1 = (bf16[320,2048]{1,0:T(8,128)(2,1)}, bf16[1088,2048]{1,0:T(8,128)(2,1)}) custom-call(s32[1]{0:T(128)} %bitcast.1.place_ref, bf16[320,2048]{1,0:T(8,128)(2,1)} %get-tuple-element.86.query_ref, bf16[1088,2048]{1,0:T(8,128)(2,1)} %get-tuple-element.87.key_ref.value_ref, bf16[1088,2048]{1,0:T(8,128)(2,1)} %get-tuple-element.87.key_ref.value_ref, ...), custom_call_target="tpu_custom_call" | custom-call | tf_op jit(solution)/shard_map/attend_back/pallas_call | solution.py:610
  632.2 40.2 %weights_back.1 = (bf16[2048,2048]{1,0:T(8,128)(2,1)}, bf16[2048,2048]{1,0:T(8,128)(2,1)}, bf16[2048,2048]{1,0:T(8,128)(2,1)}, f32[320,2048]{1,0:T(8,128)}, bf16...) custom-call(s32[1]{0:T(128)} %bitcast.1.place_ref, bf16[320,2048]{1,0:T(8,128)(2,1)} %get-tuple-element.117.query_ref, ...), custom_call_target="tpu_custom_call" | custom-call | tf_op jit(solution)/shard_map/weights_back/pallas_call | solution.py:689
  674.7 167.7 %finish.1 = (f32[64,4096]{1,0:T(8,128)}, f32[64,4096]{1,0:T(8,128)}, f32[64,4096]{1,0:T(8,128)}, f32[64,4096]{1,0:T(8,128)}, f32[64,2048]{1,0:T(8,128)}, /*index...) custom-call(bf16[4,4,2,64,2048]{4,3,2,1,0:T(8,128)(2,1)} %bitcast.60, ...), custom_call_target="tpu_custom_call" | custom-call | tf_op jit(solution)/shard_map/finish/pallas_call | solution.py:1429
  846.0 2.9 fusion.20
  849.0 4.2 fusion.24
  860.9 3.2 copy.126
  864.1 3.2 copy.127
  868.9 3.0 copy.128
  872.7 2.7 copy.129
  (227 shorter events, 61.2 us)
Async XLA Ops:
  7.2 300.4 %all-gather.3.cloned.1.call-start = ((), (), s32[]{:S(2)}) async-start(), calls=%async_computation.4 | async-start | bytes 10485760 | tf_op jit(solution)/shard_map/all_gather | solution.py:1514
  13.3 148.7 %copy-start.11 = (bf16[1,1,320,2048]{3,2,1,0:T(8,128)(2,1)S(1)}, bf16[1,1,320,2048]{3,2,1,0:T(8,128)(2,1)}, u32[]{:S(2)}) copy-start(bf16[1,1,320,2048]{3,2,1,0:T(8,128)(2,1)} %param.17) | copy-start | bytes 3932164
  161.9 226.6 %all-gather.5.cloned.1.call-start = ((), (), s32[]{:S(2)}) async-start(), calls=%async_computation.5 | async-start | bytes 5242880 | tf_op jit(solution)/shard_map/all_gather | solution.py:1518
  162.0 68.1 %collective-permute-start = (bf16[320,2048]{1,0:T(8,128)(2,1)S(1)}, bf16[320,2048]{1,0:T(8,128)(2,1)}, u32[]{:S(2)}, u32[]{:S(2)}) collective-permute-start(bf16[320,2048]{1,0:T(8,128)(2,1)S(1)} %bitcast.71), channel_id=1, source_target_pairs={{0,1},{1,0},{2,3},{3,2},{4,5},{5,4},{6,7},{7,6},{8,9},{9,8},{10,11... | collective-permute-start | bytes 3932168 | tf_op jit(solution)/shard_map/ppermute | solution.py:986
  162.2 65.8 %collective-permute-start.1 = (bf16[320,2048]{1,0:T(8,128)(2,1)S(1)}, bf16[320,2048]{1,0:T(8,128)(2,1)}, u32[]{:S(2)}, u32[]{:S(2)}) collective-permute-start(bf16[320,2048]{1,0:T(8,128)(2,1)S(1)} %bitcast.72), channel_id=1, source_target_pairs={{0,2},{1,3},{2,0},{3,1},{4,6},{5,7},{6,4},{7,5},{8,10},{9,11},{10,... | collective-permute-start | bytes 3932168 | tf_op jit(solution)/shard_map/ppermute | solution.py:986
  163.5 65.8 %collective-permute-start.3 = (bf16[320,2048]{1,0:T(8,128)(2,1)S(1)}, bf16[320,2048]{1,0:T(8,128)(2,1)}, u32[]{:S(2)}, u32[]{:S(2)}) collective-permute-start(bf16[320,2048]{1,0:T(8,128)(2,1)S(1)} %bitcast.73), channel_id=1, source_target_pairs={{0,4},{1,5},{2,6},{3,7},{4,0},{5,1},{6,2},{7,3},{8,12},{9,13},{10,... | collective-permute-start | bytes 3932168 | tf_op jit(solution)/shard_map/ppermute | solution.py:986
  163.6 65.9 %collective-permute-start.5 = (bf16[320,2048]{1,0:T(8,128)(2,1)S(1)}, bf16[320,2048]{1,0:T(8,128)(2,1)}, u32[]{:S(2)}, u32[]{:S(2)}) collective-permute-start(bf16[320,2048]{1,0:T(8,128)(2,1)S(1)} %bitcast.74), channel_id=1, source_target_pairs={{0,6},{1,7},{2,4},{3,5},{4,2},{5,3},{6,0},{7,1},{8,14},{9,15},{10,... | collective-permute-start | bytes 3932168 | tf_op jit(solution)/shard_map/ppermute | solution.py:986
  228.0 5.1 collective-permute-start.2
  229.3 5.4 collective-permute-start.4
  229.6 6.7 collective-permute-start.6
  236.5 30.5 %collective-permute-start.8 = (bf16[320,2048]{1,0:T(8,128)(2,1)S(1)}, bf16[320,2048]{1,0:T(8,128)(2,1)S(1)}, u32[]{:S(2)}, u32[]{:S(2)}) collective-permute-start(bf16[320,2048]{1,0:T(8,128)(2,1)S(1)} %multiply_convert_fusion), channel_id=1, source_target_pairs={{0,2},{1,3},{2,0},{3,1},{4,6},{5,7},{6,4},{7,5},{8,10},{9,11},{10,... | collective-permute-start | bytes 3932168 | tf_op jit(solution)/shard_map/ppermute | solution.py:986
  237.8 30.4 %collective-permute-start.10 = (bf16[320,2048]{1,0:T(8,128)(2,1)S(1)}, bf16[320,2048]{1,0:T(8,128)(2,1)S(1)}, u32[]{:S(2)}, u32[]{:S(2)}) collective-permute-start(bf16[320,2048]{1,0:T(8,128)(2,1)S(1)} %multiply_convert_fusion), channel_id=1, source_target_pairs={{0,4},{1,5},{2,6},{3,7},{4,0},{5,1},{6,2},{7,3},{8,12},{9,13},{10,... | collective-permute-start | bytes 3932168 | tf_op jit(solution)/shard_map/ppermute | solution.py:986
  238.2 60.1 %collective-permute-start.12 = (bf16[320,2048]{1,0:T(8,128)(2,1)S(1)}, bf16[320,2048]{1,0:T(8,128)(2,1)S(1)}, u32[]{:S(2)}, u32[]{:S(2)}) collective-permute-start(bf16[320,2048]{1,0:T(8,128)(2,1)S(1)} %multiply_convert_fusion), channel_id=1, source_target_pairs={{0,6},{1,7},{2,4},{3,5},{4,2},{5,3},{6,0},{7,1},{8,14},{9,15},{10,... | collective-permute-start | bytes 3932168 | tf_op jit(solution)/shard_map/ppermute | solution.py:986
  239.2 59.2 %collective-permute-start.7 = (bf16[320,2048]{1,0:T(8,128)(2,1)S(1)}, bf16[320,2048]{1,0:T(8,128)(2,1)S(1)}, u32[]{:S(2)}, u32[]{:S(2)}) collective-permute-start(bf16[320,2048]{1,0:T(8,128)(2,1)S(1)} %multiply_convert_fusion), channel_id=1, source_target_pairs={{0,1},{1,0},{2,3},{3,2},{4,5},{5,4},{6,7},{7,6},{8,9},{9,8},{10,11... | collective-permute-start | bytes 3932168 | tf_op jit(solution)/shard_map/ppermute | solution.py:986
  267.0 33.8 %collective-permute-start.9 = (bf16[320,2048]{1,0:T(8,128)(2,1)S(1)}, bf16[320,2048]{1,0:T(8,128)(2,1)S(1)}, u32[]{:S(2)}, u32[]{:S(2)}) collective-permute-start(bf16[320,2048]{1,0:T(8,128)(2,1)S(1)} %collective-permute-done.8), channel_id=1, source_target_pairs={{0,1},{1,0},{2,3},{3,2},{4,5},{5,4},{6,7},{7,6},{8,9},{9,8},{10,11... | collective-permute-start | bytes 3932168 | tf_op jit(solution)/shard_map/ppermute | solution.py:986
  268.1 35.1 %collective-permute-start.11 = (bf16[320,2048]{1,0:T(8,128)(2,1)S(1)}, bf16[320,2048]{1,0:T(8,128)(2,1)S(1)}, u32[]{:S(2)}, u32[]{:S(2)}) collective-permute-start(bf16[320,2048]{1,0:T(8,128)(2,1)S(1)} %collective-permute-done.10), channel_id=1, source_target_pairs={{0,1},{1,0},{2,3},{3,2},{4,5},{5,4},{6,7},{7,6},{8,9},{9,8},{10,11... | collective-permute-start | bytes 3932168 | tf_op jit(solution)/shard_map/ppermute | solution.py:986
  298.3 7.4 collective-permute-start.13
  307.7 161.6 %reduce-scatter.5.cloned.1.call-start = ((), (), s32[]{:S(2)}) async-start(), calls=%async_computation.6 | async-start | bytes 5242880 | tf_op jit(solution)/shard_map/reduce_scatter | solution.py:996
  388.5 224.8 %reduce-scatter.7.cloned.1.call-start = ((), (), s32[]{:S(2)}) async-start(), calls=%async_computation.7 | async-start | bytes 5242880 | tf_op jit(solution)/shard_map/reduce_scatter | solution.py:996
  430.7 17.4 %collective-permute-start.14 = (bf16[320,2048]{1,0:T(8,128)(2,1)}, bf16[320,2048]{1,0:T(8,128)(2,1)S(1)}, u32[]{:S(2)}, u32[]{:S(2)}) collective-permute-start(bf16[320,2048]{1,0:T(8,128)(2,1)} %get-tuple-element.238), channel_id=1, source_target_pairs={{0,1},{1,0},{2,3},{3,2},{4,5},{5,4},{6,7},{7,6},{8,9},{9,8},{10,11... | collective-permute-start | bytes 3932168 | tf_op jit(solution)/shard_map/ppermute | solution.py:986
  431.3 16.9 %collective-permute-start.15 = (bf16[320,2048]{1,0:T(8,128)(2,1)}, bf16[320,2048]{1,0:T(8,128)(2,1)}, u32[]{:S(2)}, u32[]{:S(2)}) collective-permute-start(bf16[320,2048]{1,0:T(8,128)(2,1)} %get-tuple-element.237), channel_id=1, source_target_pairs={{0,1},{1,0},{2,3},{3,2},{4,5},{5,4},{6,7},{7,6},{8,9},{9,8},{10,11... | collective-permute-start | bytes 3932168 | tf_op jit(solution)/shard_map/ppermute | solution.py:986
  431.3 16.9 %collective-permute-start.16 = (bf16[320,2048]{1,0:T(8,128)(2,1)}, bf16[320,2048]{1,0:T(8,128)(2,1)}, u32[]{:S(2)}, u32[]{:S(2)}) collective-permute-start(bf16[320,2048]{1,0:T(8,128)(2,1)} %get-tuple-element.236), channel_id=1, source_target_pairs={{0,1},{1,0},{2,3},{3,2},{4,5},{5,4},{6,7},{7,6},{8,9},{9,8},{10,11... | collective-permute-start | bytes 3932168 | tf_op jit(solution)/shard_map/ppermute | solution.py:986
  431.8 16.4 %collective-permute-start.17 = (bf16[320,2048]{1,0:T(8,128)(2,1)S(1)}, bf16[320,2048]{1,0:T(8,128)(2,1)}, u32[]{:S(2)}, u32[]{:S(2)}) collective-permute-start(bf16[320,2048]{1,0:T(8,128)(2,1)S(1)} %get-tuple-element.235), channel_id=1, source_target_pairs={{0,1},{1,0},{2,3},{3,2},{4,5},{5,4},{6,7},{7,6},{8,9},{9,8},{10,11... | collective-permute-start | bytes 3932168 | tf_op jit(solution)/shard_map/ppermute | solution.py:986
  469.3 203.2 %reduce-scatter.9.cloned.1.call-start = ((), (), s32[]{:S(2)}) async-start(), calls=%async_computation.8 | async-start | bytes 5242880 | tf_op jit(solution)/shard_map/reduce_scatter | solution.py:996
  493.0 350.2 %reduce-scatter.11.cloned.1.call-start = ((), (), s32[]{:S(2)}) async-start(), calls=%async_computation.9 | async-start | bytes 5242880 | tf_op jit(solution)/shard_map/reduce_scatter | solution.py:996
  493.2 103.3 %collective-permute-start.18 = (bf16[320,2048]{1,0:T(8,128)(2,1)}, bf16[320,2048]{1,0:T(8,128)(2,1)S(1)}, u32[]{:S(2)}, u32[]{:S(2)}) collective-permute-start(bf16[320,2048]{1,0:T(8,128)(2,1)} %get-tuple-element.105), channel_id=1, source_target_pairs={{0,2},{1,3},{2,0},{3,1},{4,6},{5,7},{6,4},{7,5},{8,10},{9,11},{10,... | collective-permute-start | bytes 3932168 | tf_op jit(solution)/shard_map/ppermute | solution.py:986
  494.5 102.0 %collective-permute-start.19 = (bf16[320,2048]{1,0:T(8,128)(2,1)}, bf16[320,2048]{1,0:T(8,128)(2,1)}, u32[]{:S(2)}, u32[]{:S(2)}) collective-permute-start(bf16[320,2048]{1,0:T(8,128)(2,1)} %get-tuple-element.106), channel_id=1, source_target_pairs={{0,4},{1,5},{2,6},{3,7},{4,0},{5,1},{6,2},{7,3},{8,12},{9,13},{10,... | collective-permute-start | bytes 3932168 | tf_op jit(solution)/shard_map/ppermute | solution.py:986
  495.7 100.8 %collective-permute-start.20 = (bf16[320,2048]{1,0:T(8,128)(2,1)}, bf16[320,2048]{1,0:T(8,128)(2,1)}, u32[]{:S(2)}, u32[]{:S(2)}) collective-permute-start(bf16[320,2048]{1,0:T(8,128)(2,1)} %get-tuple-element.107), channel_id=1, source_target_pairs={{0,6},{1,7},{2,4},{3,5},{4,2},{5,3},{6,0},{7,1},{8,14},{9,15},{10,... | collective-permute-start | bytes 3932168 | tf_op jit(solution)/shard_map/ppermute | solution.py:986
  495.9 100.6 %copy-start.33 = (f32[320]{0:T(512)S(1)}, f32[320]{0:T(512)}, u32[]{:S(2)}) copy-start(f32[320]{0:T(512)} %copy-done.32) | copy-start | bytes 3844
  674.7 169.3 %copy-start.39 = (f32[2,64]{1,0:T(2,128)S(1)}, f32[2,64]{1,0:T(2,128)}, u32[]{:S(2)}) copy-start(f32[2,64]{1,0:T(2,128)} %param.20) | copy-start | bytes 1540
  674.7 171.4 %copy-start.2 = (bf16[1,1,320,2048]{3,2,1,0:T(8,128)(2,1)S(1)}, bf16[1,1,320,2048]{3,2,1,0:T(8,128)(2,1)}, u32[]{:S(2)}) copy-start(bf16[1,1,320,2048]{3,2,1,0:T(8,128)(2,1)} %param.16) | copy-start | bytes 3932164
  674.7 171.4 %copy-start.30 = (f32[2048]{0:T(1024)S(1)}, f32[2048]{0:T(1024)}, u32[]{:S(2)}) copy-start(f32[2048]{0:T(1024)} %get-tuple-element.224) | copy-start | bytes 24580
  (43 other events, 525.5 us)
Sparse Core Ops, SparseCore 0:
  162.1 145.5 all-gather.2
  309.2 79.2 all-gather.4
  391.4 77.8 reduce-scatter.4
  472.1 77.2 reduce-scatter.6
  552.1 77.2 reduce-scatter.8
  672.7 77.9 reduce-scatter.10

commit v7 on v6

--- a/solution.py
+++ b/solution.py
@@ -1387,7 +1387,7 @@
     for which in range(4):
         for slab in range(2):
             a_made_copy(which, slab).start()
-    gain_made[...] = owned(pl.ds(a_width + m_width, GAIN_PAD))
+    gain_made[...] = owned(pl.ds(a_width + m_width, GAIN_PAD)).T[:8]
     gain_copy = pltpu.make_async_copy(gain_made, gain_out, gain_sem.at[0])
     gain_copy.start()
     for turn in range(lines):
@@ -1430,7 +1430,7 @@
         functools.partial(finish_kernel, lines, plane),
         out_shape=(like(attention[0]),) * 4
         + (like(merge[0]),) * 4
-        + (jax.ShapeDtypeStruct((rows, GAIN_PAD), FULL),)
+        + (jax.ShapeDtypeStruct((8, rows), FULL),)
         + (like(forward[0]),) * 4,
         in_specs=[anywhere] * 16,
         out_specs=(anywhere,) * 13,
@@ -1444,7 +1444,7 @@
             vmem((2, 4, rows, own_hidden), FULL),
             vmem((3, rows, a_width + m_width), FULL),
             vmem((4, rows, a_width + m_width), FULL),
-            vmem((rows, GAIN_PAD), FULL),
+            vmem((8, rows), FULL),
             dma((lines, 4)),
             dma((lines, 4)),
             dma((lines, 4)),
@@ -1562,33 +1562,29 @@
     down_term = contract(down_grad, activated, 0, 0).astype(LOW)
     down_term, down_weight = lax.optimization_barrier((down_term, down_weight))
     out_term, gate_up_grad = forward_back(row_count, activated, down_grad, gate_up, down_weight)
+    down_part = line_scatter(down_term)
+    gate_term = contract(normed_all, gate_up_grad[:, :own_hidden], 0, 0).astype(LOW)
+    up_term = contract(normed_all, gate_up_grad[:, own_hidden:], 0, 0).astype(LOW)
+    gate_up_grad, gate_term, up_term, down_part = lax.optimization_barrier(
+        (gate_up_grad, gate_term, up_term, down_part)
+    )
+    gate_part = line_scatter(gate_term)
+    up_part = line_scatter(up_term)
+    normed_two_grad = plane_back(row_count, gate_up_grad, gate_weight)
+    normed_two_grad, out_term = lax.optimization_barrier((normed_two_grad, out_term))
     out_chunks = out_term.reshape(dp_size, row_count, D)
     out_swapped = [plane_swap(out_chunks[offset + 1], 1) for offset in range(0, dp_size, 2)]
-    down_part = line_scatter(down_term)
-    gate_term = contract(normed_all, gate_up_grad[:, :own_hidden], 0, 0).astype(LOW)
-    gate_term, out_swapped = lax.optimization_barrier((gate_term, out_swapped))
+    middle_grad = grad_rows + norm_back(middle, second_scale, gain_float[1], normed_two_grad)
+    gain_two_part = jnp.sum(normed_two_grad * middle * second_scale, axis=0)
+    branch_grad = middle_grad.astype(LOW)
+    attended_grad = contract(branch_grad, merge_weight, 1, 0).astype(LOW)
+    attended_grad, out_swapped = lax.optimization_barrier((attended_grad, out_swapped))
     out_sums = [
         out_chunks[2 * at].astype(FULL) + one.astype(FULL) for at, one in enumerate(out_swapped)
     ]
     out_low = [one.astype(LOW) for one in out_sums[1:]]
-    normed_all, out_low = lax.optimization_barrier((normed_all, out_low))
+    attended_grad, out_low = lax.optimization_barrier((attended_grad, out_low))
     out_arrived = [plane_swap(one, 2 * at + 2) for at, one in enumerate(out_low)]
-    up_term = contract(normed_all, gate_up_grad[:, own_hidden:], 0, 0).astype(LOW)
-    gate_term, down_part = lax.optimization_barrier((gate_term, down_part))
-    gate_part = line_scatter(gate_term)
-    gate_up_grad, up_term = lax.optimization_barrier((gate_up_grad, up_term))
-    normed_two_grad = plane_back(row_count, gate_up_grad, gate_weight)
-    normed_two_grad, out_arrived = lax.optimization_barrier((normed_two_grad, out_arrived))
-    result = middle + out_sums[0]
-    for one in out_arrived:
-        result = result + one.astype(FULL)
-    block_output = result.astype(LOW).reshape(hidden.shape)
-    middle_grad = grad_rows + norm_back(middle, second_scale, gain_float[1], normed_two_grad)
-    gain_two_part = jnp.sum(normed_two_grad * middle * second_scale, axis=0)
-    branch_grad = middle_grad.astype(LOW)
-    attended_grad = contract(branch_grad, merge_weight, 1, 0).astype(LOW)
-    attended_grad, gate_part = lax.optimization_barrier((attended_grad, gate_part))
-    up_part = line_scatter(up_term)
     query_project, pair_project = attend_back(
         place, queries, pairs, seen, row_logsum, attended_grad, cosine, sine_part
     )
@@ -1608,7 +1604,11 @@
     gain_term = jnp.pad(
         jnp.stack([gain_one_part[0], gain_two_part], axis=1), ((0, 0), (0, GAIN_PAD - 2))
     )
-    pair_back, up_part = lax.optimization_barrier((pair_back, up_part))
+    pair_back, up_part, out_arrived = lax.optimization_barrier((pair_back, up_part, out_arrived))
+    result = middle + out_sums[0]
+    for one in out_arrived:
+        result = result + one.astype(FULL)
+    block_output = result.astype(LOW).reshape(hidden.shape)
     pair_sum = line_scatter(pair_back)
     finished = finish(
         (query_term, pair_term, merge_term, gain_term.astype(LOW)),
@@ -1617,7 +1617,7 @@
         (merge_master, merge_first, merge_second),
         (feedforward_master, feedforward_first, feedforward_second),
     )
-    gain_grad = finished[8][:, :2].T
+    gain_grad = finished[8][:2]
     pair_sum, gain_grad = lax.optimization_barrier((pair_sum, gain_grad))
     pair_sum = pair_sum.astype(FULL)
     normed_grad = normed_grad + jnp.pad(pair_sum, ((0, CONT), (0, 0)))

time: 895 us -> 855 us (0.955)
  Pallas kernels: 559 us -> 522 us
    pallas_call x1, Pallas kernels: 101 us -> 62.7 us  [plane_back(): pl.pallas_call(functools.partial(plane_back_kernel, plane), out_shape=jax...]
    unnamed x127 -> x111, local copies, waits for them, and re-layouts: 49.3 us -> 44.4 us
  transfers between devices with their start and end apart: 27 -> 27, of which waited for: 4 -> 5; matrix products, arithmetic and copies ran while one was open for 16% -> 17% of each run, Pallas kernels for 46% -> 44%
where the time goes in v7:
time: 855 us; the launch traced here: 843 us
  Pallas kernels  522 us (61%)
  matrix products  89.7 us (10%)
  waiting for transfers between devices  75.5 us (9%)
  local copies, waits for them, and re-layouts  52.7 us (6%)
  starting transfers between devices  44.1 us (5%)
  other arithmetic  43.3 us (5%)
  between operations  15.8 us (2%)
    pallas_call x1, Pallas kernels, finish(): pl.pallas_call(functools.partial(finish_kernel, lines, plane), out_shape=...  168 us
    pallas_call x1, Pallas kernels, gather_start(): pl.pallas_call(functools.partial(gather_kernel, lines, plane, prompt_rows...  149 us
    dot_general x5, matrix products, contract(): lax.dot_general(left, right, (((left_axis,), (right_axis,)), ((), ())), p...  63 us
    pallas_call x1, Pallas kernels, plane_back(): pl.pallas_call(functools.partial(plane_back_kernel, plane), out_shape=jax...  62.7 us
    unnamed x111, local copies, waits for them, and re-layouts  44.4 us
    ppermute x21, starting transfers between devices, plane_swap(): return lax.ppermute(block, 'dp', [(i, i ^ offset) for i in range(size)])  43.2 us
    pallas_call x1, Pallas kernels, weights_back(): pl.pallas_call(weights_back_kernel, grid_spec=pltpu.PrefetchScalarGridSpe...  40.3 us
    pallas_call x1, Pallas kernels, forward_back(): pl.pallas_call(forward_back_kernel, grid=(count // rows,), in_specs=[bloc...  36.8 us
  transfers between devices with their start and end apart: 27, of which 5 were waited for; matrix products, arithmetic and copies ran while one was open for 17% of the time, Pallas kernels for 44%

profile of v7, /device:TPU:9, one launch (start us, length us, event | category | flops | bytes accessed | tf_op | source)
XLA Modules:
  0.0 843.3 jit_solution(7197524556193421771)
XLA Ops:
  10.4 4.8 convert_element_type.111.forward_ref
  16.1 148.6 %gather_start.1 = (bf16[4,8,64,6272]{3,2,1,0:T(8,128)(2,1)}, bf16[4,256,2048]{2,1,0:T(8,128)(2,1)}, bf16[8,64,2048]{2,1,0:T(8,128)(2,1)}, bf16[8,64,1024]{2,1,0:T(8,128)(2,1)}) custom-call(bf16[64,6272]{1,0:T(8,128)(2,1)} %fusion.30.weight_ref, bf16[320,2048]{1,0:T(8,128)(2,1)} %bitcast.52, bf16[64,24576]{1,0:T(8,128)(2,1)} %convert_element_type.111.forward_ref), custom_call_target="tpu_custom_call" | custom-call | tf_op jit(solution)/shard_map/gather_start/pallas_call | solution.py:371
  174.1 3.1 multiply_sine_fusion
  177.3 34.3 %project_heads.1 = (bf16[320,2048]{1,0:T(8,128)(2,1)}, bf16[1088,2048]{1,0:T(8,128)(2,1)}, bf16[1088,2048]{1,0:T(8,128)(2,1)}, bf16[320,2048]{1,0:T(8,128)(2,1)}, f32[1088,128]{1,0:T(8,128)}) custom-call(s32[1]{0:T(128)} %bitcast.1.place_ref, bf16[1024,2048]{1,0:T(8,128)(2,1)} %bitcast.55, bf16[320,2048]{1,0:T(8,128)(2,1)} %bitcast.53, ...), custom_call_target="tpu_custom_call" | custom-call | tf_op jit(solution)/shard_map/project_heads/pallas_call | solution.py:469
  213.4 11.4 %attend.1 = (bf16[320,2048]{1,0:T(8,128)(2,1)}, f32[320,1024]{1,0:T(8,128)}) custom-call(bf16[320,2048]{1,0:T(8,128)(2,1)} %get-tuple-element.85.query_ref, bf16[1088,2048]{1,0:T(8,128)(2,1)} %get-tuple-element.86.key_ref.value_ref, bf16[1088,2048]{1,0:T(8,128)(2,1)} %get-tuple-element.86.key_ref.value_ref, f32[320,1088]{1,0:T(8,128)} %add_convert_fusion.4.seen_ref), custom_call_target="tpu_custom_call" | custom-call | tf_op jit(solution)/shard_map/attend/pallas_call | solution.py:531
  224.8 5.9 multiply_reduce_fusion.2
  243.0 26.1 %collective-permute-done.8 = bf16[320,2048]{1,0:T(8,128)(2,1)S(1)} collective-permute-done((bf16[320,2048]{1,0:T(8,128)(2,1)S(1)}, bf16[320,2048]{1,0:T(8,128)(2,1)S(1)}, u32[]{:S(2)}, u32[]{:S(2)}) %collective-permute-start.8) | collective-permute-done | bytes 1310752 | tf_op jit(solution)/shard_map/ppermute | solution.py:986
  271.1 28.4 %collective-permute-start.11 = (bf16[320,2048]{1,0:T(8,128)(2,1)S(1)}, bf16[320,2048]{1,0:T(8,128)(2,1)S(1)}, u32[]{:S(2)}, u32[]{:S(2)}) collective-permute-start(bf16[320,2048]{1,0:T(8,128)(2,1)S(1)} %collective-permute-done.10), channel_id=1, source_target_pairs={{0,1},{1,0},{2,3},{3,2},{4,5},{5,4},{6,7},{7,6},{8,9},{9,8},{10,11... | collective-permute-start | bytes 3932168 | tf_op jit(solution)/shard_map/ppermute | solution.py:986
  310.7 26.7 %fusion.38.gate_up_ref = f32[2560,2048]{1,0:T(8,128)S(1)} fusion(bf16[2560,2048]{1,0:T(8,128)(2,1)} %constant_dynamic-update-slice_fusion.8, bf16[2048,2048]{1,0:T(8,128)(2,1)} %all-gather.3.cloned.1.call-done.weight_ref), kind=kOutput, calls=%fused_computation.95 | convolution fusion | flops 21474836480 | bytes 39845888 | tf_op jit(solution)/shard_map/dot_general | solution.py:1558
  337.4 3.6 fusion.activated_ref
  341.0 3.5 copy-done
  346.8 15.4 %convolution_convert_fusion = bf16[2048,1024]{1,0:T(8,128)(2,1)} fusion(bf16[2560,2048]{1,0:T(8,128)(2,1)} %copy-done.7, bf16[2560,1024]{1,0:T(8,128)(2,1)S(1)} %fusion.activated_ref), kind=kOutput, calls=%fused_computation.14 | convolution fusion | flops 10739515392 | bytes 19922944 | tf_op jit(solution)/shard_map/dot_general | solution.py:35
  362.2 29.0 %all-gather.5.cloned.1.call-done.down_ref = bf16[2048,1024]{1,0:T(8,128)(2,1)} async-done(((bf16[512,1024]{1,0:T(8,128)(2,1)}), bf16[2048,1024]{1,0:T(8,128)(2,1)}) %all-gather.5.cloned.1.call-update) | async-done | bytes 4194320 | tf_op jit(solution)/shard_map/all_gather | solution.py:1518
  391.8 36.8 %forward_back.1 = (bf16[2560,2048]{1,0:T(8,128)(2,1)}, bf16[2560,2048]{1,0:T(8,128)(2,1)}) custom-call(bf16[2560,1024]{1,0:T(8,128)(2,1)} %copy-done.6, bf16[2560,2048]{1,0:T(8,128)(2,1)} %copy-done.7, f32[2560,2048]{1,0:T(8,128)} %copy-done, bf16[2048,1024]{1,0:T(8,128)(2,1)} %all-gather.5.cloned.1.call-done.down_ref), custom_call_target="tpu_custom_call" | custom-call | tf_op jit(solution)/shard_map/forward_back/pallas_call | solution.py:765
  428.6 16.9 %fusion.12 = bf16[2048,1024]{1,0:T(8,128)(2,1)} fusion(bf16[2560,2048]{1,0:T(8,128)(2,1)} %constant_dynamic-update-slice_fusion.8, bf16[2560,2048]{1,0:T(8,128)(2,1)} %get-tuple-element.98), kind=kOutput, calls=%fused_computation.16 | convolution fusion | flops 10739515392 | bytes 19922944 | tf_op jit(solution)/shard_map/dot_general | solution.py:35
  445.5 16.8 %fusion.9 = bf16[2048,1024]{1,0:T(8,128)(2,1)} fusion(bf16[2560,2048]{1,0:T(8,128)(2,1)} %constant_dynamic-update-slice_fusion.8, bf16[2560,2048]{1,0:T(8,128)(2,1)} %get-tuple-element.98), kind=kOutput, calls=%fused_computation.15 | convolution fusion | flops 10739515392 | bytes 19922944 | tf_op jit(solution)/shard_map/dot_general | solution.py:35
  462.3 9.2 %reduce-scatter.5.cloned.1.call-done = bf16[512,1024]{1,0:T(8,128)(2,1)} async-done(((bf16[2048,1024]{1,0:T(8,128)(2,1)}), bf16[512,1024]{1,0:T(8,128)(2,1)}) %reduce-scatter.5.cloned.1.call-update) | async-done | bytes 1048592 | tf_op jit(solution)/shard_map/reduce_scatter | solution.py:996
  472.1 62.7 %plane_back.1 = f32[320,2048]{1,0:T(8,128)} custom-call(bf16[8,320,2048]{2,1,0:T(8,128)(2,1)} %bitcast.57, bf16[2048,2048]{1,0:T(8,128)(2,1)} %all-gather.3.cloned.1.call-done.weight_ref), custom_call_target="tpu_custom_call" | custom-call | tf_op jit(solution)/shard_map/plane_back/pallas_call | solution.py:956
  534.9 3.1 fusion.37
  543.3 7.9 fusion.17.grad_ref
  551.3 5.6 add_convert_fusion.1
  559.5 19.6 %attend_back.1 = (bf16[320,2048]{1,0:T(8,128)(2,1)}, bf16[1088,2048]{1,0:T(8,128)(2,1)}) custom-call(s32[1]{0:T(128)} %bitcast.1.place_ref, bf16[320,2048]{1,0:T(8,128)(2,1)} %get-tuple-element.85.query_ref, bf16[1088,2048]{1,0:T(8,128)(2,1)} %get-tuple-element.86.key_ref.value_ref, bf16[1088,2048]{1,0:T(8,128)(2,1)} %get-tuple-element.86.key_ref.value_ref, ...), custom_call_target="tpu_custom_call" | custom-call | tf_op jit(solution)/shard_map/attend_back/pallas_call | solution.py:610
  579.1 40.3 %weights_back.1 = (bf16[2048,2048]{1,0:T(8,128)(2,1)}, bf16[2048,2048]{1,0:T(8,128)(2,1)}, bf16[2048,2048]{1,0:T(8,128)(2,1)}, f32[320,2048]{1,0:T(8,128)}, bf16...) custom-call(s32[1]{0:T(128)} %bitcast.1.place_ref, bf16[320,2048]{1,0:T(8,128)(2,1)} %get-tuple-element.109.query_ref, ...), custom_call_target="tpu_custom_call" | custom-call | tf_op jit(solution)/shard_map/weights_back/pallas_call | solution.py:689
  621.4 9.6 %reduce-scatter.11.cloned.1.call-done = bf16[512,1024]{1,0:T(8,128)(2,1)} async-done(((bf16[2048,1024]{1,0:T(8,128)(2,1)}), bf16[512,1024]{1,0:T(8,128)(2,1)}) %reduce-scatter.11.cloned.1.call-update) | async-done | bytes 1048592 | tf_op jit(solution)/shard_map/reduce_scatter | solution.py:996
  631.0 168.4 %finish.1 = (f32[64,4096]{1,0:T(8,128)}, f32[64,4096]{1,0:T(8,128)}, f32[64,4096]{1,0:T(8,128)}, f32[64,4096]{1,0:T(8,128)}, f32[64,2048]{1,0:T(8,128)}, /*index...) custom-call(bf16[4,4,2,64,2048]{4,3,2,1,0:T(8,128)(2,1)} %bitcast.58, ...), custom_call_target="tpu_custom_call" | custom-call | tf_op jit(solution)/shard_map/finish/pallas_call | solution.py:1429
  800.1 5.5 fusion.27
  805.6 3.3 fusion.20
  809.6 4.2 fusion.24
  821.6 3.2 copy.78
  824.8 3.2 copy.79
  829.6 3.0 copy.80
  833.3 2.7 copy.81
  (203 shorter events, 64.6 us)
Async XLA Ops:
  7.2 303.2 %all-gather.3.cloned.1.call-start = ((), (), s32[]{:S(2)}) async-start(), calls=%async_computation.4 | async-start | bytes 10485760 | tf_op jit(solution)/shard_map/all_gather | solution.py:1514
  16.1 148.7 %copy-start.9 = (bf16[1,1,320,2048]{3,2,1,0:T(8,128)(2,1)S(1)}, bf16[1,1,320,2048]{3,2,1,0:T(8,128)(2,1)}, u32[]{:S(2)}) copy-start(bf16[1,1,320,2048]{3,2,1,0:T(8,128)(2,1)} %param.17) | copy-start | bytes 3932164
  164.7 226.6 %all-gather.5.cloned.1.call-start = ((), (), s32[]{:S(2)}) async-start(), calls=%async_computation.5 | async-start | bytes 5242880 | tf_op jit(solution)/shard_map/all_gather | solution.py:1518
  164.8 67.7 %collective-permute-start.5 = (bf16[320,2048]{1,0:T(8,128)(2,1)S(1)}, bf16[320,2048]{1,0:T(8,128)(2,1)}, u32[]{:S(2)}, u32[]{:S(2)}) collective-permute-start(bf16[320,2048]{1,0:T(8,128)(2,1)S(1)} %bitcast.69), channel_id=1, source_target_pairs={{0,6},{1,7},{2,4},{3,5},{4,2},{5,3},{6,0},{7,1},{8,14},{9,15},{10,... | collective-permute-start | bytes 3932168 | tf_op jit(solution)/shard_map/ppermute | solution.py:986
  166.0 65.9 %collective-permute-start.3 = (bf16[320,2048]{1,0:T(8,128)(2,1)S(1)}, bf16[320,2048]{1,0:T(8,128)(2,1)}, u32[]{:S(2)}, u32[]{:S(2)}) collective-permute-start(bf16[320,2048]{1,0:T(8,128)(2,1)S(1)} %bitcast.70), channel_id=1, source_target_pairs={{0,4},{1,5},{2,6},{3,7},{4,0},{5,1},{6,2},{7,3},{8,12},{9,13},{10,... | collective-permute-start | bytes 3932168 | tf_op jit(solution)/shard_map/ppermute | solution.py:986
  167.3 64.2 %collective-permute-start.1 = (bf16[320,2048]{1,0:T(8,128)(2,1)S(1)}, bf16[320,2048]{1,0:T(8,128)(2,1)}, u32[]{:S(2)}, u32[]{:S(2)}) collective-permute-start(bf16[320,2048]{1,0:T(8,128)(2,1)S(1)} %bitcast.71), channel_id=1, source_target_pairs={{0,2},{1,3},{2,0},{3,1},{4,6},{5,7},{6,4},{7,5},{8,10},{9,11},{10,... | collective-permute-start | bytes 3932168 | tf_op jit(solution)/shard_map/ppermute | solution.py:986
  167.5 65.2 %collective-permute-start = (bf16[320,2048]{1,0:T(8,128)(2,1)S(1)}, bf16[320,2048]{1,0:T(8,128)(2,1)}, u32[]{:S(2)}, u32[]{:S(2)}) collective-permute-start(bf16[320,2048]{1,0:T(8,128)(2,1)S(1)} %bitcast.72), channel_id=1, source_target_pairs={{0,1},{1,0},{2,3},{3,2},{4,5},{5,4},{6,7},{7,6},{8,9},{9,8},{10,11... | collective-permute-start | bytes 3932168 | tf_op jit(solution)/shard_map/ppermute | solution.py:986
  171.5 60.0 %copy-start.22 = (f32[2048]{0:T(1024)}, f32[2048]{0:T(1024)S(1)}, u32[]{:S(2)}) copy-start(f32[2048]{0:T(1024)S(1)} %get-tuple-element.151) | copy-start | bytes 24580
  213.4 11.4 %copy-start.3 = (bf16[1,1,320,2048]{3,2,1,0:T(8,128)(2,1)S(1)}, bf16[1,1,320,2048]{3,2,1,0:T(8,128)(2,1)}, u32[]{:S(2)}) copy-start(bf16[1,1,320,2048]{3,2,1,0:T(8,128)(2,1)} %param.16) | copy-start | bytes 3932164
  231.5 4.1 collective-permute-start.2
  231.8 5.4 collective-permute-start.4
  232.5 6.3 collective-permute-start.6
  239.0 68.1 %copy-start.7 = (bf16[2560,2048]{1,0:T(8,128)(2,1)}, bf16[2560,2048]{1,0:T(8,128)(2,1)S(1)}, u32[]{:S(2)}) copy-start(bf16[2560,2048]{1,0:T(8,128)(2,1)S(1)} %constant_dynamic-update-slice_fusion.grad_ref) | copy-start | bytes 31457284
  239.0 30.1 %collective-permute-start.8 = (bf16[320,2048]{1,0:T(8,128)(2,1)S(1)}, bf16[320,2048]{1,0:T(8,128)(2,1)S(1)}, u32[]{:S(2)}, u32[]{:S(2)}) collective-permute-start(bf16[320,2048]{1,0:T(8,128)(2,1)S(1)} %multiply_convert_fusion), channel_id=1, source_target_pairs={{0,2},{1,3},{2,0},{3,1},{4,6},{5,7},{6,4},{7,5},{8,10},{9,11},{10,... | collective-permute-start | bytes 3932168 | tf_op jit(solution)/shard_map/ppermute | solution.py:986
  240.3 30.8 %collective-permute-start.10 = (bf16[320,2048]{1,0:T(8,128)(2,1)S(1)}, bf16[320,2048]{1,0:T(8,128)(2,1)S(1)}, u32[]{:S(2)}, u32[]{:S(2)}) collective-permute-start(bf16[320,2048]{1,0:T(8,128)(2,1)S(1)} %multiply_convert_fusion), channel_id=1, source_target_pairs={{0,4},{1,5},{2,6},{3,7},{4,0},{5,1},{6,2},{7,3},{8,12},{9,13},{10,... | collective-permute-start | bytes 3932168 | tf_op jit(solution)/shard_map/ppermute | solution.py:986
  240.7 60.1 %collective-permute-start.12 = (bf16[320,2048]{1,0:T(8,128)(2,1)S(1)}, bf16[320,2048]{1,0:T(8,128)(2,1)S(1)}, u32[]{:S(2)}, u32[]{:S(2)}) collective-permute-start(bf16[320,2048]{1,0:T(8,128)(2,1)S(1)} %multiply_convert_fusion), channel_id=1, source_target_pairs={{0,6},{1,7},{2,4},{3,5},{4,2},{5,3},{6,0},{7,1},{8,14},{9,15},{10,... | collective-permute-start | bytes 3932168 | tf_op jit(solution)/shard_map/ppermute | solution.py:986
  241.7 59.1 %collective-permute-start.7 = (bf16[320,2048]{1,0:T(8,128)(2,1)S(1)}, bf16[320,2048]{1,0:T(8,128)(2,1)S(1)}, u32[]{:S(2)}, u32[]{:S(2)}) collective-permute-start(bf16[320,2048]{1,0:T(8,128)(2,1)S(1)} %multiply_convert_fusion), channel_id=1, source_target_pairs={{0,1},{1,0},{2,3},{3,2},{4,5},{5,4},{6,7},{7,6},{8,9},{9,8},{10,11... | collective-permute-start | bytes 3932168 | tf_op jit(solution)/shard_map/ppermute | solution.py:986
  269.1 34.2 %collective-permute-start.9 = (bf16[320,2048]{1,0:T(8,128)(2,1)S(1)}, bf16[320,2048]{1,0:T(8,128)(2,1)S(1)}, u32[]{:S(2)}, u32[]{:S(2)}) collective-permute-start(bf16[320,2048]{1,0:T(8,128)(2,1)S(1)} %collective-permute-done.8), channel_id=1, source_target_pairs={{0,1},{1,0},{2,3},{3,2},{4,5},{5,4},{6,7},{7,6},{8,9},{9,8},{10,11... | collective-permute-start | bytes 3932168 | tf_op jit(solution)/shard_map/ppermute | solution.py:986
  271.1 34.7 %collective-permute-start.11 = (bf16[320,2048]{1,0:T(8,128)(2,1)S(1)}, bf16[320,2048]{1,0:T(8,128)(2,1)S(1)}, u32[]{:S(2)}, u32[]{:S(2)}) collective-permute-start(bf16[320,2048]{1,0:T(8,128)(2,1)S(1)} %collective-permute-done.10), channel_id=1, source_target_pairs={{0,1},{1,0},{2,3},{3,2},{4,5},{5,4},{6,7},{7,6},{8,9},{9,8},{10,11... | collective-permute-start | bytes 3932168 | tf_op jit(solution)/shard_map/ppermute | solution.py:986
  300.9 7.4 collective-permute-start.13
  310.4 161.1 %reduce-scatter.5.cloned.1.call-start = ((), (), s32[]{:S(2)}) async-start(), calls=%async_computation.6 | async-start | bytes 5242880 | tf_op jit(solution)/shard_map/reduce_scatter | solution.py:996
  391.3 228.2 %reduce-scatter.7.cloned.1.call-start = ((), (), s32[]{:S(2)}) async-start(), calls=%async_computation.7 | async-start | bytes 5242880 | tf_op jit(solution)/shard_map/reduce_scatter | solution.py:996
  471.5 159.5 %reduce-scatter.11.cloned.1.call-start = ((), (), s32[]{:S(2)}) async-start(), calls=%async_computation.9 | async-start | bytes 5242880 | tf_op jit(solution)/shard_map/reduce_scatter | solution.py:996
  472.1 333.5 %reduce-scatter.9.cloned.1.call-start = ((), (), s32[]{:S(2)}) async-start(), calls=%async_computation.8 | async-start | bytes 5242880 | tf_op jit(solution)/shard_map/reduce_scatter | solution.py:996
  538.0 13.3 %collective-permute-start.17 = (bf16[320,2048]{1,0:T(8,128)(2,1)S(1)}, bf16[320,2048]{1,0:T(8,128)(2,1)S(1)}, u32[]{:S(2)}, u32[]{:S(2)}) collective-permute-start(bf16[320,2048]{1,0:T(8,128)(2,1)S(1)} %get-tuple-element.160), channel_id=1, source_target_pairs={{0,1},{1,0},{2,3},{3,2},{4,5},{5,4},{6,7},{7,6},{8,9},{9,8},{10,11... | collective-permute-start | bytes 3932168 | tf_op jit(solution)/shard_map/ppermute | solution.py:986
  539.1 12.2 %collective-permute-start.16 = (bf16[320,2048]{1,0:T(8,128)(2,1)S(1)}, bf16[320,2048]{1,0:T(8,128)(2,1)S(1)}, u32[]{:S(2)}, u32[]{:S(2)}) collective-permute-start(bf16[320,2048]{1,0:T(8,128)(2,1)S(1)} %get-tuple-element.161), channel_id=1, source_target_pairs={{0,1},{1,0},{2,3},{3,2},{4,5},{5,4},{6,7},{7,6},{8,9},{9,8},{10,11... | collective-permute-start | bytes 3932168 | tf_op jit(solution)/shard_map/ppermute | solution.py:986
  539.1 12.1 %collective-permute-start.15 = (bf16[320,2048]{1,0:T(8,128)(2,1)S(1)}, bf16[320,2048]{1,0:T(8,128)(2,1)S(1)}, u32[]{:S(2)}, u32[]{:S(2)}) collective-permute-start(bf16[320,2048]{1,0:T(8,128)(2,1)S(1)} %get-tuple-element.162), channel_id=1, source_target_pairs={{0,1},{1,0},{2,3},{3,2},{4,5},{5,4},{6,7},{7,6},{8,9},{9,8},{10,11... | collective-permute-start | bytes 3932168 | tf_op jit(solution)/shard_map/ppermute | solution.py:986
  539.6 11.7 %collective-permute-start.14 = (bf16[320,2048]{1,0:T(8,128)(2,1)S(1)}, bf16[320,2048]{1,0:T(8,128)(2,1)S(1)}, u32[]{:S(2)}, u32[]{:S(2)}) collective-permute-start(bf16[320,2048]{1,0:T(8,128)(2,1)S(1)} %get-tuple-element.163), channel_id=1, source_target_pairs={{0,1},{1,0},{2,3},{3,2},{4,5},{5,4},{6,7},{7,6},{8,9},{9,8},{10,11... | collective-permute-start | bytes 3932168 | tf_op jit(solution)/shard_map/ppermute | solution.py:986
  556.9 62.6 %collective-permute-start.18 = (bf16[320,2048]{1,0:T(8,128)(2,1)}, bf16[320,2048]{1,0:T(8,128)(2,1)}, u32[]{:S(2)}, u32[]{:S(2)}) collective-permute-start(bf16[320,2048]{1,0:T(8,128)(2,1)} %get-tuple-element.116), channel_id=1, source_target_pairs={{0,2},{1,3},{2,0},{3,1},{4,6},{5,7},{6,4},{7,5},{8,10},{9,11},{10,... | collective-permute-start | bytes 3932168 | tf_op jit(solution)/shard_map/ppermute | solution.py:986
  558.1 61.4 %collective-permute-start.19 = (bf16[320,2048]{1,0:T(8,128)(2,1)}, bf16[320,2048]{1,0:T(8,128)(2,1)}, u32[]{:S(2)}, u32[]{:S(2)}) collective-permute-start(bf16[320,2048]{1,0:T(8,128)(2,1)} %get-tuple-element.117), channel_id=1, source_target_pairs={{0,4},{1,5},{2,6},{3,7},{4,0},{5,1},{6,2},{7,3},{8,12},{9,13},{10,... | collective-permute-start | bytes 3932168 | tf_op jit(solution)/shard_map/ppermute | solution.py:986
  558.4 61.1 %collective-permute-start.20 = (bf16[320,2048]{1,0:T(8,128)(2,1)}, bf16[320,2048]{1,0:T(8,128)(2,1)}, u32[]{:S(2)}, u32[]{:S(2)}) collective-permute-start(bf16[320,2048]{1,0:T(8,128)(2,1)} %get-tuple-element.118), channel_id=1, source_target_pairs={{0,6},{1,7},{2,4},{3,5},{4,2},{5,3},{6,0},{7,1},{8,14},{9,15},{10,... | collective-permute-start | bytes 3932168 | tf_op jit(solution)/shard_map/ppermute | solution.py:986
  809.6 12.0 %slice-start.6 = ((s8[6291456]{0:T(1024)(128)(4,1)}), s8[4194304]{0:T(1024)(128)(4,1)S(1)}, s32[]{:S(2)}) async-start(s8[6291456]{0:T(1024)(128)(4,1)} %bitcast.67), calls=%async_computation.16 | async-start | bytes 8388608
  (37 other events, 149.2 us)
Sparse Core Ops, SparseCore 0:
  164.8 145.5 all-gather.2
  312.0 79.2 all-gather.4
  393.6 77.8 reduce-scatter.4
  473.7 77.2 reduce-scatter.6
  553.8 77.2 reduce-scatter.10
  633.9 77.2 reduce-scatter.8

commit v8 on v7

--- a/solution.py
+++ b/solution.py
@@ -125,12 +125,15 @@
     weights_ref,
     rows_ref,
     gate_ref,
-    down_ref,
+    first_ref,
+    second_ref,
     local_sem,
     line_send,
     line_recv,
     rows_send,
     rows_recv,
+    first_send,
+    first_recv,
     near_send,
     near_recv,
     half_send,
@@ -182,6 +185,16 @@
             (g + 1 if way == 0 else g - 1, d),
         )
 
+    def line_first(way, step):
+        block = g - step + 1 if way == 0 else g + step - 1
+        return copy(
+            first_ref.at[block],
+            first_ref.at[block],
+            first_send.at[way, step],
+            first_recv.at[way, step],
+            (g + 1 if way == 0 else g - 1, d),
+        )
+
     def sends(way, step):
         if way == 0:
             return (g < lines - 1) & (g >= step - 1)
@@ -220,13 +233,16 @@
             (g, flip(d, 1)),
         )
 
-    own_hidden = down_ref.shape[2]
+    half_hidden = second_ref.shape[2]
+    own_hidden = 2 * half_hidden
 
     def swap_piece(owner, part, source_index):
-        source = forward_ref.at[:, pl.ds(part * FF + owner * own_hidden, own_hidden)]
-        if part == 2:
-            return source, down_ref.at[source_index]
-        return source, gate_ref.at[source_index, :, pl.ds(part * own_hidden, own_hidden)]
+        if part < 2:
+            source = forward_ref.at[:, pl.ds(part * FF + owner * own_hidden, own_hidden)]
+            return source, gate_ref.at[source_index, :, pl.ds(part * own_hidden, own_hidden)]
+        start = 2 * FF + owner * own_hidden + (part - 2) * half_hidden
+        source = forward_ref.at[:, pl.ds(start, half_hidden)]
+        return source, first_ref.at[g, source_index] if part == 2 else second_ref.at[source_index]
 
     def swap_copy(offset, part):
         source, target = swap_piece(flip(d, offset), part, d)
@@ -243,7 +259,7 @@
         pltpu.make_async_copy(own_rows, rows_ref.at[g], local_sem.at[1]),
         *(
             pltpu.make_async_copy(*swap_piece(d, part, d), local_sem.at[2 + part])
-            for part in range(3)
+            for part in range(4)
         ),
     )
 
@@ -307,15 +323,34 @@
         if step == 1:
             relay(g)
             for offset in range(1, plane):
-                for part in range(3):
+                for part in (2, 0, 1, 3):
                     swap_copy(offset, part).start()
     for step in range(1, lines):
         take_rows(step)
+        if step == lines - 1:
+            locals_[4].wait()
+            for offset in range(1, plane):
+                swap_copy(offset, 2).wait_recv()
+            for way in (0, 1):
+                pl.when(sends(way, 1))(lambda way=way: line_first(way, 1).start())
         both(step, relay)
         if step == 1:
             finish(g)
-        else:
+        elif step < lines - 1:
             both(step - 1, finish)
+    for step in range(1, lines):
+        for way in (0, 1):
+
+            @pl.when(receives(way, step))
+            def _(way=way, step=step):
+                line_first(way, step).wait_recv()
+
+            if step + 1 < lines:
+                pl.when(sends(way, step + 1))(
+                    lambda way=way, step=step: line_first(way, step + 1).start()
+                )
+        if step == 1:
+            both(lines - 2, finish)
     both(lines - 1, finish)
 
     def drain(block):
@@ -338,12 +373,15 @@
             def _(way=way, step=step):
                 line_weight(way, step).wait_send()
                 line_rows(way, step).wait_send()
+                line_first(way, step).wait_send()
 
     for offset in range(1, plane):
-        for part in range(3):
+        for part in (0, 1, 3):
             swap_copy(offset, part).wait()
-    for one in locals_:
-        one.wait()
+        swap_copy(offset, 2).wait_send()
+    for at, one in enumerate(locals_):
+        if at != 4:
+            one.wait()
 
 
 def gather_start(weight, hidden, forward):
@@ -358,14 +396,16 @@
         (2, lines),
         (2, lines),
         (2, lines),
+        (2, lines),
+        (2, lines),
         (lines, near_count),
         (lines, near_count),
         (lines, 2),
         (lines, 2),
         (lines, plane // 2),
         (lines, plane // 2),
-        (plane, 3),
-        (plane, 3),
+        (plane, 4),
+        (plane, 4),
     )
     own_hidden = FF // plane
     return pl.pallas_call(
@@ -374,11 +414,12 @@
             jax.ShapeDtypeStruct((lines, plane, own_rows, width), weight.dtype),
             jax.ShapeDtypeStruct((lines, prompt_rows, D), hidden.dtype),
             jax.ShapeDtypeStruct((plane, own_rows, 2 * own_hidden), forward.dtype),
-            jax.ShapeDtypeStruct((plane, own_rows, own_hidden), forward.dtype),
+            jax.ShapeDtypeStruct((lines, plane, own_rows, own_hidden // 2), forward.dtype),
+            jax.ShapeDtypeStruct((plane, own_rows, own_hidden // 2), forward.dtype),
         ),
         in_specs=[anywhere] * 3,
-        out_specs=(anywhere,) * 4,
-        scratch_shapes=[dma((5,))] + [dma(shape) for shape in pairs],
+        out_specs=(anywhere,) * 5,
+        scratch_shapes=[dma((6,))] + [dma(shape) for shape in pairs],
         compiler_params=pltpu.CompilerParams(collective_id=0, has_side_effects=True),
         name="gather_start",
     )(weight, hidden, forward)
@@ -733,23 +774,24 @@
 
 
 def forward_back_kernel(
-    activated_ref, grad_ref, gate_up_ref, down_ref, out_ref, gate_up_grad_ref
+    activated_ref, grad_ref, gate_up_ref, first_ref, second_ref, out_ref, gate_up_grad_ref
 ):
     own_hidden = activated_ref.shape[1]
-    part = down_ref.shape[0] // 4
+    part = first_ref.shape[0] // 4
+    piece = own_hidden // 2
 
     @pl.loop(0, 4)
     def _(at):
         columns = pl.ds(pl.multiple_of(at * part, part), part)
-        out_ref[:, columns] = across(activated_ref[...], down_ref[columns]).astype(LOW)
-
-    piece = own_hidden // 2
-    for at in range(2):
+        out_ref[:, columns] = (
+            across(activated_ref[:, :piece], first_ref[columns])
+            + across(activated_ref[:, piece:], second_ref[columns])
+        ).astype(LOW)
+
+    for at, down_ref in enumerate((first_ref, second_ref)):
         columns = slice(at * piece, (at + 1) * piece)
         upper = slice(own_hidden + at * piece, own_hidden + (at + 1) * piece)
-        activated_grad = jnp.dot(
-            grad_ref[...], down_ref[:, columns], preferred_element_type=FULL
-        )
+        activated_grad = jnp.dot(grad_ref[...], down_ref[...], preferred_element_type=FULL)
         gate_values, up_values = gate_up_ref[:, columns], gate_up_ref[:, upper]
         gate_sigmoid = jax.nn.sigmoid(gate_values)
         gate_grad, up_grad = gate_backward(
@@ -759,7 +801,7 @@
         gate_up_grad_ref[:, upper] = up_grad
 
 
-def forward_back(rows, activated, grads, gate_up, down_weight):
+def forward_back(rows, activated, grads, gate_up, first_down, second_down):
     count, own_hidden = activated.shape
     block = lambda width: pl.BlockSpec((rows, width), lambda j: (j, 0))
     return pl.pallas_call(
@@ -769,7 +811,8 @@
             block(own_hidden),
             block(D),
             block(2 * own_hidden),
-            pl.BlockSpec(down_weight.shape, lambda j: (0, 0)),
+            pl.BlockSpec(first_down.shape, lambda j: (0, 0)),
+            pl.BlockSpec(second_down.shape, lambda j: (0, 0)),
         ],
         out_specs=[block(D), block(2 * own_hidden)],
         out_shape=[
@@ -778,14 +821,16 @@
         ],
         compiler_params=pltpu.CompilerParams(vmem_limit_bytes=VMEM_LIMIT),
         name="forward_back",
-    )(activated, grads, gate_up, down_weight)
+    )(activated, grads, gate_up, first_down, second_down)
 
 
 def plane_back_kernel(
     plane,
     rows_ref,
     weight_ref,
+    down_ref,
     out_ref,
+    swapped_ref,
     weight,
     tiles,
     keep,
@@ -800,6 +845,8 @@
     plane_send,
     plane_recv,
     out_sem,
+    swap_send,
+    swap_recv,
 ):
     g = lax.axis_index("grp")
     d = lax.axis_index("dp")
@@ -858,9 +905,23 @@
             (g, flip(d, 2 * there)),
         )
 
+    def swap_copy(offset):
+        there = flip(d, offset)
+        return remote(
+            down_ref.at[there],
+            swapped_ref.at[d],
+            swap_send.at[offset],
+            swap_recv.at[offset],
+            (g, there),
+        )
+
+    own_swap = pltpu.make_async_copy(down_ref.at[d], swapped_ref.at[d], out_sem.at[1])
     tile_copy(0).start()
     tile_copy(1).start()
     pl.semaphore_wait(barrier, plane - 1)
+    for offset in range(1, plane):
+        swap_copy(offset).start()
+    own_swap.start()
     load.wait()
     part_width = 512
 
@@ -944,10 +1005,13 @@
     else:
         for at in range(1, chips):
             plane_copy(at).wait_send()
+    for offset in range(1, plane):
+        swap_copy(offset).wait()
+    own_swap.wait()
     out.wait()
 
 
-def plane_back(rows, gate_up_grad, gate_weight):
+def plane_back(rows, gate_up_grad, gate_weight, down_part):
     plane = lax.axis_size("dp")
     chips = plane // 2
     inner = gate_up_grad.shape[1]
@@ -955,9 +1019,12 @@
     dma = pltpu.SemaphoreType.DMA
     return pl.pallas_call(
         functools.partial(plane_back_kernel, plane),
-        out_shape=jax.ShapeDtypeStruct((rows, D), FULL),
-        in_specs=[anywhere] * 2,
-        out_specs=anywhere,
+        out_shape=(
+            jax.ShapeDtypeStruct((rows, D), FULL),
+            jax.ShapeDtypeStruct(down_part.shape, LOW),
+        ),
+        in_specs=[anywhere] * 3,
+        out_specs=(anywhere,) * 2,
         scratch_shapes=[
             pltpu.VMEM((D, inner), LOW),
             pltpu.VMEM((2, 2, rows, inner), LOW),
@@ -972,13 +1039,15 @@
             dma((chips,)),
             dma((max(6, chips),)),
             dma((max(6, chips),)),
-            dma((1,)),
+            dma((2,)),
+            dma((plane,)),
+            dma((plane,)),
         ],
         compiler_params=pltpu.CompilerParams(
             collective_id=2, has_side_effects=True, vmem_limit_bytes=VMEM_LIMIT
         ),
         name="plane_back",
-    )(gate_up_grad.reshape(plane, rows, inner), gate_weight)
+    )(gate_up_grad.reshape(plane, rows, inner), gate_weight, down_part)
 
 
 def plane_swap(block, offset):
@@ -1158,8 +1227,8 @@
 
     own_swap = [
         pltpu.make_async_copy(forward_refs[part].at[d], swap_in.at[part, d], own_sem.at[part])
-        for part in range(3)
-    ]
+        for part in range(2)
+    ] + [pltpu.make_async_copy(down_ref, swap_in.at[2], own_sem.at[2])]
 
     def f_columns(turn):
         block = lax.rem(d + lax.div(turn, 3), plane)
@@ -1208,7 +1277,7 @@
                 mine_copy(turn, part).start()
         if turn == 0:
             for step in range(1, plane):
-                for part in range(3):
+                for part in range(2):
                     swap_copy(step, part).start()
             for one in own_swap:
                 one.start()
@@ -1346,7 +1415,7 @@
             for one in own_swap:
                 one.wait()
             for step in range(1, plane):
-                for part in range(3):
+                for part in range(2):
                     swap_copy(step, part).wait_recv()
         near_done(turn)
         line_done(turn - 1)
@@ -1404,7 +1473,7 @@
         if turn < lines - 1:
             line_copy(turn).wait_send()
     for step in range(1, plane):
-        for part in range(3):
+        for part in range(2):
             swap_copy(step, part).wait_send()
     for which in range(4):
         for slab in range(2):
@@ -1417,7 +1486,7 @@
     chips = plane // 2
     rows, a_width = attention[0].shape
     m_width = merge[0].shape[1]
-    own_hidden = forward_parts[0].shape[1]
+    own_hidden = forward_parts[0].shape[-1]
     width = a_width + m_width + GAIN_PAD
     anywhere = pl.BlockSpec(memory_space=pl.ANY)
     dma = pltpu.SemaphoreType.DMA
@@ -1452,8 +1521,8 @@
             dma((lines, max(6, chips))),
             dma((lines,)),
             dma((lines,)),
-            dma((plane, 3)),
-            dma((plane, 3)),
+            dma((plane, 2)),
+            dma((plane, 2)),
             dma((3,)),
             dma((2, 3)),
             dma((2, 4)),
@@ -1466,7 +1535,7 @@
         name="finish",
     )(
         *(term.reshape(lines, chips, 2, rows, term.shape[1]) for term in terms),
-        *(part.reshape(plane, rows, -1) for part in forward_parts),
+        *(part.reshape(plane, rows, own_hidden) for part in forward_parts),
         *attention,
         *merge,
         *forward,
@@ -1504,7 +1573,7 @@
     weight_low = jnp.concatenate(
         [attention_master.astype(LOW), merge_master.astype(LOW), gain_columns.astype(LOW)], axis=1
     )
-    weights, group_rows, gate_rows, down_rows = gather_start(
+    weights, group_rows, gate_rows, first_rows, second_rows = gather_start(
         weight_low, own_inputs, feedforward_master.astype(LOW)
     )
     weights, late_cotangent = lax.optimization_barrier((weights, cotangent))
@@ -1514,9 +1583,10 @@
     gate_weight = lax.all_gather(
         gate_rows.reshape(dp_size * own_rows, 2 * own_hidden), "grp", axis=0, tiled=True
     )
-    gate_weight, down_rows = lax.optimization_barrier((gate_weight, down_rows))
-    down_weight = lax.all_gather(
-        down_rows.reshape(dp_size * own_rows, own_hidden), "grp", axis=0, tiled=True
+    gate_weight, second_rows = lax.optimization_barrier((gate_weight, second_rows))
+    first_down = first_rows.reshape(D, own_hidden // 2)
+    second_down = lax.all_gather(
+        second_rows.reshape(dp_size * own_rows, own_hidden // 2), "grp", axis=0, tiled=True
     )
     down_grad = plane_gather(late_cotangent.reshape(row_count, D))
 
@@ -1560,8 +1630,10 @@
     up_values = gate_up[:, own_hidden:]
     gate_sigmoid, gate_silu, activated = gate_parts(gate_values, up_values)
     down_term = contract(down_grad, activated, 0, 0).astype(LOW)
-    down_term, down_weight = lax.optimization_barrier((down_term, down_weight))
-    out_term, gate_up_grad = forward_back(row_count, activated, down_grad, gate_up, down_weight)
+    down_term, second_down = lax.optimization_barrier((down_term, second_down))
+    out_term, gate_up_grad = forward_back(
+        row_count, activated, down_grad, gate_up, first_down, second_down
+    )
     down_part = line_scatter(down_term)
     gate_term = contract(normed_all, gate_up_grad[:, :own_hidden], 0, 0).astype(LOW)
     up_term = contract(normed_all, gate_up_grad[:, own_hidden:], 0, 0).astype(LOW)
@@ -1570,7 +1642,9 @@
     )
     gate_part = line_scatter(gate_term)
     up_part = line_scatter(up_term)
-    normed_two_grad = plane_back(row_count, gate_up_grad, gate_weight)
+    normed_two_grad, down_swapped = plane_back(
+        row_count, gate_up_grad, gate_weight, down_part.reshape(dp_size, own_rows, own_hidden)
+    )
     normed_two_grad, out_term = lax.optimization_barrier((normed_two_grad, out_term))
     out_chunks = out_term.reshape(dp_size, row_count, D)
     out_swapped = [plane_swap(out_chunks[offset + 1], 1) for offset in range(0, dp_size, 2)]
@@ -1608,11 +1682,12 @@
     result = middle + out_sums[0]
     for one in out_arrived:
         result = result + one.astype(FULL)
-    block_output = result.astype(LOW).reshape(hidden.shape)
+    block_output, query_term = lax.optimization_barrier((result.astype(LOW), query_term))
+    block_output = block_output.reshape(hidden.shape)
     pair_sum = line_scatter(pair_back)
     finished = finish(
         (query_term, pair_term, merge_term, gain_term.astype(LOW)),
-        (gate_part, up_part, down_part),
+        (gate_part, up_part, down_swapped),
         (attention_master, attention_first, attention_second),
         (merge_master, merge_first, merge_second),
         (feedforward_master, feedforward_first, feedforward_second),

time: 855 us -> 833 us (0.974)
  waiting for transfers between devices: 75.5 us -> 42.1 us
    all_gather x1, waiting for transfers between devices: 29 us -> 0.01 us  [body(): lax.all_gather(second_rows.reshape(dp_size * own_rows, own_hidden // 2),...]
    pallas_call x1, Pallas kernels: 149 us -> 168 us  [gather_start(): pl.pallas_call(functools.partial(gather_kernel, lines, plane, prompt_rows...]
    pallas_call x1, Pallas kernels: 168 us -> 157 us  [finish(): pl.pallas_call(functools.partial(finish_kernel, lines, plane), out_shape=...]
  transfers between devices with their start and end apart: 27 -> 27, of which waited for: 5 -> 4; matrix products, arithmetic and copies ran while one was open for 17% -> 17% of each run, Pallas kernels for 44% -> 44%
where the time goes in v8:
time: 833 us; the launch traced here: 821 us
  Pallas kernels  530 us (64%)
  matrix products  89.6 us (11%)
  local copies, waits for them, and re-layouts  52.7 us (6%)
  starting transfers between devices  47.5 us (6%)
  other arithmetic  42.9 us (5%)
  waiting for transfers between devices  42.1 us (5%)
  between operations  15.8 us (2%)
    pallas_call x1, Pallas kernels, gather_start(): pl.pallas_call(functools.partial(gather_kernel, lines, plane, prompt_rows...  168 us
    pallas_call x1, Pallas kernels, finish(): pl.pallas_call(functools.partial(finish_kernel, lines, plane), out_shape=...  157 us
    dot_general x5, matrix products, contract(): lax.dot_general(left, right, (((left_axis,), (right_axis,)), ((), ())), p...  62.9 us
    pallas_call x1, Pallas kernels, plane_back(): pl.pallas_call(functools.partial(plane_back_kernel, plane), out_shape=(ja...  62.8 us
    ppermute x21, starting transfers between devices, plane_swap(): return lax.ppermute(block, 'dp', [(i, i ^ offset) for i in range(size)])  46.7 us
    unnamed x111, local copies, waits for them, and re-layouts  44.4 us
    pallas_call x1, Pallas kernels, weights_back(): pl.pallas_call(weights_back_kernel, grid_spec=pltpu.PrefetchScalarGridSpe...  40.3 us
    pallas_call x1, Pallas kernels, forward_back(): pl.pallas_call(forward_back_kernel, grid=(count // rows,), in_specs=[bloc...  36.6 us
  transfers between devices with their start and end apart: 27, of which 4 were waited for; matrix products, arithmetic and copies ran while one was open for 17% of the time, Pallas kernels for 44%

profile of v8, /device:TPU:9, one launch (start us, length us, event | category | flops | bytes accessed | tf_op | source)
XLA Modules:
  0.0 821.1 jit_solution(10791288781715809741)
XLA Ops:
  10.4 4.8 convert_element_type.111.forward_ref
  16.1 168.2 %gather_start.1 = (bf16[4,8,64,6272]{3,2,1,0:T(8,128)(2,1)}, bf16[4,256,2048]{2,1,0:T(8,128)(2,1)}, bf16[8,64,2048]{2,1,0:T(8,128)(2,1)}, bf16[4,8,64,512]{3,2,1,0:T(8,128)(2,1)}, bf16[8,64,512]{2,1,0:T(8,128)(2,1)}) custom-call(bf16[64,6272]{1,0:T(8,128)(2,1)} %fusion.29.weight_ref, bf16[320,2048]{1,0:T(8,128)(2,1)} %bitcast.52, ...), custom_call_target="tpu_custom_call" | custom-call | tf_op jit(solution)/shard_map/gather_start/pallas_call | solution.py:411
  187.1 4.4 collective-permute-start
  197.2 3.1 multiply_sine_fusion
  200.3 34.9 %project_heads.1 = (bf16[320,2048]{1,0:T(8,128)(2,1)}, bf16[1088,2048]{1,0:T(8,128)(2,1)}, bf16[1088,2048]{1,0:T(8,128)(2,1)}, bf16[320,2048]{1,0:T(8,128)(2,1)}, f32[1088,128]{1,0:T(8,128)}) custom-call(s32[1]{0:T(128)} %bitcast.1.place_ref, bf16[1024,2048]{1,0:T(8,128)(2,1)} %bitcast.55, bf16[320,2048]{1,0:T(8,128)(2,1)} %bitcast.53, ...), custom_call_target="tpu_custom_call" | custom-call | tf_op jit(solution)/shard_map/project_heads/pallas_call | solution.py:510
  237.1 11.4 %attend.1 = (bf16[320,2048]{1,0:T(8,128)(2,1)}, f32[320,1024]{1,0:T(8,128)}) custom-call(bf16[320,2048]{1,0:T(8,128)(2,1)} %get-tuple-element.90.query_ref, bf16[1088,2048]{1,0:T(8,128)(2,1)} %get-tuple-element.91.key_ref.value_ref, bf16[1088,2048]{1,0:T(8,128)(2,1)} %get-tuple-element.91.key_ref.value_ref, f32[320,1088]{1,0:T(8,128)} %add_convert_fusion.4.seen_ref), custom_call_target="tpu_custom_call" | custom-call | tf_op jit(solution)/shard_map/attend/pallas_call | solution.py:572
  248.5 6.0 multiply_reduce_fusion.2
  266.7 25.9 %collective-permute-done.8 = bf16[320,2048]{1,0:T(8,128)(2,1)S(1)} collective-permute-done((bf16[320,2048]{1,0:T(8,128)(2,1)S(1)}, bf16[320,2048]{1,0:T(8,128)(2,1)S(1)}, u32[]{:S(2)}, u32[]{:S(2)}) %collective-permute-start.8) | collective-permute-done | bytes 1310752 | tf_op jit(solution)/shard_map/ppermute | solution.py:1055
  294.9 28.2 %collective-permute-start.11 = (bf16[320,2048]{1,0:T(8,128)(2,1)S(1)}, bf16[320,2048]{1,0:T(8,128)(2,1)S(1)}, u32[]{:S(2)}, u32[]{:S(2)}) collective-permute-start(bf16[320,2048]{1,0:T(8,128)(2,1)S(1)} %collective-permute-done.10), channel_id=1, source_target_pairs={{0,1},{1,0},{2,3},{3,2},{4,5},{5,4},{6,7},{7,6},{8,9},{9,8},{10,11... | collective-permute-start | bytes 3932168 | tf_op jit(solution)/shard_map/ppermute | solution.py:1055
  333.0 4.3 all-gather.3.cloned.1.call-done.weight_ref
  337.6 26.7 %fusion.37.gate_up_ref = f32[2560,2048]{1,0:T(8,128)S(1)} fusion(bf16[2560,2048]{1,0:T(8,128)(2,1)} %constant_dynamic-update-slice_fusion.8, bf16[2048,2048]{1,0:T(8,128)(2,1)} %all-gather.3.cloned.1.call-done.weight_ref), kind=kOutput, calls=%fused_computation.94 | convolution fusion | flops 21474836480 | bytes 39845888 | tf_op jit(solution)/shard_map/dot_general | solution.py:1628
  364.3 3.6 fusion.activated_ref
  367.9 3.5 copy-done
  373.8 15.4 %convolution_convert_fusion = bf16[2048,1024]{1,0:T(8,128)(2,1)} fusion(bf16[2560,2048]{1,0:T(8,128)(2,1)} %copy-done.6, bf16[2560,1024]{1,0:T(8,128)(2,1)S(1)} %fusion.activated_ref), kind=kOutput, calls=%fused_computation.14 | convolution fusion | flops 10739515392 | bytes 19922944 | tf_op jit(solution)/shard_map/dot_general | solution.py:35
  389.7 36.6 %forward_back.1 = (bf16[2560,2048]{1,0:T(8,128)(2,1)}, bf16[2560,2048]{1,0:T(8,128)(2,1)}) custom-call(bf16[2560,1024]{1,0:T(8,128)(2,1)} %copy-done.5, bf16[2560,2048]{1,0:T(8,128)(2,1)} %copy-done.6, f32[2560,2048]{1,0:T(8,128)} %copy-done, bf16[2048,512]{1,0:T(8,128)(2,1)} %bitcast.74, bf16[2048,512]{1,0:T(8,128)(2,1)} %all-gather.5.cloned.1.call-done.second_ref), custom_call_target="tpu_custom_call" | custom-call | tf_op jit(solution)/shard_map/forward_back/pallas_call | solution.py:807
  426.2 16.8 %fusion.12 = bf16[2048,1024]{1,0:T(8,128)(2,1)} fusion(bf16[2560,2048]{1,0:T(8,128)(2,1)} %constant_dynamic-update-slice_fusion.8, bf16[2560,2048]{1,0:T(8,128)(2,1)} %get-tuple-element.104), kind=kOutput, calls=%fused_computation.16 | convolution fusion | flops 10739515392 | bytes 19922944 | tf_op jit(solution)/shard_map/dot_general | solution.py:35
  443.0 16.8 %fusion.9 = bf16[2048,1024]{1,0:T(8,128)(2,1)} fusion(bf16[2560,2048]{1,0:T(8,128)(2,1)} %constant_dynamic-update-slice_fusion.8, bf16[2560,2048]{1,0:T(8,128)(2,1)} %get-tuple-element.104), kind=kOutput, calls=%fused_computation.15 | convolution fusion | flops 10739515392 | bytes 19922944 | tf_op jit(solution)/shard_map/dot_general | solution.py:35
  459.8 7.4 reduce-scatter.5.cloned.1.call-done
  467.9 62.8 %plane_back.1 = (f32[320,2048]{1,0:T(8,128)}, bf16[8,64,1024]{2,1,0:T(8,128)(2,1)}) custom-call(bf16[8,320,2048]{2,1,0:T(8,128)(2,1)} %bitcast.57, bf16[2048,2048]{1,0:T(8,128)(2,1)} %all-gather.3.cloned.1.call-done.weight_ref, bf16[8,64,1024]{2,1,0:T(8,128)(2,1)} %bitcast.79), custom_call_target="tpu_custom_call" | custom-call | tf_op jit(solution)/shard_map/plane_back/pallas_call | solution.py:1020
  530.7 3.1 fusion.36
  539.1 7.9 fusion.17.grad_ref
  547.1 5.6 add_convert_fusion.1
  555.4 19.3 %attend_back.1 = (bf16[320,2048]{1,0:T(8,128)(2,1)}, bf16[1088,2048]{1,0:T(8,128)(2,1)}) custom-call(s32[1]{0:T(128)} %bitcast.1.place_ref, bf16[320,2048]{1,0:T(8,128)(2,1)} %get-tuple-element.90.query_ref, bf16[1088,2048]{1,0:T(8,128)(2,1)} %get-tuple-element.91.key_ref.value_ref, bf16[1088,2048]{1,0:T(8,128)(2,1)} %get-tuple-element.91.key_ref.value_ref, ...), custom_call_target="tpu_custom_call" | custom-call | tf_op jit(solution)/shard_map/attend_back/pallas_call | solution.py:651
  574.7 40.3 %weights_back.1 = (bf16[2048,2048]{1,0:T(8,128)(2,1)}, bf16[2048,2048]{1,0:T(8,128)(2,1)}, bf16[2048,2048]{1,0:T(8,128)(2,1)}, f32[320,2048]{1,0:T(8,128)}, bf16...) custom-call(s32[1]{0:T(128)} %bitcast.1.place_ref, bf16[320,2048]{1,0:T(8,128)(2,1)} %get-tuple-element.117.query_ref, ...), custom_call_target="tpu_custom_call" | custom-call | tf_op jit(solution)/shard_map/weights_back/pallas_call | solution.py:730
  617.0 5.4 add_convert_fusion
  622.4 3.8 reduce-scatter.11.cloned.1.call-done
  626.2 156.9 %finish.1 = (f32[64,4096]{1,0:T(8,128)}, f32[64,4096]{1,0:T(8,128)}, f32[64,4096]{1,0:T(8,128)}, f32[64,4096]{1,0:T(8,128)}, f32[64,2048]{1,0:T(8,128)}, /*index...) custom-call(bf16[4,4,2,64,2048]{4,3,2,1,0:T(8,128)(2,1)} %bitcast.58, ...), custom_call_target="tpu_custom_call" | custom-call | tf_op jit(solution)/shard_map/finish/pallas_call | solution.py:1498
  783.9 2.9 fusion.20
  787.4 4.2 fusion.24
  799.4 3.2 copy.78
  802.6 3.2 copy.79
  807.4 3.0 copy.80
  (203 shorter events, 65.6 us)
Async XLA Ops:
  7.2 330.1 %all-gather.3.cloned.1.call-start = ((), (), s32[]{:S(2)}) async-start(), calls=%async_computation.4 | async-start | bytes 10485760 | tf_op jit(solution)/shard_map/all_gather | solution.py:1583
  16.1 168.3 %copy-start.9 = (bf16[1,1,320,2048]{3,2,1,0:T(8,128)(2,1)S(1)}, bf16[1,1,320,2048]{3,2,1,0:T(8,128)(2,1)}, u32[]{:S(2)}) copy-start(bf16[1,1,320,2048]{3,2,1,0:T(8,128)(2,1)} %param.17) | copy-start | bytes 3932164
  184.3 204.8 %all-gather.5.cloned.1.call-start = ((), (), s32[]{:S(2)}) async-start(), calls=%async_computation.5 | async-start | bytes 2621440 | tf_op jit(solution)/shard_map/all_gather | solution.py:1588
  184.4 71.8 %collective-permute-start.5 = (bf16[320,2048]{1,0:T(8,128)(2,1)S(1)}, bf16[320,2048]{1,0:T(8,128)(2,1)}, u32[]{:S(2)}, u32[]{:S(2)}) collective-permute-start(bf16[320,2048]{1,0:T(8,128)(2,1)S(1)} %bitcast.69), channel_id=1, source_target_pairs={{0,6},{1,7},{2,4},{3,5},{4,2},{5,3},{6,0},{7,1},{8,14},{9,15},{10,... | collective-permute-start | bytes 3932168 | tf_op jit(solution)/shard_map/ppermute | solution.py:1055
  185.9 69.6 %collective-permute-start.3 = (bf16[320,2048]{1,0:T(8,128)(2,1)S(1)}, bf16[320,2048]{1,0:T(8,128)(2,1)}, u32[]{:S(2)}, u32[]{:S(2)}) collective-permute-start(bf16[320,2048]{1,0:T(8,128)(2,1)S(1)} %bitcast.70), channel_id=1, source_target_pairs={{0,4},{1,5},{2,6},{3,7},{4,0},{5,1},{6,2},{7,3},{8,12},{9,13},{10,... | collective-permute-start | bytes 3932168 | tf_op jit(solution)/shard_map/ppermute | solution.py:1055
  186.4 68.7 %collective-permute-start.1 = (bf16[320,2048]{1,0:T(8,128)(2,1)S(1)}, bf16[320,2048]{1,0:T(8,128)(2,1)}, u32[]{:S(2)}, u32[]{:S(2)}) collective-permute-start(bf16[320,2048]{1,0:T(8,128)(2,1)S(1)} %bitcast.71), channel_id=1, source_target_pairs={{0,2},{1,3},{2,0},{3,1},{4,6},{5,7},{6,4},{7,5},{8,10},{9,11},{10,... | collective-permute-start | bytes 3932168 | tf_op jit(solution)/shard_map/ppermute | solution.py:1055
  187.1 69.2 %collective-permute-start = (bf16[320,2048]{1,0:T(8,128)(2,1)S(1)}, bf16[320,2048]{1,0:T(8,128)(2,1)}, u32[]{:S(2)}, u32[]{:S(2)}) collective-permute-start(bf16[320,2048]{1,0:T(8,128)(2,1)S(1)} %bitcast.72), channel_id=1, source_target_pairs={{0,1},{1,0},{2,3},{3,2},{4,5},{5,4},{6,7},{7,6},{8,9},{9,8},{10,11... | collective-permute-start | bytes 3932168 | tf_op jit(solution)/shard_map/ppermute | solution.py:1055
  194.6 60.6 %copy-start.22 = (f32[2048]{0:T(1024)}, f32[2048]{0:T(1024)S(1)}, u32[]{:S(2)}) copy-start(f32[2048]{0:T(1024)S(1)} %get-tuple-element.161) | copy-start | bytes 24580
  255.2 4.1 collective-permute-start.2
  255.5 5.4 collective-permute-start.4
  256.2 6.3 collective-permute-start.6
  262.7 67.9 %copy-start.6 = (bf16[2560,2048]{1,0:T(8,128)(2,1)}, bf16[2560,2048]{1,0:T(8,128)(2,1)S(1)}, u32[]{:S(2)}) copy-start(bf16[2560,2048]{1,0:T(8,128)(2,1)S(1)} %constant_dynamic-update-slice_fusion.grad_ref) | copy-start | bytes 31457284
  262.7 29.9 %collective-permute-start.8 = (bf16[320,2048]{1,0:T(8,128)(2,1)S(1)}, bf16[320,2048]{1,0:T(8,128)(2,1)S(1)}, u32[]{:S(2)}, u32[]{:S(2)}) collective-permute-start(bf16[320,2048]{1,0:T(8,128)(2,1)S(1)} %multiply_convert_fusion), channel_id=1, source_target_pairs={{0,2},{1,3},{2,0},{3,1},{4,6},{5,7},{6,4},{7,5},{8,10},{9,11},{10,... | collective-permute-start | bytes 3932168 | tf_op jit(solution)/shard_map/ppermute | solution.py:1055
  263.8 31.1 %collective-permute-start.10 = (bf16[320,2048]{1,0:T(8,128)(2,1)S(1)}, bf16[320,2048]{1,0:T(8,128)(2,1)S(1)}, u32[]{:S(2)}, u32[]{:S(2)}) collective-permute-start(bf16[320,2048]{1,0:T(8,128)(2,1)S(1)} %multiply_convert_fusion), channel_id=1, source_target_pairs={{0,4},{1,5},{2,6},{3,7},{4,0},{5,1},{6,2},{7,3},{8,12},{9,13},{10,... | collective-permute-start | bytes 3932168 | tf_op jit(solution)/shard_map/ppermute | solution.py:1055
  264.6 59.8 %collective-permute-start.12 = (bf16[320,2048]{1,0:T(8,128)(2,1)S(1)}, bf16[320,2048]{1,0:T(8,128)(2,1)S(1)}, u32[]{:S(2)}, u32[]{:S(2)}) collective-permute-start(bf16[320,2048]{1,0:T(8,128)(2,1)S(1)} %multiply_convert_fusion), channel_id=1, source_target_pairs={{0,6},{1,7},{2,4},{3,5},{4,2},{5,3},{6,0},{7,1},{8,14},{9,15},{10,... | collective-permute-start | bytes 3932168 | tf_op jit(solution)/shard_map/ppermute | solution.py:1055
  265.4 59.0 %collective-permute-start.7 = (bf16[320,2048]{1,0:T(8,128)(2,1)S(1)}, bf16[320,2048]{1,0:T(8,128)(2,1)S(1)}, u32[]{:S(2)}, u32[]{:S(2)}) collective-permute-start(bf16[320,2048]{1,0:T(8,128)(2,1)S(1)} %multiply_convert_fusion), channel_id=1, source_target_pairs={{0,1},{1,0},{2,3},{3,2},{4,5},{5,4},{6,7},{7,6},{8,9},{9,8},{10,11... | collective-permute-start | bytes 3932168 | tf_op jit(solution)/shard_map/ppermute | solution.py:1055
  292.6 34.2 %collective-permute-start.9 = (bf16[320,2048]{1,0:T(8,128)(2,1)S(1)}, bf16[320,2048]{1,0:T(8,128)(2,1)S(1)}, u32[]{:S(2)}, u32[]{:S(2)}) collective-permute-start(bf16[320,2048]{1,0:T(8,128)(2,1)S(1)} %collective-permute-done.8), channel_id=1, source_target_pairs={{0,1},{1,0},{2,3},{3,2},{4,5},{5,4},{6,7},{7,6},{8,9},{9,8},{10,11... | collective-permute-start | bytes 3932168 | tf_op jit(solution)/shard_map/ppermute | solution.py:1055
  294.9 34.4 %collective-permute-start.11 = (bf16[320,2048]{1,0:T(8,128)(2,1)S(1)}, bf16[320,2048]{1,0:T(8,128)(2,1)S(1)}, u32[]{:S(2)}, u32[]{:S(2)}) collective-permute-start(bf16[320,2048]{1,0:T(8,128)(2,1)S(1)} %collective-permute-done.10), channel_id=1, source_target_pairs={{0,1},{1,0},{2,3},{3,2},{4,5},{5,4},{6,7},{7,6},{8,9},{9,8},{10,11... | collective-permute-start | bytes 3932168 | tf_op jit(solution)/shard_map/ppermute | solution.py:1055
  324.3 7.4 collective-permute-start.13
  337.3 129.9 %reduce-scatter.5.cloned.1.call-start = ((), (), s32[]{:S(2)}) async-start(), calls=%async_computation.6 | async-start | bytes 5242880 | tf_op jit(solution)/shard_map/reduce_scatter | solution.py:1065
  389.2 225.9 %reduce-scatter.7.cloned.1.call-start = ((), (), s32[]{:S(2)}) async-start(), calls=%async_computation.7 | async-start | bytes 5242880 | tf_op jit(solution)/shard_map/reduce_scatter | solution.py:1065
  467.2 159.0 %reduce-scatter.11.cloned.1.call-start = ((), (), s32[]{:S(2)}) async-start(), calls=%async_computation.9 | async-start | bytes 5242880 | tf_op jit(solution)/shard_map/reduce_scatter | solution.py:1065
  467.8 316.0 %reduce-scatter.9.cloned.1.call-start = ((), (), s32[]{:S(2)}) async-start(), calls=%async_computation.8 | async-start | bytes 5242880 | tf_op jit(solution)/shard_map/reduce_scatter | solution.py:1065
  533.8 13.2 %collective-permute-start.17 = (bf16[320,2048]{1,0:T(8,128)(2,1)S(1)}, bf16[320,2048]{1,0:T(8,128)(2,1)S(1)}, u32[]{:S(2)}, u32[]{:S(2)}) collective-permute-start(bf16[320,2048]{1,0:T(8,128)(2,1)S(1)} %get-tuple-element.170), channel_id=1, source_target_pairs={{0,1},{1,0},{2,3},{3,2},{4,5},{5,4},{6,7},{7,6},{8,9},{9,8},{10,11... | collective-permute-start | bytes 3932168 | tf_op jit(solution)/shard_map/ppermute | solution.py:1055
  534.9 12.1 %collective-permute-start.16 = (bf16[320,2048]{1,0:T(8,128)(2,1)S(1)}, bf16[320,2048]{1,0:T(8,128)(2,1)S(1)}, u32[]{:S(2)}, u32[]{:S(2)}) collective-permute-start(bf16[320,2048]{1,0:T(8,128)(2,1)S(1)} %get-tuple-element.171), channel_id=1, source_target_pairs={{0,1},{1,0},{2,3},{3,2},{4,5},{5,4},{6,7},{7,6},{8,9},{9,8},{10,11... | collective-permute-start | bytes 3932168 | tf_op jit(solution)/shard_map/ppermute | solution.py:1055
  535.0 12.0 %collective-permute-start.15 = (bf16[320,2048]{1,0:T(8,128)(2,1)S(1)}, bf16[320,2048]{1,0:T(8,128)(2,1)S(1)}, u32[]{:S(2)}, u32[]{:S(2)}) collective-permute-start(bf16[320,2048]{1,0:T(8,128)(2,1)S(1)} %get-tuple-element.172), channel_id=1, source_target_pairs={{0,1},{1,0},{2,3},{3,2},{4,5},{5,4},{6,7},{7,6},{8,9},{9,8},{10,11... | collective-permute-start | bytes 3932168 | tf_op jit(solution)/shard_map/ppermute | solution.py:1055
  535.4 11.6 %collective-permute-start.14 = (bf16[320,2048]{1,0:T(8,128)(2,1)S(1)}, bf16[320,2048]{1,0:T(8,128)(2,1)S(1)}, u32[]{:S(2)}, u32[]{:S(2)}) collective-permute-start(bf16[320,2048]{1,0:T(8,128)(2,1)S(1)} %get-tuple-element.173), channel_id=1, source_target_pairs={{0,1},{1,0},{2,3},{3,2},{4,5},{5,4},{6,7},{7,6},{8,9},{9,8},{10,11... | collective-permute-start | bytes 3932168 | tf_op jit(solution)/shard_map/ppermute | solution.py:1055
  552.7 62.3 %collective-permute-start.18 = (bf16[320,2048]{1,0:T(8,128)(2,1)}, bf16[320,2048]{1,0:T(8,128)(2,1)}, u32[]{:S(2)}, u32[]{:S(2)}) collective-permute-start(bf16[320,2048]{1,0:T(8,128)(2,1)} %get-tuple-element.124), channel_id=1, source_target_pairs={{0,2},{1,3},{2,0},{3,1},{4,6},{5,7},{6,4},{7,5},{8,10},{9,11},{10,... | collective-permute-start | bytes 3932168 | tf_op jit(solution)/shard_map/ppermute | solution.py:1055
  553.9 61.2 %collective-permute-start.19 = (bf16[320,2048]{1,0:T(8,128)(2,1)}, bf16[320,2048]{1,0:T(8,128)(2,1)}, u32[]{:S(2)}, u32[]{:S(2)}) collective-permute-start(bf16[320,2048]{1,0:T(8,128)(2,1)} %get-tuple-element.125), channel_id=1, source_target_pairs={{0,4},{1,5},{2,6},{3,7},{4,0},{5,1},{6,2},{7,3},{8,12},{9,13},{10,... | collective-permute-start | bytes 3932168 | tf_op jit(solution)/shard_map/ppermute | solution.py:1055
  554.2 60.8 %collective-permute-start.20 = (bf16[320,2048]{1,0:T(8,128)(2,1)}, bf16[320,2048]{1,0:T(8,128)(2,1)}, u32[]{:S(2)}, u32[]{:S(2)}) collective-permute-start(bf16[320,2048]{1,0:T(8,128)(2,1)} %get-tuple-element.126), channel_id=1, source_target_pairs={{0,6},{1,7},{2,4},{3,5},{4,2},{5,3},{6,0},{7,1},{8,14},{9,15},{10,... | collective-permute-start | bytes 3932168 | tf_op jit(solution)/shard_map/ppermute | solution.py:1055
  626.2 157.6 %copy-start.4 = (bf16[1,1,320,2048]{3,2,1,0:T(8,128)(2,1)S(1)}, bf16[1,1,320,2048]{3,2,1,0:T(8,128)(2,1)}, u32[]{:S(2)}) copy-start(bf16[1,1,320,2048]{3,2,1,0:T(8,128)(2,1)} %param.16) | copy-start | bytes 3932164
  626.2 157.7 %copy-start.24 = (f32[2048]{0:T(1024)S(1)}, f32[2048]{0:T(1024)}, u32[]{:S(2)}) copy-start(f32[2048]{0:T(1024)} %get-tuple-element.160) | copy-start | bytes 24580
  (37 other events, 162.1 us)
Sparse Core Ops, SparseCore 0:
  184.5 152.8 all-gather.2
  338.9 45.1 all-gather.4
  389.3 77.8 reduce-scatter.4
  469.5 77.2 reduce-scatter.6
  548.9 77.2 reduce-scatter.10
  629.0 82.1 reduce-scatter.8

commit v9 on v8

--- a/solution.py
+++ b/solution.py
@@ -851,6 +851,7 @@
     g = lax.axis_index("grp")
     d = lax.axis_index("dp")
     chips = plane // 2
+    own_hidden = down_ref.shape[2]
     halves = plane == 8
     order = (3, 1, 2, 0) if halves else tuple(range(chips - 1, -1, -1))
     cut = D // 2
@@ -909,13 +910,15 @@
         there = flip(d, offset)
         return remote(
             down_ref.at[there],
-            swapped_ref.at[d],
+            swapped_ref.at[:, pl.ds(d * own_hidden, own_hidden)],
             swap_send.at[offset],
             swap_recv.at[offset],
             (g, there),
         )
 
-    own_swap = pltpu.make_async_copy(down_ref.at[d], swapped_ref.at[d], out_sem.at[1])
+    own_swap = pltpu.make_async_copy(
+        down_ref.at[d], swapped_ref.at[:, pl.ds(d * own_hidden, own_hidden)], out_sem.at[1]
+    )
     tile_copy(0).start()
     tile_copy(1).start()
     pl.semaphore_wait(barrier, plane - 1)
@@ -1021,7 +1024,7 @@
         functools.partial(plane_back_kernel, plane),
         out_shape=(
             jax.ShapeDtypeStruct((rows, D), FULL),
-            jax.ShapeDtypeStruct(down_part.shape, LOW),
+            jax.ShapeDtypeStruct((down_part.shape[1], FF), LOW),
         ),
         in_specs=[anywhere] * 3,
         out_specs=(anywhere,) * 2,
@@ -1075,37 +1078,15 @@
     gate_ref,
     up_ref,
     down_ref,
-    a_master,
-    a_first,
-    a_second,
-    m_master,
-    m_first,
-    m_second,
-    f_master,
-    f_first,
-    f_second,
-    a_grad,
-    a_update,
-    a_first_new,
-    a_second_new,
-    m_grad,
-    m_update,
-    m_first_new,
-    m_second_new,
+    a_out,
+    m_out,
     gain_out,
-    f_grad,
-    f_update,
-    f_first_new,
-    f_second_new,
+    f_out,
     mine,
     core_in,
     plane_in,
     line_in,
-    swap_in,
-    state,
-    made,
-    a_state,
-    a_made,
+    owned,
     gain_made,
     mine_sem,
     core_send,
@@ -1117,20 +1098,16 @@
     swap_send,
     swap_recv,
     own_sem,
-    state_sem,
-    made_sem,
-    a_sem,
-    gain_sem,
+    out_sem,
 ):
     g = lax.axis_index("grp")
     d = lax.axis_index("dp")
     chips = plane // 2
     chip, core = lax.div(d, 2), lax.rem(d, 2)
     partner = d + 1 - 2 * core
-    rows = a_master.shape[0]
     own_hidden = gate_ref.shape[2]
     width = core_in.shape[3]
-    a_width, m_width = a_master.shape[1], m_master.shape[1]
+    a_width, m_width = a_out.shape[1], m_out.shape[1]
     parts, begin = [], 0
     for ref in (query_ref, pair_ref, merge_ref, gain_ref):
         parts.append((ref, pl.ds(begin, ref.shape[4])))
@@ -1213,61 +1190,25 @@
             (line, d),
         )
 
-    forward_refs = (gate_ref, up_ref, down_ref)
+    forward_refs = (gate_ref, up_ref)
+
+    def swap_place(part):
+        return f_out.at[:, pl.ds(part * FF + d * own_hidden, own_hidden)]
 
     def swap_copy(step, part):
         there = lax.rem(d + step, plane)
         return remote(
             forward_refs[part].at[there],
-            swap_in.at[part, d],
+            swap_place(part),
             swap_send.at[step, part],
             swap_recv.at[step, part],
             (g, there),
         )
 
     own_swap = [
-        pltpu.make_async_copy(forward_refs[part].at[d], swap_in.at[part, d], own_sem.at[part])
+        pltpu.make_async_copy(forward_refs[part].at[d], swap_place(part), own_sem.at[part])
         for part in range(2)
-    ] + [pltpu.make_async_copy(down_ref, swap_in.at[2], own_sem.at[2])]
-
-    def f_columns(turn):
-        block = lax.rem(d + lax.div(turn, 3), plane)
-        return pl.ds(
-            pl.multiple_of(lax.rem(turn, 3) * FF + block * own_hidden, own_hidden), own_hidden
-        )
-
-    def state_copy(turn, which):
-        slot = lax.rem(turn, 2)
-        return pltpu.make_async_copy(
-            (f_master, f_first, f_second)[which].at[:, f_columns(turn)],
-            state.at[slot, which],
-            state_sem.at[slot, which],
-        )
-
-    def made_copy(turn, which):
-        slot = lax.rem(turn, 2)
-        return pltpu.make_async_copy(
-            made.at[slot, which],
-            (f_grad, f_update, f_first_new, f_second_new)[which].at[:, f_columns(turn)],
-            made_sem.at[slot, which],
-        )
-
-    slabs = (pl.ds(0, a_width), pl.ds(a_width, m_width))
-
-    def a_state_copy(which, slab):
-        source = ((a_master, a_first, a_second), (m_master, m_first, m_second))[slab][which]
-        return pltpu.make_async_copy(
-            source, a_state.at[which, :, slabs[slab]], a_sem.at[slab, which]
-        )
-
-    def a_made_copy(which, slab):
-        target = (
-            (a_grad, a_update, a_first_new, a_second_new),
-            (m_grad, m_update, m_first_new, m_second_new),
-        )[slab][which]
-        return pltpu.make_async_copy(
-            a_made.at[which, :, slabs[slab]], target, a_sem.at[slab, 3 + which]
-        )
+    ] + [pltpu.make_async_copy(down_ref, f_out.at[:, pl.ds(2 * FF, FF)], own_sem.at[2])]
 
     every = range(len(parts))
     for turn in range(lines):
@@ -1281,11 +1222,6 @@
                     swap_copy(step, part).start()
             for one in own_swap:
                 one.start()
-    for which in range(3):
-        state_copy(0, which).start()
-        for slab in range(2):
-            a_state_copy(which, slab).start()
-
     tile = 896 if width % 896 == 0 else 128
     halves = plane == 8
 
@@ -1336,43 +1272,6 @@
             )
             relay_copy(turn, part).start()
 
-    def forward_turn(turn):
-        slot = lax.rem(turn, 2)
-        block = lax.rem(d + lax.div(turn, 3), plane)
-        part = lax.rem(turn, 3)
-
-        @pl.when(turn + 1 < 3 * plane)
-        def _():
-            for which in range(3):
-                state_copy(turn + 1, which).start()
-
-        @pl.when(turn > 1)
-        def _():
-            for which in range(4):
-                made_copy(turn - 2, which).wait()
-
-        for which in range(3):
-            state_copy(turn, which).wait()
-
-        @pl.loop(0, rows // 16)
-        def _(at):
-            rows_at = pl.ds(pl.multiple_of(at * 16, 16), 16)
-            gradient = swap_in[part, block, rows_at].astype(FULL)
-            update, first_new, second_new = adam_step(
-                state[slot, 0, rows_at],
-                state[slot, 1, rows_at],
-                state[slot, 2, rows_at],
-                gradient,
-                WEIGHT_DECAY,
-            )
-            made[slot, 0, rows_at] = gradient
-            made[slot, 1, rows_at] = update
-            made[slot, 2, rows_at] = first_new
-            made[slot, 3, rows_at] = second_new
-
-        for which in range(4):
-            made_copy(turn, which).start()
-
     def near_done(turn):
         if halves:
             pass_on(turn)
@@ -1404,34 +1303,15 @@
         if turn < lines - 1:
             line_copy(turn).start()
 
-    each = 3 * plane // lines
-
-    def forward_some(turn):
-        lax.fori_loop(turn * each, (turn + 1) * each, lambda k, c: (forward_turn(k), c)[1], 0)
-
     near_done(0)
     for turn in range(1, lines):
-        if turn == 1:
-            for one in own_swap:
-                one.wait()
-            for step in range(1, plane):
-                for part in range(2):
-                    swap_copy(step, part).wait_recv()
         near_done(turn)
         line_done(turn - 1)
-        forward_some(turn - 1)
     line_done(lines - 1)
-    forward_some(lines - 1)
-    for which in range(4):
-        for turn in (3 * plane - 2, 3 * plane - 1):
-            made_copy(turn, which).wait()
     for turn in range(lines - 1):
         line_copy(turn).wait_recv()
-    for which in range(3):
-        for slab in range(2):
-            a_state_copy(which, slab).wait()
-
-    def owned(columns):
+
+    def total_of(columns):
         total = core_in[g, chip, :, columns].astype(FULL)
         for step in range(1, lines):
             total = total + line_in[lax.rem(g + step, lines), :, columns].astype(FULL)
@@ -1440,25 +1320,16 @@
     @pl.loop(0, (a_width + m_width) // 256)
     def _(at):
         columns = pl.ds(pl.multiple_of(at * 256, 256), 256)
-        gradient = owned(columns)
-        update, first_new, second_new = adam_step(
-            a_state[0, :, columns],
-            a_state[1, :, columns],
-            a_state[2, :, columns],
-            gradient,
-            WEIGHT_DECAY,
-        )
-        a_made[0, :, columns] = gradient
-        a_made[1, :, columns] = update
-        a_made[2, :, columns] = first_new
-        a_made[3, :, columns] = second_new
-
-    for which in range(4):
-        for slab in range(2):
-            a_made_copy(which, slab).start()
-    gain_made[...] = owned(pl.ds(a_width + m_width, GAIN_PAD)).T[:8]
-    gain_copy = pltpu.make_async_copy(gain_made, gain_out, gain_sem.at[0])
-    gain_copy.start()
+        owned[:, columns] = total_of(columns)
+
+    gain_made[...] = total_of(pl.ds(a_width + m_width, GAIN_PAD)).T[:8]
+    outs = (
+        pltpu.make_async_copy(owned.at[:, pl.ds(0, a_width)], a_out, out_sem.at[0]),
+        pltpu.make_async_copy(owned.at[:, pl.ds(a_width, m_width)], m_out, out_sem.at[1]),
+        pltpu.make_async_copy(gain_made, gain_out, out_sem.at[2]),
+    )
+    for one in outs:
+        one.start()
     for turn in range(lines):
         for part in every:
             core_copy(turn, part).wait_send()
@@ -1474,45 +1345,39 @@
             line_copy(turn).wait_send()
     for step in range(1, plane):
         for part in range(2):
-            swap_copy(step, part).wait_send()
-    for which in range(4):
-        for slab in range(2):
-            a_made_copy(which, slab).wait()
-    gain_copy.wait()
-
-
-def finish(terms, forward_parts, attention, merge, forward):
+            swap_copy(step, part).wait()
+    for one in own_swap:
+        one.wait()
+    for one in outs:
+        one.wait()
+
+
+def finish(terms, gate_part, up_part, down_swapped):
     lines, plane = lax.axis_size("grp"), lax.axis_size("dp")
     chips = plane // 2
-    rows, a_width = attention[0].shape
-    m_width = merge[0].shape[1]
-    own_hidden = forward_parts[0].shape[-1]
+    rows = D // (lines * plane)
+    m_width = terms[2].shape[1]
+    a_width = terms[0].shape[1] + terms[1].shape[1]
     width = a_width + m_width + GAIN_PAD
     anywhere = pl.BlockSpec(memory_space=pl.ANY)
     dma = pltpu.SemaphoreType.DMA
     vmem = pltpu.VMEM
-
-    def like(array):
-        return jax.ShapeDtypeStruct(array.shape, array.dtype)
-
     return pl.pallas_call(
         functools.partial(finish_kernel, lines, plane),
-        out_shape=(like(attention[0]),) * 4
-        + (like(merge[0]),) * 4
-        + (jax.ShapeDtypeStruct((8, rows), FULL),)
-        + (like(forward[0]),) * 4,
-        in_specs=[anywhere] * 16,
-        out_specs=(anywhere,) * 13,
+        out_shape=(
+            jax.ShapeDtypeStruct((rows, a_width), FULL),
+            jax.ShapeDtypeStruct((rows, m_width), FULL),
+            jax.ShapeDtypeStruct((8, rows), FULL),
+            jax.ShapeDtypeStruct((rows, 3 * FF), LOW),
+        ),
+        in_specs=[anywhere] * 7,
+        out_specs=(anywhere,) * 4,
         scratch_shapes=[
             vmem((2, chips, rows, width), LOW),
             vmem((lines, chips, rows, width), LOW),
             vmem((lines, 3 if plane == 8 else chips, rows, width), LOW),
             vmem((lines, rows, width), LOW),
-            vmem((3, plane, rows, own_hidden), LOW),
-            vmem((2, 3, rows, own_hidden), FULL),
-            vmem((2, 4, rows, own_hidden), FULL),
-            vmem((3, rows, a_width + m_width), FULL),
-            vmem((4, rows, a_width + m_width), FULL),
+            vmem((rows, a_width + m_width), FULL),
             vmem((8, rows), FULL),
             dma((lines, 4)),
             dma((lines, 4)),
@@ -1524,10 +1389,7 @@
             dma((plane, 2)),
             dma((plane, 2)),
             dma((3,)),
-            dma((2, 3)),
-            dma((2, 4)),
-            dma((2, 7)),
-            dma((1,)),
+            dma((3,)),
         ],
         compiler_params=pltpu.CompilerParams(
             collective_id=1, has_side_effects=True, vmem_limit_bytes=VMEM_LIMIT
@@ -1535,10 +1397,9 @@
         name="finish",
     )(
         *(term.reshape(lines, chips, 2, rows, term.shape[1]) for term in terms),
-        *(part.reshape(plane, rows, own_hidden) for part in forward_parts),
-        *attention,
-        *merge,
-        *forward,
+        gate_part.reshape(plane, rows, -1),
+        up_part.reshape(plane, rows, -1),
+        down_swapped,
     )
 
 
@@ -1685,28 +1546,39 @@
     block_output, query_term = lax.optimization_barrier((result.astype(LOW), query_term))
     block_output = block_output.reshape(hidden.shape)
     pair_sum = line_scatter(pair_back)
-    finished = finish(
+    attention_grad, merge_grad, gain_sums, forward_low = finish(
         (query_term, pair_term, merge_term, gain_term.astype(LOW)),
-        (gate_part, up_part, down_swapped),
-        (attention_master, attention_first, attention_second),
-        (merge_master, merge_first, merge_second),
-        (feedforward_master, feedforward_first, feedforward_second),
-    )
-    gain_grad = finished[8][:2]
+        gate_part,
+        up_part,
+        down_swapped,
+    )
+    gain_grad = gain_sums[:2]
     pair_sum, gain_grad = lax.optimization_barrier((pair_sum, gain_grad))
     pair_sum = pair_sum.astype(FULL)
     normed_grad = normed_grad + jnp.pad(pair_sum, ((0, CONT), (0, 0)))
     input_grad = (middle_grad + norm_back(inputs, first_scale, gain_float[0], normed_grad)).reshape(
         hidden.shape
     )
+    feedforward_grad = forward_low.astype(FULL)
     gain_new = adam_step(gain_master, gain_first, gain_second, gain_grad, 0.0)
+    attention_new = adam_step(
+        attention_master, attention_first, attention_second, attention_grad, WEIGHT_DECAY
+    )
+    merge_new = adam_step(merge_master, merge_first, merge_second, merge_grad, WEIGHT_DECAY)
+    feedforward_new = adam_step(
+        feedforward_master, feedforward_first, feedforward_second, feedforward_grad, WEIGHT_DECAY
+    )
     return (
         block_output,
         input_grad,
         gain_grad,
         *gain_new,
-        *finished[:8],
-        *finished[9:],
+        attention_grad,
+        *attention_new,
+        merge_grad,
+        *merge_new,
+        feedforward_grad,
+        *feedforward_new,
     )
 
 

time: 833 us -> 829 us (level)
  local copies, waits for them, and re-layouts: 52.7 us -> 32.7 us
  other arithmetic: 42.9 us -> 62.7 us
    unnamed x111 -> x81, local copies, waits for them, and re-layouts: 44.4 us -> 24.2 us
    mul x1 -> x4, other arithmetic: 0.59 us -> 19.7 us  [adam_step(): return (-LEARN_RATE * (update + decay_rate * master), first_new, second_new)]
  transfers between devices with their start and end apart: 27 -> 27, of which waited for: 4 -> 4; matrix products, arithmetic and copies ran while one was open for 17% -> 20% of each run, Pallas kernels for 44% -> 44%
where the time goes in v9:
time: 829 us; the launch traced here: 817 us
  Pallas kernels  527 us (64%)
  matrix products  89.6 us (11%)
  other arithmetic  62.7 us (8%)
  starting transfers between devices  47.6 us (6%)
  waiting for transfers between devices  42 us (5%)
  local copies, waits for them, and re-layouts  32.7 us (4%)
  between operations  15.8 us (2%)
    pallas_call x1, Pallas kernels, gather_start(): pl.pallas_call(functools.partial(gather_kernel, lines, plane, prompt_rows...  168 us
    pallas_call x1, Pallas kernels, finish(): pl.pallas_call(functools.partial(finish_kernel, lines, plane), out_shape=...  154 us
    dot_general x5, matrix products, contract(): lax.dot_general(left, right, (((left_axis,), (right_axis,)), ((), ())), p...  62.9 us
    pallas_call x1, Pallas kernels, plane_back(): pl.pallas_call(functools.partial(plane_back_kernel, plane), out_shape=(ja...  62.7 us
    ppermute x21, starting transfers between devices, plane_swap(): return lax.ppermute(block, 'dp', [(i, i ^ offset) for i in range(size)])  46.7 us
    pallas_call x1, Pallas kernels, weights_back(): pl.pallas_call(weights_back_kernel, grid_spec=pltpu.PrefetchScalarGridSpe...  40.4 us
    pallas_call x1, Pallas kernels, forward_back(): pl.pallas_call(forward_back_kernel, grid=(count // rows,), in_specs=[bloc...  36.6 us
    pallas_call x1, Pallas kernels, project_heads(): pl.pallas_call(project_kernel, grid_spec=pltpu.PrefetchScalarGridSpec(num...  34.9 us
  transfers between devices with their start and end apart: 27, of which 4 were waited for; matrix products, arithmetic and copies ran while one was open for 20% of the time, Pallas kernels for 44%

profile of v9, /device:TPU:9, one launch (start us, length us, event | category | flops | bytes accessed | tf_op | source)
XLA Modules:
  0.0 817.5 jit_solution(15950624899945998769)
XLA Ops:
  10.4 4.8 convert_element_type.114.forward_ref
  16.1 168.2 %gather_start.1 = (bf16[4,8,64,6272]{3,2,1,0:T(8,128)(2,1)}, bf16[4,256,2048]{2,1,0:T(8,128)(2,1)}, bf16[8,64,2048]{2,1,0:T(8,128)(2,1)}, bf16[4,8,64,512]{3,2,1,0:T(8,128)(2,1)}, bf16[8,64,512]{2,1,0:T(8,128)(2,1)}) custom-call(bf16[64,6272]{1,0:T(8,128)(2,1)} %fusion.31.weight_ref, bf16[320,2048]{1,0:T(8,128)(2,1)} %bitcast.52, ...), custom_call_target="tpu_custom_call" | custom-call | tf_op jit(solution)/shard_map/gather_start/pallas_call | solution.py:411
  187.1 4.4 collective-permute-start
  197.2 3.1 multiply_sine_fusion
  200.3 34.9 %project_heads.1 = (bf16[320,2048]{1,0:T(8,128)(2,1)}, bf16[1088,2048]{1,0:T(8,128)(2,1)}, bf16[1088,2048]{1,0:T(8,128)(2,1)}, bf16[320,2048]{1,0:T(8,128)(2,1)}, f32[1088,128]{1,0:T(8,128)}) custom-call(s32[1]{0:T(128)} %bitcast.1.place_ref, bf16[1024,2048]{1,0:T(8,128)(2,1)} %bitcast.55, bf16[320,2048]{1,0:T(8,128)(2,1)} %bitcast.53, ...), custom_call_target="tpu_custom_call" | custom-call | tf_op jit(solution)/shard_map/project_heads/pallas_call | solution.py:510
  237.1 11.4 %attend.1 = (bf16[320,2048]{1,0:T(8,128)(2,1)}, f32[320,1024]{1,0:T(8,128)}) custom-call(bf16[320,2048]{1,0:T(8,128)(2,1)} %get-tuple-element.81.query_ref, bf16[1088,2048]{1,0:T(8,128)(2,1)} %get-tuple-element.82.key_ref.value_ref, bf16[1088,2048]{1,0:T(8,128)(2,1)} %get-tuple-element.82.key_ref.value_ref, f32[320,1088]{1,0:T(8,128)} %add_convert_fusion.4.seen_ref), custom_call_target="tpu_custom_call" | custom-call | tf_op jit(solution)/shard_map/attend/pallas_call | solution.py:572
  248.5 6.0 multiply_reduce_fusion.2
  266.7 25.9 %collective-permute-done.8 = bf16[320,2048]{1,0:T(8,128)(2,1)S(1)} collective-permute-done((bf16[320,2048]{1,0:T(8,128)(2,1)S(1)}, bf16[320,2048]{1,0:T(8,128)(2,1)S(1)}, u32[]{:S(2)}, u32[]{:S(2)}) %collective-permute-start.8) | collective-permute-done | bytes 1310752 | tf_op jit(solution)/shard_map/ppermute | solution.py:1058
  294.9 28.2 %collective-permute-start.11 = (bf16[320,2048]{1,0:T(8,128)(2,1)S(1)}, bf16[320,2048]{1,0:T(8,128)(2,1)S(1)}, u32[]{:S(2)}, u32[]{:S(2)}) collective-permute-start(bf16[320,2048]{1,0:T(8,128)(2,1)S(1)} %collective-permute-done.10), channel_id=1, source_target_pairs={{0,1},{1,0},{2,3},{3,2},{4,5},{5,4},{6,7},{7,6},{8,9},{9,8},{10,11... | collective-permute-start | bytes 3932168 | tf_op jit(solution)/shard_map/ppermute | solution.py:1058
  332.9 4.4 all-gather.3.cloned.1.call-done.weight_ref
  337.6 26.7 %fusion.43.gate_up_ref = f32[2560,2048]{1,0:T(8,128)S(1)} fusion(bf16[2560,2048]{1,0:T(8,128)(2,1)} %constant_dynamic-update-slice_fusion.8, bf16[2048,2048]{1,0:T(8,128)(2,1)} %all-gather.3.cloned.1.call-done.weight_ref), kind=kOutput, calls=%fused_computation.106 | convolution fusion | flops 21474836480 | bytes 39845888 | tf_op jit(solution)/shard_map/dot_general | solution.py:1489
  364.3 3.6 fusion.activated_ref
  367.9 3.5 copy-done
  373.8 15.4 %convolution_convert_fusion = bf16[2048,1024]{1,0:T(8,128)(2,1)} fusion(bf16[2560,2048]{1,0:T(8,128)(2,1)} %copy-done.6, bf16[2560,1024]{1,0:T(8,128)(2,1)S(1)} %fusion.activated_ref), kind=kOutput, calls=%fused_computation.18 | convolution fusion | flops 10739515392 | bytes 19922944 | tf_op jit(solution)/shard_map/dot_general | solution.py:35
  389.7 36.6 %forward_back.1 = (bf16[2560,2048]{1,0:T(8,128)(2,1)}, bf16[2560,2048]{1,0:T(8,128)(2,1)}) custom-call(bf16[2560,1024]{1,0:T(8,128)(2,1)} %copy-done.5, bf16[2560,2048]{1,0:T(8,128)(2,1)} %copy-done.6, f32[2560,2048]{1,0:T(8,128)} %copy-done, bf16[2048,512]{1,0:T(8,128)(2,1)} %bitcast.66, bf16[2048,512]{1,0:T(8,128)(2,1)} %all-gather.5.cloned.1.call-done.second_ref), custom_call_target="tpu_custom_call" | custom-call | tf_op jit(solution)/shard_map/forward_back/pallas_call | solution.py:807
  426.3 16.8 %fusion.13 = bf16[2048,1024]{1,0:T(8,128)(2,1)} fusion(bf16[2560,2048]{1,0:T(8,128)(2,1)} %constant_dynamic-update-slice_fusion.8, bf16[2560,2048]{1,0:T(8,128)(2,1)} %get-tuple-element.95), kind=kOutput, calls=%fused_computation.20 | convolution fusion | flops 10739515392 | bytes 19922944 | tf_op jit(solution)/shard_map/dot_general | solution.py:35
  443.1 16.8 %fusion.10 = bf16[2048,1024]{1,0:T(8,128)(2,1)} fusion(bf16[2560,2048]{1,0:T(8,128)(2,1)} %constant_dynamic-update-slice_fusion.8, bf16[2560,2048]{1,0:T(8,128)(2,1)} %get-tuple-element.95), kind=kOutput, calls=%fused_computation.19 | convolution fusion | flops 10739515392 | bytes 19922944 | tf_op jit(solution)/shard_map/dot_general | solution.py:35
  459.9 7.3 reduce-scatter.5.cloned.1.call-done
  467.9 62.7 %plane_back.1 = (f32[320,2048]{1,0:T(8,128)}, bf16[64,8192]{1,0:T(8,128)(2,1)}) custom-call(bf16[8,320,2048]{2,1,0:T(8,128)(2,1)} %bitcast.57, bf16[2048,2048]{1,0:T(8,128)(2,1)} %all-gather.3.cloned.1.call-done.weight_ref, bf16[8,64,1024]{2,1,0:T(8,128)(2,1)} %bitcast.71), custom_call_target="tpu_custom_call" | custom-call | tf_op jit(solution)/shard_map/plane_back/pallas_call | solution.py:1023
  530.6 3.1 fusion.42
  536.7 2.4 fusion.41
  539.1 7.9 fusion.18.grad_ref
  547.0 5.6 add_convert_fusion.1
  555.4 19.3 %attend_back.1 = (bf16[320,2048]{1,0:T(8,128)(2,1)}, bf16[1088,2048]{1,0:T(8,128)(2,1)}) custom-call(s32[1]{0:T(128)} %bitcast.1.place_ref, bf16[320,2048]{1,0:T(8,128)(2,1)} %get-tuple-element.81.query_ref, bf16[1088,2048]{1,0:T(8,128)(2,1)} %get-tuple-element.82.key_ref.value_ref, bf16[1088,2048]{1,0:T(8,128)(2,1)} %get-tuple-element.82.key_ref.value_ref, ...), custom_call_target="tpu_custom_call" | custom-call | tf_op jit(solution)/shard_map/attend_back/pallas_call | solution.py:651
  574.7 40.4 %weights_back.1 = (bf16[2048,2048]{1,0:T(8,128)(2,1)}, bf16[2048,2048]{1,0:T(8,128)(2,1)}, bf16[2048,2048]{1,0:T(8,128)(2,1)}, f32[320,2048]{1,0:T(8,128)}, bf16...) custom-call(s32[1]{0:T(128)} %bitcast.1.place_ref, bf16[320,2048]{1,0:T(8,128)(2,1)} %get-tuple-element.108.query_ref, ...), custom_call_target="tpu_custom_call" | custom-call | tf_op jit(solution)/shard_map/weights_back/pallas_call | solution.py:730
  617.1 5.4 add_convert_fusion
  622.6 3.6 reduce-scatter.11.cloned.1.call-done
  626.2 153.6 %finish.1 = (f32[64,4096]{1,0:T(8,128)}, f32[64,2048]{1,0:T(8,128)}, f32[8,64]{1,0:T(8,128)}, bf16[64,24576]{1,0:T(8,128)(2,1)}) custom-call(bf16[4,4,2,64,2048]{4,3,2,1,0:T(8,128)(2,1)} %bitcast.58, bf16[4,4,2,64,2048]{4,3,2,1,0:T(8,128)(2,1)} %bitcast.59, bf16[4,4,2,64,2048]{4,3,2,1,0:T(8,128)(2,1)} %bitcast.60, bf16[4,4,2,64,128]{4,3,2,1,0:T(8,128)(2,1)} %bitcast.65, ...), custom_call_target="tpu_custom_call" | custom-call | tf_op jit(solution)/shard_map/finish/pallas_call | solution.py:1365
  780.7 2.8 add_multiply_fusion.3
  786.5 14.1 %add_multiply_fusion = (f32[64,24576]{1,0:T(8,128)}, f32[64,24576]{1,0:T(8,128)}, f32[64,24576]{1,0:T(8,128)}, f32[64,24576]{1,0:T(8,128)}) fusion(f32[64,24576]{1,0:T(8,128)} %param.29, f32[64,24576]{1,0:T(8,128)} %param.30, f32[64,24576]{1,0:T(8,128)} %param.31, bf16[64,24576]{1,0:T(8,128)(2,1)S(1)} %copy-done.15), kind=kLoop, calls=%fused_computation.8 | loop fusion | flops 23592960 | bytes 47185920 | tf_op jit(solution)/shard_map/mul | solution.py:81
  800.7 2.9 fusion.21
  804.3 4.1 fusion.25
  (172 shorter events, 55.5 us)
Async XLA Ops:
  7.2 330.1 %all-gather.3.cloned.1.call-start = ((), (), s32[]{:S(2)}) async-start(), calls=%async_computation.4 | async-start | bytes 10485760 | tf_op jit(solution)/shard_map/all_gather | solution.py:1444
  16.1 168.3 %copy-start.9 = (bf16[1,1,320,2048]{3,2,1,0:T(8,128)(2,1)S(1)}, bf16[1,1,320,2048]{3,2,1,0:T(8,128)(2,1)}, u32[]{:S(2)}) copy-start(bf16[1,1,320,2048]{3,2,1,0:T(8,128)(2,1)} %param.17) | copy-start | bytes 3932164
  184.3 204.8 %all-gather.5.cloned.1.call-start = ((), (), s32[]{:S(2)}) async-start(), calls=%async_computation.5 | async-start | bytes 2621440 | tf_op jit(solution)/shard_map/all_gather | solution.py:1449
  184.4 71.8 %collective-permute-start.5 = (bf16[320,2048]{1,0:T(8,128)(2,1)S(1)}, bf16[320,2048]{1,0:T(8,128)(2,1)}, u32[]{:S(2)}, u32[]{:S(2)}) collective-permute-start(bf16[320,2048]{1,0:T(8,128)(2,1)S(1)} %bitcast.61), channel_id=1, source_target_pairs={{0,6},{1,7},{2,4},{3,5},{4,2},{5,3},{6,0},{7,1},{8,14},{9,15},{10,... | collective-permute-start | bytes 3932168 | tf_op jit(solution)/shard_map/ppermute | solution.py:1058
  185.9 69.6 %collective-permute-start.3 = (bf16[320,2048]{1,0:T(8,128)(2,1)S(1)}, bf16[320,2048]{1,0:T(8,128)(2,1)}, u32[]{:S(2)}, u32[]{:S(2)}) collective-permute-start(bf16[320,2048]{1,0:T(8,128)(2,1)S(1)} %bitcast.62), channel_id=1, source_target_pairs={{0,4},{1,5},{2,6},{3,7},{4,0},{5,1},{6,2},{7,3},{8,12},{9,13},{10,... | collective-permute-start | bytes 3932168 | tf_op jit(solution)/shard_map/ppermute | solution.py:1058
  186.4 68.7 %collective-permute-start.1 = (bf16[320,2048]{1,0:T(8,128)(2,1)S(1)}, bf16[320,2048]{1,0:T(8,128)(2,1)}, u32[]{:S(2)}, u32[]{:S(2)}) collective-permute-start(bf16[320,2048]{1,0:T(8,128)(2,1)S(1)} %bitcast.63), channel_id=1, source_target_pairs={{0,2},{1,3},{2,0},{3,1},{4,6},{5,7},{6,4},{7,5},{8,10},{9,11},{10,... | collective-permute-start | bytes 3932168 | tf_op jit(solution)/shard_map/ppermute | solution.py:1058
  187.1 69.2 %collective-permute-start = (bf16[320,2048]{1,0:T(8,128)(2,1)S(1)}, bf16[320,2048]{1,0:T(8,128)(2,1)}, u32[]{:S(2)}, u32[]{:S(2)}) collective-permute-start(bf16[320,2048]{1,0:T(8,128)(2,1)S(1)} %bitcast.64), channel_id=1, source_target_pairs={{0,1},{1,0},{2,3},{3,2},{4,5},{5,4},{6,7},{7,6},{8,9},{9,8},{10,11... | collective-permute-start | bytes 3932168 | tf_op jit(solution)/shard_map/ppermute | solution.py:1058
  194.6 60.6 %copy-start.21 = (f32[2048]{0:T(1024)}, f32[2048]{0:T(1024)S(1)}, u32[]{:S(2)}) copy-start(f32[2048]{0:T(1024)S(1)} %get-tuple-element.143) | copy-start | bytes 24580
  255.2 4.1 collective-permute-start.2
  255.5 5.4 collective-permute-start.4
  256.2 6.3 collective-permute-start.6
  262.7 67.8 %copy-start.6 = (bf16[2560,2048]{1,0:T(8,128)(2,1)}, bf16[2560,2048]{1,0:T(8,128)(2,1)S(1)}, u32[]{:S(2)}) copy-start(bf16[2560,2048]{1,0:T(8,128)(2,1)S(1)} %constant_dynamic-update-slice_fusion.grad_ref) | copy-start | bytes 31457284
  262.7 29.9 %collective-permute-start.8 = (bf16[320,2048]{1,0:T(8,128)(2,1)S(1)}, bf16[320,2048]{1,0:T(8,128)(2,1)S(1)}, u32[]{:S(2)}, u32[]{:S(2)}) collective-permute-start(bf16[320,2048]{1,0:T(8,128)(2,1)S(1)} %multiply_convert_fusion), channel_id=1, source_target_pairs={{0,2},{1,3},{2,0},{3,1},{4,6},{5,7},{6,4},{7,5},{8,10},{9,11},{10,... | collective-permute-start | bytes 3932168 | tf_op jit(solution)/shard_map/ppermute | solution.py:1058
  263.8 31.1 %collective-permute-start.10 = (bf16[320,2048]{1,0:T(8,128)(2,1)S(1)}, bf16[320,2048]{1,0:T(8,128)(2,1)S(1)}, u32[]{:S(2)}, u32[]{:S(2)}) collective-permute-start(bf16[320,2048]{1,0:T(8,128)(2,1)S(1)} %multiply_convert_fusion), channel_id=1, source_target_pairs={{0,4},{1,5},{2,6},{3,7},{4,0},{5,1},{6,2},{7,3},{8,12},{9,13},{10,... | collective-permute-start | bytes 3932168 | tf_op jit(solution)/shard_map/ppermute | solution.py:1058
  264.6 59.7 %collective-permute-start.12 = (bf16[320,2048]{1,0:T(8,128)(2,1)S(1)}, bf16[320,2048]{1,0:T(8,128)(2,1)S(1)}, u32[]{:S(2)}, u32[]{:S(2)}) collective-permute-start(bf16[320,2048]{1,0:T(8,128)(2,1)S(1)} %multiply_convert_fusion), channel_id=1, source_target_pairs={{0,6},{1,7},{2,4},{3,5},{4,2},{5,3},{6,0},{7,1},{8,14},{9,15},{10,... | collective-permute-start | bytes 3932168 | tf_op jit(solution)/shard_map/ppermute | solution.py:1058
  265.4 58.9 %collective-permute-start.7 = (bf16[320,2048]{1,0:T(8,128)(2,1)S(1)}, bf16[320,2048]{1,0:T(8,128)(2,1)S(1)}, u32[]{:S(2)}, u32[]{:S(2)}) collective-permute-start(bf16[320,2048]{1,0:T(8,128)(2,1)S(1)} %multiply_convert_fusion), channel_id=1, source_target_pairs={{0,1},{1,0},{2,3},{3,2},{4,5},{5,4},{6,7},{7,6},{8,9},{9,8},{10,11... | collective-permute-start | bytes 3932168 | tf_op jit(solution)/shard_map/ppermute | solution.py:1058
  292.6 34.2 %collective-permute-start.9 = (bf16[320,2048]{1,0:T(8,128)(2,1)S(1)}, bf16[320,2048]{1,0:T(8,128)(2,1)S(1)}, u32[]{:S(2)}, u32[]{:S(2)}) collective-permute-start(bf16[320,2048]{1,0:T(8,128)(2,1)S(1)} %collective-permute-done.8), channel_id=1, source_target_pairs={{0,1},{1,0},{2,3},{3,2},{4,5},{5,4},{6,7},{7,6},{8,9},{9,8},{10,11... | collective-permute-start | bytes 3932168 | tf_op jit(solution)/shard_map/ppermute | solution.py:1058
  294.9 34.4 %collective-permute-start.11 = (bf16[320,2048]{1,0:T(8,128)(2,1)S(1)}, bf16[320,2048]{1,0:T(8,128)(2,1)S(1)}, u32[]{:S(2)}, u32[]{:S(2)}) collective-permute-start(bf16[320,2048]{1,0:T(8,128)(2,1)S(1)} %collective-permute-done.10), channel_id=1, source_target_pairs={{0,1},{1,0},{2,3},{3,2},{4,5},{5,4},{6,7},{7,6},{8,9},{9,8},{10,11... | collective-permute-start | bytes 3932168 | tf_op jit(solution)/shard_map/ppermute | solution.py:1058
  324.3 7.4 collective-permute-start.13
  337.3 129.9 %reduce-scatter.5.cloned.1.call-start = ((), (), s32[]{:S(2)}) async-start(), calls=%async_computation.6 | async-start | bytes 5242880 | tf_op jit(solution)/shard_map/reduce_scatter | solution.py:1068
  389.2 227.9 %reduce-scatter.7.cloned.1.call-start = ((), (), s32[]{:S(2)}) async-start(), calls=%async_computation.7 | async-start | bytes 5242880 | tf_op jit(solution)/shard_map/reduce_scatter | solution.py:1068
  467.2 159.0 %reduce-scatter.11.cloned.1.call-start = ((), (), s32[]{:S(2)}) async-start(), calls=%async_computation.9 | async-start | bytes 5242880 | tf_op jit(solution)/shard_map/reduce_scatter | solution.py:1068
  467.8 332.8 %reduce-scatter.9.cloned.1.call-start = ((), (), s32[]{:S(2)}) async-start(), calls=%async_computation.8 | async-start | bytes 5242880 | tf_op jit(solution)/shard_map/reduce_scatter | solution.py:1068
  533.7 13.3 %collective-permute-start.17 = (bf16[320,2048]{1,0:T(8,128)(2,1)S(1)}, bf16[320,2048]{1,0:T(8,128)(2,1)S(1)}, u32[]{:S(2)}, u32[]{:S(2)}) collective-permute-start(bf16[320,2048]{1,0:T(8,128)(2,1)S(1)} %get-tuple-element.162), channel_id=1, source_target_pairs={{0,1},{1,0},{2,3},{3,2},{4,5},{5,4},{6,7},{7,6},{8,9},{9,8},{10,11... | collective-permute-start | bytes 3932168 | tf_op jit(solution)/shard_map/ppermute | solution.py:1058
  534.9 12.1 %collective-permute-start.16 = (bf16[320,2048]{1,0:T(8,128)(2,1)S(1)}, bf16[320,2048]{1,0:T(8,128)(2,1)S(1)}, u32[]{:S(2)}, u32[]{:S(2)}) collective-permute-start(bf16[320,2048]{1,0:T(8,128)(2,1)S(1)} %get-tuple-element.163), channel_id=1, source_target_pairs={{0,1},{1,0},{2,3},{3,2},{4,5},{5,4},{6,7},{7,6},{8,9},{9,8},{10,11... | collective-permute-start | bytes 3932168 | tf_op jit(solution)/shard_map/ppermute | solution.py:1058
  535.0 12.1 %collective-permute-start.15 = (bf16[320,2048]{1,0:T(8,128)(2,1)S(1)}, bf16[320,2048]{1,0:T(8,128)(2,1)S(1)}, u32[]{:S(2)}, u32[]{:S(2)}) collective-permute-start(bf16[320,2048]{1,0:T(8,128)(2,1)S(1)} %get-tuple-element.164), channel_id=1, source_target_pairs={{0,1},{1,0},{2,3},{3,2},{4,5},{5,4},{6,7},{7,6},{8,9},{9,8},{10,11... | collective-permute-start | bytes 3932168 | tf_op jit(solution)/shard_map/ppermute | solution.py:1058
  535.4 11.6 %collective-permute-start.14 = (bf16[320,2048]{1,0:T(8,128)(2,1)S(1)}, bf16[320,2048]{1,0:T(8,128)(2,1)S(1)}, u32[]{:S(2)}, u32[]{:S(2)}) collective-permute-start(bf16[320,2048]{1,0:T(8,128)(2,1)S(1)} %get-tuple-element.165), channel_id=1, source_target_pairs={{0,1},{1,0},{2,3},{3,2},{4,5},{5,4},{6,7},{7,6},{8,9},{9,8},{10,11... | collective-permute-start | bytes 3932168 | tf_op jit(solution)/shard_map/ppermute | solution.py:1058
  552.7 64.4 %collective-permute-start.18 = (bf16[320,2048]{1,0:T(8,128)(2,1)}, bf16[320,2048]{1,0:T(8,128)(2,1)}, u32[]{:S(2)}, u32[]{:S(2)}) collective-permute-start(bf16[320,2048]{1,0:T(8,128)(2,1)} %get-tuple-element.115), channel_id=1, source_target_pairs={{0,2},{1,3},{2,0},{3,1},{4,6},{5,7},{6,4},{7,5},{8,10},{9,11},{10,... | collective-permute-start | bytes 3932168 | tf_op jit(solution)/shard_map/ppermute | solution.py:1058
  553.9 63.2 %collective-permute-start.19 = (bf16[320,2048]{1,0:T(8,128)(2,1)}, bf16[320,2048]{1,0:T(8,128)(2,1)}, u32[]{:S(2)}, u32[]{:S(2)}) collective-permute-start(bf16[320,2048]{1,0:T(8,128)(2,1)} %get-tuple-element.116), channel_id=1, source_target_pairs={{0,4},{1,5},{2,6},{3,7},{4,0},{5,1},{6,2},{7,3},{8,12},{9,13},{10,... | collective-permute-start | bytes 3932168 | tf_op jit(solution)/shard_map/ppermute | solution.py:1058
  554.2 62.9 %collective-permute-start.20 = (bf16[320,2048]{1,0:T(8,128)(2,1)}, bf16[320,2048]{1,0:T(8,128)(2,1)}, u32[]{:S(2)}, u32[]{:S(2)}) collective-permute-start(bf16[320,2048]{1,0:T(8,128)(2,1)} %get-tuple-element.117), channel_id=1, source_target_pairs={{0,6},{1,7},{2,4},{3,5},{4,2},{5,3},{6,0},{7,1},{8,14},{9,15},{10,... | collective-permute-start | bytes 3932168 | tf_op jit(solution)/shard_map/ppermute | solution.py:1058
  626.2 154.5 %copy-start.16 = (f32[64,2048]{1,0:T(8,128)S(1)}, f32[64,2048]{1,0:T(8,128)}, u32[]{:S(2)}) copy-start(f32[64,2048]{1,0:T(8,128)} %param.26) | copy-start | bytes 1572868
  626.2 157.3 %copy-start.20 = (f32[64,4096]{1,0:T(8,128)S(1)}, f32[64,4096]{1,0:T(8,128)}, u32[]{:S(2)}) copy-start(f32[64,4096]{1,0:T(8,128)} %param.25) | copy-start | bytes 3145732
  (27 other events, 149.3 us)
Sparse Core Ops, SparseCore 0:
  184.5 152.8 all-gather.2
  338.9 45.1 all-gather.4
  389.3 77.8 reduce-scatter.4
  469.5 77.2 reduce-scatter.6
  548.9 77.2 reduce-scatter.10
  628.5 81.5 reduce-scatter.8

commit v10 on v9

--- a/solution.py
+++ b/solution.py
@@ -323,8 +323,7 @@
         if step == 1:
             relay(g)
             for offset in range(1, plane):
-                for part in (2, 0, 1, 3):
-                    swap_copy(offset, part).start()
+                swap_copy(offset, 2).start()
     for step in range(1, lines):
         take_rows(step)
         if step == lines - 1:
@@ -338,6 +337,10 @@
             finish(g)
         elif step < lines - 1:
             both(step - 1, finish)
+        if step == 1:
+            for offset in range(1, plane):
+                for part in (0, 1, 3):
+                    swap_copy(offset, part).start()
     for step in range(1, lines):
         for way in (0, 1):
 
@@ -1216,12 +1219,6 @@
             core_copy(turn, part).start()
             if turn < 2:
                 mine_copy(turn, part).start()
-        if turn == 0:
-            for step in range(1, plane):
-                for part in range(2):
-                    swap_copy(step, part).start()
-            for one in own_swap:
-                one.start()
     tile = 896 if width % 896 == 0 else 128
     halves = plane == 8
 
@@ -1307,6 +1304,12 @@
     for turn in range(1, lines):
         near_done(turn)
         line_done(turn - 1)
+        if turn == lines - 2:
+            for step in range(1, plane):
+                for part in range(2):
+                    swap_copy(step, part).start()
+            for one in own_swap:
+                one.start()
     line_done(lines - 1)
     for turn in range(lines - 1):
         line_copy(turn).wait_recv()

time: 829 us -> 815 us (0.983)
  Pallas kernels: 527 us -> 515 us
    pallas_call x1, Pallas kernels: 168 us -> 159 us  [gather_start(): pl.pallas_call(functools.partial(gather_kernel, lines, plane, prompt_rows...]
where the time goes in v10:
time: 815 us; the launch traced here: 803 us
  Pallas kernels  515 us (63%)
  matrix products  89.6 us (11%)
  other arithmetic  62.7 us (8%)
  starting transfers between devices  46.4 us (6%)
  waiting for transfers between devices  41.2 us (5%)
  local copies, waits for them, and re-layouts  32.6 us (4%)
  between operations  15.8 us (2%)
    pallas_call x1, Pallas kernels, gather_start(): pl.pallas_call(functools.partial(gather_kernel, lines, plane, prompt_rows...  159 us
    pallas_call x1, Pallas kernels, finish(): pl.pallas_call(functools.partial(finish_kernel, lines, plane), out_shape=...  150 us
    dot_general x5, matrix products, contract(): lax.dot_general(left, right, (((left_axis,), (right_axis,)), ((), ())), p...  62.9 us
    pallas_call x1, Pallas kernels, plane_back(): pl.pallas_call(functools.partial(plane_back_kernel, plane), out_shape=(ja...  62.7 us
    ppermute x21, starting transfers between devices, plane_swap(): return lax.ppermute(block, 'dp', [(i, i ^ offset) for i in range(size)])  45.6 us
    pallas_call x1, Pallas kernels, weights_back(): pl.pallas_call(weights_back_kernel, grid_spec=pltpu.PrefetchScalarGridSpe...  40.4 us
    pallas_call x1, Pallas kernels, forward_back(): pl.pallas_call(forward_back_kernel, grid=(count // rows,), in_specs=[bloc...  36.6 us
    pallas_call x1, Pallas kernels, project_heads(): pl.pallas_call(project_kernel, grid_spec=pltpu.PrefetchScalarGridSpec(num...  34.8 us
  transfers between devices with their start and end apart: 27, of which 4 were waited for; matrix products, arithmetic and copies ran while one was open for 20% of the time, Pallas kernels for 44%

profile of v10, /device:TPU:9, one launch (start us, length us, event | category | flops | bytes accessed | tf_op | source)
XLA Modules:
  0.0 803.1 jit_solution(539953936923725340)
XLA Ops:
  10.4 4.8 convert_element_type.114.forward_ref
  16.1 159.3 %gather_start.1 = (bf16[4,8,64,6272]{3,2,1,0:T(8,128)(2,1)}, bf16[4,256,2048]{2,1,0:T(8,128)(2,1)}, bf16[8,64,2048]{2,1,0:T(8,128)(2,1)}, bf16[4,8,64,512]{3,2,1,0:T(8,128)(2,1)}, bf16[8,64,512]{2,1,0:T(8,128)(2,1)}) custom-call(bf16[64,6272]{1,0:T(8,128)(2,1)} %fusion.31.weight_ref, bf16[320,2048]{1,0:T(8,128)(2,1)} %bitcast.52, ...), custom_call_target="tpu_custom_call" | custom-call | tf_op jit(solution)/shard_map/gather_start/pallas_call | solution.py:414
  178.2 4.2 collective-permute-start
  188.0 3.1 multiply_sine_fusion
  191.1 34.8 %project_heads.1 = (bf16[320,2048]{1,0:T(8,128)(2,1)}, bf16[1088,2048]{1,0:T(8,128)(2,1)}, bf16[1088,2048]{1,0:T(8,128)(2,1)}, bf16[320,2048]{1,0:T(8,128)(2,1)}, f32[1088,128]{1,0:T(8,128)}) custom-call(s32[1]{0:T(128)} %bitcast.1.place_ref, bf16[1024,2048]{1,0:T(8,128)(2,1)} %bitcast.55, bf16[320,2048]{1,0:T(8,128)(2,1)} %bitcast.53, ...), custom_call_target="tpu_custom_call" | custom-call | tf_op jit(solution)/shard_map/project_heads/pallas_call | solution.py:513
  227.8 11.4 %attend.1 = (bf16[320,2048]{1,0:T(8,128)(2,1)}, f32[320,1024]{1,0:T(8,128)}) custom-call(bf16[320,2048]{1,0:T(8,128)(2,1)} %get-tuple-element.81.query_ref, bf16[1088,2048]{1,0:T(8,128)(2,1)} %get-tuple-element.82.key_ref.value_ref, bf16[1088,2048]{1,0:T(8,128)(2,1)} %get-tuple-element.82.key_ref.value_ref, f32[320,1088]{1,0:T(8,128)} %add_convert_fusion.4.seen_ref), custom_call_target="tpu_custom_call" | custom-call | tf_op jit(solution)/shard_map/attend/pallas_call | solution.py:575
  239.2 5.9 multiply_reduce_fusion.2
  257.3 26.2 %collective-permute-done.8 = bf16[320,2048]{1,0:T(8,128)(2,1)S(1)} collective-permute-done((bf16[320,2048]{1,0:T(8,128)(2,1)S(1)}, bf16[320,2048]{1,0:T(8,128)(2,1)S(1)}, u32[]{:S(2)}, u32[]{:S(2)}) %collective-permute-start.8) | collective-permute-done | bytes 1310752 | tf_op jit(solution)/shard_map/ppermute | solution.py:1061
  285.5 27.6 %collective-permute-start.11 = (bf16[320,2048]{1,0:T(8,128)(2,1)S(1)}, bf16[320,2048]{1,0:T(8,128)(2,1)S(1)}, u32[]{:S(2)}, u32[]{:S(2)}) collective-permute-start(bf16[320,2048]{1,0:T(8,128)(2,1)S(1)} %collective-permute-done.10), channel_id=1, source_target_pairs={{0,1},{1,0},{2,3},{3,2},{4,5},{5,4},{6,7},{7,6},{8,9},{9,8},{10,11... | collective-permute-start | bytes 3932168 | tf_op jit(solution)/shard_map/ppermute | solution.py:1061
  322.9 3.4 all-gather.3.cloned.1.call-done.weight_ref
  326.6 26.7 %fusion.43.gate_up_ref = f32[2560,2048]{1,0:T(8,128)S(1)} fusion(bf16[2560,2048]{1,0:T(8,128)(2,1)} %constant_dynamic-update-slice_fusion.8, bf16[2048,2048]{1,0:T(8,128)(2,1)} %all-gather.3.cloned.1.call-done.weight_ref), kind=kOutput, calls=%fused_computation.106 | convolution fusion | flops 21474836480 | bytes 39845888 | tf_op jit(solution)/shard_map/dot_general | solution.py:1492
  353.3 3.6 fusion.activated_ref
  356.9 3.5 copy-done
  362.7 15.4 %convolution_convert_fusion = bf16[2048,1024]{1,0:T(8,128)(2,1)} fusion(bf16[2560,2048]{1,0:T(8,128)(2,1)} %copy-done.6, bf16[2560,1024]{1,0:T(8,128)(2,1)S(1)} %fusion.activated_ref), kind=kOutput, calls=%fused_computation.18 | convolution fusion | flops 10739515392 | bytes 19922944 | tf_op jit(solution)/shard_map/dot_general | solution.py:35
  378.6 36.6 %forward_back.1 = (bf16[2560,2048]{1,0:T(8,128)(2,1)}, bf16[2560,2048]{1,0:T(8,128)(2,1)}) custom-call(bf16[2560,1024]{1,0:T(8,128)(2,1)} %copy-done.5, bf16[2560,2048]{1,0:T(8,128)(2,1)} %copy-done.6, f32[2560,2048]{1,0:T(8,128)} %copy-done, bf16[2048,512]{1,0:T(8,128)(2,1)} %bitcast.66, bf16[2048,512]{1,0:T(8,128)(2,1)} %all-gather.5.cloned.1.call-done.second_ref), custom_call_target="tpu_custom_call" | custom-call | tf_op jit(solution)/shard_map/forward_back/pallas_call | solution.py:810
  415.3 16.8 %fusion.13 = bf16[2048,1024]{1,0:T(8,128)(2,1)} fusion(bf16[2560,2048]{1,0:T(8,128)(2,1)} %constant_dynamic-update-slice_fusion.8, bf16[2560,2048]{1,0:T(8,128)(2,1)} %get-tuple-element.95), kind=kOutput, calls=%fused_computation.20 | convolution fusion | flops 10739515392 | bytes 19922944 | tf_op jit(solution)/shard_map/dot_general | solution.py:35
  432.1 16.8 %fusion.10 = bf16[2048,1024]{1,0:T(8,128)(2,1)} fusion(bf16[2560,2048]{1,0:T(8,128)(2,1)} %constant_dynamic-update-slice_fusion.8, bf16[2560,2048]{1,0:T(8,128)(2,1)} %get-tuple-element.95), kind=kOutput, calls=%fused_computation.19 | convolution fusion | flops 10739515392 | bytes 19922944 | tf_op jit(solution)/shard_map/dot_general | solution.py:35
  448.9 7.3 reduce-scatter.5.cloned.1.call-done
  456.9 62.7 %plane_back.1 = (f32[320,2048]{1,0:T(8,128)}, bf16[64,8192]{1,0:T(8,128)(2,1)}) custom-call(bf16[8,320,2048]{2,1,0:T(8,128)(2,1)} %bitcast.57, bf16[2048,2048]{1,0:T(8,128)(2,1)} %all-gather.3.cloned.1.call-done.weight_ref, bf16[8,64,1024]{2,1,0:T(8,128)(2,1)} %bitcast.71), custom_call_target="tpu_custom_call" | custom-call | tf_op jit(solution)/shard_map/plane_back/pallas_call | solution.py:1026
  519.6 3.1 fusion.42
  525.7 2.4 fusion.41
  528.1 7.9 fusion.18.grad_ref
  536.0 5.6 add_convert_fusion.1
  544.3 19.3 %attend_back.1 = (bf16[320,2048]{1,0:T(8,128)(2,1)}, bf16[1088,2048]{1,0:T(8,128)(2,1)}) custom-call(s32[1]{0:T(128)} %bitcast.1.place_ref, bf16[320,2048]{1,0:T(8,128)(2,1)} %get-tuple-element.81.query_ref, bf16[1088,2048]{1,0:T(8,128)(2,1)} %get-tuple-element.82.key_ref.value_ref, bf16[1088,2048]{1,0:T(8,128)(2,1)} %get-tuple-element.82.key_ref.value_ref, ...), custom_call_target="tpu_custom_call" | custom-call | tf_op jit(solution)/shard_map/attend_back/pallas_call | solution.py:654
  563.7 40.4 %weights_back.1 = (bf16[2048,2048]{1,0:T(8,128)(2,1)}, bf16[2048,2048]{1,0:T(8,128)(2,1)}, bf16[2048,2048]{1,0:T(8,128)(2,1)}, f32[320,2048]{1,0:T(8,128)}, bf16...) custom-call(s32[1]{0:T(128)} %bitcast.1.place_ref, bf16[320,2048]{1,0:T(8,128)(2,1)} %get-tuple-element.108.query_ref, ...), custom_call_target="tpu_custom_call" | custom-call | tf_op jit(solution)/shard_map/weights_back/pallas_call | solution.py:733
  606.1 5.4 add_convert_fusion
  611.6 3.6 reduce-scatter.11.cloned.1.call-done
  615.2 150.3 %finish.1 = (f32[64,4096]{1,0:T(8,128)}, f32[64,2048]{1,0:T(8,128)}, f32[8,64]{1,0:T(8,128)}, bf16[64,24576]{1,0:T(8,128)(2,1)}) custom-call(bf16[4,4,2,64,2048]{4,3,2,1,0:T(8,128)(2,1)} %bitcast.58, bf16[4,4,2,64,2048]{4,3,2,1,0:T(8,128)(2,1)} %bitcast.59, bf16[4,4,2,64,2048]{4,3,2,1,0:T(8,128)(2,1)} %bitcast.60, bf16[4,4,2,64,128]{4,3,2,1,0:T(8,128)(2,1)} %bitcast.65, ...), custom_call_target="tpu_custom_call" | custom-call | tf_op jit(solution)/shard_map/finish/pallas_call | solution.py:1368
  766.3 2.8 add_multiply_fusion.3
  772.2 14.1 %add_multiply_fusion = (f32[64,24576]{1,0:T(8,128)}, f32[64,24576]{1,0:T(8,128)}, f32[64,24576]{1,0:T(8,128)}, f32[64,24576]{1,0:T(8,128)}) fusion(f32[64,24576]{1,0:T(8,128)} %param.29, f32[64,24576]{1,0:T(8,128)} %param.30, f32[64,24576]{1,0:T(8,128)} %param.31, bf16[64,24576]{1,0:T(8,128)(2,1)S(1)} %copy-done.15), kind=kLoop, calls=%fused_computation.8 | loop fusion | flops 23592960 | bytes 47185920 | tf_op jit(solution)/shard_map/mul | solution.py:81
  786.4 2.9 fusion.21
  789.9 4.1 fusion.25
  (172 shorter events, 55.2 us)
Async XLA Ops:
  7.2 319.1 %all-gather.3.cloned.1.call-start = ((), (), s32[]{:S(2)}) async-start(), calls=%async_computation.4 | async-start | bytes 10485760 | tf_op jit(solution)/shard_map/all_gather | solution.py:1447
  16.1 159.3 %copy-start.9 = (bf16[1,1,320,2048]{3,2,1,0:T(8,128)(2,1)S(1)}, bf16[1,1,320,2048]{3,2,1,0:T(8,128)(2,1)}, u32[]{:S(2)}) copy-start(bf16[1,1,320,2048]{3,2,1,0:T(8,128)(2,1)} %param.17) | copy-start | bytes 3932164
  175.4 202.8 %all-gather.5.cloned.1.call-start = ((), (), s32[]{:S(2)}) async-start(), calls=%async_computation.5 | async-start | bytes 2621440 | tf_op jit(solution)/shard_map/all_gather | solution.py:1452
  175.4 71.4 %collective-permute-start.5 = (bf16[320,2048]{1,0:T(8,128)(2,1)S(1)}, bf16[320,2048]{1,0:T(8,128)(2,1)}, u32[]{:S(2)}, u32[]{:S(2)}) collective-permute-start(bf16[320,2048]{1,0:T(8,128)(2,1)S(1)} %bitcast.61), channel_id=1, source_target_pairs={{0,6},{1,7},{2,4},{3,5},{4,2},{5,3},{6,0},{7,1},{8,14},{9,15},{10,... | collective-permute-start | bytes 3932168 | tf_op jit(solution)/shard_map/ppermute | solution.py:1061
  175.5 70.7 %collective-permute-start.3 = (bf16[320,2048]{1,0:T(8,128)(2,1)S(1)}, bf16[320,2048]{1,0:T(8,128)(2,1)}, u32[]{:S(2)}, u32[]{:S(2)}) collective-permute-start(bf16[320,2048]{1,0:T(8,128)(2,1)S(1)} %bitcast.62), channel_id=1, source_target_pairs={{0,4},{1,5},{2,6},{3,7},{4,0},{5,1},{6,2},{7,3},{8,12},{9,13},{10,... | collective-permute-start | bytes 3932168 | tf_op jit(solution)/shard_map/ppermute | solution.py:1061
  176.7 69.1 %collective-permute-start.1 = (bf16[320,2048]{1,0:T(8,128)(2,1)S(1)}, bf16[320,2048]{1,0:T(8,128)(2,1)}, u32[]{:S(2)}, u32[]{:S(2)}) collective-permute-start(bf16[320,2048]{1,0:T(8,128)(2,1)S(1)} %bitcast.63), channel_id=1, source_target_pairs={{0,2},{1,3},{2,0},{3,1},{4,6},{5,7},{6,4},{7,5},{8,10},{9,11},{10,... | collective-permute-start | bytes 3932168 | tf_op jit(solution)/shard_map/ppermute | solution.py:1061
  178.2 68.8 %collective-permute-start = (bf16[320,2048]{1,0:T(8,128)(2,1)S(1)}, bf16[320,2048]{1,0:T(8,128)(2,1)}, u32[]{:S(2)}, u32[]{:S(2)}) collective-permute-start(bf16[320,2048]{1,0:T(8,128)(2,1)S(1)} %bitcast.64), channel_id=1, source_target_pairs={{0,1},{1,0},{2,3},{3,2},{4,5},{5,4},{6,7},{7,6},{8,9},{9,8},{10,11... | collective-permute-start | bytes 3932168 | tf_op jit(solution)/shard_map/ppermute | solution.py:1061
  185.4 60.5 %copy-start.21 = (f32[2048]{0:T(1024)}, f32[2048]{0:T(1024)S(1)}, u32[]{:S(2)}) copy-start(f32[2048]{0:T(1024)S(1)} %get-tuple-element.143) | copy-start | bytes 24580
  245.8 4.2 collective-permute-start.2
  246.2 5.4 collective-permute-start.4
  246.8 6.4 collective-permute-start.6
  253.3 67.1 %copy-start.6 = (bf16[2560,2048]{1,0:T(8,128)(2,1)}, bf16[2560,2048]{1,0:T(8,128)(2,1)S(1)}, u32[]{:S(2)}) copy-start(bf16[2560,2048]{1,0:T(8,128)(2,1)S(1)} %constant_dynamic-update-slice_fusion.grad_ref) | copy-start | bytes 31457284
  253.4 30.1 %collective-permute-start.8 = (bf16[320,2048]{1,0:T(8,128)(2,1)S(1)}, bf16[320,2048]{1,0:T(8,128)(2,1)S(1)}, u32[]{:S(2)}, u32[]{:S(2)}) collective-permute-start(bf16[320,2048]{1,0:T(8,128)(2,1)S(1)} %multiply_convert_fusion), channel_id=1, source_target_pairs={{0,2},{1,3},{2,0},{3,1},{4,6},{5,7},{6,4},{7,5},{8,10},{9,11},{10,... | collective-permute-start | bytes 3932168 | tf_op jit(solution)/shard_map/ppermute | solution.py:1061
  253.8 31.7 %collective-permute-start.10 = (bf16[320,2048]{1,0:T(8,128)(2,1)S(1)}, bf16[320,2048]{1,0:T(8,128)(2,1)S(1)}, u32[]{:S(2)}, u32[]{:S(2)}) collective-permute-start(bf16[320,2048]{1,0:T(8,128)(2,1)S(1)} %multiply_convert_fusion), channel_id=1, source_target_pairs={{0,4},{1,5},{2,6},{3,7},{4,0},{5,1},{6,2},{7,3},{8,12},{9,13},{10,... | collective-permute-start | bytes 3932168 | tf_op jit(solution)/shard_map/ppermute | solution.py:1061
  253.9 60.5 %collective-permute-start.12 = (bf16[320,2048]{1,0:T(8,128)(2,1)S(1)}, bf16[320,2048]{1,0:T(8,128)(2,1)S(1)}, u32[]{:S(2)}, u32[]{:S(2)}) collective-permute-start(bf16[320,2048]{1,0:T(8,128)(2,1)S(1)} %multiply_convert_fusion), channel_id=1, source_target_pairs={{0,6},{1,7},{2,4},{3,5},{4,2},{5,3},{6,0},{7,1},{8,14},{9,15},{10,... | collective-permute-start | bytes 3932168 | tf_op jit(solution)/shard_map/ppermute | solution.py:1061
  256.1 58.3 %collective-permute-start.7 = (bf16[320,2048]{1,0:T(8,128)(2,1)S(1)}, bf16[320,2048]{1,0:T(8,128)(2,1)S(1)}, u32[]{:S(2)}, u32[]{:S(2)}) collective-permute-start(bf16[320,2048]{1,0:T(8,128)(2,1)S(1)} %multiply_convert_fusion), channel_id=1, source_target_pairs={{0,1},{1,0},{2,3},{3,2},{4,5},{5,4},{6,7},{7,6},{8,9},{9,8},{10,11... | collective-permute-start | bytes 3932168 | tf_op jit(solution)/shard_map/ppermute | solution.py:1061
  283.5 33.3 %collective-permute-start.9 = (bf16[320,2048]{1,0:T(8,128)(2,1)S(1)}, bf16[320,2048]{1,0:T(8,128)(2,1)S(1)}, u32[]{:S(2)}, u32[]{:S(2)}) collective-permute-start(bf16[320,2048]{1,0:T(8,128)(2,1)S(1)} %collective-permute-done.8), channel_id=1, source_target_pairs={{0,1},{1,0},{2,3},{3,2},{4,5},{5,4},{6,7},{7,6},{8,9},{9,8},{10,11... | collective-permute-start | bytes 3932168 | tf_op jit(solution)/shard_map/ppermute | solution.py:1061
  285.5 33.8 %collective-permute-start.11 = (bf16[320,2048]{1,0:T(8,128)(2,1)S(1)}, bf16[320,2048]{1,0:T(8,128)(2,1)S(1)}, u32[]{:S(2)}, u32[]{:S(2)}) collective-permute-start(bf16[320,2048]{1,0:T(8,128)(2,1)S(1)} %collective-permute-done.10), channel_id=1, source_target_pairs={{0,1},{1,0},{2,3},{3,2},{4,5},{5,4},{6,7},{7,6},{8,9},{9,8},{10,11... | collective-permute-start | bytes 3932168 | tf_op jit(solution)/shard_map/ppermute | solution.py:1061
  314.3 7.4 collective-permute-start.13
  326.3 129.9 %reduce-scatter.5.cloned.1.call-start = ((), (), s32[]{:S(2)}) async-start(), calls=%async_computation.6 | async-start | bytes 5242880 | tf_op jit(solution)/shard_map/reduce_scatter | solution.py:1071
  378.2 227.9 %reduce-scatter.7.cloned.1.call-start = ((), (), s32[]{:S(2)}) async-start(), calls=%async_computation.7 | async-start | bytes 5242880 | tf_op jit(solution)/shard_map/reduce_scatter | solution.py:1071
  456.2 159.0 %reduce-scatter.11.cloned.1.call-start = ((), (), s32[]{:S(2)}) async-start(), calls=%async_computation.9 | async-start | bytes 5242880 | tf_op jit(solution)/shard_map/reduce_scatter | solution.py:1071
  456.8 329.5 %reduce-scatter.9.cloned.1.call-start = ((), (), s32[]{:S(2)}) async-start(), calls=%async_computation.8 | async-start | bytes 5242880 | tf_op jit(solution)/shard_map/reduce_scatter | solution.py:1071
  522.7 13.3 %collective-permute-start.17 = (bf16[320,2048]{1,0:T(8,128)(2,1)S(1)}, bf16[320,2048]{1,0:T(8,128)(2,1)S(1)}, u32[]{:S(2)}, u32[]{:S(2)}) collective-permute-start(bf16[320,2048]{1,0:T(8,128)(2,1)S(1)} %get-tuple-element.162), channel_id=1, source_target_pairs={{0,1},{1,0},{2,3},{3,2},{4,5},{5,4},{6,7},{7,6},{8,9},{9,8},{10,11... | collective-permute-start | bytes 3932168 | tf_op jit(solution)/shard_map/ppermute | solution.py:1061
  523.9 12.1 %collective-permute-start.16 = (bf16[320,2048]{1,0:T(8,128)(2,1)S(1)}, bf16[320,2048]{1,0:T(8,128)(2,1)S(1)}, u32[]{:S(2)}, u32[]{:S(2)}) collective-permute-start(bf16[320,2048]{1,0:T(8,128)(2,1)S(1)} %get-tuple-element.163), channel_id=1, source_target_pairs={{0,1},{1,0},{2,3},{3,2},{4,5},{5,4},{6,7},{7,6},{8,9},{9,8},{10,11... | collective-permute-start | bytes 3932168 | tf_op jit(solution)/shard_map/ppermute | solution.py:1061
  524.0 12.1 %collective-permute-start.15 = (bf16[320,2048]{1,0:T(8,128)(2,1)S(1)}, bf16[320,2048]{1,0:T(8,128)(2,1)S(1)}, u32[]{:S(2)}, u32[]{:S(2)}) collective-permute-start(bf16[320,2048]{1,0:T(8,128)(2,1)S(1)} %get-tuple-element.164), channel_id=1, source_target_pairs={{0,1},{1,0},{2,3},{3,2},{4,5},{5,4},{6,7},{7,6},{8,9},{9,8},{10,11... | collective-permute-start | bytes 3932168 | tf_op jit(solution)/shard_map/ppermute | solution.py:1061
  524.4 11.6 %collective-permute-start.14 = (bf16[320,2048]{1,0:T(8,128)(2,1)S(1)}, bf16[320,2048]{1,0:T(8,128)(2,1)S(1)}, u32[]{:S(2)}, u32[]{:S(2)}) collective-permute-start(bf16[320,2048]{1,0:T(8,128)(2,1)S(1)} %get-tuple-element.165), channel_id=1, source_target_pairs={{0,1},{1,0},{2,3},{3,2},{4,5},{5,4},{6,7},{7,6},{8,9},{9,8},{10,11... | collective-permute-start | bytes 3932168 | tf_op jit(solution)/shard_map/ppermute | solution.py:1061
  541.7 64.4 %collective-permute-start.18 = (bf16[320,2048]{1,0:T(8,128)(2,1)}, bf16[320,2048]{1,0:T(8,128)(2,1)}, u32[]{:S(2)}, u32[]{:S(2)}) collective-permute-start(bf16[320,2048]{1,0:T(8,128)(2,1)} %get-tuple-element.115), channel_id=1, source_target_pairs={{0,2},{1,3},{2,0},{3,1},{4,6},{5,7},{6,4},{7,5},{8,10},{9,11},{10,... | collective-permute-start | bytes 3932168 | tf_op jit(solution)/shard_map/ppermute | solution.py:1061
  542.9 63.2 %collective-permute-start.19 = (bf16[320,2048]{1,0:T(8,128)(2,1)}, bf16[320,2048]{1,0:T(8,128)(2,1)}, u32[]{:S(2)}, u32[]{:S(2)}) collective-permute-start(bf16[320,2048]{1,0:T(8,128)(2,1)} %get-tuple-element.116), channel_id=1, source_target_pairs={{0,4},{1,5},{2,6},{3,7},{4,0},{5,1},{6,2},{7,3},{8,12},{9,13},{10,... | collective-permute-start | bytes 3932168 | tf_op jit(solution)/shard_map/ppermute | solution.py:1061
  543.2 62.9 %collective-permute-start.20 = (bf16[320,2048]{1,0:T(8,128)(2,1)}, bf16[320,2048]{1,0:T(8,128)(2,1)}, u32[]{:S(2)}, u32[]{:S(2)}) collective-permute-start(bf16[320,2048]{1,0:T(8,128)(2,1)} %get-tuple-element.117), channel_id=1, source_target_pairs={{0,6},{1,7},{2,4},{3,5},{4,2},{5,3},{6,0},{7,1},{8,14},{9,15},{10,... | collective-permute-start | bytes 3932168 | tf_op jit(solution)/shard_map/ppermute | solution.py:1061
  615.2 151.1 %copy-start.16 = (f32[64,2048]{1,0:T(8,128)S(1)}, f32[64,2048]{1,0:T(8,128)}, u32[]{:S(2)}) copy-start(f32[64,2048]{1,0:T(8,128)} %param.26) | copy-start | bytes 1572868
  615.2 154.0 %copy-start.20 = (f32[64,4096]{1,0:T(8,128)S(1)}, f32[64,4096]{1,0:T(8,128)}, u32[]{:S(2)}) copy-start(f32[64,4096]{1,0:T(8,128)} %param.25) | copy-start | bytes 3145732
  (27 other events, 149.2 us)
Sparse Core Ops, SparseCore 0:
  175.5 150.7 all-gather.2
  327.9 45.1 all-gather.4
  378.3 77.8 reduce-scatter.4
  458.4 77.2 reduce-scatter.6
  537.9 77.2 reduce-scatter.10
  617.4 115.5 reduce-scatter.8

commit v11 on v10

--- a/solution.py
+++ b/solution.py
@@ -1079,7 +1079,6 @@
     merge_ref,
     gain_ref,
     gate_ref,
-    up_ref,
     down_ref,
     a_out,
     m_out,
@@ -1108,7 +1107,7 @@
     chips = plane // 2
     chip, core = lax.div(d, 2), lax.rem(d, 2)
     partner = d + 1 - 2 * core
-    own_hidden = gate_ref.shape[2]
+    own_hidden = gate_ref.shape[2] // 2
     width = core_in.shape[3]
     a_width, m_width = a_out.shape[1], m_out.shape[1]
     parts, begin = [], 0
@@ -1193,7 +1192,8 @@
             (line, d),
         )
 
-    forward_refs = (gate_ref, up_ref)
+    def swap_source(owner, part):
+        return gate_ref.at[owner, :, pl.ds(part * own_hidden, own_hidden)]
 
     def swap_place(part):
         return f_out.at[:, pl.ds(part * FF + d * own_hidden, own_hidden)]
@@ -1201,7 +1201,7 @@
     def swap_copy(step, part):
         there = lax.rem(d + step, plane)
         return remote(
-            forward_refs[part].at[there],
+            swap_source(there, part),
             swap_place(part),
             swap_send.at[step, part],
             swap_recv.at[step, part],
@@ -1209,7 +1209,7 @@
         )
 
     own_swap = [
-        pltpu.make_async_copy(forward_refs[part].at[d], swap_place(part), own_sem.at[part])
+        pltpu.make_async_copy(swap_source(d, part), swap_place(part), own_sem.at[part])
         for part in range(2)
     ] + [pltpu.make_async_copy(down_ref, f_out.at[:, pl.ds(2 * FF, FF)], own_sem.at[2])]
 
@@ -1355,7 +1355,7 @@
         one.wait()
 
 
-def finish(terms, gate_part, up_part, down_swapped):
+def finish(terms, gate_part, down_swapped):
     lines, plane = lax.axis_size("grp"), lax.axis_size("dp")
     chips = plane // 2
     rows = D // (lines * plane)
@@ -1373,7 +1373,7 @@
             jax.ShapeDtypeStruct((8, rows), FULL),
             jax.ShapeDtypeStruct((rows, 3 * FF), LOW),
         ),
-        in_specs=[anywhere] * 7,
+        in_specs=[anywhere] * 6,
         out_specs=(anywhere,) * 4,
         scratch_shapes=[
             vmem((2, chips, rows, width), LOW),
@@ -1401,7 +1401,6 @@
     )(
         *(term.reshape(lines, chips, 2, rows, term.shape[1]) for term in terms),
         gate_part.reshape(plane, rows, -1),
-        up_part.reshape(plane, rows, -1),
         down_swapped,
     )
 
@@ -1499,13 +1498,11 @@
         row_count, activated, down_grad, gate_up, first_down, second_down
     )
     down_part = line_scatter(down_term)
-    gate_term = contract(normed_all, gate_up_grad[:, :own_hidden], 0, 0).astype(LOW)
-    up_term = contract(normed_all, gate_up_grad[:, own_hidden:], 0, 0).astype(LOW)
-    gate_up_grad, gate_term, up_term, down_part = lax.optimization_barrier(
-        (gate_up_grad, gate_term, up_term, down_part)
+    gate_term = contract(normed_all, gate_up_grad, 0, 0).astype(LOW)
+    gate_up_grad, gate_term, down_part = lax.optimization_barrier(
+        (gate_up_grad, gate_term, down_part)
     )
     gate_part = line_scatter(gate_term)
-    up_part = line_scatter(up_term)
     normed_two_grad, down_swapped = plane_back(
         row_count, gate_up_grad, gate_weight, down_part.reshape(dp_size, own_rows, own_hidden)
     )
@@ -1542,7 +1539,9 @@
     gain_term = jnp.pad(
         jnp.stack([gain_one_part[0], gain_two_part], axis=1), ((0, 0), (0, GAIN_PAD - 2))
     )
-    pair_back, up_part, out_arrived = lax.optimization_barrier((pair_back, up_part, out_arrived))
+    pair_back, gate_part, out_arrived = lax.optimization_barrier(
+        (pair_back, gate_part, out_arrived)
+    )
     result = middle + out_sums[0]
     for one in out_arrived:
         result = result + one.astype(FULL)
@@ -1552,7 +1551,6 @@
     attention_grad, merge_grad, gain_sums, forward_low = finish(
         (query_term, pair_term, merge_term, gain_term.astype(LOW)),
         gate_part,
-        up_part,
         down_swapped,
     )
     gain_grad = gain_sums[:2]

time: 815 us -> 804 us (0.987)
    dot_general x5 -> x4, matrix products: 62.9 us -> 58.2 us  [contract(): lax.dot_general(left, right, (((left_axis,), (right_axis,)), ((), ())), p...]
    unnamed x81 -> x61, local copies, waits for them, and re-layouts: 24.2 us -> 24.2 us
  transfers between devices with their start and end apart: 27 -> 26, of which waited for: 4 -> 3; matrix products, arithmetic and copies ran while one was open for 20% -> 20% of each run, Pallas kernels for 44% -> 44%
where the time goes in v11:
time: 804 us; the launch traced here: 791 us
  Pallas kernels  507 us (63%)
  matrix products  84.9 us (11%)
  other arithmetic  64 us (8%)
  starting transfers between devices  46.6 us (6%)
  waiting for transfers between devices  41.2 us (5%)
  local copies, waits for them, and re-layouts  32.7 us (4%)
  between operations  15.4 us (2%)
    pallas_call x1, Pallas kernels, gather_start(): pl.pallas_call(functools.partial(gather_kernel, lines, plane, prompt_rows...  159 us
    pallas_call x1, Pallas kernels, finish(): pl.pallas_call(functools.partial(finish_kernel, lines, plane), out_shape=...  143 us
    pallas_call x1, Pallas kernels, plane_back(): pl.pallas_call(functools.partial(plane_back_kernel, plane), out_shape=(ja...  62.8 us
    dot_general x4, matrix products, contract(): lax.dot_general(left, right, (((left_axis,), (right_axis,)), ((), ())), p...  58.2 us
    ppermute x21, starting transfers between devices, plane_swap(): return lax.ppermute(block, 'dp', [(i, i ^ offset) for i in range(size)])  45.6 us
    pallas_call x1, Pallas kernels, weights_back(): pl.pallas_call(weights_back_kernel, grid_spec=pltpu.PrefetchScalarGridSpe...  40.4 us
    pallas_call x1, Pallas kernels, forward_back(): pl.pallas_call(forward_back_kernel, grid=(count // rows,), in_specs=[bloc...  36.6 us
    pallas_call x1, Pallas kernels, project_heads(): pl.pallas_call(project_kernel, grid_spec=pltpu.PrefetchScalarGridSpec(num...  34.8 us
  transfers between devices with their start and end apart: 26, of which 3 were waited for; matrix products, arithmetic and copies ran while one was open for 20% of the time, Pallas kernels for 44%

profile of v11, /device:TPU:9, one launch (start us, length us, event | category | flops | bytes accessed | tf_op | source)
XLA Modules:
  0.0 791.5 jit_solution(16365682936655207216)
XLA Ops:
  10.4 4.8 convert_element_type.111.forward_ref
  16.1 159.3 %gather_start.1 = (bf16[4,8,64,6272]{3,2,1,0:T(8,128)(2,1)}, bf16[4,256,2048]{2,1,0:T(8,128)(2,1)}, bf16[8,64,2048]{2,1,0:T(8,128)(2,1)}, bf16[4,8,64,512]{3,2,1,0:T(8,128)(2,1)}, bf16[8,64,512]{2,1,0:T(8,128)(2,1)}) custom-call(bf16[64,6272]{1,0:T(8,128)(2,1)} %fusion.21.weight_ref, bf16[320,2048]{1,0:T(8,128)(2,1)} %bitcast.51, ...), custom_call_target="tpu_custom_call" | custom-call | tf_op jit(solution)/shard_map/gather_start/pallas_call | solution.py:414
  178.1 4.2 collective-permute-start
  187.9 3.1 multiply_sine_fusion
  191.1 34.8 %project_heads.1 = (bf16[320,2048]{1,0:T(8,128)(2,1)}, bf16[1088,2048]{1,0:T(8,128)(2,1)}, bf16[1088,2048]{1,0:T(8,128)(2,1)}, bf16[320,2048]{1,0:T(8,128)(2,1)}, f32[1088,128]{1,0:T(8,128)}) custom-call(s32[1]{0:T(128)} %bitcast.1.place_ref, bf16[1024,2048]{1,0:T(8,128)(2,1)} %bitcast.54, bf16[320,2048]{1,0:T(8,128)(2,1)} %bitcast.52, ...), custom_call_target="tpu_custom_call" | custom-call | tf_op jit(solution)/shard_map/project_heads/pallas_call | solution.py:513
  227.8 11.4 %attend.1 = (bf16[320,2048]{1,0:T(8,128)(2,1)}, f32[320,1024]{1,0:T(8,128)}) custom-call(bf16[320,2048]{1,0:T(8,128)(2,1)} %get-tuple-element.80.query_ref, bf16[1088,2048]{1,0:T(8,128)(2,1)} %get-tuple-element.81.key_ref.value_ref, bf16[1088,2048]{1,0:T(8,128)(2,1)} %get-tuple-element.81.key_ref.value_ref, f32[320,1088]{1,0:T(8,128)} %add_convert_fusion.4.seen_ref), custom_call_target="tpu_custom_call" | custom-call | tf_op jit(solution)/shard_map/attend/pallas_call | solution.py:575
  239.1 5.9 multiply_reduce_fusion.2
  258.0 26.2 %collective-permute-done.8 = bf16[320,2048]{1,0:T(8,128)(2,1)S(1)} collective-permute-done((bf16[320,2048]{1,0:T(8,128)(2,1)S(1)}, bf16[320,2048]{1,0:T(8,128)(2,1)S(1)}, u32[]{:S(2)}, u32[]{:S(2)}) %collective-permute-start.8) | collective-permute-done | bytes 1310752 | tf_op jit(solution)/shard_map/ppermute | solution.py:1061
  286.2 27.6 %collective-permute-start.11 = (bf16[320,2048]{1,0:T(8,128)(2,1)S(1)}, bf16[320,2048]{1,0:T(8,128)(2,1)S(1)}, u32[]{:S(2)}, u32[]{:S(2)}) collective-permute-start(bf16[320,2048]{1,0:T(8,128)(2,1)S(1)} %collective-permute-done.10), channel_id=1, source_target_pairs={{0,1},{1,0},{2,3},{3,2},{4,5},{5,4},{6,7},{7,6},{8,9},{9,8},{10,11... | collective-permute-start | bytes 3932168 | tf_op jit(solution)/shard_map/ppermute | solution.py:1061
  323.6 2.7 all-gather.3.cloned.1.call-done.weight_ref
  326.6 26.7 %fusion.33.gate_up_ref = f32[2560,2048]{1,0:T(8,128)S(1)} fusion(bf16[2560,2048]{1,0:T(8,128)(2,1)} %constant_dynamic-update-slice_fusion.8, bf16[2048,2048]{1,0:T(8,128)(2,1)} %all-gather.3.cloned.1.call-done.weight_ref), kind=kOutput, calls=%fused_computation.101 | convolution fusion | flops 21474836480 | bytes 39845888 | tf_op jit(solution)/shard_map/dot_general | solution.py:1491
  353.3 3.6 fusion.activated_ref
  356.9 3.5 copy-done
  360.4 2.4 copy-done.3
  362.7 15.4 %convolution_convert_fusion.1 = bf16[2048,1024]{1,0:T(8,128)(2,1)} fusion(bf16[2560,2048]{1,0:T(8,128)(2,1)} %copy-done.4, bf16[2560,1024]{1,0:T(8,128)(2,1)S(1)} %fusion.activated_ref), kind=kOutput, calls=%fused_computation.15 | convolution fusion | flops 10739515392 | bytes 19922944 | tf_op jit(solution)/shard_map/dot_general | solution.py:35
  378.6 36.6 %forward_back.1 = (bf16[2560,2048]{1,0:T(8,128)(2,1)}, bf16[2560,2048]{1,0:T(8,128)(2,1)}) custom-call(bf16[2560,1024]{1,0:T(8,128)(2,1)} %copy-done.3, bf16[2560,2048]{1,0:T(8,128)(2,1)} %copy-done.4, f32[2560,2048]{1,0:T(8,128)} %copy-done, bf16[2048,512]{1,0:T(8,128)(2,1)} %bitcast.61, bf16[2048,512]{1,0:T(8,128)(2,1)} %all-gather.5.cloned.1.call-done.second_ref), custom_call_target="tpu_custom_call" | custom-call | tf_op jit(solution)/shard_map/forward_back/pallas_call | solution.py:810
  415.2 28.8 %convolution_convert_fusion = bf16[2048,2048]{1,0:T(8,128)(2,1)} fusion(bf16[2560,2048]{1,0:T(8,128)(2,1)} %constant_dynamic-update-slice_fusion.8, bf16[2560,2048]{1,0:T(8,128)(2,1)} %get-tuple-element.94), kind=kOutput, calls=%fused_computation.3 | convolution fusion | flops 21479030784 | bytes 29360128 | tf_op jit(solution)/shard_map/dot_general | solution.py:35
  444.0 12.2 %reduce-scatter.4.cloned.1.call-done = bf16[512,1024]{1,0:T(8,128)(2,1)} async-done(((bf16[2048,1024]{1,0:T(8,128)(2,1)}), bf16[512,1024]{1,0:T(8,128)(2,1)}) %reduce-scatter.4.cloned.1.call-update) | async-done | bytes 1048592 | tf_op jit(solution)/shard_map/reduce_scatter | solution.py:1071
  456.4 62.8 %plane_back.1 = (f32[320,2048]{1,0:T(8,128)}, bf16[64,8192]{1,0:T(8,128)(2,1)}) custom-call(bf16[8,320,2048]{2,1,0:T(8,128)(2,1)} %bitcast.56, bf16[2048,2048]{1,0:T(8,128)(2,1)} %all-gather.3.cloned.1.call-done.weight_ref, bf16[8,64,1024]{2,1,0:T(8,128)(2,1)} %bitcast.65), custom_call_target="tpu_custom_call" | custom-call | tf_op jit(solution)/shard_map/plane_back/pallas_call | solution.py:1026
  519.2 3.1 fusion.32
  524.8 3.7 fusion.31
  528.5 8.1 %fusion.8.grad_ref = bf16[320,2048]{1,0:T(8,128)(2,1)} fusion(bf16[320,2048]{1,0:T(8,128)(2,1)S(1)} %get-tuple-element.155.branch_ref, bf16[2048,6272]{1,0:T(8,128)(2,1)} %bitcast.48), kind=kOutput, calls=%fused_computation.16 | convolution fusion | flops 2685009920 | bytes 11010048 | tf_op jit(solution)/shard_map/dot_general | solution.py:35
  536.6 5.1 add_convert_fusion.1
  544.4 18.8 %attend_back.1 = (bf16[320,2048]{1,0:T(8,128)(2,1)}, bf16[1088,2048]{1,0:T(8,128)(2,1)}) custom-call(s32[1]{0:T(128)} %bitcast.1.place_ref, bf16[320,2048]{1,0:T(8,128)(2,1)} %get-tuple-element.80.query_ref, bf16[1088,2048]{1,0:T(8,128)(2,1)} %get-tuple-element.81.key_ref.value_ref, bf16[1088,2048]{1,0:T(8,128)(2,1)} %get-tuple-element.81.key_ref.value_ref, ...), custom_call_target="tpu_custom_call" | custom-call | tf_op jit(solution)/shard_map/attend_back/pallas_call | solution.py:654
  563.2 40.4 %weights_back.1 = (bf16[2048,2048]{1,0:T(8,128)(2,1)}, bf16[2048,2048]{1,0:T(8,128)(2,1)}, bf16[2048,2048]{1,0:T(8,128)(2,1)}, f32[320,2048]{1,0:T(8,128)}, bf16...) custom-call(s32[1]{0:T(128)} %bitcast.1.place_ref, bf16[320,2048]{1,0:T(8,128)(2,1)} %get-tuple-element.107.query_ref, ...), custom_call_target="tpu_custom_call" | custom-call | tf_op jit(solution)/shard_map/weights_back/pallas_call | solution.py:733
  605.6 5.4 add_convert_fusion
  611.1 142.7 %finish.1 = (f32[64,4096]{1,0:T(8,128)}, f32[64,2048]{1,0:T(8,128)}, f32[8,64]{1,0:T(8,128)}, bf16[64,24576]{1,0:T(8,128)(2,1)}) custom-call(bf16[4,4,2,64,2048]{4,3,2,1,0:T(8,128)(2,1)} %bitcast.57, bf16[4,4,2,64,2048]{4,3,2,1,0:T(8,128)(2,1)} %bitcast.58, bf16[4,4,2,64,2048]{4,3,2,1,0:T(8,128)(2,1)} %bitcast.59, bf16[4,4,2,64,128]{4,3,2,1,0:T(8,128)(2,1)} %bitcast.60, ...), custom_call_target="tpu_custom_call" | custom-call | tf_op jit(solution)/shard_map/finish/pallas_call | solution.py:1368
  754.6 2.6 add_multiply_fusion.3
  757.3 3.5 add_multiply_fusion.2
  760.9 14.1 %add_multiply_fusion = (f32[64,24576]{1,0:T(8,128)}, f32[64,24576]{1,0:T(8,128)}, f32[64,24576]{1,0:T(8,128)}, f32[64,24576]{1,0:T(8,128)}) fusion(f32[64,24576]{1,0:T(8,128)} %param.29, f32[64,24576]{1,0:T(8,128)} %param.30, f32[64,24576]{1,0:T(8,128)} %param.31, bf16[64,24576]{1,0:T(8,128)(2,1)S(1)} %copy-done.11), kind=kLoop, calls=%fused_computation.9 | loop fusion | flops 23592960 | bytes 47185920 | tf_op jit(solution)/shard_map/mul | solution.py:81
  775.0 2.9 fusion.11
  778.6 4.1 fusion.15
  (148 shorter events, 49.7 us)
Async XLA Ops:
  7.2 319.1 %all-gather.3.cloned.1.call-start = ((), (), s32[]{:S(2)}) async-start(), calls=%async_computation.3 | async-start | bytes 10485760 | tf_op jit(solution)/shard_map/all_gather | solution.py:1446
  175.4 202.7 %all-gather.5.cloned.1.call-start = ((), (), s32[]{:S(2)}) async-start(), calls=%async_computation.4 | async-start | bytes 2621440 | tf_op jit(solution)/shard_map/all_gather | solution.py:1451
  175.4 72.1 %collective-permute-start.5 = (bf16[320,2048]{1,0:T(8,128)(2,1)}, bf16[320,2048]{1,0:T(8,128)(2,1)}, u32[]{:S(2)}, u32[]{:S(2)}) collective-permute-start(bf16[320,2048]{1,0:T(8,128)(2,1)} %bitcast.9), channel_id=1, source_target_pairs={{0,6},{1,7},{2,4},{3,5},{4,2},{5,3},{6,0},{7,1},{8,14},{9,15},{10,... | collective-permute-start | bytes 3932168 | tf_op jit(solution)/shard_map/ppermute | solution.py:1061
  175.5 70.1 %collective-permute-start.3 = (bf16[320,2048]{1,0:T(8,128)(2,1)}, bf16[320,2048]{1,0:T(8,128)(2,1)}, u32[]{:S(2)}, u32[]{:S(2)}) collective-permute-start(bf16[320,2048]{1,0:T(8,128)(2,1)} %bitcast.9), channel_id=1, source_target_pairs={{0,4},{1,5},{2,6},{3,7},{4,0},{5,1},{6,2},{7,3},{8,12},{9,13},{10,... | collective-permute-start | bytes 3932168 | tf_op jit(solution)/shard_map/ppermute | solution.py:1061
  176.6 68.5 %collective-permute-start.1 = (bf16[320,2048]{1,0:T(8,128)(2,1)}, bf16[320,2048]{1,0:T(8,128)(2,1)}, u32[]{:S(2)}, u32[]{:S(2)}) collective-permute-start(bf16[320,2048]{1,0:T(8,128)(2,1)} %bitcast.9), channel_id=1, source_target_pairs={{0,2},{1,3},{2,0},{3,1},{4,6},{5,7},{6,4},{7,5},{8,10},{9,11},{10,... | collective-permute-start | bytes 3932168 | tf_op jit(solution)/shard_map/ppermute | solution.py:1061
  178.1 69.6 %collective-permute-start = (bf16[320,2048]{1,0:T(8,128)(2,1)}, bf16[320,2048]{1,0:T(8,128)(2,1)}, u32[]{:S(2)}, u32[]{:S(2)}) collective-permute-start(bf16[320,2048]{1,0:T(8,128)(2,1)} %bitcast.9), channel_id=1, source_target_pairs={{0,1},{1,0},{2,3},{3,2},{4,5},{5,4},{6,7},{7,6},{8,9},{9,8},{10,11... | collective-permute-start | bytes 3932168 | tf_op jit(solution)/shard_map/ppermute | solution.py:1061
  245.1 5.5 collective-permute-start.2
  245.6 6.7 collective-permute-start.4
  247.5 6.4 collective-permute-start.6
  254.0 67.2 %copy-start.4 = (bf16[2560,2048]{1,0:T(8,128)(2,1)}, bf16[2560,2048]{1,0:T(8,128)(2,1)S(1)}, u32[]{:S(2)}) copy-start(bf16[2560,2048]{1,0:T(8,128)(2,1)S(1)} %constant_dynamic-update-slice_fusion.grad_ref) | copy-start | bytes 31457284
  254.1 30.1 %collective-permute-start.8 = (bf16[320,2048]{1,0:T(8,128)(2,1)S(1)}, bf16[320,2048]{1,0:T(8,128)(2,1)S(1)}, u32[]{:S(2)}, u32[]{:S(2)}) collective-permute-start(bf16[320,2048]{1,0:T(8,128)(2,1)S(1)} %multiply_convert_fusion), channel_id=1, source_target_pairs={{0,2},{1,3},{2,0},{3,1},{4,6},{5,7},{6,4},{7,5},{8,10},{9,11},{10,... | collective-permute-start | bytes 3932168 | tf_op jit(solution)/shard_map/ppermute | solution.py:1061
  254.5 31.7 %collective-permute-start.10 = (bf16[320,2048]{1,0:T(8,128)(2,1)S(1)}, bf16[320,2048]{1,0:T(8,128)(2,1)S(1)}, u32[]{:S(2)}, u32[]{:S(2)}) collective-permute-start(bf16[320,2048]{1,0:T(8,128)(2,1)S(1)} %multiply_convert_fusion), channel_id=1, source_target_pairs={{0,4},{1,5},{2,6},{3,7},{4,0},{5,1},{6,2},{7,3},{8,12},{9,13},{10,... | collective-permute-start | bytes 3932168 | tf_op jit(solution)/shard_map/ppermute | solution.py:1061
  254.5 60.5 %collective-permute-start.12 = (bf16[320,2048]{1,0:T(8,128)(2,1)S(1)}, bf16[320,2048]{1,0:T(8,128)(2,1)S(1)}, u32[]{:S(2)}, u32[]{:S(2)}) collective-permute-start(bf16[320,2048]{1,0:T(8,128)(2,1)S(1)} %multiply_convert_fusion), channel_id=1, source_target_pairs={{0,6},{1,7},{2,4},{3,5},{4,2},{5,3},{6,0},{7,1},{8,14},{9,15},{10,... | collective-permute-start | bytes 3932168 | tf_op jit(solution)/shard_map/ppermute | solution.py:1061
  256.8 58.3 %collective-permute-start.7 = (bf16[320,2048]{1,0:T(8,128)(2,1)S(1)}, bf16[320,2048]{1,0:T(8,128)(2,1)S(1)}, u32[]{:S(2)}, u32[]{:S(2)}) collective-permute-start(bf16[320,2048]{1,0:T(8,128)(2,1)S(1)} %multiply_convert_fusion), channel_id=1, source_target_pairs={{0,1},{1,0},{2,3},{3,2},{4,5},{5,4},{6,7},{7,6},{8,9},{9,8},{10,11... | collective-permute-start | bytes 3932168 | tf_op jit(solution)/shard_map/ppermute | solution.py:1061
  284.2 33.3 %collective-permute-start.9 = (bf16[320,2048]{1,0:T(8,128)(2,1)S(1)}, bf16[320,2048]{1,0:T(8,128)(2,1)S(1)}, u32[]{:S(2)}, u32[]{:S(2)}) collective-permute-start(bf16[320,2048]{1,0:T(8,128)(2,1)S(1)} %collective-permute-done.8), channel_id=1, source_target_pairs={{0,1},{1,0},{2,3},{3,2},{4,5},{5,4},{6,7},{7,6},{8,9},{9,8},{10,11... | collective-permute-start | bytes 3932168 | tf_op jit(solution)/shard_map/ppermute | solution.py:1061
  286.2 33.8 %collective-permute-start.11 = (bf16[320,2048]{1,0:T(8,128)(2,1)S(1)}, bf16[320,2048]{1,0:T(8,128)(2,1)S(1)}, u32[]{:S(2)}, u32[]{:S(2)}) collective-permute-start(bf16[320,2048]{1,0:T(8,128)(2,1)S(1)} %collective-permute-done.10), channel_id=1, source_target_pairs={{0,1},{1,0},{2,3},{3,2},{4,5},{5,4},{6,7},{7,6},{8,9},{9,8},{10,11... | collective-permute-start | bytes 3932168 | tf_op jit(solution)/shard_map/ppermute | solution.py:1061
  315.0 7.4 collective-permute-start.13
  326.3 129.8 %reduce-scatter.4.cloned.1.call-start = ((), (), s32[]{:S(2)}) async-start(), calls=%async_computation.5 | async-start | bytes 5242880 | tf_op jit(solution)/shard_map/reduce_scatter | solution.py:1071
  378.2 227.4 %reduce-scatter.6.cloned.1.call-start = ((), (), s32[]{:S(2)}) async-start(), calls=%async_computation.6 | async-start | bytes 10485760 | tf_op jit(solution)/shard_map/reduce_scatter | solution.py:1071
  456.2 318.8 %reduce-scatter.8.cloned.1.call-start = ((), (), s32[]{:S(2)}) async-start(), calls=%async_computation.7 | async-start | bytes 5242880 | tf_op jit(solution)/shard_map/reduce_scatter | solution.py:1071
  522.3 14.3 %collective-permute-start.17 = (bf16[320,2048]{1,0:T(8,128)(2,1)S(1)}, bf16[320,2048]{1,0:T(8,128)(2,1)S(1)}, u32[]{:S(2)}, u32[]{:S(2)}) collective-permute-start(bf16[320,2048]{1,0:T(8,128)(2,1)S(1)} %get-tuple-element.160), channel_id=1, source_target_pairs={{0,1},{1,0},{2,3},{3,2},{4,5},{5,4},{6,7},{7,6},{8,9},{9,8},{10,11... | collective-permute-start | bytes 3932168 | tf_op jit(solution)/shard_map/ppermute | solution.py:1061
  523.4 13.2 %collective-permute-start.16 = (bf16[320,2048]{1,0:T(8,128)(2,1)S(1)}, bf16[320,2048]{1,0:T(8,128)(2,1)S(1)}, u32[]{:S(2)}, u32[]{:S(2)}) collective-permute-start(bf16[320,2048]{1,0:T(8,128)(2,1)S(1)} %get-tuple-element.161), channel_id=1, source_target_pairs={{0,1},{1,0},{2,3},{3,2},{4,5},{5,4},{6,7},{7,6},{8,9},{9,8},{10,11... | collective-permute-start | bytes 3932168 | tf_op jit(solution)/shard_map/ppermute | solution.py:1061
  523.5 13.1 %collective-permute-start.15 = (bf16[320,2048]{1,0:T(8,128)(2,1)S(1)}, bf16[320,2048]{1,0:T(8,128)(2,1)S(1)}, u32[]{:S(2)}, u32[]{:S(2)}) collective-permute-start(bf16[320,2048]{1,0:T(8,128)(2,1)S(1)} %get-tuple-element.162), channel_id=1, source_target_pairs={{0,1},{1,0},{2,3},{3,2},{4,5},{5,4},{6,7},{7,6},{8,9},{9,8},{10,11... | collective-permute-start | bytes 3932168 | tf_op jit(solution)/shard_map/ppermute | solution.py:1061
  523.9 12.7 %collective-permute-start.14 = (bf16[320,2048]{1,0:T(8,128)(2,1)S(1)}, bf16[320,2048]{1,0:T(8,128)(2,1)}, u32[]{:S(2)}, u32[]{:S(2)}) collective-permute-start(bf16[320,2048]{1,0:T(8,128)(2,1)S(1)} %get-tuple-element.163), channel_id=1, source_target_pairs={{0,1},{1,0},{2,3},{3,2},{4,5},{5,4},{6,7},{7,6},{8,9},{9,8},{10,11... | collective-permute-start | bytes 3932168 | tf_op jit(solution)/shard_map/ppermute | solution.py:1061
  541.7 63.8 %collective-permute-start.18 = (bf16[320,2048]{1,0:T(8,128)(2,1)}, bf16[320,2048]{1,0:T(8,128)(2,1)}, u32[]{:S(2)}, u32[]{:S(2)}) collective-permute-start(bf16[320,2048]{1,0:T(8,128)(2,1)} %get-tuple-element.114), channel_id=1, source_target_pairs={{0,2},{1,3},{2,0},{3,1},{4,6},{5,7},{6,4},{7,5},{8,10},{9,11},{10,... | collective-permute-start | bytes 3932168 | tf_op jit(solution)/shard_map/ppermute | solution.py:1061
  542.9 62.7 %collective-permute-start.19 = (bf16[320,2048]{1,0:T(8,128)(2,1)}, bf16[320,2048]{1,0:T(8,128)(2,1)}, u32[]{:S(2)}, u32[]{:S(2)}) collective-permute-start(bf16[320,2048]{1,0:T(8,128)(2,1)} %get-tuple-element.115), channel_id=1, source_target_pairs={{0,4},{1,5},{2,6},{3,7},{4,0},{5,1},{6,2},{7,3},{8,12},{9,13},{10,... | collective-permute-start | bytes 3932168 | tf_op jit(solution)/shard_map/ppermute | solution.py:1061
  543.4 62.1 %collective-permute-start.20 = (bf16[320,2048]{1,0:T(8,128)(2,1)}, bf16[320,2048]{1,0:T(8,128)(2,1)}, u32[]{:S(2)}, u32[]{:S(2)}) collective-permute-start(bf16[320,2048]{1,0:T(8,128)(2,1)} %get-tuple-element.116), channel_id=1, source_target_pairs={{0,6},{1,7},{2,4},{3,5},{4,2},{5,3},{6,0},{7,1},{8,14},{9,15},{10,... | collective-permute-start | bytes 3932168 | tf_op jit(solution)/shard_map/ppermute | solution.py:1061
  611.0 143.6 %copy-start.12 = (f32[64,2048]{1,0:T(8,128)S(1)}, f32[64,2048]{1,0:T(8,128)}, u32[]{:S(2)}) copy-start(f32[64,2048]{1,0:T(8,128)} %param.26) | copy-start | bytes 1572868
  611.1 143.6 %copy-start.15 = (f32[64,2048]{1,0:T(8,128)S(1)}, f32[64,2048]{1,0:T(8,128)}, u32[]{:S(2)}) copy-start(f32[64,2048]{1,0:T(8,128)} %param.27) | copy-start | bytes 1572868
  754.6 23.3 %copy-start.18 = (f32[2,64]{1,0:T(2,128)}, f32[2,64]{1,0:T(2,128)S(1)}, u32[]{:S(2)}) copy-start(f32[2,64]{1,0:T(2,128)S(1)} %slice.69) | copy-start | bytes 1540
  760.8 14.2 %copy-start.2 = (bf16[1,1,320,2048]{3,2,1,0:T(8,128)(2,1)S(1)}, bf16[1,1,320,2048]{3,2,1,0:T(8,128)(2,1)}, u32[]{:S(2)}) copy-start(bf16[1,1,320,2048]{3,2,1,0:T(8,128)(2,1)} %param.16) | copy-start | bytes 3932164
  760.8 14.2 %copy-start.16 = (f32[2048]{0:T(1024)S(1)}, f32[2048]{0:T(1024)}, u32[]{:S(2)}) copy-start(f32[2048]{0:T(1024)} %get-tuple-element.140) | copy-start | bytes 24580
  (16 other events, 72.4 us)
Sparse Core Ops, SparseCore 0:
  175.5 150.7 all-gather.2
  327.9 45.1 all-gather.4
  378.3 77.8 reduce-scatter.3
  458.5 144.6 reduce-scatter.5
  605.7 89.7 reduce-scatter.7

commit v12 on v11

--- a/solution.py
+++ b/solution.py
@@ -316,17 +316,18 @@
                 pl.when(sends(way, step + 1))(
                     lambda way=way, step=step: line_weight(way, step + 1).start()
                 )
-            else:
+
+        both(step, lambda block: launch(block, False))
+        if step == 1:
+            for way in (0, 1):
                 pl.when(sends(way, 1))(lambda way=way: line_rows(way, 1).start())
-
-        both(step, lambda block: launch(block, False))
         if step == 1:
             relay(g)
             for offset in range(1, plane):
                 swap_copy(offset, 2).start()
     for step in range(1, lines):
         take_rows(step)
-        if step == lines - 1:
+        if step == lines - 2:
             locals_[4].wait()
             for offset in range(1, plane):
                 swap_copy(offset, 2).wait_recv()

time: 804 us -> 803 us (level)
  no operation moved by 1% of the time
where the time goes in v12:
time: 803 us; the launch traced here: 791 us
  Pallas kernels  507 us (63%)
  matrix products  85 us (11%)
  other arithmetic  64 us (8%)
  starting transfers between devices  44.8 us (6%)
  waiting for transfers between devices  41.8 us (5%)
  local copies, waits for them, and re-layouts  32.7 us (4%)
  between operations  15.4 us (2%)
    pallas_call x1, Pallas kernels, gather_start(): pl.pallas_call(functools.partial(gather_kernel, lines, plane, prompt_rows...  159 us
    pallas_call x1, Pallas kernels, finish(): pl.pallas_call(functools.partial(finish_kernel, lines, plane), out_shape=...  143 us
    pallas_call x1, Pallas kernels, plane_back(): pl.pallas_call(functools.partial(plane_back_kernel, plane), out_shape=(ja...  62.7 us
    dot_general x4, matrix products, contract(): lax.dot_general(left, right, (((left_axis,), (right_axis,)), ((), ())), p...  58.2 us
    ppermute x21, starting transfers between devices, plane_swap(): return lax.ppermute(block, 'dp', [(i, i ^ offset) for i in range(size)])  43.8 us
    pallas_call x1, Pallas kernels, weights_back(): pl.pallas_call(weights_back_kernel, grid_spec=pltpu.PrefetchScalarGridSpe...  40.4 us
    pallas_call x1, Pallas kernels, forward_back(): pl.pallas_call(forward_back_kernel, grid=(count // rows,), in_specs=[bloc...  36.6 us
    pallas_call x1, Pallas kernels, project_heads(): pl.pallas_call(project_kernel, grid_spec=pltpu.PrefetchScalarGridSpec(num...  34.8 us
  transfers between devices with their start and end apart: 26, of which 3 were waited for; matrix products, arithmetic and copies ran while one was open for 20% of the time, Pallas kernels for 44%

profile of v12, /device:TPU:9, one launch (start us, length us, event | category | flops | bytes accessed | tf_op | source)
XLA Modules:
  0.0 790.5 jit_solution(14179024802993958678)
XLA Ops:
  10.4 4.8 convert_element_type.111.forward_ref
  16.1 159.4 %gather_start.1 = (bf16[4,8,64,6272]{3,2,1,0:T(8,128)(2,1)}, bf16[4,256,2048]{2,1,0:T(8,128)(2,1)}, bf16[8,64,2048]{2,1,0:T(8,128)(2,1)}, bf16[4,8,64,512]{3,2,1,0:T(8,128)(2,1)}, bf16[8,64,512]{2,1,0:T(8,128)(2,1)}) custom-call(bf16[64,6272]{1,0:T(8,128)(2,1)} %fusion.21.weight_ref, bf16[320,2048]{1,0:T(8,128)(2,1)} %bitcast.51, ...), custom_call_target="tpu_custom_call" | custom-call | tf_op jit(solution)/shard_map/gather_start/pallas_call | solution.py:415
  178.3 2.3 collective-permute-start
  186.2 3.1 multiply_sine_fusion
  189.3 34.8 %project_heads.1 = (bf16[320,2048]{1,0:T(8,128)(2,1)}, bf16[1088,2048]{1,0:T(8,128)(2,1)}, bf16[1088,2048]{1,0:T(8,128)(2,1)}, bf16[320,2048]{1,0:T(8,128)(2,1)}, f32[1088,128]{1,0:T(8,128)}) custom-call(s32[1]{0:T(128)} %bitcast.1.place_ref, bf16[1024,2048]{1,0:T(8,128)(2,1)} %bitcast.54, bf16[320,2048]{1,0:T(8,128)(2,1)} %bitcast.52, ...), custom_call_target="tpu_custom_call" | custom-call | tf_op jit(solution)/shard_map/project_heads/pallas_call | solution.py:514
  226.1 11.4 %attend.1 = (bf16[320,2048]{1,0:T(8,128)(2,1)}, f32[320,1024]{1,0:T(8,128)}) custom-call(bf16[320,2048]{1,0:T(8,128)(2,1)} %get-tuple-element.80.query_ref, bf16[1088,2048]{1,0:T(8,128)(2,1)} %get-tuple-element.81.key_ref.value_ref, bf16[1088,2048]{1,0:T(8,128)(2,1)} %get-tuple-element.81.key_ref.value_ref, f32[320,1088]{1,0:T(8,128)} %add_convert_fusion.4.seen_ref), custom_call_target="tpu_custom_call" | custom-call | tf_op jit(solution)/shard_map/attend/pallas_call | solution.py:576
  237.5 5.9 multiply_reduce_fusion.2
  256.3 26.0 %collective-permute-done.8 = bf16[320,2048]{1,0:T(8,128)(2,1)S(1)} collective-permute-done((bf16[320,2048]{1,0:T(8,128)(2,1)S(1)}, bf16[320,2048]{1,0:T(8,128)(2,1)S(1)}, u32[]{:S(2)}, u32[]{:S(2)}) %collective-permute-start.8) | collective-permute-done | bytes 1310752 | tf_op jit(solution)/shard_map/ppermute | solution.py:1062
  284.5 27.5 %collective-permute-start.11 = (bf16[320,2048]{1,0:T(8,128)(2,1)S(1)}, bf16[320,2048]{1,0:T(8,128)(2,1)S(1)}, u32[]{:S(2)}, u32[]{:S(2)}) collective-permute-start(bf16[320,2048]{1,0:T(8,128)(2,1)S(1)} %collective-permute-done.10), channel_id=1, source_target_pairs={{0,1},{1,0},{2,3},{3,2},{4,5},{5,4},{6,7},{7,6},{8,9},{9,8},{10,11... | collective-permute-start | bytes 3932168 | tf_op jit(solution)/shard_map/ppermute | solution.py:1062
  321.8 3.5 all-gather.3.cloned.1.call-done.weight_ref
  325.6 26.7 %fusion.33.gate_up_ref = f32[2560,2048]{1,0:T(8,128)S(1)} fusion(bf16[2560,2048]{1,0:T(8,128)(2,1)} %constant_dynamic-update-slice_fusion.8, bf16[2048,2048]{1,0:T(8,128)(2,1)} %all-gather.3.cloned.1.call-done.weight_ref), kind=kOutput, calls=%fused_computation.101 | convolution fusion | flops 21474836480 | bytes 39845888 | tf_op jit(solution)/shard_map/dot_general | solution.py:1492
  352.4 3.6 fusion.activated_ref
  355.9 3.5 copy-done
  359.4 2.4 copy-done.3
  361.8 15.4 %convolution_convert_fusion.1 = bf16[2048,1024]{1,0:T(8,128)(2,1)} fusion(bf16[2560,2048]{1,0:T(8,128)(2,1)} %copy-done.4, bf16[2560,1024]{1,0:T(8,128)(2,1)S(1)} %fusion.activated_ref), kind=kOutput, calls=%fused_computation.15 | convolution fusion | flops 10739515392 | bytes 19922944 | tf_op jit(solution)/shard_map/dot_general | solution.py:35
  377.7 36.6 %forward_back.1 = (bf16[2560,2048]{1,0:T(8,128)(2,1)}, bf16[2560,2048]{1,0:T(8,128)(2,1)}) custom-call(bf16[2560,1024]{1,0:T(8,128)(2,1)} %copy-done.3, bf16[2560,2048]{1,0:T(8,128)(2,1)} %copy-done.4, f32[2560,2048]{1,0:T(8,128)} %copy-done, bf16[2048,512]{1,0:T(8,128)(2,1)} %bitcast.61, bf16[2048,512]{1,0:T(8,128)(2,1)} %all-gather.5.cloned.1.call-done.second_ref), custom_call_target="tpu_custom_call" | custom-call | tf_op jit(solution)/shard_map/forward_back/pallas_call | solution.py:811
  414.3 28.8 %convolution_convert_fusion = bf16[2048,2048]{1,0:T(8,128)(2,1)} fusion(bf16[2560,2048]{1,0:T(8,128)(2,1)} %constant_dynamic-update-slice_fusion.8, bf16[2560,2048]{1,0:T(8,128)(2,1)} %get-tuple-element.94), kind=kOutput, calls=%fused_computation.3 | convolution fusion | flops 21479030784 | bytes 29360128 | tf_op jit(solution)/shard_map/dot_general | solution.py:35
  443.1 12.2 %reduce-scatter.4.cloned.1.call-done = bf16[512,1024]{1,0:T(8,128)(2,1)} async-done(((bf16[2048,1024]{1,0:T(8,128)(2,1)}), bf16[512,1024]{1,0:T(8,128)(2,1)}) %reduce-scatter.4.cloned.1.call-update) | async-done | bytes 1048592 | tf_op jit(solution)/shard_map/reduce_scatter | solution.py:1072
  455.5 62.7 %plane_back.1 = (f32[320,2048]{1,0:T(8,128)}, bf16[64,8192]{1,0:T(8,128)(2,1)}) custom-call(bf16[8,320,2048]{2,1,0:T(8,128)(2,1)} %bitcast.56, bf16[2048,2048]{1,0:T(8,128)(2,1)} %all-gather.3.cloned.1.call-done.weight_ref, bf16[8,64,1024]{2,1,0:T(8,128)(2,1)} %bitcast.65), custom_call_target="tpu_custom_call" | custom-call | tf_op jit(solution)/shard_map/plane_back/pallas_call | solution.py:1027
  518.2 3.1 fusion.32
  523.8 3.7 fusion.31
  527.5 8.1 %fusion.8.grad_ref = bf16[320,2048]{1,0:T(8,128)(2,1)} fusion(bf16[320,2048]{1,0:T(8,128)(2,1)S(1)} %get-tuple-element.155.branch_ref, bf16[2048,6272]{1,0:T(8,128)(2,1)} %bitcast.48), kind=kOutput, calls=%fused_computation.16 | convolution fusion | flops 2685009920 | bytes 11010048 | tf_op jit(solution)/shard_map/dot_general | solution.py:35
  535.6 5.1 add_convert_fusion.1
  543.4 18.8 %attend_back.1 = (bf16[320,2048]{1,0:T(8,128)(2,1)}, bf16[1088,2048]{1,0:T(8,128)(2,1)}) custom-call(s32[1]{0:T(128)} %bitcast.1.place_ref, bf16[320,2048]{1,0:T(8,128)(2,1)} %get-tuple-element.80.query_ref, bf16[1088,2048]{1,0:T(8,128)(2,1)} %get-tuple-element.81.key_ref.value_ref, bf16[1088,2048]{1,0:T(8,128)(2,1)} %get-tuple-element.81.key_ref.value_ref, ...), custom_call_target="tpu_custom_call" | custom-call | tf_op jit(solution)/shard_map/attend_back/pallas_call | solution.py:655
  562.2 40.4 %weights_back.1 = (bf16[2048,2048]{1,0:T(8,128)(2,1)}, bf16[2048,2048]{1,0:T(8,128)(2,1)}, bf16[2048,2048]{1,0:T(8,128)(2,1)}, f32[320,2048]{1,0:T(8,128)}, bf16...) custom-call(s32[1]{0:T(128)} %bitcast.1.place_ref, bf16[320,2048]{1,0:T(8,128)(2,1)} %get-tuple-element.107.query_ref, ...), custom_call_target="tpu_custom_call" | custom-call | tf_op jit(solution)/shard_map/weights_back/pallas_call | solution.py:734
  604.6 5.4 add_convert_fusion
  610.1 142.7 %finish.1 = (f32[64,4096]{1,0:T(8,128)}, f32[64,2048]{1,0:T(8,128)}, f32[8,64]{1,0:T(8,128)}, bf16[64,24576]{1,0:T(8,128)(2,1)}) custom-call(bf16[4,4,2,64,2048]{4,3,2,1,0:T(8,128)(2,1)} %bitcast.57, bf16[4,4,2,64,2048]{4,3,2,1,0:T(8,128)(2,1)} %bitcast.58, bf16[4,4,2,64,2048]{4,3,2,1,0:T(8,128)(2,1)} %bitcast.59, bf16[4,4,2,64,128]{4,3,2,1,0:T(8,128)(2,1)} %bitcast.60, ...), custom_call_target="tpu_custom_call" | custom-call | tf_op jit(solution)/shard_map/finish/pallas_call | solution.py:1369
  753.7 2.6 add_multiply_fusion.3
  756.4 3.5 add_multiply_fusion.2
  759.9 14.1 %add_multiply_fusion = (f32[64,24576]{1,0:T(8,128)}, f32[64,24576]{1,0:T(8,128)}, f32[64,24576]{1,0:T(8,128)}, f32[64,24576]{1,0:T(8,128)}) fusion(f32[64,24576]{1,0:T(8,128)} %param.29, f32[64,24576]{1,0:T(8,128)} %param.30, f32[64,24576]{1,0:T(8,128)} %param.31, bf16[64,24576]{1,0:T(8,128)(2,1)S(1)} %copy-done.11), kind=kLoop, calls=%fused_computation.9 | loop fusion | flops 23592960 | bytes 47185920 | tf_op jit(solution)/shard_map/mul | solution.py:81
  774.1 2.9 fusion.11
  777.7 4.1 fusion.15
  (148 shorter events, 49.9 us)
Async XLA Ops:
  7.2 318.2 %all-gather.3.cloned.1.call-start = ((), (), s32[]{:S(2)}) async-start(), calls=%async_computation.3 | async-start | bytes 10485760 | tf_op jit(solution)/shard_map/all_gather | solution.py:1447
  175.5 201.7 %all-gather.5.cloned.1.call-start = ((), (), s32[]{:S(2)}) async-start(), calls=%async_computation.4 | async-start | bytes 2621440 | tf_op jit(solution)/shard_map/all_gather | solution.py:1452
  175.6 70.3 %collective-permute-start.5 = (bf16[320,2048]{1,0:T(8,128)(2,1)}, bf16[320,2048]{1,0:T(8,128)(2,1)}, u32[]{:S(2)}, u32[]{:S(2)}) collective-permute-start(bf16[320,2048]{1,0:T(8,128)(2,1)} %bitcast.9), channel_id=1, source_target_pairs={{0,6},{1,7},{2,4},{3,5},{4,2},{5,3},{6,0},{7,1},{8,14},{9,15},{10,... | collective-permute-start | bytes 3932168 | tf_op jit(solution)/shard_map/ppermute | solution.py:1062
  175.8 68.1 %collective-permute-start.3 = (bf16[320,2048]{1,0:T(8,128)(2,1)}, bf16[320,2048]{1,0:T(8,128)(2,1)}, u32[]{:S(2)}, u32[]{:S(2)}) collective-permute-start(bf16[320,2048]{1,0:T(8,128)(2,1)} %bitcast.9), channel_id=1, source_target_pairs={{0,4},{1,5},{2,6},{3,7},{4,0},{5,1},{6,2},{7,3},{8,12},{9,13},{10,... | collective-permute-start | bytes 3932168 | tf_op jit(solution)/shard_map/ppermute | solution.py:1062
  176.6 66.9 %collective-permute-start.1 = (bf16[320,2048]{1,0:T(8,128)(2,1)}, bf16[320,2048]{1,0:T(8,128)(2,1)}, u32[]{:S(2)}, u32[]{:S(2)}) collective-permute-start(bf16[320,2048]{1,0:T(8,128)(2,1)} %bitcast.9), channel_id=1, source_target_pairs={{0,2},{1,3},{2,0},{3,1},{4,6},{5,7},{6,4},{7,5},{8,10},{9,11},{10,... | collective-permute-start | bytes 3932168 | tf_op jit(solution)/shard_map/ppermute | solution.py:1062
  178.3 67.7 %collective-permute-start = (bf16[320,2048]{1,0:T(8,128)(2,1)}, bf16[320,2048]{1,0:T(8,128)(2,1)}, u32[]{:S(2)}, u32[]{:S(2)}) collective-permute-start(bf16[320,2048]{1,0:T(8,128)(2,1)} %bitcast.9), channel_id=1, source_target_pairs={{0,1},{1,0},{2,3},{3,2},{4,5},{5,4},{6,7},{7,6},{8,9},{9,8},{10,11... | collective-permute-start | bytes 3932168 | tf_op jit(solution)/shard_map/ppermute | solution.py:1062
  243.4 5.5 collective-permute-start.2
  243.9 6.7 collective-permute-start.4
  245.9 6.3 collective-permute-start.6
  252.3 67.1 %copy-start.4 = (bf16[2560,2048]{1,0:T(8,128)(2,1)}, bf16[2560,2048]{1,0:T(8,128)(2,1)S(1)}, u32[]{:S(2)}) copy-start(bf16[2560,2048]{1,0:T(8,128)(2,1)S(1)} %constant_dynamic-update-slice_fusion.grad_ref) | copy-start | bytes 31457284
  252.3 30.0 %collective-permute-start.8 = (bf16[320,2048]{1,0:T(8,128)(2,1)S(1)}, bf16[320,2048]{1,0:T(8,128)(2,1)S(1)}, u32[]{:S(2)}, u32[]{:S(2)}) collective-permute-start(bf16[320,2048]{1,0:T(8,128)(2,1)S(1)} %multiply_convert_fusion), channel_id=1, source_target_pairs={{0,2},{1,3},{2,0},{3,1},{4,6},{5,7},{6,4},{7,5},{8,10},{9,11},{10,... | collective-permute-start | bytes 3932168 | tf_op jit(solution)/shard_map/ppermute | solution.py:1062
  252.7 31.8 %collective-permute-start.10 = (bf16[320,2048]{1,0:T(8,128)(2,1)S(1)}, bf16[320,2048]{1,0:T(8,128)(2,1)S(1)}, u32[]{:S(2)}, u32[]{:S(2)}) collective-permute-start(bf16[320,2048]{1,0:T(8,128)(2,1)S(1)} %multiply_convert_fusion), channel_id=1, source_target_pairs={{0,4},{1,5},{2,6},{3,7},{4,0},{5,1},{6,2},{7,3},{8,12},{9,13},{10,... | collective-permute-start | bytes 3932168 | tf_op jit(solution)/shard_map/ppermute | solution.py:1062
  253.7 59.5 %collective-permute-start.12 = (bf16[320,2048]{1,0:T(8,128)(2,1)S(1)}, bf16[320,2048]{1,0:T(8,128)(2,1)S(1)}, u32[]{:S(2)}, u32[]{:S(2)}) collective-permute-start(bf16[320,2048]{1,0:T(8,128)(2,1)S(1)} %multiply_convert_fusion), channel_id=1, source_target_pairs={{0,6},{1,7},{2,4},{3,5},{4,2},{5,3},{6,0},{7,1},{8,14},{9,15},{10,... | collective-permute-start | bytes 3932168 | tf_op jit(solution)/shard_map/ppermute | solution.py:1062
  255.1 58.2 %collective-permute-start.7 = (bf16[320,2048]{1,0:T(8,128)(2,1)S(1)}, bf16[320,2048]{1,0:T(8,128)(2,1)S(1)}, u32[]{:S(2)}, u32[]{:S(2)}) collective-permute-start(bf16[320,2048]{1,0:T(8,128)(2,1)S(1)} %multiply_convert_fusion), channel_id=1, source_target_pairs={{0,1},{1,0},{2,3},{3,2},{4,5},{5,4},{6,7},{7,6},{8,9},{9,8},{10,11... | collective-permute-start | bytes 3932168 | tf_op jit(solution)/shard_map/ppermute | solution.py:1062
  282.3 33.4 %collective-permute-start.9 = (bf16[320,2048]{1,0:T(8,128)(2,1)S(1)}, bf16[320,2048]{1,0:T(8,128)(2,1)S(1)}, u32[]{:S(2)}, u32[]{:S(2)}) collective-permute-start(bf16[320,2048]{1,0:T(8,128)(2,1)S(1)} %collective-permute-done.8), channel_id=1, source_target_pairs={{0,1},{1,0},{2,3},{3,2},{4,5},{5,4},{6,7},{7,6},{8,9},{9,8},{10,11... | collective-permute-start | bytes 3932168 | tf_op jit(solution)/shard_map/ppermute | solution.py:1062
  284.5 33.7 %collective-permute-start.11 = (bf16[320,2048]{1,0:T(8,128)(2,1)S(1)}, bf16[320,2048]{1,0:T(8,128)(2,1)S(1)}, u32[]{:S(2)}, u32[]{:S(2)}) collective-permute-start(bf16[320,2048]{1,0:T(8,128)(2,1)S(1)} %collective-permute-done.10), channel_id=1, source_target_pairs={{0,1},{1,0},{2,3},{3,2},{4,5},{5,4},{6,7},{7,6},{8,9},{9,8},{10,11... | collective-permute-start | bytes 3932168 | tf_op jit(solution)/shard_map/ppermute | solution.py:1062
  313.2 7.4 collective-permute-start.13
  325.4 129.9 %reduce-scatter.4.cloned.1.call-start = ((), (), s32[]{:S(2)}) async-start(), calls=%async_computation.5 | async-start | bytes 5242880 | tf_op jit(solution)/shard_map/reduce_scatter | solution.py:1072
  377.2 227.4 %reduce-scatter.6.cloned.1.call-start = ((), (), s32[]{:S(2)}) async-start(), calls=%async_computation.6 | async-start | bytes 10485760 | tf_op jit(solution)/shard_map/reduce_scatter | solution.py:1072
  455.3 318.8 %reduce-scatter.8.cloned.1.call-start = ((), (), s32[]{:S(2)}) async-start(), calls=%async_computation.7 | async-start | bytes 5242880 | tf_op jit(solution)/shard_map/reduce_scatter | solution.py:1072
  521.3 14.3 %collective-permute-start.17 = (bf16[320,2048]{1,0:T(8,128)(2,1)S(1)}, bf16[320,2048]{1,0:T(8,128)(2,1)S(1)}, u32[]{:S(2)}, u32[]{:S(2)}) collective-permute-start(bf16[320,2048]{1,0:T(8,128)(2,1)S(1)} %get-tuple-element.160), channel_id=1, source_target_pairs={{0,1},{1,0},{2,3},{3,2},{4,5},{5,4},{6,7},{7,6},{8,9},{9,8},{10,11... | collective-permute-start | bytes 3932168 | tf_op jit(solution)/shard_map/ppermute | solution.py:1062
  522.4 13.2 %collective-permute-start.16 = (bf16[320,2048]{1,0:T(8,128)(2,1)S(1)}, bf16[320,2048]{1,0:T(8,128)(2,1)S(1)}, u32[]{:S(2)}, u32[]{:S(2)}) collective-permute-start(bf16[320,2048]{1,0:T(8,128)(2,1)S(1)} %get-tuple-element.161), channel_id=1, source_target_pairs={{0,1},{1,0},{2,3},{3,2},{4,5},{5,4},{6,7},{7,6},{8,9},{9,8},{10,11... | collective-permute-start | bytes 3932168 | tf_op jit(solution)/shard_map/ppermute | solution.py:1062
  522.5 13.1 %collective-permute-start.15 = (bf16[320,2048]{1,0:T(8,128)(2,1)S(1)}, bf16[320,2048]{1,0:T(8,128)(2,1)S(1)}, u32[]{:S(2)}, u32[]{:S(2)}) collective-permute-start(bf16[320,2048]{1,0:T(8,128)(2,1)S(1)} %get-tuple-element.162), channel_id=1, source_target_pairs={{0,1},{1,0},{2,3},{3,2},{4,5},{5,4},{6,7},{7,6},{8,9},{9,8},{10,11... | collective-permute-start | bytes 3932168 | tf_op jit(solution)/shard_map/ppermute | solution.py:1062
  523.0 12.7 %collective-permute-start.14 = (bf16[320,2048]{1,0:T(8,128)(2,1)S(1)}, bf16[320,2048]{1,0:T(8,128)(2,1)}, u32[]{:S(2)}, u32[]{:S(2)}) collective-permute-start(bf16[320,2048]{1,0:T(8,128)(2,1)S(1)} %get-tuple-element.163), channel_id=1, source_target_pairs={{0,1},{1,0},{2,3},{3,2},{4,5},{5,4},{6,7},{7,6},{8,9},{9,8},{10,11... | collective-permute-start | bytes 3932168 | tf_op jit(solution)/shard_map/ppermute | solution.py:1062
  540.8 63.8 %collective-permute-start.18 = (bf16[320,2048]{1,0:T(8,128)(2,1)}, bf16[320,2048]{1,0:T(8,128)(2,1)}, u32[]{:S(2)}, u32[]{:S(2)}) collective-permute-start(bf16[320,2048]{1,0:T(8,128)(2,1)} %get-tuple-element.114), channel_id=1, source_target_pairs={{0,2},{1,3},{2,0},{3,1},{4,6},{5,7},{6,4},{7,5},{8,10},{9,11},{10,... | collective-permute-start | bytes 3932168 | tf_op jit(solution)/shard_map/ppermute | solution.py:1062
  541.9 62.6 %collective-permute-start.19 = (bf16[320,2048]{1,0:T(8,128)(2,1)}, bf16[320,2048]{1,0:T(8,128)(2,1)}, u32[]{:S(2)}, u32[]{:S(2)}) collective-permute-start(bf16[320,2048]{1,0:T(8,128)(2,1)} %get-tuple-element.115), channel_id=1, source_target_pairs={{0,4},{1,5},{2,6},{3,7},{4,0},{5,1},{6,2},{7,3},{8,12},{9,13},{10,... | collective-permute-start | bytes 3932168 | tf_op jit(solution)/shard_map/ppermute | solution.py:1062
  542.5 62.1 %collective-permute-start.20 = (bf16[320,2048]{1,0:T(8,128)(2,1)}, bf16[320,2048]{1,0:T(8,128)(2,1)}, u32[]{:S(2)}, u32[]{:S(2)}) collective-permute-start(bf16[320,2048]{1,0:T(8,128)(2,1)} %get-tuple-element.116), channel_id=1, source_target_pairs={{0,6},{1,7},{2,4},{3,5},{4,2},{5,3},{6,0},{7,1},{8,14},{9,15},{10,... | collective-permute-start | bytes 3932168 | tf_op jit(solution)/shard_map/ppermute | solution.py:1062
  610.1 143.6 %copy-start.12 = (f32[64,2048]{1,0:T(8,128)S(1)}, f32[64,2048]{1,0:T(8,128)}, u32[]{:S(2)}) copy-start(f32[64,2048]{1,0:T(8,128)} %param.26) | copy-start | bytes 1572868
  610.1 143.6 %copy-start.15 = (f32[64,2048]{1,0:T(8,128)S(1)}, f32[64,2048]{1,0:T(8,128)}, u32[]{:S(2)}) copy-start(f32[64,2048]{1,0:T(8,128)} %param.27) | copy-start | bytes 1572868
  753.7 23.3 %copy-start.18 = (f32[2,64]{1,0:T(2,128)}, f32[2,64]{1,0:T(2,128)S(1)}, u32[]{:S(2)}) copy-start(f32[2,64]{1,0:T(2,128)S(1)} %slice.69) | copy-start | bytes 1540
  759.9 14.2 %copy-start.2 = (bf16[1,1,320,2048]{3,2,1,0:T(8,128)(2,1)S(1)}, bf16[1,1,320,2048]{3,2,1,0:T(8,128)(2,1)}, u32[]{:S(2)}) copy-start(bf16[1,1,320,2048]{3,2,1,0:T(8,128)(2,1)} %param.16) | copy-start | bytes 3932164
  759.9 14.2 %copy-start.16 = (f32[2048]{0:T(1024)S(1)}, f32[2048]{0:T(1024)}, u32[]{:S(2)}) copy-start(f32[2048]{0:T(1024)} %get-tuple-element.140) | copy-start | bytes 24580
  (16 other events, 72.4 us)
Sparse Core Ops, SparseCore 0:
  175.6 149.6 all-gather.2
  326.9 45.1 all-gather.4
  377.3 77.8 reduce-scatter.3
  457.6 144.6 reduce-scatter.5
  604.8 89.7 reduce-scatter.7

commit v13 on v12

--- a/solution.py
+++ b/solution.py
@@ -930,7 +930,7 @@
         swap_copy(offset).start()
     own_swap.start()
     load.wait()
-    part_width = 512
+    part_width = 1024
 
     def product(turn, which, target):
         @pl.loop(0, D // part_width)

time: 803 us -> 802 us (level)
  no operation moved by 1% of the time
where the time goes in v13:
time: 802 us; the launch traced here: 790 us
  Pallas kernels  507 us (63%)
  matrix products  84.8 us (11%)
  other arithmetic  64.1 us (8%)
  starting transfers between devices  44.6 us (6%)
  waiting for transfers between devices  41.8 us (5%)
  local copies, waits for them, and re-layouts  32.9 us (4%)
  between operations  15.4 us (2%)
    pallas_call x1, Pallas kernels, gather_start(): pl.pallas_call(functools.partial(gather_kernel, lines, plane, prompt_rows...  159 us
    pallas_call x1, Pallas kernels, finish(): pl.pallas_call(functools.partial(finish_kernel, lines, plane), out_shape=...  144 us
    pallas_call x1, Pallas kernels, plane_back(): pl.pallas_call(functools.partial(plane_back_kernel, plane), out_shape=(ja...  61 us
    dot_general x4, matrix products, contract(): lax.dot_general(left, right, (((left_axis,), (right_axis,)), ((), ())), p...  58.1 us
    ppermute x21, starting transfers between devices, plane_swap(): return lax.ppermute(block, 'dp', [(i, i ^ offset) for i in range(size)])  43.6 us
    pallas_call x1, Pallas kernels, weights_back(): pl.pallas_call(weights_back_kernel, grid_spec=pltpu.PrefetchScalarGridSpe...  40.6 us
    pallas_call x1, Pallas kernels, forward_back(): pl.pallas_call(forward_back_kernel, grid=(count // rows,), in_specs=[bloc...  36.6 us
    pallas_call x1, Pallas kernels, project_heads(): pl.pallas_call(project_kernel, grid_spec=pltpu.PrefetchScalarGridSpec(num...  34.8 us
  transfers between devices with their start and end apart: 26, of which 3 were waited for; matrix products, arithmetic and copies ran while one was open for 20% of the time, Pallas kernels for 44%

profile of v13, /device:TPU:9, one launch (start us, length us, event | category | flops | bytes accessed | tf_op | source)
XLA Modules:
  0.0 790.4 jit_solution(15689119288704616020)
XLA Ops:
  10.4 4.8 convert_element_type.111.forward_ref
  16.1 159.4 %gather_start.1 = (bf16[4,8,64,6272]{3,2,1,0:T(8,128)(2,1)}, bf16[4,256,2048]{2,1,0:T(8,128)(2,1)}, bf16[8,64,2048]{2,1,0:T(8,128)(2,1)}, bf16[4,8,64,512]{3,2,1,0:T(8,128)(2,1)}, bf16[8,64,512]{2,1,0:T(8,128)(2,1)}) custom-call(bf16[64,6272]{1,0:T(8,128)(2,1)} %fusion.21.weight_ref, bf16[320,2048]{1,0:T(8,128)(2,1)} %bitcast.51, ...), custom_call_target="tpu_custom_call" | custom-call | tf_op jit(solution)/shard_map/gather_start/pallas_call | solution.py:415
  178.3 2.3 collective-permute-start
  186.2 3.1 multiply_sine_fusion
  189.3 34.8 %project_heads.1 = (bf16[320,2048]{1,0:T(8,128)(2,1)}, bf16[1088,2048]{1,0:T(8,128)(2,1)}, bf16[1088,2048]{1,0:T(8,128)(2,1)}, bf16[320,2048]{1,0:T(8,128)(2,1)}, f32[1088,128]{1,0:T(8,128)}) custom-call(s32[1]{0:T(128)} %bitcast.1.place_ref, bf16[1024,2048]{1,0:T(8,128)(2,1)} %bitcast.54, bf16[320,2048]{1,0:T(8,128)(2,1)} %bitcast.52, ...), custom_call_target="tpu_custom_call" | custom-call | tf_op jit(solution)/shard_map/project_heads/pallas_call | solution.py:514
  226.1 11.4 %attend.1 = (bf16[320,2048]{1,0:T(8,128)(2,1)}, f32[320,1024]{1,0:T(8,128)}) custom-call(bf16[320,2048]{1,0:T(8,128)(2,1)} %get-tuple-element.80.query_ref, bf16[1088,2048]{1,0:T(8,128)(2,1)} %get-tuple-element.81.key_ref.value_ref, bf16[1088,2048]{1,0:T(8,128)(2,1)} %get-tuple-element.81.key_ref.value_ref, f32[320,1088]{1,0:T(8,128)} %add_convert_fusion.4.seen_ref), custom_call_target="tpu_custom_call" | custom-call | tf_op jit(solution)/shard_map/attend/pallas_call | solution.py:576
  237.5 5.9 multiply_reduce_fusion.2
  256.3 26.0 %collective-permute-done.8 = bf16[320,2048]{1,0:T(8,128)(2,1)S(1)} collective-permute-done((bf16[320,2048]{1,0:T(8,128)(2,1)S(1)}, bf16[320,2048]{1,0:T(8,128)(2,1)S(1)}, u32[]{:S(2)}, u32[]{:S(2)}) %collective-permute-start.8) | collective-permute-done | bytes 1310752 | tf_op jit(solution)/shard_map/ppermute | solution.py:1062
  284.5 27.5 %collective-permute-start.11 = (bf16[320,2048]{1,0:T(8,128)(2,1)S(1)}, bf16[320,2048]{1,0:T(8,128)(2,1)S(1)}, u32[]{:S(2)}, u32[]{:S(2)}) collective-permute-start(bf16[320,2048]{1,0:T(8,128)(2,1)S(1)} %collective-permute-done.10), channel_id=1, source_target_pairs={{0,1},{1,0},{2,3},{3,2},{4,5},{5,4},{6,7},{7,6},{8,9},{9,8},{10,11... | collective-permute-start | bytes 3932168 | tf_op jit(solution)/shard_map/ppermute | solution.py:1062
  321.8 3.5 all-gather.3.cloned.1.call-done.weight_ref
  325.6 26.7 %fusion.33.gate_up_ref = f32[2560,2048]{1,0:T(8,128)S(1)} fusion(bf16[2560,2048]{1,0:T(8,128)(2,1)} %constant_dynamic-update-slice_fusion.8, bf16[2048,2048]{1,0:T(8,128)(2,1)} %all-gather.3.cloned.1.call-done.weight_ref), kind=kOutput, calls=%fused_computation.101 | convolution fusion | flops 21474836480 | bytes 39845888 | tf_op jit(solution)/shard_map/dot_general | solution.py:1492
  352.4 3.6 fusion.activated_ref
  355.9 3.5 copy-done
  359.4 2.4 copy-done.3
  361.8 15.4 %convolution_convert_fusion.1 = bf16[2048,1024]{1,0:T(8,128)(2,1)} fusion(bf16[2560,2048]{1,0:T(8,128)(2,1)} %copy-done.4, bf16[2560,1024]{1,0:T(8,128)(2,1)S(1)} %fusion.activated_ref), kind=kOutput, calls=%fused_computation.15 | convolution fusion | flops 10739515392 | bytes 19922944 | tf_op jit(solution)/shard_map/dot_general | solution.py:35
  377.7 36.6 %forward_back.1 = (bf16[2560,2048]{1,0:T(8,128)(2,1)}, bf16[2560,2048]{1,0:T(8,128)(2,1)}) custom-call(bf16[2560,1024]{1,0:T(8,128)(2,1)} %copy-done.3, bf16[2560,2048]{1,0:T(8,128)(2,1)} %copy-done.4, f32[2560,2048]{1,0:T(8,128)} %copy-done, bf16[2048,512]{1,0:T(8,128)(2,1)} %bitcast.61, bf16[2048,512]{1,0:T(8,128)(2,1)} %all-gather.5.cloned.1.call-done.second_ref), custom_call_target="tpu_custom_call" | custom-call | tf_op jit(solution)/shard_map/forward_back/pallas_call | solution.py:811
  414.3 28.8 %convolution_convert_fusion = bf16[2048,2048]{1,0:T(8,128)(2,1)} fusion(bf16[2560,2048]{1,0:T(8,128)(2,1)} %constant_dynamic-update-slice_fusion.8, bf16[2560,2048]{1,0:T(8,128)(2,1)} %get-tuple-element.94), kind=kOutput, calls=%fused_computation.3 | convolution fusion | flops 21479030784 | bytes 29360128 | tf_op jit(solution)/shard_map/dot_general | solution.py:35
  443.1 12.2 %reduce-scatter.4.cloned.1.call-done = bf16[512,1024]{1,0:T(8,128)(2,1)} async-done(((bf16[2048,1024]{1,0:T(8,128)(2,1)}), bf16[512,1024]{1,0:T(8,128)(2,1)}) %reduce-scatter.4.cloned.1.call-update) | async-done | bytes 1048592 | tf_op jit(solution)/shard_map/reduce_scatter | solution.py:1072
  455.5 61.0 %plane_back.1 = (f32[320,2048]{1,0:T(8,128)}, bf16[64,8192]{1,0:T(8,128)(2,1)}) custom-call(bf16[8,320,2048]{2,1,0:T(8,128)(2,1)} %bitcast.56, bf16[2048,2048]{1,0:T(8,128)(2,1)} %all-gather.3.cloned.1.call-done.weight_ref, bf16[8,64,1024]{2,1,0:T(8,128)(2,1)} %bitcast.65), custom_call_target="tpu_custom_call" | custom-call | tf_op jit(solution)/shard_map/plane_back/pallas_call | solution.py:1027
  516.5 3.4 fusion.32
  522.1 3.7 fusion.31
  525.8 7.9 %fusion.8.grad_ref = bf16[320,2048]{1,0:T(8,128)(2,1)} fusion(bf16[320,2048]{1,0:T(8,128)(2,1)S(1)} %get-tuple-element.155.branch_ref, bf16[2048,6272]{1,0:T(8,128)(2,1)} %bitcast.48), kind=kOutput, calls=%fused_computation.16 | convolution fusion | flops 2685009920 | bytes 11010048 | tf_op jit(solution)/shard_map/dot_general | solution.py:35
  533.8 5.5 add_convert_fusion.1
  541.9 18.6 %attend_back.1 = (bf16[320,2048]{1,0:T(8,128)(2,1)}, bf16[1088,2048]{1,0:T(8,128)(2,1)}) custom-call(s32[1]{0:T(128)} %bitcast.1.place_ref, bf16[320,2048]{1,0:T(8,128)(2,1)} %get-tuple-element.80.query_ref, bf16[1088,2048]{1,0:T(8,128)(2,1)} %get-tuple-element.81.key_ref.value_ref, bf16[1088,2048]{1,0:T(8,128)(2,1)} %get-tuple-element.81.key_ref.value_ref, ...), custom_call_target="tpu_custom_call" | custom-call | tf_op jit(solution)/shard_map/attend_back/pallas_call | solution.py:655
  560.5 40.6 %weights_back.1 = (bf16[2048,2048]{1,0:T(8,128)(2,1)}, bf16[2048,2048]{1,0:T(8,128)(2,1)}, bf16[2048,2048]{1,0:T(8,128)(2,1)}, f32[320,2048]{1,0:T(8,128)}, bf16...) custom-call(s32[1]{0:T(128)} %bitcast.1.place_ref, bf16[320,2048]{1,0:T(8,128)(2,1)} %get-tuple-element.107.query_ref, ...), custom_call_target="tpu_custom_call" | custom-call | tf_op jit(solution)/shard_map/weights_back/pallas_call | solution.py:734
  603.2 5.4 add_convert_fusion
  608.6 144.3 %finish.1 = (f32[64,4096]{1,0:T(8,128)}, f32[64,2048]{1,0:T(8,128)}, f32[8,64]{1,0:T(8,128)}, bf16[64,24576]{1,0:T(8,128)(2,1)}) custom-call(bf16[4,4,2,64,2048]{4,3,2,1,0:T(8,128)(2,1)} %bitcast.57, bf16[4,4,2,64,2048]{4,3,2,1,0:T(8,128)(2,1)} %bitcast.58, bf16[4,4,2,64,2048]{4,3,2,1,0:T(8,128)(2,1)} %bitcast.59, bf16[4,4,2,64,128]{4,3,2,1,0:T(8,128)(2,1)} %bitcast.60, ...), custom_call_target="tpu_custom_call" | custom-call | tf_op jit(solution)/shard_map/finish/pallas_call | solution.py:1369
  753.8 2.6 add_multiply_fusion.3
  756.5 3.5 add_multiply_fusion.2
  760.0 13.8 %add_multiply_fusion = (f32[64,24576]{1,0:T(8,128)}, f32[64,24576]{1,0:T(8,128)}, f32[64,24576]{1,0:T(8,128)}, f32[64,24576]{1,0:T(8,128)}) fusion(f32[64,24576]{1,0:T(8,128)} %param.29, f32[64,24576]{1,0:T(8,128)} %param.30, f32[64,24576]{1,0:T(8,128)} %param.31, bf16[64,24576]{1,0:T(8,128)(2,1)S(1)} %copy-done.11), kind=kLoop, calls=%fused_computation.9 | loop fusion | flops 23592960 | bytes 47185920 | tf_op jit(solution)/shard_map/mul | solution.py:81
  773.9 2.9 fusion.11
  777.5 4.1 fusion.15
  (148 shorter events, 49.7 us)
Async XLA Ops:
  7.2 318.2 %all-gather.3.cloned.1.call-start = ((), (), s32[]{:S(2)}) async-start(), calls=%async_computation.3 | async-start | bytes 10485760 | tf_op jit(solution)/shard_map/all_gather | solution.py:1447
  175.5 201.7 %all-gather.5.cloned.1.call-start = ((), (), s32[]{:S(2)}) async-start(), calls=%async_computation.4 | async-start | bytes 2621440 | tf_op jit(solution)/shard_map/all_gather | solution.py:1452
  175.6 70.3 %collective-permute-start.5 = (bf16[320,2048]{1,0:T(8,128)(2,1)}, bf16[320,2048]{1,0:T(8,128)(2,1)}, u32[]{:S(2)}, u32[]{:S(2)}) collective-permute-start(bf16[320,2048]{1,0:T(8,128)(2,1)} %bitcast.9), channel_id=1, source_target_pairs={{0,6},{1,7},{2,4},{3,5},{4,2},{5,3},{6,0},{7,1},{8,14},{9,15},{10,... | collective-permute-start | bytes 3932168 | tf_op jit(solution)/shard_map/ppermute | solution.py:1062
  175.8 68.1 %collective-permute-start.3 = (bf16[320,2048]{1,0:T(8,128)(2,1)}, bf16[320,2048]{1,0:T(8,128)(2,1)}, u32[]{:S(2)}, u32[]{:S(2)}) collective-permute-start(bf16[320,2048]{1,0:T(8,128)(2,1)} %bitcast.9), channel_id=1, source_target_pairs={{0,4},{1,5},{2,6},{3,7},{4,0},{5,1},{6,2},{7,3},{8,12},{9,13},{10,... | collective-permute-start | bytes 3932168 | tf_op jit(solution)/shard_map/ppermute | solution.py:1062
  176.6 66.9 %collective-permute-start.1 = (bf16[320,2048]{1,0:T(8,128)(2,1)}, bf16[320,2048]{1,0:T(8,128)(2,1)}, u32[]{:S(2)}, u32[]{:S(2)}) collective-permute-start(bf16[320,2048]{1,0:T(8,128)(2,1)} %bitcast.9), channel_id=1, source_target_pairs={{0,2},{1,3},{2,0},{3,1},{4,6},{5,7},{6,4},{7,5},{8,10},{9,11},{10,... | collective-permute-start | bytes 3932168 | tf_op jit(solution)/shard_map/ppermute | solution.py:1062
  178.3 67.7 %collective-permute-start = (bf16[320,2048]{1,0:T(8,128)(2,1)}, bf16[320,2048]{1,0:T(8,128)(2,1)}, u32[]{:S(2)}, u32[]{:S(2)}) collective-permute-start(bf16[320,2048]{1,0:T(8,128)(2,1)} %bitcast.9), channel_id=1, source_target_pairs={{0,1},{1,0},{2,3},{3,2},{4,5},{5,4},{6,7},{7,6},{8,9},{9,8},{10,11... | collective-permute-start | bytes 3932168 | tf_op jit(solution)/shard_map/ppermute | solution.py:1062
  243.4 5.5 collective-permute-start.2
  243.9 6.7 collective-permute-start.4
  245.9 6.3 collective-permute-start.6
  252.3 67.1 %copy-start.4 = (bf16[2560,2048]{1,0:T(8,128)(2,1)}, bf16[2560,2048]{1,0:T(8,128)(2,1)S(1)}, u32[]{:S(2)}) copy-start(bf16[2560,2048]{1,0:T(8,128)(2,1)S(1)} %constant_dynamic-update-slice_fusion.grad_ref) | copy-start | bytes 31457284
  252.3 30.0 %collective-permute-start.8 = (bf16[320,2048]{1,0:T(8,128)(2,1)S(1)}, bf16[320,2048]{1,0:T(8,128)(2,1)S(1)}, u32[]{:S(2)}, u32[]{:S(2)}) collective-permute-start(bf16[320,2048]{1,0:T(8,128)(2,1)S(1)} %multiply_convert_fusion), channel_id=1, source_target_pairs={{0,2},{1,3},{2,0},{3,1},{4,6},{5,7},{6,4},{7,5},{8,10},{9,11},{10,... | collective-permute-start | bytes 3932168 | tf_op jit(solution)/shard_map/ppermute | solution.py:1062
  252.7 31.8 %collective-permute-start.10 = (bf16[320,2048]{1,0:T(8,128)(2,1)S(1)}, bf16[320,2048]{1,0:T(8,128)(2,1)S(1)}, u32[]{:S(2)}, u32[]{:S(2)}) collective-permute-start(bf16[320,2048]{1,0:T(8,128)(2,1)S(1)} %multiply_convert_fusion), channel_id=1, source_target_pairs={{0,4},{1,5},{2,6},{3,7},{4,0},{5,1},{6,2},{7,3},{8,12},{9,13},{10,... | collective-permute-start | bytes 3932168 | tf_op jit(solution)/shard_map/ppermute | solution.py:1062
  253.7 59.5 %collective-permute-start.12 = (bf16[320,2048]{1,0:T(8,128)(2,1)S(1)}, bf16[320,2048]{1,0:T(8,128)(2,1)S(1)}, u32[]{:S(2)}, u32[]{:S(2)}) collective-permute-start(bf16[320,2048]{1,0:T(8,128)(2,1)S(1)} %multiply_convert_fusion), channel_id=1, source_target_pairs={{0,6},{1,7},{2,4},{3,5},{4,2},{5,3},{6,0},{7,1},{8,14},{9,15},{10,... | collective-permute-start | bytes 3932168 | tf_op jit(solution)/shard_map/ppermute | solution.py:1062
  255.1 58.2 %collective-permute-start.7 = (bf16[320,2048]{1,0:T(8,128)(2,1)S(1)}, bf16[320,2048]{1,0:T(8,128)(2,1)S(1)}, u32[]{:S(2)}, u32[]{:S(2)}) collective-permute-start(bf16[320,2048]{1,0:T(8,128)(2,1)S(1)} %multiply_convert_fusion), channel_id=1, source_target_pairs={{0,1},{1,0},{2,3},{3,2},{4,5},{5,4},{6,7},{7,6},{8,9},{9,8},{10,11... | collective-permute-start | bytes 3932168 | tf_op jit(solution)/shard_map/ppermute | solution.py:1062
  282.3 33.4 %collective-permute-start.9 = (bf16[320,2048]{1,0:T(8,128)(2,1)S(1)}, bf16[320,2048]{1,0:T(8,128)(2,1)S(1)}, u32[]{:S(2)}, u32[]{:S(2)}) collective-permute-start(bf16[320,2048]{1,0:T(8,128)(2,1)S(1)} %collective-permute-done.8), channel_id=1, source_target_pairs={{0,1},{1,0},{2,3},{3,2},{4,5},{5,4},{6,7},{7,6},{8,9},{9,8},{10,11... | collective-permute-start | bytes 3932168 | tf_op jit(solution)/shard_map/ppermute | solution.py:1062
  284.5 33.7 %collective-permute-start.11 = (bf16[320,2048]{1,0:T(8,128)(2,1)S(1)}, bf16[320,2048]{1,0:T(8,128)(2,1)S(1)}, u32[]{:S(2)}, u32[]{:S(2)}) collective-permute-start(bf16[320,2048]{1,0:T(8,128)(2,1)S(1)} %collective-permute-done.10), channel_id=1, source_target_pairs={{0,1},{1,0},{2,3},{3,2},{4,5},{5,4},{6,7},{7,6},{8,9},{9,8},{10,11... | collective-permute-start | bytes 3932168 | tf_op jit(solution)/shard_map/ppermute | solution.py:1062
  313.2 7.4 collective-permute-start.13
  325.4 129.9 %reduce-scatter.4.cloned.1.call-start = ((), (), s32[]{:S(2)}) async-start(), calls=%async_computation.5 | async-start | bytes 5242880 | tf_op jit(solution)/shard_map/reduce_scatter | solution.py:1072
  377.2 225.9 %reduce-scatter.6.cloned.1.call-start = ((), (), s32[]{:S(2)}) async-start(), calls=%async_computation.6 | async-start | bytes 10485760 | tf_op jit(solution)/shard_map/reduce_scatter | solution.py:1072
  455.3 318.6 %reduce-scatter.8.cloned.1.call-start = ((), (), s32[]{:S(2)}) async-start(), calls=%async_computation.7 | async-start | bytes 5242880 | tf_op jit(solution)/shard_map/reduce_scatter | solution.py:1072
  519.8 13.9 %collective-permute-start.17 = (bf16[320,2048]{1,0:T(8,128)(2,1)S(1)}, bf16[320,2048]{1,0:T(8,128)(2,1)S(1)}, u32[]{:S(2)}, u32[]{:S(2)}) collective-permute-start(bf16[320,2048]{1,0:T(8,128)(2,1)S(1)} %get-tuple-element.160), channel_id=1, source_target_pairs={{0,1},{1,0},{2,3},{3,2},{4,5},{5,4},{6,7},{7,6},{8,9},{9,8},{10,11... | collective-permute-start | bytes 3932168 | tf_op jit(solution)/shard_map/ppermute | solution.py:1062
  520.8 13.0 %collective-permute-start.16 = (bf16[320,2048]{1,0:T(8,128)(2,1)S(1)}, bf16[320,2048]{1,0:T(8,128)(2,1)S(1)}, u32[]{:S(2)}, u32[]{:S(2)}) collective-permute-start(bf16[320,2048]{1,0:T(8,128)(2,1)S(1)} %get-tuple-element.161), channel_id=1, source_target_pairs={{0,1},{1,0},{2,3},{3,2},{4,5},{5,4},{6,7},{7,6},{8,9},{9,8},{10,11... | collective-permute-start | bytes 3932168 | tf_op jit(solution)/shard_map/ppermute | solution.py:1062
  520.8 12.9 %collective-permute-start.15 = (bf16[320,2048]{1,0:T(8,128)(2,1)S(1)}, bf16[320,2048]{1,0:T(8,128)(2,1)S(1)}, u32[]{:S(2)}, u32[]{:S(2)}) collective-permute-start(bf16[320,2048]{1,0:T(8,128)(2,1)S(1)} %get-tuple-element.162), channel_id=1, source_target_pairs={{0,1},{1,0},{2,3},{3,2},{4,5},{5,4},{6,7},{7,6},{8,9},{9,8},{10,11... | collective-permute-start | bytes 3932168 | tf_op jit(solution)/shard_map/ppermute | solution.py:1062
  521.3 12.5 %collective-permute-start.14 = (bf16[320,2048]{1,0:T(8,128)(2,1)S(1)}, bf16[320,2048]{1,0:T(8,128)(2,1)}, u32[]{:S(2)}, u32[]{:S(2)}) collective-permute-start(bf16[320,2048]{1,0:T(8,128)(2,1)S(1)} %get-tuple-element.163), channel_id=1, source_target_pairs={{0,1},{1,0},{2,3},{3,2},{4,5},{5,4},{6,7},{7,6},{8,9},{9,8},{10,11... | collective-permute-start | bytes 3932168 | tf_op jit(solution)/shard_map/ppermute | solution.py:1062
  539.3 63.9 %collective-permute-start.18 = (bf16[320,2048]{1,0:T(8,128)(2,1)}, bf16[320,2048]{1,0:T(8,128)(2,1)}, u32[]{:S(2)}, u32[]{:S(2)}) collective-permute-start(bf16[320,2048]{1,0:T(8,128)(2,1)} %get-tuple-element.114), channel_id=1, source_target_pairs={{0,2},{1,3},{2,0},{3,1},{4,6},{5,7},{6,4},{7,5},{8,10},{9,11},{10,... | collective-permute-start | bytes 3932168 | tf_op jit(solution)/shard_map/ppermute | solution.py:1062
  540.4 62.7 %collective-permute-start.19 = (bf16[320,2048]{1,0:T(8,128)(2,1)}, bf16[320,2048]{1,0:T(8,128)(2,1)}, u32[]{:S(2)}, u32[]{:S(2)}) collective-permute-start(bf16[320,2048]{1,0:T(8,128)(2,1)} %get-tuple-element.115), channel_id=1, source_target_pairs={{0,4},{1,5},{2,6},{3,7},{4,0},{5,1},{6,2},{7,3},{8,12},{9,13},{10,... | collective-permute-start | bytes 3932168 | tf_op jit(solution)/shard_map/ppermute | solution.py:1062
  540.4 62.7 %collective-permute-start.20 = (bf16[320,2048]{1,0:T(8,128)(2,1)}, bf16[320,2048]{1,0:T(8,128)(2,1)}, u32[]{:S(2)}, u32[]{:S(2)}) collective-permute-start(bf16[320,2048]{1,0:T(8,128)(2,1)} %get-tuple-element.116), channel_id=1, source_target_pairs={{0,6},{1,7},{2,4},{3,5},{4,2},{5,3},{6,0},{7,1},{8,14},{9,15},{10,... | collective-permute-start | bytes 3932168 | tf_op jit(solution)/shard_map/ppermute | solution.py:1062
  608.6 145.2 %copy-start.12 = (f32[64,2048]{1,0:T(8,128)S(1)}, f32[64,2048]{1,0:T(8,128)}, u32[]{:S(2)}) copy-start(f32[64,2048]{1,0:T(8,128)} %param.26) | copy-start | bytes 1572868
  608.6 145.2 %copy-start.15 = (f32[64,2048]{1,0:T(8,128)S(1)}, f32[64,2048]{1,0:T(8,128)}, u32[]{:S(2)}) copy-start(f32[64,2048]{1,0:T(8,128)} %param.27) | copy-start | bytes 1572868
  753.8 23.0 %copy-start.18 = (f32[2,64]{1,0:T(2,128)}, f32[2,64]{1,0:T(2,128)S(1)}, u32[]{:S(2)}) copy-start(f32[2,64]{1,0:T(2,128)S(1)} %slice.69) | copy-start | bytes 1540
  760.0 13.9 %copy-start.2 = (bf16[1,1,320,2048]{3,2,1,0:T(8,128)(2,1)S(1)}, bf16[1,1,320,2048]{3,2,1,0:T(8,128)(2,1)}, u32[]{:S(2)}) copy-start(bf16[1,1,320,2048]{3,2,1,0:T(8,128)(2,1)} %param.16) | copy-start | bytes 3932164
  760.0 13.9 %copy-start.16 = (f32[2048]{0:T(1024)S(1)}, f32[2048]{0:T(1024)}, u32[]{:S(2)}) copy-start(f32[2048]{0:T(1024)} %get-tuple-element.140) | copy-start | bytes 24580
  (16 other events, 72.4 us)
Sparse Core Ops, SparseCore 0:
  175.6 149.6 all-gather.2
  326.9 45.1 all-gather.4
  377.3 77.8 reduce-scatter.3
  457.6 144.6 reduce-scatter.5
  604.5 93.2 reduce-scatter.7
